TPU v7x, 32 devices: a whole 2x2x4 slice. The times are simulated.
32 devices in a mesh: wide: 8 (over z, x), narrow: 4 (over y, core).
Axes of the slice: x: 2, y: 2, z: 4, core: 2. Of those that a mesh axis runs over, the one named last changes fastest.
Arguments:
- token_ids: int32 [8, 2, 1024], P('wide'), may hold values from 0 to 50686
- mask_slots: int32 [8, 2, 256], P('wide'), may hold values from 0 to 1023, as said below
- mask_counts: int32 [8, 2], P('wide'), may hold values from 64 to 256, as said below
- embedding: float32 [50688, 768], P('narrow', 'wide'), may hold values from -6 to 6
- out_table: float32 [768, 50688], P('wide', 'narrow')
- qkv_weight: float32 [3, 768, 768], P(None, 'wide', 'narrow'), may hold values from -0.21875 to 0.21875
- proj_weight: float32 [768, 768], P('narrow', 'wide'), may hold values from -1.75 to 1.75
- up_weight: float32 [768, 3072], P('wide', 'narrow'), may hold values from -0.21875 to 0.21875
- down_weight: float32 [3072, 768], P('narrow', 'wide'), may hold values from -0.109375 to 0.109375
- mod_weight: float32 [128, 6144], P(None, 'wide'), may hold values from -0.5 to 0.5
- vectors: float32 [9216], P('wide')
- embedding_first: float32 [50688, 768], P('narrow', 'wide'), may hold values from -3.5762787e-07 to 3.5762787e-07
- out_table_first: float32 [768, 50688], P('wide', 'narrow'), may hold values from -3.5762787e-07 to 3.5762787e-07
- qkv_first: float32 [3, 768, 768], P(None, 'wide', 'narrow'), may hold values from -3.5762787e-07 to 3.5762787e-07
- proj_first: float32 [768, 768], P('narrow', 'wide'), may hold values from -3.5762787e-07 to 3.5762787e-07
- up_first: float32 [768, 3072], P('wide', 'narrow'), may hold values from -3.5762787e-07 to 3.5762787e-07
- down_first: float32 [3072, 768], P('narrow', 'wide'), may hold values from -3.5762787e-07 to 3.5762787e-07
- mod_first: float32 [128, 6144], P(None, 'wide'), may hold values from -3.5762787e-07 to 3.5762787e-07
- vectors_first: float32 [9216], P('wide'), may hold values from -3.8146973e-06 to 3.8146973e-06
- embedding_second: float32 [50688, 768], P('narrow', 'wide'), may hold values from 1.53388e-14 to 6.13552e-14
- out_table_second: float32 [768, 50688], P('wide', 'narrow'), may hold values from 1.53388e-14 to 6.13552e-14
- qkv_second: float32 [3, 768, 768], P(None, 'wide', 'narrow'), may hold values from 1.53388e-14 to 6.13552e-14
- proj_second: float32 [768, 768], P('narrow', 'wide'), may hold values from 1.53388e-14 to 6.13552e-14
- up_second: float32 [768, 3072], P('wide', 'narrow'), may hold values from 1.53388e-14 to 6.13552e-14
- down_second: float32 [3072, 768], P('narrow', 'wide'), may hold values from 1.53388e-14 to 6.13552e-14
- mod_second: float32 [128, 6144], P(None, 'wide'), may hold values from 1.53388e-14 to 6.13552e-14
- vectors_second: float32 [9216], P('wide'), may hold values from 1.53388e-12 to 6.13552e-12
Outputs:
- loss_sum: float32 [], replicated
- grad_norm: float32 [], replicated
- embedding_next: float32 [50688, 768], P('narrow', 'wide')
- embedding_first_next: float32 [50688, 768], P('narrow', 'wide')
- embedding_second_next: float32 [50688, 768], P('narrow', 'wide')
- out_table_next: float32 [768, 50688], P('wide', 'narrow')
- out_table_first_next: float32 [768, 50688], P('wide', 'narrow')
- out_table_second_next: float32 [768, 50688], P('wide', 'narrow')
- qkv_next: float32 [3, 768, 768], P(None, 'wide', 'narrow')
- qkv_first_next: float32 [3, 768, 768], P(None, 'wide', 'narrow')
- qkv_second_next: float32 [3, 768, 768], P(None, 'wide', 'narrow')
- proj_next: float32 [768, 768], P('narrow', 'wide')
- proj_first_next: float32 [768, 768], P('narrow', 'wide')
- proj_second_next: float32 [768, 768], P('narrow', 'wide')
- up_next: float32 [768, 3072], P('wide', 'narrow')
- up_first_next: float32 [768, 3072], P('wide', 'narrow')
- up_second_next: float32 [768, 3072], P('wide', 'narrow')
- down_next: float32 [3072, 768], P('narrow', 'wide')
- down_first_next: float32 [3072, 768], P('narrow', 'wide')
- down_second_next: float32 [3072, 768], P('narrow', 'wide')
- mod_next: float32 [128, 6144], P(None, 'wide')
- mod_first_next: float32 [128, 6144], P(None, 'wide')
- mod_second_next: float32 [128, 6144], P(None, 'wide')
- vectors_next: float32 [9216], P('wide')
- vectors_first_next: float32 [9216], P('wide')
- vectors_second_next: float32 [9216], P('wide')
Inputs may be any that keep to these rules, and one draw needn't show every extreme that they name: `mask_counts`: in each micro-batch, the counts of rows w and w + 4 sum to 320; row 4 holds 256 in every micro-batch. `mask_slots`: the 256 positions of one sequence are distinct.
All inputs are finite; a program needn't handle non-finite values.
Results may differ from a plain program's by a relative error of at most 0.012.
The roundings to bfloat16 on the way count: a program that leaves them out, or rounds other values in their place, can miss the bound.
Values may be sent and summed in bfloat16 or wider, within the bound.
No kernel may reach another device: no remote copies, remote signals or barrier semaphores. Data moves between devices by JAX's collectives and lax.ppermute only.
A program may use at most 448 MiB of HBM per device.

v0:
```python
import math

import jax
import jax.numpy as jnp
from jax import lax
from jax.sharding import PartitionSpec as P

HD = 64
STEP = 10


HIGHEST = lax.Precision.HIGHEST
NORM_EPS = 1e-06
CLIP_NORM = 0.005
BETA_ONE = 0.9
BETA_TWO = 0.95
ADAM_EPS = 1e-08
WEIGHT_DECAY = 0.1
LEARN_RATES = (1.0, 0.1, 0.07, 0.5, 0.07, 0.04, 0.2, 0.5)


def combined_all(value, axis, join):
    pieces = jax.tree.map(lambda part: lax.all_gather(part, axis), value)
    head = jax.tree.map(lambda part: part[0], pieces)
    tail = jax.tree.map(lambda part: part[1:], pieces)
    so_far, _ = lax.scan(lambda so_far, piece: (join(so_far, piece), None), head, tail)
    return so_far


def layer_norm(values):
    centered = values - jnp.mean(values, axis=-1, keepdims=True)
    inverse = lax.rsqrt(jnp.mean(centered * centered, axis=-1, keepdims=True) + NORM_EPS)
    return (centered * inverse, inverse)


def norm_back(grad, normed, inverse):
    return inverse * (
        grad
        - jnp.mean(grad, axis=-1, keepdims=True)
        - normed * jnp.mean(grad * normed, axis=-1, keepdims=True)
    )


def gelu_tanh(values):
    inner = 0.7978845608 * (values + 0.044715 * values * values * values)
    return 0.5 * values * (1.0 + jnp.tanh(inner))


def gelu_slope(values):
    tangent = jnp.tanh(0.7978845608 * (values + 0.044715 * values * values * values))
    return 0.5 * (1.0 + tangent) + 0.5 * values * (1.0 - tangent * tangent) * 0.7978845608 * (
        1.0 + 0.134145 * values * values
    )


def rotary_tables(length, width):
    freqs = jnp.exp(jnp.arange(width // 2, dtype=jnp.float32) * (-2.0 * math.log(10000.0) / width))
    angle = jnp.arange(length, dtype=jnp.float32)[:, None] * freqs[None, :]
    return (jnp.cos(angle), jnp.sin(angle))


def rotate(values, cosine, sine):
    middle = values.shape[-1] // 2
    first = values[..., :middle]
    second = values[..., middle:]
    return jnp.concatenate(
        [first * cosine - second * sine, second * cosine + first * sine], axis=-1
    )


def time_features(moment, width):
    freqs = jnp.exp(jnp.arange(width // 2, dtype=jnp.float32) * (-math.log(10000.0) / (width // 2)))
    angle = 1000.0 * moment * freqs
    return jnp.concatenate([jnp.cos(angle), jnp.sin(angle)])


def attention_forward(query, keys, values):
    length, heads, head_size = query.shape
    block = min(512, length)
    scale = head_size ** (-0.5)

    def one_block(query_block):
        scores = (
            jnp.einsum("qhe,khe->hqk", query_block, keys, preferred_element_type=jnp.float32)
            * scale
        )
        top = jnp.max(scores, axis=-1, keepdims=True)
        shifted = jnp.exp(scores - top)
        total = jnp.sum(shifted, axis=-1, keepdims=True)
        weights = (shifted / total).astype(jnp.bfloat16)
        mixed = jnp.einsum("hqk,khe->qhe", weights, values, preferred_element_type=jnp.float32)
        return (mixed, (top + jnp.log(total))[..., 0])

    mixed, log_totals = lax.map(one_block, query.reshape(length // block, block, heads, head_size))
    return (mixed.reshape(length, heads, head_size), log_totals)


def attention_backward(query, keys, values, d_mixed, log_totals):
    length, heads, head_size = query.shape
    block = min(512, length)
    scale = head_size ** (-0.5)

    def one_block(carry, item):
        key_grad, value_grad = carry
        query_block, grad_block, total_block = item
        scores = (
            jnp.einsum("qhe,khe->hqk", query_block, keys, preferred_element_type=jnp.float32)
            * scale
        )
        weights = jnp.exp(scores - total_block[..., None])
        d_weights = jnp.einsum(
            "qhe,khe->hqk", grad_block, values, preferred_element_type=jnp.float32
        )
        delta = jnp.sum(weights * d_weights, axis=-1, keepdims=True)
        d_scores = (weights * (d_weights - delta)).astype(jnp.bfloat16)
        query_grad = (
            jnp.einsum("hqk,khe->qhe", d_scores, keys, preferred_element_type=jnp.float32) * scale
        )
        key_grad = (
            key_grad
            + jnp.einsum("hqk,qhe->khe", d_scores, query_block, preferred_element_type=jnp.float32)
            * scale
        )
        value_grad = value_grad + jnp.einsum(
            "hqk,qhe->khe",
            weights.astype(jnp.bfloat16),
            grad_block,
            preferred_element_type=jnp.float32,
        )
        return ((key_grad, value_grad), query_grad)

    zeros = jnp.zeros((length, heads, head_size), jnp.float32)
    blocks = length // block
    (key_grad, value_grad), query_grad = lax.scan(
        one_block,
        (zeros, zeros),
        (
            query.reshape(blocks, block, heads, head_size),
            d_mixed.reshape(blocks, block, heads, head_size),
            log_totals,
        ),
    )
    return (query_grad.reshape(length, heads, head_size), key_grad, value_grad)


def layer_forward(
    start, modulation, vector_full, qkv_copy, proj_copy, up_copy, down_copy, cosine, sine
):
    length, width = start.shape
    shift_one, scale_one, gate_one, shift_two, scale_two, gate_two = jnp.split(
        modulation[: 6 * width], 6
    )
    gain_one, gain_two, gain_last, bias_down = jnp.split(vector_full[: 4 * width], 4)
    normed_one, inverse_one = layer_norm(start)
    hidden_one = (normed_one * gain_one * (1.0 + scale_one) + shift_one).astype(jnp.bfloat16)
    projected = jnp.einsum("rd,kde->kre", hidden_one, qkv_copy, preferred_element_type=jnp.float32)
    heads = projected.shape[2] // HD
    projected = projected.reshape(3, length, heads, HD)
    cos_rows = cosine[:, None, :]
    sin_rows = sine[:, None, :]
    query = rotate(projected[0], cos_rows, sin_rows).astype(jnp.bfloat16)
    keys = rotate(projected[1], cos_rows, sin_rows).astype(jnp.bfloat16)
    values = projected[2].astype(jnp.bfloat16)
    mixed, log_totals = attention_forward(query, keys, values)
    mixed = mixed.reshape(length, heads * HD).astype(jnp.bfloat16)
    attended = lax.psum(jnp.dot(mixed, proj_copy, preferred_element_type=jnp.float32), "narrow")
    middle = start + gate_one * attended
    normed_two, inverse_two = layer_norm(middle)
    hidden_two = (normed_two * gain_two * (1.0 + scale_two) + shift_two).astype(jnp.bfloat16)
    inner = jnp.dot(hidden_two, up_copy, preferred_element_type=jnp.float32)
    active = gelu_tanh(inner).astype(jnp.bfloat16)
    output = lax.psum(jnp.dot(active, down_copy, preferred_element_type=jnp.float32), "narrow")
    final = middle + gate_two * (output + bias_down)
    saved = (
        normed_one,
        inverse_one,
        hidden_one,
        query,
        keys,
        values,
        mixed,
        log_totals,
        attended,
        normed_two,
        inverse_two,
        hidden_two,
        inner,
        active,
        output,
    )
    return (final, saved)


def layer_backward(
    d_final, saved, modulation, vector_full, qkv_copy, proj_copy, up_copy, down_copy, cosine, sine
):
    (
        normed_one,
        inverse_one,
        hidden_one,
        query,
        keys,
        values,
        mixed,
        log_totals,
        attended,
        normed_two,
        inverse_two,
        hidden_two,
        inner,
        active,
        output,
    ) = saved
    length, width = d_final.shape
    shift_one, scale_one, gate_one, shift_two, scale_two, gate_two = jnp.split(
        modulation[: 6 * width], 6
    )
    gain_one, gain_two, gain_last, bias_down = jnp.split(vector_full[: 4 * width], 4)
    d_bias = jnp.sum(d_final, axis=0) * gate_two
    d_gate_two = jnp.sum(d_final * (output + bias_down), axis=0)
    d_output = (d_final * gate_two).astype(jnp.bfloat16)
    d_down = jnp.einsum("rf,rd->fd", active, d_output, preferred_element_type=jnp.float32)
    d_active = jnp.einsum("rd,fd->rf", d_output, down_copy, preferred_element_type=jnp.float32)
    d_inner = (d_active * gelu_slope(inner)).astype(jnp.bfloat16)
    d_up = jnp.einsum("rd,rf->df", hidden_two, d_inner, preferred_element_type=jnp.float32)
    d_hidden_two = lax.psum(
        jnp.einsum("rf,df->rd", d_inner, up_copy, preferred_element_type=jnp.float32).astype(
            jnp.bfloat16
        ),
        "narrow",
    ).astype(jnp.float32)
    d_shift_two = jnp.sum(d_hidden_two, axis=0)
    d_scale_two = jnp.sum(d_hidden_two * normed_two * gain_two, axis=0)
    d_gain_two = jnp.sum(d_hidden_two * normed_two * (1.0 + scale_two), axis=0)
    d_middle = d_final + norm_back(
        d_hidden_two * gain_two * (1.0 + scale_two), normed_two, inverse_two
    )
    d_gate_one = jnp.sum(d_middle * attended, axis=0)
    d_attended = (d_middle * gate_one).astype(jnp.bfloat16)
    d_proj = jnp.einsum("rw,rd->wd", mixed, d_attended, preferred_element_type=jnp.float32)
    heads = query.shape[1]
    d_mixed = (
        jnp.einsum("rd,wd->rw", d_attended, proj_copy, preferred_element_type=jnp.float32)
        .astype(jnp.bfloat16)
        .reshape(length, heads, HD)
    )
    d_query, d_keys, d_values = attention_backward(query, keys, values, d_mixed, log_totals)
    cos_rows = cosine[:, None, :]
    sin_rows = sine[:, None, :]
    d_projected = (
        jnp.stack(
            [rotate(d_query, cos_rows, -sin_rows), rotate(d_keys, cos_rows, -sin_rows), d_values]
        )
        .reshape(3, length, heads * HD)
        .astype(jnp.bfloat16)
    )
    d_qkv = jnp.einsum("rd,kre->kde", hidden_one, d_projected, preferred_element_type=jnp.float32)
    d_hidden_one = lax.psum(
        jnp.einsum("kre,kde->rd", d_projected, qkv_copy, preferred_element_type=jnp.float32).astype(
            jnp.bfloat16
        ),
        "narrow",
    ).astype(jnp.float32)
    d_shift_one = jnp.sum(d_hidden_one, axis=0)
    d_scale_one = jnp.sum(d_hidden_one * normed_one * gain_one, axis=0)
    d_gain_one = jnp.sum(d_hidden_one * normed_one * (1.0 + scale_one), axis=0)
    d_start = d_middle + norm_back(
        d_hidden_one * gain_one * (1.0 + scale_one), normed_one, inverse_one
    )
    return (
        d_start,
        (d_qkv, d_proj, d_up, d_down),
        (d_gain_one, d_gain_two, d_bias),
        (d_shift_one, d_scale_one, d_gate_one, d_shift_two, d_scale_two, d_gate_two),
    )


def head_loss(row_block, targets, valid, table_copy, offset, loss_scale):
    vocab_local = table_copy.shape[1]
    logits = jnp.dot(row_block, table_copy, preferred_element_type=jnp.float32)
    local_targets = targets - offset
    hitting = jnp.arange(vocab_local)[None, :] == local_targets[:, None]
    top = jnp.max(logits, axis=-1)
    total = jnp.sum(jnp.exp(logits - top[:, None]), axis=-1)
    target_logit = jnp.sum(jnp.where(hitting, logits, 0.0), axis=-1)

    def combine(first, second):
        highest = jnp.maximum(first[0], second[0])
        summed = first[1] * jnp.exp(first[0] - highest) + second[1] * jnp.exp(second[0] - highest)
        return (highest, summed, first[2] + second[2])

    top_all, total_all, target_all = combined_all((top, total, target_logit), "narrow", combine)
    log_total = top_all + jnp.log(total_all)
    loss_part = jnp.sum(jnp.where(valid, log_total - target_all, 0.0))
    weight_rows = valid.astype(jnp.float32) * loss_scale
    d_logits = (
        (jnp.exp(logits - log_total[:, None]) - hitting.astype(jnp.float32)) * weight_rows[:, None]
    ).astype(jnp.bfloat16)
    d_table = jnp.einsum("nd,nv->dv", row_block, d_logits, preferred_element_type=jnp.float32)
    d_rows = lax.psum(
        jnp.einsum("nv,dv->nd", d_logits, table_copy, preferred_element_type=jnp.float32), "narrow"
    )
    return (loss_part, d_rows, d_table)


def reduce_wide(grads):
    return (
        lax.psum_scatter(grads[0], "wide", scatter_dimension=1, tiled=True),
        lax.psum_scatter(grads[1], "wide", scatter_dimension=0, tiled=True),
        lax.psum_scatter(grads[2], "wide", scatter_dimension=1, tiled=True),
        lax.psum_scatter(grads[3], "wide", scatter_dimension=1, tiled=True),
        lax.psum_scatter(grads[4], "wide", scatter_dimension=0, tiled=True),
        lax.psum_scatter(grads[5], "wide", scatter_dimension=1, tiled=True),
        lax.psum_scatter(grads[6], "wide", scatter_dimension=1, tiled=True),
        lax.psum_scatter(grads[7], "wide", scatter_dimension=0, tiled=True),
    )


def local(
    token_ids,
    mask_slots,
    mask_counts,
    embedding,
    out_table,
    qkv_weight,
    proj_weight,
    up_weight,
    down_weight,
    mod_weight,
    vectors,
    embedding_first,
    out_table_first,
    qkv_first,
    proj_first,
    up_first,
    down_first,
    mod_first,
    vectors_first,
    embedding_second,
    out_table_second,
    qkv_second,
    proj_second,
    up_second,
    down_second,
    mod_second,
    vectors_second,
):
    masters = (
        embedding,
        out_table,
        qkv_weight,
        proj_weight,
        up_weight,
        down_weight,
        mod_weight,
        vectors,
    )
    firsts = (
        embedding_first,
        out_table_first,
        qkv_first,
        proj_first,
        up_first,
        down_first,
        mod_first,
        vectors_first,
    )
    seconds = (
        embedding_second,
        out_table_second,
        qkv_second,
        proj_second,
        up_second,
        down_second,
        mod_second,
        vectors_second,
    )
    copies = (
        lax.all_gather(embedding.astype(jnp.bfloat16), "wide", axis=1, tiled=True),
        lax.all_gather(out_table.astype(jnp.bfloat16), "wide", axis=0, tiled=True),
        lax.all_gather(qkv_weight.astype(jnp.bfloat16), "wide", axis=1, tiled=True),
        lax.all_gather(proj_weight.astype(jnp.bfloat16), "wide", axis=1, tiled=True),
        lax.all_gather(up_weight.astype(jnp.bfloat16), "wide", axis=0, tiled=True),
        lax.all_gather(down_weight.astype(jnp.bfloat16), "wide", axis=1, tiled=True),
        lax.all_gather(mod_weight.astype(jnp.bfloat16), "wide", axis=1, tiled=True),
        lax.all_gather(vectors.astype(jnp.bfloat16), "wide", axis=0, tiled=True),
    )
    embed_copy, table_copy, qkv_copy, proj_copy, up_copy, down_copy, mod_copy, vector_copy = copies
    mod_full = mod_copy.astype(jnp.float32)
    vector_full = vector_copy.astype(jnp.float32)
    narrow_count = lax.axis_size("narrow")
    wide_count = lax.axis_size("wide")
    vocab_local = embed_copy.shape[0]
    offset = lax.axis_index("narrow") * vocab_local
    length = token_ids.shape[2]
    capacity = mask_slots.shape[2]
    micro_count = token_ids.shape[1]
    width = embed_copy.shape[1]
    cosine, sine = rotary_tables(length, HD)
    loss_scale = 1.0 / (length * micro_count * wide_count)
    pair_total = 5 * length // 16
    gain_last = vector_full[2 * width : 3 * width]
    summed_grads = None
    shards = None
    loss_local = jnp.zeros((), jnp.float32)
    for micro in range(micro_count):
        token_row = token_ids[0, micro]
        slot_row = mask_slots[0, micro]
        mask_count = mask_counts[0, micro]
        valid = jnp.arange(capacity) < mask_count
        masked = jnp.zeros((length,), jnp.int32).at[slot_row].set(valid.astype(jnp.int32))
        inputs = jnp.where(masked > 0, vocab_local * narrow_count - 1, token_row)
        local_ids = inputs - offset
        inside = (local_ids >= 0) & (local_ids < vocab_local)
        looked = jnp.where(
            inside[:, None],
            embed_copy[jnp.clip(local_ids, 0, vocab_local - 1)].astype(jnp.float32),
            0.0,
        )
        start = lax.psum(looked.astype(jnp.bfloat16), "narrow").astype(jnp.float32)
        condition = jax.nn.silu(
            time_features(mask_count.astype(jnp.float32) / pair_total, mod_full.shape[0])
        )
        modulation = jnp.dot(condition, mod_full, precision=HIGHEST) + vector_full[4 * width :]
        final, saved = layer_forward(
            start, modulation, vector_full, qkv_copy, proj_copy, up_copy, down_copy, cosine, sine
        )
        shift_last = modulation[6 * width : 7 * width]
        scale_last = modulation[7 * width :]
        normed, inverse = layer_norm(final)
        lifted = gain_last * (1.0 + scale_last)
        hidden = (normed * lifted + shift_last).astype(jnp.bfloat16)
        picked = hidden[slot_row]
        targets = token_row[slot_row]
        loss_part, d_rows, d_table = head_loss(
            picked, targets, valid, table_copy, offset, loss_scale
        )
        loss_local = loss_local + loss_part
        d_hidden = jnp.zeros((length, width), jnp.float32).at[slot_row].add(d_rows)
        d_shift_last = jnp.sum(d_hidden, axis=0)
        d_scale_last = jnp.sum(d_hidden * normed * gain_last, axis=0)
        d_gain_last = jnp.sum(d_hidden * normed * (1.0 + scale_last), axis=0)
        d_final = norm_back(d_hidden * lifted, normed, inverse)
        d_start, matrix_grads, gain_grads, mod_grads = layer_backward(
            d_final,
            saved,
            modulation,
            vector_full,
            qkv_copy,
            proj_copy,
            up_copy,
            down_copy,
            cosine,
            sine,
        )
        d_embed = jax.ops.segment_sum(
            d_start, jnp.where(inside, local_ids, vocab_local), num_segments=vocab_local
        )
        d_modulation = jnp.concatenate(mod_grads + (d_shift_last, d_scale_last))
        d_mod_weight = condition[:, None] * d_modulation[None, :]
        d_vectors = jnp.concatenate(
            (gain_grads[0], gain_grads[1], d_gain_last, gain_grads[2], d_modulation)
        )
        grads = (
            d_embed,
            d_table,
            matrix_grads[0],
            matrix_grads[1],
            matrix_grads[2],
            matrix_grads[3],
            d_mod_weight,
            d_vectors,
        )
        summed_grads = (
            grads
            if summed_grads is None
            else tuple((older + newer for older, newer in zip(summed_grads, grads)))
        )
    shards = reduce_wide(summed_grads)
    loss_sum = lax.psum(loss_local, "wide")
    split_square = jnp.zeros((), jnp.float32)
    for grad in shards[:6]:
        split_square = split_square + jnp.sum(grad * grad)
    shared_square = jnp.sum(shards[6] * shards[6]) + jnp.sum(shards[7] * shards[7])
    square = lax.psum(split_square + shared_square / narrow_count, ("wide", "narrow"))
    grad_norm = jnp.sqrt(square)
    factor = CLIP_NORM / jnp.maximum(grad_norm, CLIP_NORM)
    results = []
    for member in range(8):
        grad = shards[member] * factor
        first = BETA_ONE * firsts[member] + (1.0 - BETA_ONE) * grad
        second = BETA_TWO * seconds[member] + (1.0 - BETA_TWO) * grad * grad
        stepped = (
            first / (1.0 - BETA_ONE**STEP) / (jnp.sqrt(second / (1.0 - BETA_TWO**STEP)) + ADAM_EPS)
        )
        decay = WEIGHT_DECAY if member < 7 else 0.0
        fresh = masters[member] - LEARN_RATES[member] * (stepped + decay * masters[member])
        results.extend([fresh, first, second])
    return (
        loss_sum,
        grad_norm,
        results[0],
        results[1],
        results[2],
        results[3],
        results[4],
        results[5],
        results[6],
        results[7],
        results[8],
        results[9],
        results[10],
        results[11],
        results[12],
        results[13],
        results[14],
        results[15],
        results[16],
        results[17],
        results[18],
        results[19],
        results[20],
        results[21],
        results[22],
        results[23],
    )


def solution(mesh):
    placed = (
        P("wide", None, None),
        P("wide", None, None),
        P("wide", None),
        P("narrow", "wide"),
        P("wide", "narrow"),
        P(None, "wide", "narrow"),
        P("narrow", "wide"),
        P("wide", "narrow"),
        P("narrow", "wide"),
        P(None, "wide"),
        P("wide"),
        P("narrow", "wide"),
        P("wide", "narrow"),
        P(None, "wide", "narrow"),
        P("narrow", "wide"),
        P("wide", "narrow"),
        P("narrow", "wide"),
        P(None, "wide"),
        P("wide"),
        P("narrow", "wide"),
        P("wide", "narrow"),
        P(None, "wide", "narrow"),
        P("narrow", "wide"),
        P("wide", "narrow"),
        P("narrow", "wide"),
        P(None, "wide"),
        P("wide"),
    )
    return jax.shard_map(
        local,
        mesh=mesh,
        in_specs=placed,
        out_specs=(
            P(),
            P(),
            P("narrow", "wide"),
            P("narrow", "wide"),
            P("narrow", "wide"),
            P("wide", "narrow"),
            P("wide", "narrow"),
            P("wide", "narrow"),
            P(None, "wide", "narrow"),
            P(None, "wide", "narrow"),
            P(None, "wide", "narrow"),
            P("narrow", "wide"),
            P("narrow", "wide"),
            P("narrow", "wide"),
            P("wide", "narrow"),
            P("wide", "narrow"),
            P("wide", "narrow"),
            P("narrow", "wide"),
            P("narrow", "wide"),
            P("narrow", "wide"),
            P(None, "wide"),
            P(None, "wide"),
            P(None, "wide"),
            P("wide"),
            P("wide"),
            P("wide"),
        ),
        check_vma=False,
    )
```

profile of v0, /device:TPU:0, one launch (start us, length us, event | category | flops | bytes accessed | tf_op | source)
XLA Modules:
  0.0 3435.1 jit_solution(9817219246885828774)
XLA Ops:
  20.8 90.4 %all_gather.63 = bf16[3,768,192]{2,0,1:T(4,128)(2,1)S(1)} all-gather(bf16[3,96,192]{2,0,1:T(4,128)(2,1)S(1)} %copy.132), channel_id=1, replica_groups=mesh['wide'=8,'narrow'=4] {'wide'}, dimensions={1}, use_global_device_ids=true | all-gather | bytes 995328 | tf_op jit(solution)/shard_map/all_gather | solution.py:381
  111.2 306.1 %all-gather.19.cloned.1.call-done = bf16[12672,768]{0,1:T(8,128)(2,1)} async-done(((bf16[12672,96]{0,1:T(8,128)(2,1)}), bf16[12672,768]{0,1:T(8,128)(2,1)}) %all-gather.19.cloned.1.call-update) | async-done | bytes 19464208 | tf_op jit(solution)/shard_map/all_gather | solution.py:379
  417.3 26.1 copy.131
  443.4 14.8 gather_fusion.3
  458.2 13.5 gather_fusion
  476.2 30.6 all-gather.6
  507.8 31.5 all_gather.64
  556.2 8.9 while.84
  566.0 8.6 while.82
  582.3 117.0 %all-reduce.19.cloned.1.call-done = (f32[1024,768]{1,0:T(8,128)}, f32[1024,768]{1,0:T(8,128)}) async-done(((f32[1024,768]{1,0:T(8,128)}, f32[1024,768]{1,0:T(8,128)}), (f32[1024,768]{1,0:T(8,128)}, f32[1024,768]{1,0:T(8,128)})) %all-reduce.19.cloned.1.call-update) | async-done | bytes 6291472 | tf_op jit(solution)/shard_map/psum | solution.py:166
  699.3 4.6 fusion.219
  708.7 34.5 %all-gather.23.cloned.1.call-done = bf16[768,768]{1,0:T(8,128)(2,1)} async-done(((bf16[96,768]{1,0:T(8,128)(2,1)}), bf16[768,768]{1,0:T(8,128)(2,1)}) %all-gather.23.cloned.1.call-update) | async-done | bytes 1179664 | tf_op jit(solution)/shard_map/all_gather | solution.py:383
  743.2 4.9 fusion.232
  751.2 34.4 %all-gather.25.cloned.1.call-done = bf16[768,768]{0,1:T(8,128)(2,1)} async-done(((bf16[768,96]{0,1:T(8,128)(2,1)}), bf16[768,768]{0,1:T(8,128)(2,1)}) %all-gather.25.cloned.1.call-update) | async-done | bytes 1179664 | tf_op jit(solution)/shard_map/all_gather | solution.py:384
  785.7 6.0 fusion.201
  805.7 108.4 %all-reduce.17.cloned.1.call-done = (f32[1024,768]{1,0:T(8,128)}, f32[1024,768]{1,0:T(8,128)}) async-done(((f32[1024,768]{1,0:T(8,128)}, f32[1024,768]{1,0:T(8,128)}), (f32[1024,768]{1,0:T(8,128)}, f32[1024,768]{1,0:T(8,128)})) %all-reduce.17.cloned.1.call-update) | async-done | bytes 6291472 | tf_op jit(solution)/shard_map/psum | solution.py:172
  914.1 7.0 fusion.217
  927.7 361.7 %all-gather.27.cloned.1.call-done = bf16[768,12672]{1,0:T(8,128)(2,1)} async-done(((bf16[96,12672]{1,0:T(8,128)(2,1)}), bf16[768,12672]{1,0:T(8,128)(2,1)}) %all-gather.27.cloned.1.call-update) | async-done | bytes 19464208 | tf_op jit(solution)/shard_map/all_gather | solution.py:380
  1289.4 9.6 fusion.228
  1304.5 5.2 all-gather.11
  1310.2 5.1 all-gather.12
  1315.3 5.1 all-gather.10
  1326.9 9.7 fusion.227
  1341.3 5.1 all-gather.8
  1346.4 5.1 all-gather.9
  1351.4 5.1 all-gather.7
  1359.8 15.9 fusion.204
  1375.8 16.0 fusion.203
  1391.8 43.2 %all-reduce.15.cloned.1.call-done = (f32[256,768]{1,0:T(8,128)}, f32[256,768]{1,0:T(8,128)}) async-done(((f32[256,768]{1,0:T(8,128)}, f32[256,768]{1,0:T(8,128)}), (f32[256,768]{1,0:T(8,128)}, f32[256,768]{1,0:T(8,128)})) %all-reduce.15.cloned.1.call-update) | async-done | bytes 1572880 | tf_op jit(solution)/shard_map/psum | solution.py:300
  1435.0 4.7 scatter_custom_fusion.2
  1439.7 5.0 scatter_custom_fusion.3
  1444.8 7.0 multiply_reduce_fusion.6
  1453.1 5.9 fusion.205
  1471.1 68.7 %all-reduce.23.cloned.1.call-done = (bf16[1024,768]{1,0:T(8,128)(2,1)}, bf16[1024,768]{1,0:T(8,128)(2,1)}) async-done(((bf16[1024,768]{1,0:T(8,128)(2,1)}, bf16[1024,768]{1,0:T(8,128)(2,1)}), (bf16[1024,768]{1,0:T(8,128)(2,1)}, bf16[1024,768]{1,0:T(8,128)(2,1)})) %all-reduce.23.cloned.1.call-update) | async-done | bytes 3145744 | tf_op jit(solution)/shard_map/psum | solution.py:226
  1539.8 4.9 multiply_reduce_fusion.7
  1544.8 6.6 multiply_reduce_fusion.15
  1555.1 47.1 %while.87 = (s32[]{:T(128)}, f32[1024,3,64]{0,2,1:T(8,128)}, f32[1024,3,64]{0,2,1:T(8,128)}, f32[2,512,3,64]{1,0,3,2:T(2,128)}, bf16[2,512,3,64]{1,3,2,0:T(8,128...) while((s32[]{:T(128)}, f32[1024,3,64]{0,2,1:T(8,128)}, ...), condition=%wide.region_63.64_spmd.clone, body=%wide.region_61.63_spmd.clone.sunk | while | flops 1026587136 | bytes 109360928 | solution.py:134
  1564.0 8.1 dynamic_update_slice.37
  1587.3 8.1 dynamic_update_slice.37
  1606.3 5.6 multiply_reduce_fusion.20
  1615.7 47.2 %while.86 = (s32[]{:T(128)}, f32[1024,3,64]{0,2,1:T(8,128)}, f32[1024,3,64]{0,2,1:T(8,128)}, f32[2,512,3,64]{1,0,3,2:T(2,128)}, bf16[2,512,3,64]{1,3,2,0:T(8,128...) while((s32[]{:T(128)}, f32[1024,3,64]{0,2,1:T(8,128)}, ...), condition=%wide.region_50.51_spmd.clone, body=%wide.region_48.50_spmd.clone.sunk | while | flops 1026587136 | bytes 109360928 | solution.py:134
  1624.7 8.1 dynamic_update_slice.36
  1647.9 8.1 dynamic_update_slice.36
  1682.4 4.8 fusion.157
  1703.5 4.2 copy.159
  1707.7 4.7 reshape.651
  1712.7 30.6 all-reduce.21.cloned.1.call-done
  1747.2 6.0 multiply_reduce_fusion.8
  1757.5 21.7 fusion.202
  1779.2 30.7 convolution_add_fusion
  1815.6 31.1 scatter_custom_fusion.4
  1846.7 39.0 %copy.157 = f32[12672,768]{0,1:T(8,128)} copy(f32[12672,768]{1,0:T(8,128)} %scatter_custom_fusion.4) | data formatting | bytes 77856768
  1891.1 38.4 %all-reduce.1 = (f32[]{:T(128)}, f32[9216]{0:T(1024)S(1)}) all-reduce(f32[]{:T(128)S(6)} %add.628, f32[9216]{0:T(1024)S(1)} %add.654), channel_id=1, replica_groups=mesh['wide'=8,'narrow'=4] {'wide'}, use_global_device_ids=true, to_apply=%region_40.41 | all-reduce | flops 9217 | bytes 73736 | tf_op jit(solution)/shard_map/psum | solution.py:480
  1931.9 22.4 reduce-scatter.16.cloned.1.call-done
  1955.9 67.9 %reduce-scatter.24.cloned.1.call-done = f32[96,576]{1,0:T(8,128)} async-done(((f32[768,576]{1,0:T(8,128)}), f32[96,576]{1,0:T(8,128)}) %reduce-scatter.24.cloned.1.call-update) | async-done | bytes 221200
  2025.8 75.3 %reduce-scatter.20.cloned.1.call-done = f32[128,768]{1,0:T(8,128)} async-done(((f32[128,6144]{1,0:T(8,128)}), f32[128,768]{1,0:T(8,128)}) %reduce-scatter.20.cloned.1.call-update) | async-done | bytes 393232 | tf_op jit(solution)/shard_map/reduce_scatter | solution.py:314
  2104.0 615.9 %reduce-scatter.14.cloned.1.call-done = f32[96,12672]{1,0:T(8,128)} async-done(((f32[768,12672]{1,0:T(8,128)}), f32[96,12672]{1,0:T(8,128)}) %reduce-scatter.14.cloned.1.call-update) | async-done | bytes 4866064 | tf_op jit(solution)/shard_map/reduce_scatter | solution.py:309
  2720.0 4.2 multiply_reduce_fusion.5
  2724.2 614.7 %reduce-scatter.22.cloned.1.call-done = f32[96,12672]{1,0:T(8,128)} async-done(((f32[768,12672]{1,0:T(8,128)}), f32[96,12672]{1,0:T(8,128)}) %reduce-scatter.22.cloned.1.call-update) | async-done | bytes 4866064
  3338.9 6.4 copy.158
  3345.3 4.4 multiply_reduce_fusion.4
  3353.8 39.4 %psum.111 = f32[]{:T(128)} all-reduce(f32[]{:T(128)S(6)} %add.656), channel_id=1, replica_groups=mesh['wide'=8,'narrow'=4] {'wide','narrow'}, use_global_device_ids=true, to_apply=%region_108.109 | all-reduce | flops 1 | bytes 8 | tf_op jit(solution)/shard_map/psum | solution.py:485
  3406.3 13.8 multiply_subtract_fusion
  3420.2 6.4 add_subtract_fusion
  (843 shorter events, 266.9 us)
Async XLA Ops:
  7.2 410.1 %all-gather.19.cloned.1.call-start = ((), (), s32[]{:S(2)}) async-start(), calls=%async_computation.7 | async-start | bytes 21897216 | tf_op jit(solution)/shard_map/all_gather | solution.py:379
  11.4 529.1 %all-gather.21.cloned.1.call-start = ((), (), s32[]{:S(2)}) async-start(), calls=%async_computation.8 | async-start | bytes 1769472 | tf_op jit(solution)/shard_map/all_gather | solution.py:385
  12.2 534.0 %all-reduce.25.cloned.1.call-start = ((), (), s32[]{:S(2)}) async-start(), calls=%async_computation.24 | async-start | bytes 6291456 | tf_op jit(solution)/shard_map/psum | solution.py:420
  18.8 521.7 %copy-start.209 = (f32[128]{0:T(128)}, f32[128]{0:T(128)S(1)}, u32[]{:S(2)}) copy-start(f32[128]{0:T(128)S(1)} %divide_multiply_fusion.1) | copy-start | bytes 1540
  18.9 523.8 %copy-start.211 = (f32[128]{0:T(128)}, f32[128]{0:T(128)S(1)}, u32[]{:S(2)}) copy-start(f32[128]{0:T(128)S(1)} %divide_multiply_fusion) | copy-start | bytes 1540
  476.1 31.6 copy-start.89
  476.1 223.2 %all-reduce.19.cloned.1.call-start = ((), (), s32[]{:S(2)}) async-start(), calls=%async_computation.21 | async-start | bytes 12582912 | tf_op jit(solution)/shard_map/psum | solution.py:166
  507.7 46.1 %copy-start.79 = (bf16[3,768,192]{1,2,0:T(8,128)(2,1)}, bf16[3,768,192]{1,2,0:T(8,128)(2,1)S(1)}, u32[]{:S(2)}) copy-start(bf16[3,768,192]{1,2,0:T(8,128)(2,1)S(1)} %copy.133) | copy-start | bytes 2654212
  539.3 38.1 %copy-start.51 = (bf16[192,768]{0,1:T(8,128)(2,1)}, bf16[192,768]{0,1:T(8,128)(2,1)S(1)}, u32[]{:S(2)}) copy-start(bf16[192,768]{0,1:T(8,128)(2,1)S(1)} %all_gather.64) | copy-start | bytes 884740
  545.5 153.8 %copy-start.108 = (f32[768]{0:T(1024)}, f32[768]{0:T(1024)S(1)}, u32[]{:S(2)}) copy-start(f32[768]{0:T(1024)S(1)} %get-tuple-element.777) | copy-start | bytes 9220
  545.5 159.6 %copy-start.126 = (f32[768]{0:T(1024)}, f32[768]{0:T(1024)S(1)}, u32[]{:S(2)}) copy-start(f32[768]{0:T(1024)S(1)} %get-tuple-element.774) | copy-start | bytes 9220
  546.2 153.1 %copy-start.115 = (f32[768]{0:T(1024)}, f32[768]{0:T(1024)S(1)}, u32[]{:S(2)}) copy-start(f32[768]{0:T(1024)S(1)} %get-tuple-element.769) | copy-start | bytes 9220
  546.2 158.9 %copy-start.130 = (f32[768]{0:T(1024)}, f32[768]{0:T(1024)S(1)}, u32[]{:S(2)}) copy-start(f32[768]{0:T(1024)S(1)} %get-tuple-element.765) | copy-start | bytes 9220
  579.8 163.3 %all-gather.23.cloned.1.call-start = ((), (), s32[]{:S(2)}) async-start(), calls=%async_computation.9 | async-start | bytes 1327104 | tf_op jit(solution)/shard_map/all_gather | solution.py:383
  581.5 204.2 %all-gather.25.cloned.1.call-start = ((), (), s32[]{:S(2)}) async-start(), calls=%async_computation.10 | async-start | bytes 1327104 | tf_op jit(solution)/shard_map/all_gather | solution.py:384
  582.2 331.9 %all-reduce.17.cloned.1.call-start = ((), (), s32[]{:S(2)}) async-start(), calls=%async_computation.20 | async-start | bytes 12582912 | tf_op jit(solution)/shard_map/psum | solution.py:172
  703.9 840.8 %copy-start.10 = (f32[1024,768]{1,0:T(8,128)}, f32[1024,768]{1,0:T(8,128)S(1)}, u32[]{:S(2)}) copy-start(f32[1024,768]{1,0:T(8,128)S(1)} %get-tuple-element.842) | copy-start | bytes 9437188
  795.4 494.0 %all-gather.27.cloned.1.call-start = ((), (), s32[]{:S(2)}) async-start(), calls=%async_computation.11 | async-start | bytes 21897216 | tf_op jit(solution)/shard_map/all_gather | solution.py:380
  799.6 114.5 %copy-start.149 = (f32[768]{0:T(1024)S(1)}, f32[768]{0:T(1024)}, u32[]{:S(2)}) copy-start(f32[768]{0:T(1024)} %get-tuple-element.757) | copy-start | bytes 9220
  799.6 114.5 %copy-start.164 = (f32[768]{0:T(1024)S(1)}, f32[768]{0:T(1024)}, u32[]{:S(2)}) copy-start(f32[768]{0:T(1024)} %get-tuple-element.773) | copy-start | bytes 9220
  799.6 114.5 %copy-start.167 = (f32[768]{0:T(1024)S(1)}, f32[768]{0:T(1024)}, u32[]{:S(2)}) copy-start(f32[768]{0:T(1024)} %get-tuple-element.766) | copy-start | bytes 9220
  799.6 635.4 %all-reduce.15.cloned.1.call-start = ((), (), s32[]{:S(2)}) async-start(), calls=%async_computation.19 | async-start | bytes 3145728 | tf_op jit(solution)/shard_map/psum | solution.py:300
  799.7 114.4 %copy-start.190 = (s32[1024]{0:T(1024)}, s32[1024]{0:T(1024)S(1)}, u32[]{:S(2)}) copy-start(s32[1024]{0:T(1024)S(1)} %pad_clamp_fusion.1) | copy-start | bytes 12292
  801.3 112.8 %copy-start.191 = (s32[1024]{0:T(1024)}, s32[1024]{0:T(1024)S(1)}, u32[]{:S(2)}) copy-start(s32[1024]{0:T(1024)S(1)} %pad_clamp_fusion) | copy-start | bytes 12292
  927.6 371.3 %copy-start.55 = (bf16[256,768]{1,0:T(8,128)(2,1)}, bf16[256,768]{1,0:T(8,128)(2,1)S(1)}, u32[]{:S(2)}) copy-start(bf16[256,768]{1,0:T(8,128)(2,1)S(1)} %gather_fusion.4) | copy-start | bytes 1179652
  927.6 371.4 %copy-start.192 = (s32[256]{0:T(256)S(1)}, s32[256]{0:T(256)}, u32[]{:S(2)}) copy-start(s32[256]{0:T(256)} %get-tuple-element.843) | copy-start | bytes 3076
  1299.0 21.4 copy-start.173
  1299.0 21.9 copy-start.19
  1336.8 19.8 slice-start.9
  1336.8 19.8 slice-start.11
  1336.8 23.0 copy-start.193
  1336.8 23.0 copy-start.217
  1391.8 148.0 %all-reduce.23.cloned.1.call-start = ((), (), s32[]{:S(2)}) async-start(), calls=%async_computation.23 | async-start | bytes 6291456 | tf_op jit(solution)/shard_map/psum | solution.py:226
  1470.9 68.9 %copy-start.104 = (f32[1024]{0:T(1024)S(1)}, f32[1024]{0:T(1024)}, u32[]{:S(2)}) copy-start(f32[1024]{0:T(1024)} %copy-done.103) | copy-start | bytes 12292
  1470.9 68.9 %copy-start.131 = (f32[768]{0:T(1024)S(1)}, f32[768]{0:T(1024)}, u32[]{:S(2)}) copy-start(f32[768]{0:T(1024)} %copy-done.130) | copy-start | bytes 9220
  1470.9 68.9 %copy-start.133 = (f32[1024]{0:T(1024)S(1)}, f32[1024]{0:T(1024)}, u32[]{:S(2)}) copy-start(f32[1024]{0:T(1024)} %copy-done.132) | copy-start | bytes 12292
  1471.0 73.8 %copy-start.127 = (f32[768]{0:T(1024)S(1)}, f32[768]{0:T(1024)}, u32[]{:S(2)}) copy-start(f32[768]{0:T(1024)} %copy-done.126) | copy-start | bytes 9220
  1471.0 73.8 %copy-start.129 = (f32[1024]{0:T(1024)S(1)}, f32[1024]{0:T(1024)}, u32[]{:S(2)}) copy-start(f32[1024]{0:T(1024)} %copy-done.128) | copy-start | bytes 12292
  1471.0 272.3 %all-reduce.21.cloned.1.call-start = ((), (), s32[]{:S(2)}) async-start(), calls=%async_computation.22 | async-start | bytes 6291456 | tf_op jit(solution)/shard_map/psum | solution.py:258
  1674.4 215.1 %reduce-scatter.26.cloned.1.call-start = ((), (), s32[]{:S(2)}) async-start(), calls=%async_computation.18 | async-start | bytes 884736
  1681.9 248.3 %reduce-scatter.18.cloned.1.call-start = ((), (), s32[]{:S(2)}) async-start(), calls=%async_computation.14 | async-start | bytes 2654208 | tf_op jit(solution)/shard_map/reduce_scatter | solution.py:313
  1690.5 263.8 %reduce-scatter.16.cloned.1.call-start = ((), (), s32[]{:S(2)}) async-start(), calls=%async_computation.13 | async-start | bytes 2654208 | tf_op jit(solution)/shard_map/reduce_scatter | solution.py:312
  1697.1 326.6 %reduce-scatter.24.cloned.1.call-start = ((), (), s32[]{:S(2)}) async-start(), calls=%async_computation.17 | async-start | bytes 2211840
  1707.7 35.6 %copy-start.141 = (f32[768]{0:T(1024)S(1)}, f32[768]{0:T(1024)}, u32[]{:S(2)}) copy-start(f32[768]{0:T(1024)} %copy-done.139) | copy-start | bytes 9220
  1707.7 35.6 %copy-start.146 = (f32[1024]{0:T(1024)S(1)}, f32[1024]{0:T(1024)}, u32[]{:S(2)}) copy-start(f32[1024]{0:T(1024)} %copy-done.144) | copy-start | bytes 12292
  1712.4 34.5 %copy-start.143 = (f32[1024]{0:T(1024)S(1)}, f32[1024]{0:T(1024)}, u32[]{:S(2)}) copy-start(f32[1024]{0:T(1024)} %copy-done.142) | copy-start | bytes 12292
  1712.4 388.6 %reduce-scatter.20.cloned.1.call-start = ((), (), s32[]{:S(2)}) async-start(), calls=%async_computation.15 | async-start | bytes 3538944 | tf_op jit(solution)/shard_map/reduce_scatter | solution.py:314
  1757.3 21.9 copy-start.56
  1757.3 21.8 copy-start.194
  1757.4 21.8 copy-start.208
  1757.4 21.8 copy-start.218
  1757.4 962.6 %reduce-scatter.14.cloned.1.call-start = ((), (), s32[]{:S(2)}) async-start(), calls=%async_computation.12 | async-start | bytes 43794432 | tf_op jit(solution)/shard_map/reduce_scatter | solution.py:309
  1809.9 1529.0 %reduce-scatter.22.cloned.1.call-start = ((), (), s32[]{:S(2)}) async-start(), calls=%async_computation.16 | async-start | bytes 43794432
  1929.5 95.4 %copy-start.197 = (f32[9216]{0:T(1024)}, f32[9216]{0:T(1024)S(1)}, u32[]{:S(2)}) copy-start(f32[9216]{0:T(1024)S(1)} %get-tuple-element.647) | copy-start | bytes 110596
  3349.7 47.2 %copy-start.152 = (f32[1152]{0:T(1024)S(1)}, f32[1152]{0:T(1024)}, u32[]{:S(2)}) copy-start(f32[1152]{0:T(1024)} %param.49) | copy-start | bytes 13828
  3349.7 47.2 %copy-start.195 = (f32[1152]{0:T(1024)S(1)}, f32[1152]{0:T(1024)}, u32[]{:S(2)}) copy-start(f32[1152]{0:T(1024)} %param.57) | copy-start | bytes 13828
  3349.7 48.6 %copy-start.90 = (f32[192,96]{1,0:T(8,128)S(1)}, f32[192,96]{1,0:T(8,128)}, u32[]{:S(2)}) copy-start(f32[192,96]{1,0:T(8,128)} %param.45) | copy-start | bytes 221188
  3349.7 48.6 %copy-start.105 = (f32[192,96]{1,0:T(8,128)S(1)}, f32[192,96]{1,0:T(8,128)}, u32[]{:S(2)}) copy-start(f32[192,96]{1,0:T(8,128)} %param.53) | copy-start | bytes 221188
  3349.7 50.3 %copy-start.65 = (f32[128,768]{1,0:T(8,128)S(1)}, f32[128,768]{1,0:T(8,128)}, u32[]{:S(2)}) copy-start(f32[128,768]{1,0:T(8,128)} %param.48) | copy-start | bytes 1179652
  3349.7 50.3 %copy-start.66 = (f32[128,768]{1,0:T(8,128)S(1)}, f32[128,768]{1,0:T(8,128)}, u32[]{:S(2)}) copy-start(f32[128,768]{1,0:T(8,128)} %reduce-scatter.20.cloned.1.call-done) | copy-start | bytes 1179652
  3349.7 50.3 %copy-start.94 = (f32[128,768]{1,0:T(8,128)S(1)}, f32[128,768]{1,0:T(8,128)}, u32[]{:S(2)}) copy-start(f32[128,768]{1,0:T(8,128)} %param.56) | copy-start | bytes 1179652
  3399.9 20.2 slice-start
  3400.0 20.2 slice-start.4
  3400.0 20.2 slice-start.6
  (209 other events, 1133.1 us)
Sparse Core Ops, SparseCore 0:
  11.5 405.6 all-gather.18
  420.1 44.4 all-gather.20
  476.2 68.6 all-reduce.24
  580.0 119.2 all-reduce.18
  701.9 41.2 all-gather.22
  745.8 39.8 all-gather.24
  795.5 118.5 all-reduce.16
  915.6 373.6 all-gather.26
  1391.9 43.0 all-reduce.14
  1471.1 68.6 all-reduce.22
  1674.5 68.6 all-reduce.20
  1746.4 62.5 reduce-scatter.25
  1813.5 68.0 reduce-scatter.17
  1885.9 68.3 reduce-scatter.15
  1958.0 65.7 reduce-scatter.23
  2027.8 73.1 reduce-scatter.19
  2104.8 615.1 reduce-scatter.13
  2723.8 615.0 reduce-scatter.21
where the time goes:
time: 3450 us; the launch traced here: 3440 us
  waiting for transfers between devices  2500 us (72%)
  blocking collectives  261 us (8%)
  matrix products  230 us (7%)
  other arithmetic  209 us (6%)
  local copies, waits for them, and re-layouts  203 us (6%)
    unnamed x21, waiting for transfers between devices  683 us
    reduce_scatter x1, waiting for transfers between devices, reduce_wide(): lax.psum_scatter(grads[1], 'wide', scatter_dimension=0, tiled=True)  616 us
    all_gather x1, waiting for transfers between devices, local(): lax.all_gather(out_table.astype(jnp.bfloat16), 'wide', axis=0, tiled=True)  362 us
    all_gather x1, waiting for transfers between devices, local(): lax.all_gather(embedding.astype(jnp.bfloat16), 'wide', axis=1, tiled=True)  306 us
    psum x1, waiting for transfers between devices, layer_forward(): lax.psum(jnp.dot(mixed, proj_copy, preferred_element_type=jnp.float32), '...  117 us
    psum x1, waiting for transfers between devices, layer_forward(): lax.psum(jnp.dot(active, down_copy, preferred_element_type=jnp.float32),...  108 us
    all_gather x1, blocking collectives, local(): lax.all_gather(qkv_weight.astype(jnp.bfloat16), 'wide', axis=1, tiled=True)  90.4 us
    unnamed x507, local copies, waits for them, and re-layouts  83.6 us
  transfers between devices with their start and end apart: 18, of which 14 were waited for; matrix products, arithmetic and copies ran while one was open for 9% of the time, Pallas kernels for 0%

commit v1 on v0

v1 whole, which is shorter than its diff:
```python
import functools
import math

import jax
import jax.numpy as jnp
from jax import lax
from jax.experimental import pallas as pl
from jax.experimental.pallas import tpu as pltpu
from jax.sharding import PartitionSpec as P

HD = 64
STEP = 10

HIGHEST = lax.Precision.HIGHEST
NORM_EPS = 1e-06
CLIP_NORM = 0.005
BETA_ONE = 0.9
BETA_TWO = 0.95
ADAM_EPS = 1e-08
WEIGHT_DECAY = 0.1
LEARN_RATES = (1.0, 0.1, 0.07, 0.5, 0.07, 0.04, 0.2, 0.5)
BF = jnp.bfloat16
F32 = jnp.float32
VMEM_LIMIT = 56 * 1024 * 1024


def xor_narrow(value, bits):
    return lax.ppermute(value, "narrow", [(i, i ^ bits) for i in range(lax.axis_size("narrow"))])


def xor_wide(value, bits):
    return lax.ppermute(value, "wide", [(i, i ^ bits) for i in range(lax.axis_size("wide"))])


def swap_wide(value):
    return lax.all_to_all(value, "wide", 0, 0, tiled=True)


def spread_wide(value):
    if lax.axis_size("wide") > 8:
        return lax.all_gather(value, "wide")
    return swap_wide(jnp.broadcast_to(value[None], (lax.axis_size("wide"),) + value.shape))


def swap_wide_async(value):
    count = lax.axis_size("wide")
    if count > 8:
        return swap_wide(value)
    me = lax.axis_index("wide")
    out = value
    pieces = [
        xor_wide(lax.dynamic_index_in_dim(value, me ^ k, 0, keepdims=False), k)
        for k in range(1, count)
    ]
    for k in range(1, count):
        out = lax.dynamic_update_index_in_dim(out, pieces[k - 1], me ^ k, 0)
    return out


def gather_wide(value):
    count = lax.axis_size("wide")
    if count != 8:
        return lax.all_gather(value, "wide", axis=0, tiled=True)
    me = lax.axis_index("wide")
    near = jnp.stack([value] + [xor_wide(value, k) for k in (2, 4, 6)])
    far = xor_wide(near, 1)
    out = jnp.zeros((count,) + value.shape, value.dtype)
    for k in range(4):
        out = lax.dynamic_update_index_in_dim(out, near[k], me ^ (2 * k), 0)
        out = lax.dynamic_update_index_in_dim(out, far[k], me ^ (2 * k + 1), 0)
    return out.reshape((count * value.shape[0],) + value.shape[1:])


def scatter_wide(value):
    count = lax.axis_size("wide")
    if count != 8:
        return lax.psum_scatter(value, "wide", scatter_dimension=0)
    me = lax.axis_index("wide")
    side = me & 1
    pairs = value.reshape((4, 2) + value.shape[1:])
    kept = lax.dynamic_index_in_dim(pairs, side, 1, keepdims=False)
    sent = lax.dynamic_index_in_dim(pairs, 1 - side, 1, keepdims=False).astype(BF)
    half = kept.astype(F32) + xor_wide(sent, 1).astype(F32)
    depth = me >> 1
    total = lax.dynamic_index_in_dim(half, depth, 0, keepdims=False)
    low = half.astype(BF)
    for k in (1, 2, 3):
        piece = lax.dynamic_index_in_dim(low, depth ^ k, 0, keepdims=False)
        total = total + xor_wide(piece, 2 * k).astype(F32)
    return total


def scatter_narrow(parts):
    from_core = xor_narrow(jnp.stack([parts[1], parts[3]]).astype(BF), 1)
    near = parts[0] + from_core[0].astype(F32)
    far = parts[2] + from_core[1].astype(F32)
    return near + xor_narrow(far.astype(BF), 2).astype(F32)


def gather_narrow(value):
    across = xor_narrow(value, 2)
    beside = xor_narrow(value, 1)
    corner = xor_narrow(across, 1)
    return value, beside, across, corner


def rounded(value):
    return lax.reduce_precision(value, exponent_bits=8, mantissa_bits=7)


def layer_norm(values):
    centered = values - jnp.mean(values, axis=-1, keepdims=True)
    inverse = lax.rsqrt(jnp.mean(centered * centered, axis=-1, keepdims=True) + NORM_EPS)
    return (centered * inverse, inverse)


def norm_back(grad, normed, inverse):
    return inverse * (
        grad
        - jnp.mean(grad, axis=-1, keepdims=True)
        - normed * jnp.mean(grad * normed, axis=-1, keepdims=True)
    )


def gelu_tanh(values):
    inner = 0.7978845608 * (values + 0.044715 * values * values * values)
    return 0.5 * values * (1.0 + jnp.tanh(inner))


def gelu_slope(values):
    tangent = jnp.tanh(0.7978845608 * (values + 0.044715 * values * values * values))
    return 0.5 * (1.0 + tangent) + 0.5 * values * (1.0 - tangent * tangent) * 0.7978845608 * (
        1.0 + 0.134145 * values * values
    )


def rotary_tables(positions, width):
    freqs = jnp.exp(jnp.arange(width // 2, dtype=F32) * (-2.0 * math.log(10000.0) / width))
    angle = positions.astype(F32)[:, None] * freqs[None, :]
    cosine, sine = jnp.cos(angle), jnp.sin(angle)
    return (
        jnp.concatenate([cosine] * 4, axis=1),
        jnp.concatenate([-sine, sine, -sine, sine], axis=1),
    )


def time_features(moment, width):
    freqs = jnp.exp(jnp.arange(width // 2, dtype=F32) * (-math.log(10000.0) / (width // 2)))
    angle = 1000.0 * moment[..., None] * freqs
    return jnp.concatenate([jnp.cos(angle), jnp.sin(angle)], axis=-1)


def turned(values, cosine, sine):
    lanes = lax.broadcasted_iota(jnp.int32, values.shape, 1)
    ahead = pltpu.roll(values, values.shape[1] - HD // 2, 1)
    behind = pltpu.roll(values, HD // 2, 1)
    other = jnp.where((lanes & (HD - 1)) < HD // 2, ahead, behind)
    return values * cosine + other * sine


def qkv_kernel(hidden_ref, weight_ref, cos_ref, sin_ref, out_ref):
    step = pl.program_id(0)
    block = weight_ref.shape[1]
    value = jnp.dot(hidden_ref[...], weight_ref[...], preferred_element_type=F32)

    @pl.when(step * block < 2 * hidden_ref.shape[1])
    def _():
        for part in range(block // (2 * HD)):
            lanes = slice(part * 2 * HD, (part + 1) * 2 * HD)
            out_ref[:, lanes] = turned(value[:, lanes], cos_ref[...], sin_ref[...]).astype(BF)

    @pl.when(step * block >= 2 * hidden_ref.shape[1])
    def _():
        out_ref[...] = value.astype(BF)


def project_qkv(hidden, weight, cosine, sine):
    rows, width = hidden.shape
    block = 256
    return pl.pallas_call(
        qkv_kernel,
        grid=(weight.shape[1] // block,),
        in_specs=[
            pl.BlockSpec((rows, width), lambda i: (0, 0)),
            pl.BlockSpec((width, block), lambda i: (0, i)),
            pl.BlockSpec(cosine.shape, lambda i: (0, 0)),
            pl.BlockSpec(sine.shape, lambda i: (0, 0)),
        ],
        out_specs=pl.BlockSpec((rows, block), lambda i: (0, i)),
        out_shape=jax.ShapeDtypeStruct((rows, weight.shape[1]), BF),
        compiler_params=pltpu.CompilerParams(vmem_limit_bytes=VMEM_LIMIT),
        cost_estimate=pl.CostEstimate(
            flops=2 * rows * width * weight.shape[1], bytes_accessed=8_000_000, transcendentals=0
        ),
        name="qkv",
    )(hidden, weight, cosine, sine)


NT = (((1,), (1,)), ((), ()))
NN = (((1,), (0,)), ((), ()))
TN = (((0,), (0,)), ((), ()))


def mm(a, b, dims):
    return lax.dot_general(a, b, dims, preferred_element_type=F32)


def head_mask(values, head):
    lanes = lax.broadcasted_iota(jnp.int32, values.shape, 1)
    return jnp.where((lanes >= HD) == (head == 1), values, jnp.zeros_like(values))


def attend_kernel(q_ref, k_ref, v_ref, out_ref, log_ref):
    keys, values, query = k_ref[...], v_ref[...], q_ref[...] * BF(HD**-0.5)
    halves = []
    for head in range(2):
        scores = mm(keys, head_mask(query, head), NT)
        top = jnp.max(scores, axis=0, keepdims=True)
        shifted = jnp.exp(scores - top)
        total = jnp.sum(shifted, axis=0, keepdims=True)
        weights = (shifted * (1.0 / total)).astype(BF)
        halves.append(mm(values, weights, TN)[head * HD : (head + 1) * HD])
        log_ref[0, head : head + 1, :] = top + jnp.log(total)
    out_ref[...] = jnp.concatenate(halves, axis=0).T.astype(BF)


def attend(query, keys, values):
    rows, width = query.shape
    length = keys.shape[0]
    pairs = width // (2 * HD)
    lane = pl.BlockSpec((rows, 2 * HD), lambda i: (0, i))
    wide = pl.BlockSpec((length, 2 * HD), lambda i: (0, i))
    return pl.pallas_call(
        attend_kernel,
        grid=(pairs,),
        in_specs=[lane, wide, wide],
        out_specs=[lane, pl.BlockSpec((1, 2, rows), lambda i: (i, 0, 0))],
        out_shape=[
            jax.ShapeDtypeStruct((rows, width), BF),
            jax.ShapeDtypeStruct((pairs, 2, rows), F32),
        ],
        compiler_params=pltpu.CompilerParams(vmem_limit_bytes=VMEM_LIMIT),
        cost_estimate=pl.CostEstimate(
            flops=4 * rows * length * width * 4,
            bytes_accessed=5_000_000,
            transcendentals=rows * length * width // HD,
        ),
        name="attend",
    )(query, keys, values)


def attend_back_kernel(
    q_ref, k_ref, v_ref, do_ref, log_ref, cos_ref, sin_ref, kcos_ref, ksin_ref,
    dq_ref, dk_ref, dv_ref, dk_far_ref, dv_far_ref,
):
    keys, values, query, grad = k_ref[...], v_ref[...], q_ref[...], do_ref[...]
    scale = HD**-0.5
    rows = query.shape[0]
    dq = jnp.zeros((2 * HD, rows), F32)
    dk = jnp.zeros(keys.shape, F32)
    dv = jnp.zeros(keys.shape, F32)
    for head in range(2):
        query_one = head_mask(query * BF(scale), head)
        grad_one = head_mask(grad, head)
        scores = mm(keys, query_one, NT)
        weights = jnp.exp(scores - log_ref[0, head : head + 1, :])
        d_weights = mm(values, grad_one, NT)
        delta = jnp.sum(weights * d_weights, axis=0, keepdims=True)
        d_scores = (weights * (d_weights - delta)).astype(BF)
        dq = dq + mm(head_mask(keys, head), d_scores, TN)
        dk = dk + mm(d_scores, query_one, NN)
        dv = dv + mm(weights.astype(BF), grad_one, NN)
    dq_ref[...] = turned(dq.T * scale, cos_ref[...], -sin_ref[...]).astype(BF)
    dk = turned(dk, kcos_ref[...], -ksin_ref[...])
    dk_ref[...] = dk[:rows]
    dv_ref[...] = dv[:rows]
    dk_far_ref[...] = dk[rows:].astype(BF)
    dv_far_ref[...] = dv[rows:].astype(BF)


def attend_back(query, keys, values, grad, logs, cosine, sine, key_cosine, key_sine):
    rows, width = query.shape
    length = keys.shape[0]
    pairs = width // (2 * HD)
    lane = pl.BlockSpec((rows, 2 * HD), lambda i: (0, i))
    wide = pl.BlockSpec((length, 2 * HD), lambda i: (0, i))
    whole = lambda table: pl.BlockSpec(table.shape, lambda i: (0, 0))
    return pl.pallas_call(
        attend_back_kernel,
        grid=(pairs,),
        in_specs=[
            lane, wide, wide, lane, pl.BlockSpec((1, 2, rows), lambda i: (i, 0, 0)),
            whole(cosine), whole(sine), whole(key_cosine), whole(key_sine),
        ],
        out_specs=[lane] * 5,
        out_shape=[
            jax.ShapeDtypeStruct((rows, width), BF),
            jax.ShapeDtypeStruct((rows, width), F32),
            jax.ShapeDtypeStruct((rows, width), F32),
            jax.ShapeDtypeStruct((length - rows, width), BF),
            jax.ShapeDtypeStruct((length - rows, width), BF),
        ],
        compiler_params=pltpu.CompilerParams(vmem_limit_bytes=VMEM_LIMIT),
        cost_estimate=pl.CostEstimate(
            flops=10 * rows * length * width * 4,
            bytes_accessed=10_000_000,
            transcendentals=rows * length * width // HD,
        ),
        name="attend_back",
    )(query, keys, values, grad, logs, cosine, sine, key_cosine, key_sine)


def lookup_kernel(id_ref, table_ref, out_ref, scratch):
    block = scratch.shape[0]
    unroll = 16

    def body(step, _):
        for k in range(unroll):
            place = step * unroll + k
            scratch[pl.ds(place, 1), :] = table_ref[pl.ds(id_ref[0, 0, place], 1), :]
        return 0

    lax.fori_loop(0, block // unroll, body, 0)
    out_ref[...] = scratch[...].astype(BF)


def lookup(table, ids):
    count = ids.shape[0]
    block = min(2048, count)
    width = table.shape[1]
    return pl.pallas_call(
        lookup_kernel,
        grid=(count // block,),
        in_specs=[
            pl.BlockSpec((1, 1, block), lambda i: (i, 0, 0), memory_space=pltpu.SMEM),
            pl.BlockSpec(table.shape, lambda i: (0, 0), pipeline_mode=pl.Buffered(1)),
        ],
        out_specs=pl.BlockSpec((block, width), lambda i: (i, 0)),
        out_shape=jax.ShapeDtypeStruct((count, width), BF),
        scratch_shapes=[pltpu.VMEM((block, width), F32)],
        compiler_params=pltpu.CompilerParams(vmem_limit_bytes=VMEM_LIMIT),
        cost_estimate=pl.CostEstimate(flops=0, bytes_accessed=60_000_000, transcendentals=0),
        name="lookup",
    )(ids.reshape(count // block, 1, block), table)


def collect_kernel(shift, key_ref, count_ref, grad_ref, out_ref, rows_ref):
    step = pl.program_id(0)

    @pl.when(step == 0)
    def _():
        out_ref[...] = jnp.zeros_like(out_ref)

    rows_ref[...] = grad_ref[0].astype(F32)
    mask = (1 << shift) - 1

    def body(item, _):
        key = key_ref[0, 0, item]
        target = pl.ds(lax.shift_right_logical(key, shift), 1)
        out_ref[target, :] = out_ref[target, :] + rows_ref[pl.ds(key & mask, 1), :]
        return 0

    lax.fori_loop(0, count_ref[0, 0, 0], body, 0)


def collect(keys, counts, grads, shift, entries):
    parts, tokens, width = grads.shape
    return pl.pallas_call(
        functools.partial(collect_kernel, shift),
        grid=(parts,),
        in_specs=[
            pl.BlockSpec((1, 1, tokens), lambda i: (i, 0, 0), memory_space=pltpu.SMEM),
            pl.BlockSpec((1, 1, 1), lambda i: (i, 0, 0), memory_space=pltpu.SMEM),
            pl.BlockSpec((1, tokens, width), lambda i: (i, 0, 0)),
        ],
        out_specs=pl.BlockSpec((entries, width), lambda i: (0, 0)),
        out_shape=jax.ShapeDtypeStruct((entries, width), F32),
        scratch_shapes=[pltpu.VMEM((tokens, width), F32)],
        compiler_params=pltpu.CompilerParams(vmem_limit_bytes=VMEM_LIMIT),
        cost_estimate=pl.CostEstimate(flops=0, bytes_accessed=60_000_000, transcendentals=0),
        name="collect",
    )(keys.reshape(parts, 1, tokens), counts.reshape(parts, 1, 1), grads)


def local(
    token_ids, mask_slots, mask_counts,
    embedding, out_table, qkv_weight, proj_weight, up_weight, down_weight, mod_weight, vectors,
    embedding_first, out_table_first, qkv_first, proj_first, up_first, down_first, mod_first,
    vectors_first,
    embedding_second, out_table_second, qkv_second, proj_second, up_second, down_second,
    mod_second, vectors_second,
):
    masters = (
        embedding, out_table, qkv_weight, proj_weight, up_weight, down_weight, mod_weight, vectors,
    )
    firsts = (
        embedding_first, out_table_first, qkv_first, proj_first, up_first, down_first, mod_first,
        vectors_first,
    )
    seconds = (
        embedding_second, out_table_second, qkv_second, proj_second, up_second, down_second,
        mod_second, vectors_second,
    )
    wide = lax.axis_size("wide")
    narrow = lax.axis_size("narrow")
    me = lax.axis_index("wide")
    group = lax.axis_index("narrow")
    part = group & 1
    micro = group >> 1
    entries, share = embedding.shape
    width = share * wide
    vocab = entries * narrow
    micro_count, length = token_ids.shape[1:]
    capacity = mask_slots.shape[2]
    rows = length // 2
    pair_total = 5 * length // 16
    quarter = pair_total // 4
    loss_scale = 1.0 / (length * micro_count * wide)
    positions = jnp.arange(length, dtype=jnp.int32)

    tokens, slots, counts = token_ids[0], mask_slots[0], mask_counts[0]
    at_slot = slots[:, :, None] == positions[None, None, :]
    valid = jnp.arange(capacity)[None, :] < counts[:, None]
    masked = jnp.any(at_slot & valid[:, :, None], axis=1)
    targets = jnp.sum(jnp.where(at_slot, tokens[:, None, :], 0), axis=2)
    inputs = jnp.where(masked, vocab - 1, tokens)
    packed = jnp.concatenate(
        [inputs, targets, jnp.broadcast_to(counts[:, None], (micro_count, 128))], axis=1
    )
    packed_all = spread_wide(packed)
    inputs_all = packed_all[:, :, :length]
    targets_all = packed_all[:, :, length : length + capacity]
    counts_all = packed_all[:, :, length + capacity]

    shard_a = jnp.concatenate(
        [qkv_weight[0], qkv_weight[1], qkv_weight[2], proj_weight.T], axis=1
    ).astype(BF)
    full_a = gather_narrow(gather_wide(shard_a))
    full_b = gather_narrow(gather_wide(up_weight.astype(BF)))
    full_c = gather_narrow(gather_wide(down_weight.T.astype(BF)))
    heads_width = width // narrow
    column = lambda k: [full[:, k * heads_width : (k + 1) * heads_width] for full in full_a]
    weight_qkv = jnp.concatenate(column(0) + column(1) + column(2), axis=1)
    weight_proj = jnp.concatenate(column(3), axis=1)

    chunk = entries // wide
    table_own = out_table.astype(BF).reshape(share, wide, chunk).transpose(1, 0, 2)
    tables = gather_narrow(swap_wide_async(table_own).reshape(width, chunk))

    moments = counts_all.astype(F32) / pair_total
    condition = jax.nn.silu(time_features(moments, mod_weight.shape[0]))
    condition_mine = lax.dynamic_index_in_dim(condition, micro, 1, keepdims=False)
    mod_part = jnp.dot(condition_mine, rounded(mod_weight), precision=HIGHEST)
    vector_part = jnp.broadcast_to(rounded(vectors), (wide, vectors.shape[0]))
    mod_recv = swap_wide(jnp.concatenate([mod_part, vector_part], axis=1))
    mod_share = mod_part.shape[1]
    vector_full = mod_recv[:, mod_share:].reshape(-1)
    modulation = mod_recv[:, :mod_share].reshape(-1) + vector_full[4 * width :]
    (
        shift_one, scale_one, gate_one, shift_two, scale_two, gate_two, shift_last, scale_last,
    ) = jnp.split(modulation, 8)
    gain_one, gain_two, gain_last, bias_down = jnp.split(vector_full[: 4 * width], 4)

    own_table = embedding.T.astype(BF)
    table_rows = (
        jnp.concatenate(
            [own_table, xor_narrow(own_table, 1), jnp.zeros((share, 128), BF)], axis=1
        )
        .astype(F32)
        .T
    )
    half_ids = lax.dynamic_slice_in_dim(inputs_all, part * rows, rows, axis=2)
    half_ids = jnp.stack(
        [
            lax.dynamic_index_in_dim(half_ids, micro, 1, keepdims=False),
            lax.dynamic_index_in_dim(half_ids, 1 - micro, 1, keepdims=False),
        ]
    )
    owner = half_ids // entries
    inside = half_ids - owner * entries
    places = jnp.where(
        owner == group, inside, jnp.where(owner == (group ^ 1), entries + inside, 2 * entries)
    )
    looked = lookup(table_rows, places.reshape(-1)).reshape(2, wide, rows, share)
    start_part = looked[0] + xor_narrow(looked[1], 2)
    start = swap_wide(start_part).astype(F32).transpose(1, 0, 2).reshape(rows, width)

    my_positions = part * rows + jnp.arange(rows, dtype=jnp.int32)
    far_positions = (1 - part) * rows + jnp.arange(rows, dtype=jnp.int32)
    key_cosine, key_sine = rotary_tables(jnp.concatenate([my_positions, far_positions]), HD)
    cosine, sine = key_cosine[:rows], key_sine[:rows]
    normed_one, inverse_one = layer_norm(start)
    hidden_one = (normed_one * gain_one * (1.0 + scale_one) + shift_one).astype(BF)
    projected = project_qkv(hidden_one, weight_qkv, cosine, sine)
    query = projected[:, :width]
    far = xor_narrow(projected[:, width:], 1)
    swapped = [
        far[:, kind * width + (s ^ 1) * heads_width : kind * width + ((s ^ 1) + 1) * heads_width]
        for kind in range(2)
        for s in range(narrow)
    ]
    keys = jnp.concatenate(
        [projected[:, width : 2 * width], jnp.concatenate(swapped[:narrow], axis=1)]
    )
    values = jnp.concatenate(
        [projected[:, 2 * width :], jnp.concatenate(swapped[narrow:], axis=1)]
    )
    mixed, logs = attend(query, keys, values)
    attended = mm(mixed, weight_proj, NT)
    middle = start + gate_one * attended
    normed_two, inverse_two = layer_norm(middle)
    hidden_two = (normed_two * gain_two * (1.0 + scale_two) + shift_two).astype(BF)
    inner = [mm(hidden_two, full_b[s], NN) for s in range(narrow)]
    active = [gelu_tanh(value).astype(BF) for value in inner]
    output = sum(mm(active[s], full_c[s], NT) for s in range(narrow))
    final = middle + gate_two * (output + bias_down)
    normed, inverse = layer_norm(final)
    lifted = gain_last * (1.0 + scale_last)
    hidden = (normed * lifted + shift_last).astype(BF)

    side = me // (wide // 2)
    low = me % (wide // 2)
    count_low = lax.dynamic_index_in_dim(
        lax.dynamic_index_in_dim(counts_all, low, 0, keepdims=False), micro, 0, keepdims=False
    )
    slot_row = lax.dynamic_index_in_dim(slots, micro, 0, keepdims=False)
    offset = jnp.arange(quarter, dtype=jnp.int32)
    order = jnp.concatenate(
        [
            s * (2 * quarter) + p * quarter + offset
            for p in (part, 1 - part)
            for s in (side, 1 - side)
        ]
    )
    from_low = order < count_low
    index = jnp.where(from_low, order, order - count_low)
    mine = from_low == (side == 0)
    wanted = jnp.sum(
        jnp.where(index[:, None] == jnp.arange(capacity)[None, :], slot_row[None, :], 0), axis=1
    )
    select = ((wanted[:, None] == my_positions[None, :]) & mine[:, None]).astype(BF)
    picked = mm(select, hidden, NN).astype(BF)
    picked = picked[: 2 * quarter] + xor_narrow(picked[2 * quarter :], 1)
    row_part = picked[:quarter] + xor_wide(picked[quarter:], wide // 2)
    head_rows = spread_wide(row_part).reshape(wide * quarter, width)

    targets_mine = lax.dynamic_index_in_dim(targets_all, micro, 1, keepdims=False)
    counts_mine = lax.dynamic_index_in_dim(counts_all, micro, 1, keepdims=False)
    pairs = wide // 2
    both = jnp.concatenate([targets_mine[:pairs], targets_mine[pairs:]], axis=1)
    spot = jnp.stack([s * 2 * quarter + part * quarter + offset for s in (0, 1)])
    low_counts = counts_mine[:pairs, None, None]
    spot = jnp.where(spot[None] < low_counts, spot[None], capacity + spot[None] - low_counts)
    row_targets = jnp.sum(
        jnp.where(
            spot[..., None] == jnp.arange(2 * capacity)[None, None, None, :],
            both[:, None, None, :],
            0,
        ),
        axis=-1,
    )
    row_targets = row_targets.transpose(1, 0, 2).reshape(-1)
    target_owner = row_targets // entries
    target_rest = row_targets - target_owner * entries
    target_wide = target_rest // chunk
    target_column = jnp.where(
        target_wide == me, (target_owner ^ group) * chunk + target_rest - target_wide * chunk, -1
    )

    logits = [mm(head_rows, table, NN) for table in tables]
    hitting = [
        jnp.arange(chunk)[None, :] + s * chunk == target_column[:, None] for s in range(narrow)
    ]
    top = functools.reduce(jnp.maximum, [jnp.max(value, axis=-1) for value in logits])
    total = sum(jnp.sum(jnp.exp(value - top[:, None]), axis=-1) for value in logits)
    target_logit = sum(
        jnp.sum(jnp.where(hit, value, 0.0), axis=-1) for hit, value in zip(hitting, logits)
    )
    stats = spread_wide(jnp.stack([top, total, target_logit]))
    top_all = jnp.max(stats[:, 0], axis=0)
    total_all = jnp.sum(stats[:, 1] * jnp.exp(stats[:, 0] - top_all[None]), axis=0)
    log_total = top_all + jnp.log(total_all)
    loss_part = jnp.sum(log_total - jnp.sum(stats[:, 2], axis=0))
    d_logits = [
        ((jnp.exp(value - log_total[:, None]) - hit.astype(F32)) * loss_scale).astype(BF)
        for hit, value in zip(hitting, logits)
    ]
    d_rows = sum(mm(grad, table, NT) for grad, table in zip(d_logits, tables))
    d_table_parts = [mm(head_rows, grad, TN) for grad in d_logits]
    d_table = scatter_narrow(d_table_parts).astype(BF).reshape(wide, share, chunk)
    d_table = swap_wide_async(d_table).astype(F32).transpose(1, 0, 2).reshape(share, entries)

    d_recv = swap_wide(d_rows.astype(BF).reshape(wide, quarter, width))
    d_mine = jnp.sum(d_recv.astype(F32), axis=0).astype(BF)
    d_sides = jnp.concatenate([d_mine, xor_wide(d_mine, wide // 2)])
    d_all = jnp.concatenate([d_sides, xor_narrow(d_sides, 1)])
    d_hidden = mm(select, d_all, TN)

    d_shift_last = jnp.sum(d_hidden, axis=0)
    d_hidden_normed = jnp.sum(d_hidden * normed, axis=0)
    d_scale_last = d_hidden_normed * gain_last
    d_gain_last = d_hidden_normed * (1.0 + scale_last)
    d_final = norm_back(d_hidden * lifted, normed, inverse)
    d_bias = jnp.sum(d_final, axis=0) * gate_two
    d_gate_two = jnp.sum(d_final * (output + bias_down), axis=0)
    d_output = (d_final * gate_two).astype(BF)
    d_inner = [
        (mm(d_output, full_c[s], NN) * gelu_slope(inner[s])).astype(BF) for s in range(narrow)
    ]
    d_c = [mm(d_output, active[s], TN) for s in range(narrow)]
    d_b = [mm(hidden_two, d_inner[s], TN) for s in range(narrow)]
    d_c = scatter_wide(scatter_narrow(d_c).reshape(wide, share, width))
    d_b = scatter_wide(scatter_narrow(d_b).reshape(wide, share, width))
    d_hidden_two = sum(mm(d_inner[s], full_b[s], NT) for s in range(narrow))
    d_shift_two = jnp.sum(d_hidden_two, axis=0)
    d_two_normed = jnp.sum(d_hidden_two * normed_two, axis=0)
    d_scale_two = d_two_normed * gain_two
    d_gain_two = d_two_normed * (1.0 + scale_two)
    d_middle = d_final + norm_back(
        d_hidden_two * gain_two * (1.0 + scale_two), normed_two, inverse_two
    )
    d_gate_one = jnp.sum(d_middle * attended, axis=0)
    d_attended = (d_middle * gate_one).astype(BF)
    d_proj = mm(d_attended, mixed, TN)
    d_mixed = mm(d_attended, weight_proj, NN).astype(BF)
    d_query, d_keys, d_values, d_keys_far, d_values_far = attend_back(
        query, keys, values, d_mixed, logs, cosine, sine, key_cosine, key_sine
    )
    d_far = xor_narrow(jnp.concatenate([d_keys_far, d_values_far], axis=1), 1)
    d_far = jnp.concatenate(
        [
            d_far[:, kind * width + (s ^ 1) * heads_width : kind * width + ((s ^ 1) + 1) * heads_width]
            for kind in range(2)
            for s in range(narrow)
        ],
        axis=1,
    ).astype(F32)
    d_projected = jnp.concatenate(
        [
            d_query,
            (d_keys + d_far[:, :width]).astype(BF),
            (d_values + d_far[:, width:]).astype(BF),
        ],
        axis=1,
    )
    d_qkv = mm(hidden_one, d_projected, TN)
    d_a = [
        jnp.concatenate(
            [
                d_qkv[:, kind * width + s * heads_width : kind * width + (s + 1) * heads_width]
                for kind in range(3)
            ]
            + [d_proj[:, s * heads_width : (s + 1) * heads_width]],
            axis=1,
        )
        for s in range(narrow)
    ]
    d_a = scatter_wide(scatter_narrow(d_a).reshape(wide, share, width))
    d_hidden_one = mm(d_projected, weight_qkv, NT)
    d_shift_one = jnp.sum(d_hidden_one, axis=0)
    d_one_normed = jnp.sum(d_hidden_one * normed_one, axis=0)
    d_scale_one = d_one_normed * gain_one
    d_gain_one = d_one_normed * (1.0 + scale_one)
    d_start = d_middle + norm_back(
        d_hidden_one * gain_one * (1.0 + scale_one), normed_one, inverse_one
    )

    padded = rows + 16
    mask_entry = vocab - 1
    my_inputs = lax.dynamic_slice_in_dim(
        lax.dynamic_index_in_dim(inputs, micro, 0, keepdims=False), part * rows, rows, axis=0
    )
    mask_sum = jnp.sum(jnp.where((my_inputs == mask_entry)[:, None], d_start, 0.0), axis=0)
    d_start_rows = jnp.concatenate(
        [d_start, mask_sum[None], jnp.zeros((padded - rows - 1, width), F32)]
    ).astype(BF)
    d_start_recv = swap_wide(d_start_rows.reshape(padded, wide, share).transpose(1, 0, 2))
    d_start_all = jnp.stack(gather_narrow(d_start_recv.reshape(wide * padded, share)))
    ids = jnp.stack(
        [
            lax.dynamic_slice_in_dim(
                lax.dynamic_index_in_dim(inputs_all, (group ^ s) >> 1, 1, keepdims=False),
                ((group ^ s) & 1) * rows,
                rows,
                axis=1,
            )
            for s in range(narrow)
        ]
    )
    ids = jnp.concatenate(
        [
            jnp.where(ids == mask_entry, -1, ids),
            jnp.full((narrow, wide, 1), mask_entry, jnp.int32),
            jnp.full((narrow, wide, padded - rows - 1), -1, jnp.int32),
        ],
        axis=2,
    ).reshape(narrow, wide * padded)
    local_ids = ids - group * entries
    here = (local_ids >= 0) & (local_ids < entries)
    shift = (wide * padded - 1).bit_length()
    sort_keys = jnp.where(
        here,
        local_ids * (1 << shift) + jnp.arange(wide * padded, dtype=jnp.int32)[None, :],
        jnp.iinfo(jnp.int32).max,
    )
    sort_keys = lax.sort(sort_keys, dimension=1)
    hits = jnp.sum(here.astype(jnp.int32), axis=1)
    d_embed = collect(sort_keys, hits, d_start_all, shift, entries)

    d_modulation = jnp.concatenate(
        (
            d_shift_one, d_scale_one, d_gate_one, d_shift_two, d_scale_two, d_gate_two,
            d_shift_last, d_scale_last,
        )
    )
    d_vector = jnp.concatenate((d_gain_one, d_gain_two, d_gain_last, d_bias, d_modulation))
    small = jnp.concatenate(
        [d_modulation.reshape(wide, -1), d_vector.reshape(wide, -1)], axis=1
    )
    small = swap_wide(small)
    small = small + xor_narrow(small, 1)
    small_far = xor_narrow(small, 2)
    d_vectors = jnp.sum(small[:, mod_share:] + small_far[:, mod_share:], axis=0)
    condition_far = lax.dynamic_index_in_dim(condition, 1 - micro, 1, keepdims=False)
    d_mod_weight = lax.dot_general(
        condition_mine, small[:, :mod_share], TN, precision=HIGHEST
    ) + lax.dot_general(condition_far, small_far[:, :mod_share], TN, precision=HIGHEST)

    shards = (
        d_embed,
        d_table,
        jnp.stack([d_a[:, k * heads_width : (k + 1) * heads_width] for k in range(3)]),
        d_a[:, 3 * heads_width :].T,
        d_b,
        d_c.T,
        d_mod_weight,
        d_vectors,
    )

    square = jnp.zeros((), F32)
    for grad in shards[:6]:
        square = square + jnp.sum(grad * grad)
    shared_square = jnp.sum(shards[6] * shards[6]) + jnp.sum(shards[7] * shards[7])
    square = square + shared_square / narrow
    sums = lax.all_to_all(
        jnp.broadcast_to(jnp.stack([loss_part / wide, square])[None, None], (wide * narrow, 1, 2)),
        ("wide", "narrow"),
        0,
        0,
        tiled=True,
    )
    sums = jnp.sum(sums, axis=(0, 1))
    loss_sum = sums[0]
    grad_norm = jnp.sqrt(sums[1])
    factor = CLIP_NORM / jnp.maximum(grad_norm, CLIP_NORM)
    results = []
    for member in range(8):
        grad = shards[member] * factor
        first = BETA_ONE * firsts[member] + (1.0 - BETA_ONE) * grad
        second = BETA_TWO * seconds[member] + (1.0 - BETA_TWO) * grad * grad
        stepped = (
            first / (1.0 - BETA_ONE**STEP) / (jnp.sqrt(second / (1.0 - BETA_TWO**STEP)) + ADAM_EPS)
        )
        decay = WEIGHT_DECAY if member < 7 else 0.0
        fresh = masters[member] - LEARN_RATES[member] * (stepped + decay * masters[member])
        results.extend([fresh, first, second])
    return (loss_sum, grad_norm, *results)


def solution(mesh):
    weights = (
        P("narrow", "wide"),
        P("wide", "narrow"),
        P(None, "wide", "narrow"),
        P("narrow", "wide"),
        P("wide", "narrow"),
        P("narrow", "wide"),
        P(None, "wide"),
        P("wide"),
    )
    data = (P("wide", None, None), P("wide", None, None), P("wide", None))
    outs = [P(), P()]
    for spec in weights:
        outs.extend([spec] * 3)
    return jax.shard_map(
        local,
        mesh=mesh,
        in_specs=data + weights * 3,
        out_specs=tuple(outs),
        check_vma=False,
    )
```

time: 3450 us -> 1130 us (0.33)
  waiting for transfers between devices: 2500 us -> 182 us
  blocking collectives: 261 us -> 0 us
  local copies, waits for them, and re-layouts: 203 us -> 353 us
  starting transfers between devices: 1.54 us -> 143 us
  Pallas kernels: 0 us -> 95 us
  matrix products: 230 us -> 138 us
  other arithmetic: 209 us -> 173 us
    all_gather x5 -> x0, waiting for transfers between devices: 737 us -> none  [the longest x1 362 us: local(): lax.all_gather(out_table.astype(jnp.bfloat16), 'wide', axis=0, tiled=True)]
    reduce_scatter x4 -> x0, waiting for transfers between devices: 714 us -> none  [the longest x1 616 us: reduce_wide(): lax.psum_scatter(grads[1], 'wide', scatter_dimension=0, tiled=True)]
    unnamed x21 -> x0, waiting for transfers between devices: 683 us -> none
    psum x6 -> x0, waiting for transfers between devices: 368 us -> none  [the longest x1 117 us: layer_forward(): lax.psum(jnp.dot(mixed, proj_copy, preferred_element_type=jnp.float32), '...]
    all_gather x9 -> x0, blocking collectives: 183 us -> none  [the longest x1 90.4 us: local(): lax.all_gather(qkv_weight.astype(jnp.bfloat16), 'wide', axis=1, tiled=True)]
    ppermute x0 -> x71, waiting for transfers between devices: none -> 150 us  [the longest x40 104 us: xor_wide(): lax.ppermute(value, 'wide', [(i, i ^ bits) for i in range(lax.axis_size('...]
    pallas_call x0 -> x5, Pallas kernels: none -> 95 us  [the longest x1 33 us: collect(): pl.pallas_call(functools.partial(collect_kernel, shift), grid=(parts,), i...]
    ppermute x0 -> x71, starting transfers between devices: none -> 90.9 us  [the longest x40 75.1 us: xor_wide(): lax.ppermute(value, 'wide', [(i, i ^ bits) for i in range(lax.axis_size('...]
  transfers between devices with their start and end apart: 18 -> 80, of which waited for: 14 -> 21; matrix products, arithmetic and copies ran while one was open for 9% -> 47% of each run, Pallas kernels for 0% -> 9%
where the time goes in v1:
time: 1130 us; the launch traced here: 1110 us
  local copies, waits for them, and re-layouts  353 us (31%)
  waiting for transfers between devices  182 us (16%)
  other arithmetic  173 us (15%)
  starting transfers between devices  143 us (13%)
  matrix products  138 us (12%)
  Pallas kernels  95 us (8%)
  between operations  24.9 us (2%)
    dot_general x43, matrix products, mm(): return lax.dot_general(a, b, dims, preferred_element_type=F32)  135 us
    ppermute x40, waiting for transfers between devices, xor_wide(): lax.ppermute(value, 'wide', [(i, i ^ bits) for i in range(lax.axis_size('...  104 us
    dynamic_update_slice x14, local copies, waits for them, and re-layouts, swap_wide_async(): out = lax.dynamic_update_index_in_dim(out, pieces[k - 1], me ^ k, 0)  100 us
    ppermute x40, starting transfers between devices, xor_wide(): lax.ppermute(value, 'wide', [(i, i ^ bits) for i in range(lax.axis_size('...  75.1 us
    unnamed x430, local copies, waits for them, and re-layouts  64.7 us
    all_to_all x8, starting transfers between devices, swap_wide(): return lax.all_to_all(value, 'wide', 0, 0, tiled=True)  47 us
    ppermute x31, waiting for transfers between devices, xor_narrow(): lax.ppermute(value, 'narrow', [(i, i ^ bits) for i in range(lax.axis_size...  45.9 us
    sub x8, other arithmetic, local(): masters[member] - LEARN_RATES[member] * (stepped + decay * masters[member])  35.8 us
  transfers between devices with their start and end apart: 80, of which 21 were waited for; matrix products, arithmetic and copies ran while one was open for 47% of the time, Pallas kernels for 9%

profile of v1, /device:TPU:0, one launch (start us, length us, event | category | flops | bytes accessed | tf_op | source)
XLA Modules:
  0.0 1109.0 jit_solution(17246908355088196420)
XLA Ops:
  38.5 4.7 reshape.724
  45.2 5.8 constant_dynamic-slice_fusion.11
  62.9 4.6 copy.413
  96.3 14.6 %all-to-all-start.2 = ((f32[8,1,1920]{2,1,0:T(1,128)}), f32[8,1,1920]{2,1,0:T(1,128)S(1)}, u32[]{:S(2)}, u32[]{:S(2)}) async-start(f32[8,1,1920]{2,1,0:T(1,128)} %all_to_all.39), calls=%async_computation.2 | async-start | bytes 122880 | tf_op jit(solution)/shard_map/all_to_all | solution.py:36
  111.8 6.5 all-to-all-done.2
  141.4 4.6 copy.415
  146.0 18.7 %convert_bitcast_fusion.table_ref = f32[25472,96]{1,0:T(8,128)} fusion(bf16[96,12672]{0,1:T(8,128)(2,1)} %copy.415, bf16[96,12672]{0,1:T(8,128)(2,1)} %bitcast.377, bf16[25472]{0:T(1024)(128)(2,1)S(1)} %copy-done.110), kind=kLoop, calls=%fused_computation | loop fusion | flops 14671872 | bytes 14698240 | tf_op jit(solution)/shard_map/transpose | solution.py:470
  164.7 14.8 %lookup.1 = bf16[8192,96]{1,0:T(8,128)(2,1)} custom-call(s32[4,1,2048]{2,1,0:T(1,128)} %compare_select_fusion.5.id_ref, f32[25472,96]{1,0:T(8,128)} %convert_bitcast_fusion.table_ref), custom_call_target="tpu_custom_call" | custom-call | bytes 60000000 | tf_op jit(solution)/shard_map/lookup/pallas_call | solution.py:331
  192.4 12.4 %collective-permute-done.1 = bf16[8,512,96]{1,2,0:T(8,128)(2,1)} collective-permute-done((bf16[8,512,96]{1,2,0:T(8,128)(2,1)}, bf16[8,512,96]{1,2,0:T(8,128)(2,1)}, u32[]{:S(2)}, u32[]{:S(2)}) %collective-permute-start.1) | collective-permute-done | bytes 786464 | tf_op jit(solution)/shard_map/ppermute | solution.py:28
  226.1 7.0 concatenate.142.weight_ref
  240.6 9.5 qkv.1
  263.1 20.3 %collective-permute-done.29 = bf16[96,1584]{1,0:T(8,128)(2,1)S(1)} collective-permute-done((bf16[96,1584]{1,0:T(8,128)(2,1)S(1)}, bf16[96,1584]{1,0:T(8,128)(2,1)S(1)}, u32[]{:S(2)}, u32[]{:S(2)}) %collective-permute-start.29) | collective-permute-done | bytes 304160 | tf_op jit(solution)/shard_map/ppermute | solution.py:32
  286.3 11.9 %collective-permute-done.30 = bf16[96,1584]{1,0:T(8,128)(2,1)S(1)} collective-permute-done((bf16[96,1584]{1,0:T(8,128)(2,1)S(1)}, bf16[96,1584]{1,0:T(8,128)(2,1)S(1)}, u32[]{:S(2)}, u32[]{:S(2)}) %collective-permute-start.30) | collective-permute-done | bytes 304160 | tf_op jit(solution)/shard_map/ppermute | solution.py:32
  315.0 13.7 %dynamic_update_slice.140 = bf16[8,96,1584]{2,0,1:T(8,128)(2,1)S(1)} dynamic-update-slice(bf16[8,96,1584]{2,0,1:T(8,128)(2,1)S(1)} %bitcast.374, bf16[1,96,1584]{2,0,1:T(2,128)(2,1)} %copy.423, s32[]{:T(128)S(6)} %select_n.316, s32[]{:T(128)} %constant.520.clone.1, s32[]{:T(128)} %constant.520.clone.1) | dynamic-update-slice | bytes 608260 | tf_op jit(solution)/shard_map/jit(dynamic_update_index_in_dim)/dynamic_update_slice | solution.py:56
  328.7 13.7 %dynamic_update_slice.141 = bf16[8,96,1584]{2,0,1:T(8,128)(2,1)S(1)} dynamic-update-slice(bf16[8,96,1584]{2,0,1:T(8,128)(2,1)S(1)} %dynamic_update_slice.140, bf16[1,96,1584]{2,0,1:T(2,128)(2,1)} %copy.424, s32[]{:T(128)S(6)} %select_n.317, s32[]{:T(128)} %constant.520.clone.1, s32[]{:T(128)} %constant.520.clone.1) | dynamic-update-slice | bytes 608260 | tf_op jit(solution)/shard_map/jit(dynamic_update_index_in_dim)/dynamic_update_slice | solution.py:56
  342.4 13.7 %dynamic_update_slice.142 = bf16[8,96,1584]{2,0,1:T(8,128)(2,1)S(1)} dynamic-update-slice(bf16[8,96,1584]{2,0,1:T(8,128)(2,1)S(1)} %dynamic_update_slice.141, bf16[1,96,1584]{2,0,1:T(2,128)(2,1)} %copy.425, s32[]{:T(128)S(6)} %select_n.318, s32[]{:T(128)} %constant.520.clone.1, s32[]{:T(128)} %constant.520.clone.1) | dynamic-update-slice | bytes 608260 | tf_op jit(solution)/shard_map/jit(dynamic_update_index_in_dim)/dynamic_update_slice | solution.py:56
  356.2 13.7 %dynamic_update_slice.143 = bf16[8,96,1584]{2,0,1:T(8,128)(2,1)S(1)} dynamic-update-slice(bf16[8,96,1584]{2,0,1:T(8,128)(2,1)S(1)} %dynamic_update_slice.142, bf16[1,96,1584]{2,0,1:T(2,128)(2,1)} %copy.426, s32[]{:T(128)S(6)} %select_n.319, s32[]{:T(128)} %constant.520.clone.1, s32[]{:T(128)} %constant.520.clone.1) | dynamic-update-slice | bytes 608260 | tf_op jit(solution)/shard_map/jit(dynamic_update_index_in_dim)/dynamic_update_slice | solution.py:56
  369.9 12.3 %dynamic_update_slice.144 = bf16[8,96,1584]{2,0,1:T(8,128)(2,1)S(1)} dynamic-update-slice(bf16[8,96,1584]{2,0,1:T(8,128)(2,1)S(1)} %dynamic_update_slice.143, bf16[1,96,1584]{2,0,1:T(2,128)(2,1)S(1)} %copy.427, s32[]{:T(128)S(6)} %select_n.320, s32[]{:T(128)} %constant.520.clone.1, s32[]{:T(128)} %constant.520.clone.1) | dynamic-update-slice | bytes 608260 | tf_op jit(solution)/shard_map/jit(dynamic_update_index_in_dim)/dynamic_update_slice | solution.py:56
  382.3 13.7 %dynamic_update_slice.145 = bf16[8,96,1584]{2,0,1:T(8,128)(2,1)S(1)} dynamic-update-slice(bf16[8,96,1584]{2,0,1:T(8,128)(2,1)S(1)} %dynamic_update_slice.144, bf16[1,96,1584]{2,0,1:T(2,128)(2,1)} %copy.428, s32[]{:T(128)S(6)} %select_n.321, s32[]{:T(128)} %constant.520.clone.1, s32[]{:T(128)} %constant.520.clone.1) | dynamic-update-slice | bytes 608260 | tf_op jit(solution)/shard_map/jit(dynamic_update_index_in_dim)/dynamic_update_slice | solution.py:56
  396.0 12.3 %dynamic_update_slice.146 = bf16[8,96,1584]{2,0,1:T(8,128)(2,1)S(1)} dynamic-update-slice(bf16[8,96,1584]{2,0,1:T(8,128)(2,1)S(1)} %dynamic_update_slice.145, bf16[1,96,1584]{2,0,1:T(2,128)(2,1)S(1)} %copy-done.42, s32[]{:T(128)S(6)} %select_n.322, s32[]{:T(128)} %constant.520.clone.1, s32[]{:T(128)} %constant.520.clone.1) | dynamic-update-slice | bytes 608260 | tf_op jit(solution)/shard_map/jit(dynamic_update_index_in_dim)/dynamic_update_slice | solution.py:56
  410.1 4.9 copy.431
  423.8 14.5 %attend.1 = (bf16[512,768]{1,0:T(8,128)(2,1)}, f32[6,2,512]{2,1,0:T(2,128)}) custom-call(bf16[512,768]{1,0:T(8,128)(2,1)} %get-tuple-element.361.q_ref, bf16[1024,768]{1,0:T(8,128)(2,1)} %maximum_maximum_fusion.k_ref, bf16[1024,768]{1,0:T(8,128)(2,1)} %maximum_maximum_fusion.1.v_ref), custom_call_target="tpu_custom_call" | custom-call | flops 6442450944 | bytes 5000000 | tf_op jit(solution)/shard_map/attend/pallas_call | solution.py:233
  465.4 6.8 collective-permute-start.25
  473.4 5.1 collective-permute-done.25
  479.5 4.4 all-to-all-start.3
  494.5 14.0 %all-to-all-done.3 = bf16[8,80,768]{2,1,0:T(8,128)(2,1)} async-done(((bf16[8,80,768]{2,1,0:T(8,128)(2,1)}), bf16[8,80,768]{2,1,0:T(8,128)(2,1)}, u32[]{:S(2)}, u32[]{:S(2)}) %all-to-all-start.3) | async-done | bytes 983072 | tf_op jit(solution)/shard_map/all_to_all | solution.py:36
  512.7 5.7 fusion.173
  518.4 4.2 fusion.172
  522.6 5.6 fusion.170
  528.4 4.6 exponential_reduce_fusion
  546.7 5.7 fusion.124
  560.7 5.2 add_convert_fusion
  565.9 4.4 all-to-all-start.5
  575.0 12.2 %sort.9.cloned.1.call-done = s32[4,4224]{1,0:T(4,128)} async-done(((s32[4,4224]{1,0:T(4,128)}), s32[4,4224]{1,0:T(4,128)}) %sort.9.cloned.1.call-update) | async-done | bytes 67600 | tf_op jit(solution)/shard_map/sort | solution.py:706
  588.8 6.4 fusion.19
  600.0 5.1 fusion.20
  645.5 23.3 %attend_back.1 = (bf16[512,768]{1,0:T(8,128)(2,1)}, f32[512,768]{1,0:T(8,128)}, f32[512,768]{1,0:T(8,128)}, bf16[512,768]{1,0:T(8,128)(2,1)}, bf16[512,768]{1,0:T(8,128)(2,1)}) custom-call(bf16[512,768]{1,0:T(8,128)(2,1)} %get-tuple-element.361.q_ref, bf16[1024,768]{1,0:T(8,128)(2,1)} %maximum_maximum_fusion.k_ref, ...), custom_call_target="tpu_custom_call" | custom-call | flops 16106127360 | bytes 10000000 | tf_op jit(solution)/shard_map/attend_back/pallas_call | solution.py:288
  695.2 6.2 fusion.175
  704.4 5.8 all-to-all-start.7
  722.6 6.1 all-to-all-start.6
  744.2 9.6 all-to-all-done.6
  758.3 5.2 collective-permute-done.64
  767.8 20.9 %collective-permute-done.58 = bf16[768,768]{1,0:T(8,128)(2,1)} collective-permute-done((bf16[768,768]{1,0:T(8,128)(2,1)}, bf16[768,768]{1,0:T(8,128)(2,1)}, u32[]{:S(2)}, u32[]{:S(2)}) %collective-permute-start.58) | collective-permute-done | bytes 1179680 | tf_op jit(solution)/shard_map/ppermute | solution.py:28
  793.0 5.6 fusion.4
  800.0 6.1 collective-permute-done.40
  819.4 6.6 collective-permute-done.67
  839.8 5.9 collective-permute-done.61
  854.1 33.0 %collect.1 = f32[12672,96]{1,0:T(8,128)} custom-call(s32[4,1,4224]{2,1,0:T(1,128)} %reshape.727.key_ref, s32[4,1,1]{2,1,0:T(1,128)} %copy.444.count_ref, bf16[4,4224,96]{2,1,0:T(8,128)(2,1)} %pad_maximum_fusion.1.grad_ref), custom_call_target="tpu_custom_call" | custom-call | bytes 60000000 | tf_op jit(solution)/shard_map/collect/pallas_call | solution.py:368
  891.2 7.1 fusion.6
  902.9 4.3 multiply_reduce_fusion
  926.9 9.6 collective-permute-done.45
  947.9 15.6 %collective-permute-done.48 = bf16[96,1584]{1,0:T(8,128)(2,1)} collective-permute-done((bf16[96,1584]{1,0:T(8,128)(2,1)}, bf16[96,1584]{1,0:T(8,128)(2,1)}, u32[]{:S(2)}, u32[]{:S(2)}) %collective-permute-start.48) | collective-permute-done | bytes 304160 | tf_op jit(solution)/shard_map/ppermute | solution.py:32
  970.1 19.2 %collective-permute-done.55 = bf16[96,768]{0,1:T(8,128)(2,1)} collective-permute-done((bf16[96,768]{0,1:T(8,128)(2,1)}, bf16[96,768]{0,1:T(8,128)(2,1)}, u32[]{:S(2)}, u32[]{:S(2)}) %collective-permute-start.55) | collective-permute-done | bytes 147488 | tf_op jit(solution)/shard_map/ppermute | solution.py:32
  995.8 5.6 all-to-all-start.8
  1002.5 6.4 copy.458
  1011.8 6.5 copy.454
  1018.3 6.4 copy.456
  1032.3 7.7 copy.459
  1040.0 5.7 mul.1082
  1045.7 17.4 %add_subtract_fusion = (f32[12672,96]{1,0:T(8,128)}, f32[12672,96]{1,0:T(8,128)}, f32[12672,96]{1,0:T(8,128)}) fusion(f32[12672,96]{1,0:T(8,128)} %copy.458, f32[12672,96]{1,0:T(8,128)} %collect.1, f32[]{:T(128)S(6)} %div.230, f32[12672,96]{1,0:T(8,128)} %copy.454, f32[12672,96]{1,0:T(8,128)} %copy.456), kind=kLoop, calls=%fused_computation.4 | loop fusion | flops 18247680 | bytes 34062340 | tf_op jit(solution)/shard_map/sub | solution.py:765
  1063.1 6.3 copy.464
  1069.4 6.3 copy.465
  1075.8 6.4 copy.466
  1087.4 13.4 %multiply_subtract_fusion = (f32[96,12672]{1,0:T(8,128)}, f32[96,12672]{1,0:T(8,128)}, f32[96,12672]{1,0:T(8,128)}) fusion(f32[96,12672]{1,0:T(8,128)} %param.31, f32[96,12672]{1,0:T(8,128)} %mul.1082, f32[96,12672]{1,0:T(8,128)} %param.39, f32[96,12672]{1,0:T(8,128)} %param.47), kind=kLoop, calls=%fused_computation.24 | loop fusion | flops 18247680 | bytes 34062336 | tf_op jit(solution)/shard_map/sub | solution.py:765
  (860 shorter events, 468.7 us)
Async XLA Ops:
  10.1 44.6 %collective-permute-start.2 = (bf16[96,768]{1,0:T(8,128)(2,1)}, bf16[96,768]{1,0:T(8,128)(2,1)}, u32[]{:S(2)}, u32[]{:S(2)}) collective-permute-start(bf16[96,768]{1,0:T(8,128)(2,1)} %pad_maximum_fusion.17), channel_id=1, source_target_pairs={{0,8},{4,12},{8,0},{12,4},{16,24},{20,28},{24,16},{28,20},{1,9},{5... | collective-permute-start | bytes 442376 | tf_op jit(solution)/shard_map/ppermute | solution.py:32
  13.1 62.6 %collective-permute-start.3 = (bf16[96,768]{1,0:T(8,128)(2,1)}, bf16[96,768]{1,0:T(8,128)(2,1)}, u32[]{:S(2)}, u32[]{:S(2)}) collective-permute-start(bf16[96,768]{1,0:T(8,128)(2,1)} %pad_maximum_fusion.17), channel_id=1, source_target_pairs={{0,16},{4,20},{8,24},{12,28},{16,0},{20,4},{24,8},{28,12},{1,17},{... | collective-permute-start | bytes 442376 | tf_op jit(solution)/shard_map/ppermute | solution.py:32
  15.7 60.0 %collective-permute-start.4 = (bf16[96,768]{1,0:T(8,128)(2,1)}, bf16[96,768]{1,0:T(8,128)(2,1)}, u32[]{:S(2)}, u32[]{:S(2)}) collective-permute-start(bf16[96,768]{1,0:T(8,128)(2,1)} %pad_maximum_fusion.17), channel_id=1, source_target_pairs={{0,24},{4,28},{8,16},{12,20},{16,8},{20,12},{24,0},{28,4},{1,25},{... | collective-permute-start | bytes 442376 | tf_op jit(solution)/shard_map/ppermute | solution.py:32
  17.5 58.8 %collective-permute-start.10 = (bf16[96,768]{1,0:T(8,128)(2,1)}, bf16[96,768]{1,0:T(8,128)(2,1)}, u32[]{:S(2)}, u32[]{:S(2)}) collective-permute-start(bf16[96,768]{1,0:T(8,128)(2,1)} %get-tuple-element.322), channel_id=1, source_target_pairs={{0,8},{4,12},{8,0},{12,4},{16,24},{20,28},{24,16},{28,20},{1,9},{5... | collective-permute-start | bytes 442376 | tf_op jit(solution)/shard_map/ppermute | solution.py:32
  18.4 63.6 %collective-permute-start.11 = (bf16[96,768]{1,0:T(8,128)(2,1)}, bf16[96,768]{1,0:T(8,128)(2,1)S(1)}, u32[]{:S(2)}, u32[]{:S(2)}) collective-permute-start(bf16[96,768]{1,0:T(8,128)(2,1)} %get-tuple-element.322), channel_id=1, source_target_pairs={{0,16},{4,20},{8,24},{12,28},{16,0},{20,4},{24,8},{28,12},{1,17},{... | collective-permute-start | bytes 442376 | tf_op jit(solution)/shard_map/ppermute | solution.py:32
  23.7 67.4 %all-to-all-start = ((s32[8,2,1408]{2,1,0:T(2,128)}), s32[8,2,1408]{2,1,0:T(2,128)}, u32[]{:S(2)}, u32[]{:S(2)}) async-start(s32[8,2,1408]{2,1,0:T(2,128)} %broadcast_in_dim.272), calls=%async_computation | async-start | bytes 180224 | tf_op jit(solution)/shard_map/all_to_all | solution.py:36
  54.6 27.5 %collective-permute-start.12 = (bf16[96,768]{1,0:T(8,128)(2,1)}, bf16[96,768]{1,0:T(8,128)(2,1)}, u32[]{:S(2)}, u32[]{:S(2)}) collective-permute-start(bf16[96,768]{1,0:T(8,128)(2,1)} %get-tuple-element.322), channel_id=1, source_target_pairs={{0,24},{4,28},{8,16},{12,20},{16,8},{20,12},{24,0},{28,4},{1,25},{... | collective-permute-start | bytes 442376 | tf_op jit(solution)/shard_map/ppermute | solution.py:32
  82.0 59.4 %collective-permute-start = (bf16[96,12672]{1,0:T(8,128)(2,1)}, bf16[96,12672]{1,0:T(8,128)(2,1)}, u32[]{:S(2)}, u32[]{:S(2)}) collective-permute-start(bf16[96,12672]{1,0:T(8,128)(2,1)} %convert_bitcast_fusion.6), channel_id=1, source_target_pairs={{0,1},{1,0},{2,3},{3,2},{4,5},{5,4},{6,7},{7,6},{8,9},{9,8},{10,11... | collective-permute-start | bytes 7299080 | tf_op jit(solution)/shard_map/ppermute | solution.py:28
  82.1 173.3 %collective-permute-start.26 = (bf16[96,1584]{1,0:T(8,128)(2,1)}, bf16[96,1584]{1,0:T(8,128)(2,1)}, u32[]{:S(2)}, u32[]{:S(2)}) collective-permute-start(bf16[96,1584]{1,0:T(8,128)(2,1)} %bitcast.368), channel_id=1, source_target_pairs={{0,4},{4,0},{8,12},{12,8},{16,20},{20,16},{24,28},{28,24},{1,5},{5... | collective-permute-start | bytes 912392 | tf_op jit(solution)/shard_map/ppermute | solution.py:32
  85.6 172.7 %collective-permute-start.27 = (bf16[96,1584]{1,0:T(8,128)(2,1)}, bf16[96,1584]{1,0:T(8,128)(2,1)}, u32[]{:S(2)}, u32[]{:S(2)}) collective-permute-start(bf16[96,1584]{1,0:T(8,128)(2,1)} %bitcast.367), channel_id=1, source_target_pairs={{0,8},{4,12},{8,0},{12,4},{16,24},{20,28},{24,16},{28,20},{1,9},{5... | collective-permute-start | bytes 912392 | tf_op jit(solution)/shard_map/ppermute | solution.py:32
  88.2 30.8 %collective-permute-start.5 = (bf16[4,96,768]{2,1,0:T(8,128)(2,1)}, bf16[4,96,768]{2,1,0:T(8,128)(2,1)}, u32[]{:S(2)}, u32[]{:S(2)}) collective-permute-start(bf16[4,96,768]{2,1,0:T(8,128)(2,1)} %pad_maximum_fusion.10), channel_id=1, source_target_pairs={{0,4},{4,0},{8,12},{12,8},{16,20},{20,16},{24,28},{28,24},{1,5},{5... | collective-permute-start | bytes 1769480 | tf_op jit(solution)/shard_map/ppermute | solution.py:32
  89.8 41.8 %collective-permute-start.13 = (bf16[4,96,768]{2,1,0:T(8,128)(2,1)}, bf16[4,96,768]{2,1,0:T(8,128)(2,1)}, u32[]{:S(2)}, u32[]{:S(2)}) collective-permute-start(bf16[4,96,768]{2,1,0:T(8,128)(2,1)} %pad_maximum_fusion.11), channel_id=1, source_target_pairs={{0,4},{4,0},{8,12},{12,8},{16,20},{20,16},{24,28},{28,24},{1,5},{5... | collective-permute-start | bytes 1769480 | tf_op jit(solution)/shard_map/ppermute | solution.py:32
  96.3 21.9 %all-to-all-start.2 = ((f32[8,1,1920]{2,1,0:T(1,128)}), f32[8,1,1920]{2,1,0:T(1,128)S(1)}, u32[]{:S(2)}, u32[]{:S(2)}) async-start(f32[8,1,1920]{2,1,0:T(1,128)} %all_to_all.39), calls=%async_computation.2 | async-start | bytes 122880 | tf_op jit(solution)/shard_map/all_to_all | solution.py:36
  119.0 15.2 %collective-permute-start.17 = (bf16[4,96,768]{2,1,0:T(8,128)(2,1)}, bf16[4,96,768]{2,1,0:T(8,128)(2,1)S(1)}, u32[]{:S(2)}, u32[]{:S(2)}) collective-permute-start(bf16[4,96,768]{2,1,0:T(8,128)(2,1)} %pad_maximum_fusion.12), channel_id=1, source_target_pairs={{0,4},{4,0},{8,12},{12,8},{16,20},{20,16},{24,28},{28,24},{1,5},{5... | collective-permute-start | bytes 1769480 | tf_op jit(solution)/shard_map/ppermute | solution.py:32
  131.6 60.6 %collective-permute-start.7 = (bf16[768,768]{1,0:T(8,128)(2,1)}, bf16[768,768]{1,0:T(8,128)(2,1)}, u32[]{:S(2)}, u32[]{:S(2)}) collective-permute-start(bf16[768,768]{1,0:T(8,128)(2,1)} %bitcast.25), channel_id=1, source_target_pairs={{0,2},{1,3},{2,0},{3,1},{4,6},{5,7},{6,4},{7,5},{8,10},{9,11},{10,... | collective-permute-start | bytes 3538952 | tf_op jit(solution)/shard_map/ppermute | solution.py:28
  134.1 84.5 %collective-permute-start.6 = (bf16[768,768]{1,0:T(8,128)(2,1)}, bf16[768,768]{1,0:T(8,128)(2,1)}, u32[]{:S(2)}, u32[]{:S(2)}) collective-permute-start(bf16[768,768]{1,0:T(8,128)(2,1)} %bitcast.25), channel_id=1, source_target_pairs={{0,1},{1,0},{2,3},{3,2},{4,5},{5,4},{6,7},{7,6},{8,9},{9,8},{10,11... | collective-permute-start | bytes 3538952 | tf_op jit(solution)/shard_map/ppermute | solution.py:28
  184.7 20.1 %collective-permute-start.1 = (bf16[8,512,96]{1,2,0:T(8,128)(2,1)}, bf16[8,512,96]{1,2,0:T(8,128)(2,1)}, u32[]{:S(2)}, u32[]{:S(2)}) collective-permute-start(bf16[8,512,96]{1,2,0:T(8,128)(2,1)} %copy.416), channel_id=1, source_target_pairs={{0,2},{1,3},{2,0},{3,1},{4,6},{5,7},{6,4},{7,5},{8,10},{9,11},{10,... | collective-permute-start | bytes 2359304 | tf_op jit(solution)/shard_map/ppermute | solution.py:28
  192.2 68.8 %collective-permute-start.28 = (bf16[96,1584]{1,0:T(8,128)(2,1)}, bf16[96,1584]{1,0:T(8,128)(2,1)}, u32[]{:S(2)}, u32[]{:S(2)}) collective-permute-start(bf16[96,1584]{1,0:T(8,128)(2,1)} %bitcast.406), channel_id=1, source_target_pairs={{0,12},{4,8},{8,4},{12,0},{16,28},{20,24},{24,20},{28,16},{1,13},{... | collective-permute-start | bytes 912392 | tf_op jit(solution)/shard_map/ppermute | solution.py:32
  204.8 18.4 %collective-permute-start.8 = (bf16[768,768]{1,0:T(8,128)(2,1)}, bf16[768,768]{1,0:T(8,128)(2,1)}, u32[]{:S(2)}, u32[]{:S(2)}) collective-permute-start(bf16[768,768]{1,0:T(8,128)(2,1)} %collective-permute-done.7), channel_id=1, source_target_pairs={{0,1},{1,0},{2,3},{3,2},{4,5},{5,4},{6,7},{7,6},{8,9},{9,8},{10,11... | collective-permute-start | bytes 3538952 | tf_op jit(solution)/shard_map/ppermute | solution.py:28
  207.0 26.0 %all-to-all-start.1 = ((bf16[8,512,96]{1,2,0:T(8,128)(2,1)}), bf16[8,512,96]{1,2,0:T(8,128)(2,1)S(1)}, u32[]{:S(2)}, u32[]{:S(2)}) async-start(bf16[8,512,96]{1,2,0:T(8,128)(2,1)} %add.885), calls=%async_computation.1 | async-start | bytes 1572864 | tf_op jit(solution)/shard_map/all_to_all | solution.py:36
  218.6 199.1 %collective-permute-start.20 = (bf16[768,768]{1,0:T(8,128)(2,1)}, bf16[768,768]{1,0:T(8,128)(2,1)}, u32[]{:S(2)}, u32[]{:S(2)}) collective-permute-start(bf16[768,768]{1,0:T(8,128)(2,1)} %bitcast.30), channel_id=1, source_target_pairs={{0,2},{1,3},{2,0},{3,1},{4,6},{5,7},{6,4},{7,5},{8,10},{9,11},{10,... | collective-permute-start | bytes 3538952 | tf_op jit(solution)/shard_map/ppermute | solution.py:28
  252.8 165.4 %collective-permute-start.9 = (bf16[512,1536]{1,0:T(8,128)(2,1)}, bf16[512,1536]{1,0:T(8,128)(2,1)}, u32[]{:S(2)}, u32[]{:S(2)}) collective-permute-start(bf16[512,1536]{1,0:T(8,128)(2,1)} %slice.480), channel_id=1, source_target_pairs={{0,1},{1,0},{2,3},{3,2},{4,5},{5,4},{6,7},{7,6},{8,9},{9,8},{10,11... | collective-permute-start | bytes 4718600 | tf_op jit(solution)/shard_map/ppermute | solution.py:28
  255.4 162.8 %collective-permute-start.21 = (bf16[768,768]{1,0:T(8,128)(2,1)}, bf16[768,768]{1,0:T(8,128)(2,1)}, u32[]{:S(2)}, u32[]{:S(2)}) collective-permute-start(bf16[768,768]{1,0:T(8,128)(2,1)} %bitcast.37), channel_id=1, source_target_pairs={{0,2},{1,3},{2,0},{3,1},{4,6},{5,7},{6,4},{7,5},{8,10},{9,11},{10,... | collective-permute-start | bytes 3538952 | tf_op jit(solution)/shard_map/ppermute | solution.py:28
  258.4 25.0 %collective-permute-start.29 = (bf16[96,1584]{1,0:T(8,128)(2,1)S(1)}, bf16[96,1584]{1,0:T(8,128)(2,1)S(1)}, u32[]{:S(2)}, u32[]{:S(2)}) collective-permute-start(bf16[96,1584]{1,0:T(8,128)(2,1)S(1)} %bitcast.412), channel_id=1, source_target_pairs={{0,16},{4,20},{8,24},{12,28},{16,0},{20,4},{24,8},{28,12},{1,17},{... | collective-permute-start | bytes 912392 | tf_op jit(solution)/shard_map/ppermute | solution.py:32
  261.1 37.1 %collective-permute-start.30 = (bf16[96,1584]{1,0:T(8,128)(2,1)S(1)}, bf16[96,1584]{1,0:T(8,128)(2,1)S(1)}, u32[]{:S(2)}, u32[]{:S(2)}) collective-permute-start(bf16[96,1584]{1,0:T(8,128)(2,1)S(1)} %bitcast.411), channel_id=1, source_target_pairs={{0,20},{4,16},{8,28},{12,24},{16,4},{20,0},{24,12},{28,8},{1,21},{... | collective-permute-start | bytes 912392 | tf_op jit(solution)/shard_map/ppermute | solution.py:32
  283.4 28.9 %collective-permute-start.31 = (bf16[96,1584]{1,0:T(8,128)(2,1)S(1)}, bf16[96,1584]{1,0:T(8,128)(2,1)S(1)}, u32[]{:S(2)}, u32[]{:S(2)}) collective-permute-start(bf16[96,1584]{1,0:T(8,128)(2,1)S(1)} %bitcast.408), channel_id=1, source_target_pairs={{0,24},{4,28},{8,16},{12,20},{16,8},{20,12},{24,0},{28,4},{1,25},{... | collective-permute-start | bytes 912392 | tf_op jit(solution)/shard_map/ppermute | solution.py:32
  298.2 15.5 %collective-permute-start.32 = (bf16[96,1584]{1,0:T(8,128)(2,1)S(1)}, bf16[96,1584]{1,0:T(8,128)(2,1)S(1)}, u32[]{:S(2)}, u32[]{:S(2)}) collective-permute-start(bf16[96,1584]{1,0:T(8,128)(2,1)S(1)} %bitcast.407), channel_id=1, source_target_pairs={{0,28},{4,24},{8,20},{12,16},{16,12},{20,8},{24,4},{28,0},{1,29},{... | collective-permute-start | bytes 912392 | tf_op jit(solution)/shard_map/ppermute | solution.py:32
  415.1 72.8 %collective-permute-start.34 = (bf16[768,1584]{0,1:T(8,128)(2,1)}, bf16[768,1584]{0,1:T(8,128)(2,1)}, u32[]{:S(2)}, u32[]{:S(2)}) collective-permute-start(bf16[768,1584]{0,1:T(8,128)(2,1)} %copy.431), channel_id=1, source_target_pairs={{0,2},{1,3},{2,0},{3,1},{4,6},{5,7},{6,4},{7,5},{8,10},{9,11},{10,... | collective-permute-start | bytes 7299080 | tf_op jit(solution)/shard_map/ppermute | solution.py:28
  416.6 30.9 %collective-permute-start.18 = (bf16[768,768]{1,0:T(8,128)(2,1)}, bf16[768,768]{1,0:T(8,128)(2,1)S(1)}, u32[]{:S(2)}, u32[]{:S(2)}) collective-permute-start(bf16[768,768]{1,0:T(8,128)(2,1)} %bitcast.30), channel_id=1, source_target_pairs={{0,1},{1,0},{2,3},{3,2},{4,5},{5,4},{6,7},{7,6},{8,9},{9,8},{10,11... | collective-permute-start | bytes 3538952 | tf_op jit(solution)/shard_map/ppermute | solution.py:28
  417.7 37.4 %collective-permute-start.19 = (bf16[768,768]{1,0:T(8,128)(2,1)}, bf16[768,768]{1,0:T(8,128)(2,1)}, u32[]{:S(2)}, u32[]{:S(2)}) collective-permute-start(bf16[768,768]{1,0:T(8,128)(2,1)} %bitcast.37), channel_id=1, source_target_pairs={{0,1},{1,0},{2,3},{3,2},{4,5},{5,4},{6,7},{7,6},{8,9},{9,8},{10,11... | collective-permute-start | bytes 3538952 | tf_op jit(solution)/shard_map/ppermute | solution.py:28
  418.2 30.5 %collective-permute-start.22 = (bf16[768,768]{1,0:T(8,128)(2,1)}, bf16[768,768]{1,0:T(8,128)(2,1)S(1)}, u32[]{:S(2)}, u32[]{:S(2)}) collective-permute-start(bf16[768,768]{1,0:T(8,128)(2,1)} %collective-permute-done.20), channel_id=1, source_target_pairs={{0,1},{1,0},{2,3},{3,2},{4,5},{5,4},{6,7},{7,6},{8,9},{9,8},{10,11... | collective-permute-start | bytes 3538952 | tf_op jit(solution)/shard_map/ppermute | solution.py:28
  418.3 39.2 %collective-permute-start.23 = (bf16[768,768]{1,0:T(8,128)(2,1)}, bf16[768,768]{1,0:T(8,128)(2,1)S(1)}, u32[]{:S(2)}, u32[]{:S(2)}) collective-permute-start(bf16[768,768]{1,0:T(8,128)(2,1)} %collective-permute-done.21), channel_id=1, source_target_pairs={{0,1},{1,0},{2,3},{3,2},{4,5},{5,4},{6,7},{7,6},{8,9},{9,8},{10,11... | collective-permute-start | bytes 3538952 | tf_op jit(solution)/shard_map/ppermute | solution.py:28
  473.4 39.3 %collective-permute-start.33 = (bf16[768,1584]{0,1:T(8,128)(2,1)}, bf16[768,1584]{0,1:T(8,128)(2,1)}, u32[]{:S(2)}, u32[]{:S(2)}) collective-permute-start(bf16[768,1584]{0,1:T(8,128)(2,1)} %copy.431), channel_id=1, source_target_pairs={{0,1},{1,0},{2,3},{3,2},{4,5},{5,4},{6,7},{7,6},{8,9},{9,8},{10,11... | collective-permute-start | bytes 7299080 | tf_op jit(solution)/shard_map/ppermute | solution.py:28
  479.5 29.0 %all-to-all-start.3 = ((bf16[8,80,768]{2,1,0:T(8,128)(2,1)}), bf16[8,80,768]{2,1,0:T(8,128)(2,1)}, u32[]{:S(2)}, u32[]{:S(2)}) async-start(bf16[8,80,768]{2,1,0:T(8,128)(2,1)} %broadcast_in_dim.281), calls=%async_computation.3 | async-start | bytes 1966080 | tf_op jit(solution)/shard_map/all_to_all | solution.py:36
  487.8 34.8 %collective-permute-start.35 = (bf16[768,1584]{0,1:T(8,128)(2,1)}, bf16[768,1584]{0,1:T(8,128)(2,1)}, u32[]{:S(2)}, u32[]{:S(2)}) collective-permute-start(bf16[768,1584]{0,1:T(8,128)(2,1)} %collective-permute-done.34), channel_id=1, source_target_pairs={{0,1},{1,0},{2,3},{3,2},{4,5},{5,4},{6,7},{7,6},{8,9},{9,8},{10,11... | collective-permute-start | bytes 7299080 | tf_op jit(solution)/shard_map/ppermute | solution.py:28
  565.9 29.3 %all-to-all-start.5 = ((bf16[8,80,768]{2,1,0:T(8,128)(2,1)}), bf16[8,80,768]{2,1,0:T(8,128)(2,1)}, u32[]{:S(2)}, u32[]{:S(2)}) async-start(bf16[8,80,768]{2,1,0:T(8,128)(2,1)} %bitcast.395), calls=%async_computation.5 | async-start | bytes 1966080 | tf_op jit(solution)/shard_map/all_to_all | solution.py:36
  608.6 184.3 %collective-permute-start.42 = (bf16[2,768,1584]{1,2,0:T(8,128)(2,1)}, bf16[2,768,1584]{1,2,0:T(8,128)(2,1)}, u32[]{:S(2)}, u32[]{:S(2)}) collective-permute-start(bf16[2,768,1584]{1,2,0:T(8,128)(2,1)} %pad_maximum_fusion), channel_id=1, source_target_pairs={{0,1},{1,0},{2,3},{3,2},{4,5},{5,4},{6,7},{7,6},{8,9},{9,8},{10,11... | collective-permute-start | bytes 14598152 | tf_op jit(solution)/shard_map/ppermute | solution.py:28
  672.5 57.9 %collective-permute-start.63 = (bf16[2,768,768]{2,1,0:T(8,128)(2,1)}, bf16[2,768,768]{2,1,0:T(8,128)(2,1)}, u32[]{:S(2)}, u32[]{:S(2)}) collective-permute-start(bf16[2,768,768]{2,1,0:T(8,128)(2,1)} %pad_maximum_fusion.5), channel_id=1, source_target_pairs={{0,1},{1,0},{2,3},{3,2},{4,5},{5,4},{6,7},{7,6},{8,9},{9,8},{10,11... | collective-permute-start | bytes 7077896 | tf_op jit(solution)/shard_map/ppermute | solution.py:28
  674.3 61.4 %collective-permute-start.57 = (bf16[2,768,768]{2,1,0:T(8,128)(2,1)}, bf16[2,768,768]{2,1,0:T(8,128)(2,1)}, u32[]{:S(2)}, u32[]{:S(2)}) collective-permute-start(bf16[2,768,768]{2,1,0:T(8,128)(2,1)} %pad_maximum_fusion.4), channel_id=1, source_target_pairs={{0,1},{1,0},{2,3},{3,2},{4,5},{5,4},{6,7},{7,6},{8,9},{9,8},{10,11... | collective-permute-start | bytes 7077896 | tf_op jit(solution)/shard_map/ppermute | solution.py:28
  704.4 16.2 %all-to-all-start.7 = ((f32[8,1,1920]{2,1,0:T(1,128)}), f32[8,1,1920]{2,1,0:T(1,128)}, u32[]{:S(2)}, u32[]{:S(2)}) async-start(f32[8,1,1920]{2,1,0:T(1,128)} %all_to_all.46), calls=%async_computation.7 | async-start | bytes 122880 | tf_op jit(solution)/shard_map/all_to_all | solution.py:36
  716.1 98.8 %collective-permute-start.51 = (bf16[2,768,768]{2,1,0:T(8,128)(2,1)}, bf16[2,768,768]{2,1,0:T(8,128)(2,1)}, u32[]{:S(2)}, u32[]{:S(2)}) collective-permute-start(bf16[2,768,768]{2,1,0:T(8,128)(2,1)} %pad_maximum_fusion.3), channel_id=1, source_target_pairs={{0,1},{1,0},{2,3},{3,2},{4,5},{5,4},{6,7},{7,6},{8,9},{9,8},{10,11... | collective-permute-start | bytes 7077896 | tf_op jit(solution)/shard_map/ppermute | solution.py:28
  722.6 31.2 %all-to-all-start.6 = ((bf16[8,528,96]{1,2,0:T(8,128)(2,1)}), bf16[8,528,96]{1,2,0:T(8,128)(2,1)S(1)}, u32[]{:S(2)}, u32[]{:S(2)}) async-start(bf16[8,528,96]{1,2,0:T(8,128)(2,1)} %maximum_bitcast_fusion.2), calls=%async_computation.6 | async-start | bytes 1966080 | tf_op jit(solution)/shard_map/all_to_all | solution.py:36
  734.3 29.1 %collective-permute-start.64 = (bf16[768,768]{1,0:T(8,128)(2,1)}, bf16[768,768]{1,0:T(8,128)(2,1)}, u32[]{:S(2)}, u32[]{:S(2)}) collective-permute-start(bf16[768,768]{1,0:T(8,128)(2,1)} %fusion.23), channel_id=1, source_target_pairs={{0,2},{1,3},{2,0},{3,1},{4,6},{5,7},{6,4},{7,5},{8,10},{9,11},{10,... | collective-permute-start | bytes 3538952 | tf_op jit(solution)/shard_map/ppermute | solution.py:28
  738.8 49.9 %collective-permute-start.58 = (bf16[768,768]{1,0:T(8,128)(2,1)}, bf16[768,768]{1,0:T(8,128)(2,1)}, u32[]{:S(2)}, u32[]{:S(2)}) collective-permute-start(bf16[768,768]{1,0:T(8,128)(2,1)} %fusion.25), channel_id=1, source_target_pairs={{0,2},{1,3},{2,0},{3,1},{4,6},{5,7},{6,4},{7,5},{8,10},{9,11},{10,... | collective-permute-start | bytes 3538952 | tf_op jit(solution)/shard_map/ppermute | solution.py:28
  757.8 48.3 %collective-permute-start.40 = (bf16[4224,96]{0,1:T(8,128)(2,1)}, bf16[4224,96]{0,1:T(8,128)(2,1)}, u32[]{:S(2)}, u32[]{:S(2)}) collective-permute-start(bf16[4224,96]{0,1:T(8,128)(2,1)} %reshape.730), channel_id=1, source_target_pairs={{0,2},{1,3},{2,0},{3,1},{4,6},{5,7},{6,4},{7,5},{8,10},{9,11},{10,... | collective-permute-start | bytes 2433032 | tf_op jit(solution)/shard_map/ppermute | solution.py:28
  765.6 40.5 %collective-permute-start.65 = (bf16[4,96,768]{2,1,0:T(8,128)(2,1)S(1)}, bf16[4,96,768]{2,1,0:T(8,128)(2,1)S(1)}, u32[]{:S(2)}, u32[]{:S(2)}) collective-permute-start(bf16[4,96,768]{2,1,0:T(8,128)(2,1)S(1)} %fusion.76), channel_id=1, source_target_pairs={{0,4},{4,0},{8,12},{12,8},{16,20},{20,16},{24,28},{28,24},{1,5},{5... | collective-permute-start | bytes 1769480 | tf_op jit(solution)/shard_map/ppermute | solution.py:32
  790.8 17.6 %collective-permute-start.59 = (bf16[4,96,768]{2,1,0:T(8,128)(2,1)S(1)}, bf16[4,96,768]{2,1,0:T(8,128)(2,1)S(1)}, u32[]{:S(2)}, u32[]{:S(2)}) collective-permute-start(bf16[4,96,768]{2,1,0:T(8,128)(2,1)S(1)} %fusion.75), channel_id=1, source_target_pairs={{0,4},{4,0},{8,12},{12,8},{16,20},{20,16},{24,28},{28,24},{1,5},{5... | collective-permute-start | bytes 1769480 | tf_op jit(solution)/shard_map/ppermute | solution.py:32
  798.6 92.6 %collective-permute-start.43 = (bf16[768,1584]{0,1:T(8,128)(2,1)}, bf16[768,1584]{0,1:T(8,128)(2,1)}, u32[]{:S(2)}, u32[]{:S(2)}) collective-permute-start(bf16[768,1584]{0,1:T(8,128)(2,1)} %fusion.4), channel_id=1, source_target_pairs={{0,2},{1,3},{2,0},{3,1},{4,6},{5,7},{6,4},{7,5},{8,10},{9,11},{10,... | collective-permute-start | bytes 7299080 | tf_op jit(solution)/shard_map/ppermute | solution.py:28
  806.1 42.0 %collective-permute-start.41 = (bf16[4224,96]{0,1:T(8,128)(2,1)}, bf16[4224,96]{0,1:T(8,128)(2,1)}, u32[]{:S(2)}, u32[]{:S(2)}) collective-permute-start(bf16[4224,96]{0,1:T(8,128)(2,1)} %collective-permute-done.40), channel_id=1, source_target_pairs={{0,1},{1,0},{2,3},{3,2},{4,5},{5,4},{6,7},{7,6},{8,9},{9,8},{10,11... | collective-permute-start | bytes 2433032 | tf_op jit(solution)/shard_map/ppermute | solution.py:28
  812.5 13.4 %collective-permute-start.67 = (bf16[96,768]{1,0:T(8,128)(2,1)S(1)}, bf16[96,768]{1,0:T(8,128)(2,1)S(1)}, u32[]{:S(2)}, u32[]{:S(2)}) collective-permute-start(bf16[96,768]{1,0:T(8,128)(2,1)S(1)} %get-tuple-element.400), channel_id=1, source_target_pairs={{0,16},{4,20},{8,24},{12,28},{16,0},{20,4},{24,8},{28,12},{1,17},{... | collective-permute-start | bytes 442376 | tf_op jit(solution)/shard_map/ppermute | solution.py:32
  814.9 19.4 %collective-permute-start.68 = (bf16[96,768]{1,0:T(8,128)(2,1)}, bf16[96,768]{1,0:T(8,128)(2,1)}, u32[]{:S(2)}, u32[]{:S(2)}) collective-permute-start(bf16[96,768]{1,0:T(8,128)(2,1)} %get-tuple-element.399), channel_id=1, source_target_pairs={{0,24},{4,28},{8,16},{12,20},{16,8},{20,12},{24,0},{28,4},{1,25},{... | collective-permute-start | bytes 442376 | tf_op jit(solution)/shard_map/ppermute | solution.py:32
  815.0 19.5 %collective-permute-start.60 = (bf16[96,768]{1,0:T(8,128)(2,1)}, bf16[96,768]{1,0:T(8,128)(2,1)}, u32[]{:S(2)}, u32[]{:S(2)}) collective-permute-start(bf16[96,768]{1,0:T(8,128)(2,1)} %get-tuple-element.401), channel_id=1, source_target_pairs={{0,8},{4,12},{8,0},{12,4},{16,24},{20,28},{24,16},{28,20},{1,9},{5... | collective-permute-start | bytes 442376 | tf_op jit(solution)/shard_map/ppermute | solution.py:32
  826.6 60.4 %collective-permute-start.52 = (bf16[768,768]{1,0:T(8,128)(2,1)}, bf16[768,768]{1,0:T(8,128)(2,1)}, u32[]{:S(2)}, u32[]{:S(2)}) collective-permute-start(bf16[768,768]{1,0:T(8,128)(2,1)} %fusion.22), channel_id=1, source_target_pairs={{0,2},{1,3},{2,0},{3,1},{4,6},{5,7},{6,4},{7,5},{8,10},{9,11},{10,... | collective-permute-start | bytes 3538952 | tf_op jit(solution)/shard_map/ppermute | solution.py:28
  889.6 30.3 %collective-permute-start.53 = (bf16[4,96,768]{2,1,0:T(8,128)(2,1)S(1)}, bf16[4,96,768]{2,1,0:T(8,128)(2,1)}, u32[]{:S(2)}, u32[]{:S(2)}) collective-permute-start(bf16[4,96,768]{2,1,0:T(8,128)(2,1)S(1)} %fusion.74), channel_id=1, source_target_pairs={{0,4},{4,0},{8,12},{12,8},{16,20},{20,16},{24,28},{28,24},{1,5},{5... | collective-permute-start | bytes 1769480 | tf_op jit(solution)/shard_map/ppermute | solution.py:32
  912.3 24.3 %collective-permute-start.45 = (bf16[96,1584]{1,0:T(8,128)(2,1)}, bf16[96,1584]{1,0:T(8,128)(2,1)}, u32[]{:S(2)}, u32[]{:S(2)}) collective-permute-start(bf16[96,1584]{1,0:T(8,128)(2,1)} %get-tuple-element.348), channel_id=1, source_target_pairs={{0,8},{4,12},{8,0},{12,4},{16,24},{20,28},{24,16},{28,20},{1,9},{5... | collective-permute-start | bytes 912392 | tf_op jit(solution)/shard_map/ppermute | solution.py:32
  916.1 27.2 %collective-permute-start.46 = (bf16[96,1584]{1,0:T(8,128)(2,1)}, bf16[96,1584]{1,0:T(8,128)(2,1)}, u32[]{:S(2)}, u32[]{:S(2)}) collective-permute-start(bf16[96,1584]{1,0:T(8,128)(2,1)} %get-tuple-element.347), channel_id=1, source_target_pairs={{0,12},{4,8},{8,4},{12,0},{16,28},{20,24},{24,20},{28,16},{1,13},{... | collective-permute-start | bytes 912392 | tf_op jit(solution)/shard_map/ppermute | solution.py:32
  917.0 27.3 %collective-permute-start.47 = (bf16[96,1584]{1,0:T(8,128)(2,1)}, bf16[96,1584]{1,0:T(8,128)(2,1)}, u32[]{:S(2)}, u32[]{:S(2)}) collective-permute-start(bf16[96,1584]{1,0:T(8,128)(2,1)} %get-tuple-element.346), channel_id=1, source_target_pairs={{0,16},{4,20},{8,24},{12,28},{16,0},{20,4},{24,8},{28,12},{1,17},{... | collective-permute-start | bytes 912392 | tf_op jit(solution)/shard_map/ppermute | solution.py:32
  919.3 44.2 %collective-permute-start.48 = (bf16[96,1584]{1,0:T(8,128)(2,1)}, bf16[96,1584]{1,0:T(8,128)(2,1)}, u32[]{:S(2)}, u32[]{:S(2)}) collective-permute-start(bf16[96,1584]{1,0:T(8,128)(2,1)} %get-tuple-element.345), channel_id=1, source_target_pairs={{0,20},{4,16},{8,28},{12,24},{16,4},{20,0},{24,12},{28,8},{1,21},{... | collective-permute-start | bytes 912392 | tf_op jit(solution)/shard_map/ppermute | solution.py:32
  919.9 45.9 %collective-permute-start.49 = (bf16[96,1584]{1,0:T(8,128)(2,1)}, bf16[96,1584]{1,0:T(8,128)(2,1)}, u32[]{:S(2)}, u32[]{:S(2)}) collective-permute-start(bf16[96,1584]{1,0:T(8,128)(2,1)} %get-tuple-element.344), channel_id=1, source_target_pairs={{0,24},{4,28},{8,16},{12,20},{16,8},{20,12},{24,0},{28,4},{1,25},{... | collective-permute-start | bytes 912392 | tf_op jit(solution)/shard_map/ppermute | solution.py:32
  936.5 30.3 %collective-permute-start.50 = (bf16[96,1584]{1,0:T(8,128)(2,1)}, bf16[96,1584]{1,0:T(8,128)(2,1)S(1)}, u32[]{:S(2)}, u32[]{:S(2)}) collective-permute-start(bf16[96,1584]{1,0:T(8,128)(2,1)} %get-tuple-element.343), channel_id=1, source_target_pairs={{0,28},{4,24},{8,20},{12,16},{16,12},{20,8},{24,4},{28,0},{1,29},{... | collective-permute-start | bytes 912392 | tf_op jit(solution)/shard_map/ppermute | solution.py:32
  943.3 26.8 %collective-permute-start.54 = (bf16[96,768]{0,1:T(8,128)(2,1)}, bf16[96,768]{0,1:T(8,128)(2,1)}, u32[]{:S(2)}, u32[]{:S(2)}) collective-permute-start(bf16[96,768]{0,1:T(8,128)(2,1)} %bitcast.419), channel_id=1, source_target_pairs={{0,8},{4,12},{8,0},{12,4},{16,24},{20,28},{24,16},{28,20},{1,9},{5... | collective-permute-start | bytes 442376 | tf_op jit(solution)/shard_map/ppermute | solution.py:32
  944.4 44.9 %collective-permute-start.55 = (bf16[96,768]{0,1:T(8,128)(2,1)}, bf16[96,768]{0,1:T(8,128)(2,1)}, u32[]{:S(2)}, u32[]{:S(2)}) collective-permute-start(bf16[96,768]{0,1:T(8,128)(2,1)} %bitcast.418), channel_id=1, source_target_pairs={{0,16},{4,20},{8,24},{12,28},{16,0},{20,4},{24,8},{28,12},{1,17},{... | collective-permute-start | bytes 442376 | tf_op jit(solution)/shard_map/ppermute | solution.py:32
  963.5 25.8 %collective-permute-start.56 = (bf16[96,768]{0,1:T(8,128)(2,1)S(1)}, bf16[96,768]{0,1:T(8,128)(2,1)}, u32[]{:S(2)}, u32[]{:S(2)}) collective-permute-start(bf16[96,768]{0,1:T(8,128)(2,1)S(1)} %bitcast.417), channel_id=1, source_target_pairs={{0,24},{4,28},{8,16},{12,20},{16,8},{20,12},{24,0},{28,4},{1,25},{... | collective-permute-start | bytes 442376 | tf_op jit(solution)/shard_map/ppermute | solution.py:32
  995.8 28.8 %all-to-all-start.8 = ((f32[32,1,2]{2,1,0:T(1,128)}), f32[32,1,2]{2,1,0:T(1,128)}, u32[]{:S(2)}, u32[]{:S(2)}) async-start(f32[32,1,2]{2,1,0:T(1,128)} %broadcast_in_dim.307), calls=%async_computation.8 | async-start | bytes 32768 | tf_op jit(solution)/shard_map/all_to_all | solution.py:745
  (217 other events, 1507.4 us)
Sparse Core Ops, SparseCore 0:
  574.1 12.8 sort.11.cloned.1.call-done
  (1 shorter events, 0.0 us)

commit v2 on v1

v2 whole, which is shorter than its diff:
```python
import functools
import math

import jax
import jax.numpy as jnp
from jax import lax
from jax.experimental import pallas as pl
from jax.experimental.pallas import tpu as pltpu
from jax.sharding import PartitionSpec as P

HD = 64
STEP = 10

HIGHEST = lax.Precision.HIGHEST
NORM_EPS = 1e-06
CLIP_NORM = 0.005
BETA_ONE = 0.9
BETA_TWO = 0.95
ADAM_EPS = 1e-08
WEIGHT_DECAY = 0.1
LEARN_RATES = (1.0, 0.1, 0.07, 0.5, 0.07, 0.04, 0.2, 0.5)
NARROW = ("line", "core")
BF = jnp.bfloat16
F32 = jnp.float32
VMEM_LIMIT = 56 * 1024 * 1024
FREE = pl.CostEstimate(flops=0, bytes_accessed=0, transcendentals=0)


def together(*values):
    return lax.optimization_barrier(values)


def xor_narrow(value, bits):
    return lax.ppermute(
        value, NARROW, [(i, i ^ bits) for i in range(lax.axis_size(NARROW))]
    )


def xor_wide(value, bits):
    return lax.ppermute(value, "wide", [(i, i ^ bits) for i in range(lax.axis_size("wide"))])


def swap_wide(value):
    return lax.all_to_all(value, "wide", 0, 0, tiled=True)


def spread_wide(value):
    if lax.axis_size("wide") > 8:
        return lax.all_gather(value, "wide")
    return swap_wide(jnp.broadcast_to(value[None], (lax.axis_size("wide"),) + value.shape))


def gather_wide(value, axis):
    return lax.all_gather(value, "wide", axis=axis, tiled=True)


def scatter_wide(value):
    count = lax.axis_size("wide")
    if count != 8:
        return lax.psum_scatter(value, "wide", scatter_dimension=0)
    me = lax.axis_index("wide")
    side = me & 1
    pairs = value.reshape((4, 2) + value.shape[1:])
    kept = lax.dynamic_index_in_dim(pairs, side, 1, keepdims=False)
    sent = lax.dynamic_index_in_dim(pairs, 1 - side, 1, keepdims=False).astype(BF)
    half = kept.astype(F32) + xor_wide(sent, 1).astype(F32)
    depth = me >> 1
    total = lax.dynamic_index_in_dim(half, depth, 0, keepdims=False)
    low = half.astype(BF)
    for k in (1, 2, 3):
        piece = lax.dynamic_index_in_dim(low, depth ^ k, 0, keepdims=False)
        total = total + xor_wide(piece, 2 * k).astype(F32)
    return total


def scatter_core(sent, own):
    from_core = xor_narrow(sent, 1).astype(F32)
    near = own[0].astype(F32) + from_core[0]
    far = own[1].astype(F32) + from_core[1]
    return near, far.astype(BF)


def gather_narrow(value):
    across = xor_narrow(value, 2)
    beside = xor_narrow(value, 1)
    corner = xor_narrow(across, 1)
    return value, beside, across, corner


def rounded(value):
    return lax.reduce_precision(value, exponent_bits=8, mantissa_bits=7)


def layer_norm(values):
    centered = values - jnp.mean(values, axis=-1, keepdims=True)
    inverse = lax.rsqrt(jnp.mean(centered * centered, axis=-1, keepdims=True) + NORM_EPS)
    return (centered * inverse, inverse)


def norm_back(grad, normed, inverse):
    return inverse * (
        grad
        - jnp.mean(grad, axis=-1, keepdims=True)
        - normed * jnp.mean(grad * normed, axis=-1, keepdims=True)
    )


def gelu_tanh(values):
    inner = 0.7978845608 * (values + 0.044715 * values * values * values)
    return 0.5 * values * (1.0 + jnp.tanh(inner))


def gelu_slope(values):
    tangent = jnp.tanh(0.7978845608 * (values + 0.044715 * values * values * values))
    return 0.5 * (1.0 + tangent) + 0.5 * values * (1.0 - tangent * tangent) * 0.7978845608 * (
        1.0 + 0.134145 * values * values
    )


def rotary_tables(positions, width):
    freqs = jnp.exp(jnp.arange(width // 2, dtype=F32) * (-2.0 * math.log(10000.0) / width))
    angle = positions.astype(F32)[:, None] * freqs[None, :]
    cosine, sine = jnp.cos(angle), jnp.sin(angle)
    return (
        jnp.concatenate([cosine] * 4, axis=1),
        jnp.concatenate([-sine, sine, -sine, sine], axis=1),
    )


def time_features(moment, width):
    freqs = jnp.exp(jnp.arange(width // 2, dtype=F32) * (-math.log(10000.0) / (width // 2)))
    angle = 1000.0 * moment[..., None] * freqs
    return jnp.concatenate([jnp.cos(angle), jnp.sin(angle)], axis=-1)


def turned(values, cosine, sine):
    blocks = []
    for place in range(0, values.shape[1], 2 * HD):
        block = values[:, place : place + 2 * HD]
        lanes = lax.broadcasted_iota(jnp.int32, block.shape, 1)
        ahead = pltpu.roll(block, 2 * HD - HD // 2, 1)
        behind = pltpu.roll(block, HD // 2, 1)
        other = jnp.where((lanes & (HD - 1)) < HD // 2, ahead, behind)
        blocks.append(block * cosine + other * sine)
    return jnp.concatenate(blocks, axis=1) if len(blocks) > 1 else blocks[0]


def turned_back(values, cosine, sine):
    spare = -values.shape[1] % (2 * HD)
    filled = jnp.concatenate([values, jnp.zeros((values.shape[0], spare), F32)], axis=1)
    return turned(filled, cosine, -sine)[:, : values.shape[1]]


NT = (((1,), (1,)), ((), ()))
NN = (((1,), (0,)), ((), ()))
TN = (((0,), (0,)), ((), ()))


def mm(a, b, dims):
    return lax.dot_general(a, b, dims, preferred_element_type=F32)


SHIFT_ONE, SCALE_ONE, GATE_ONE, SHIFT_TWO, SCALE_TWO, GATE_TWO, SHIFT_LAST, SCALE_LAST = range(8)
GAIN_ONE, GAIN_TWO, GAIN_LAST, BIAS_DOWN = range(8, 12)
LOCAL = dict(
    compiler_params=pltpu.CompilerParams(vmem_limit_bytes=60 * 1024 * 1024), cost_estimate=FREE
)
BUSY = dict(LOCAL, cost_estimate=pl.CostEstimate(10**10, 0, 4 * 10**7))


def column_sum(values):
    return jnp.sum(values, axis=0, keepdims=True)


def qkv_kernel(
    recv_ref, par_ref, a0, a1, a2, a3, cos_ref, sin_ref, q_ref, kv_ref, hidden_ref, start_ref
):
    par = lambda k: par_ref[k : k + 1, :]
    rows = start_ref.shape[0]
    start = jnp.concatenate(
        [recv_ref[piece, :rows, :].astype(F32) for piece in range(recv_ref.shape[0])], axis=1
    )
    start_ref[...] = start
    normed, _ = layer_norm(start)
    hidden = normed * par(GAIN_ONE) * (1.0 + par(SCALE_ONE)) + par(SHIFT_ONE)
    hidden = hidden.astype(BF)
    hidden_ref[...] = hidden
    share = q_ref.shape[2]
    for s, weight in enumerate((a0, a1, a2, a3)):
        value = mm(hidden, weight[...], NN)
        pair = turned(value[:, : 2 * share], cos_ref[...], sin_ref[...])
        q_ref[s] = pair[:, :share].astype(BF)
        kv_ref[s] = jnp.concatenate(
            [pair[:, share:], value[:, 2 * share : 3 * share]], axis=1
        ).astype(BF)


def project_qkv(recv, params, weights, cosine, sine):
    rows, width = cosine.shape[0], params.shape[1]
    share = width // 4
    return pl.pallas_call(
        qkv_kernel,
        out_shape=[
            jax.ShapeDtypeStruct((4, rows, share), BF),
            jax.ShapeDtypeStruct((4, rows, 2 * share), BF),
            jax.ShapeDtypeStruct((rows, width), BF),
            jax.ShapeDtypeStruct((rows, width), F32),
        ],
        name="qkv",
        **LOCAL,
    )(recv, params, *weights, cosine, sine)


def head_mask(values, head):
    lanes = lax.broadcasted_iota(jnp.int32, values.shape, 1)
    inside = (lanes >= head * HD) & (lanes < (head + 1) * HD)
    return jnp.where(inside, values, jnp.zeros_like(values))


def attend_kernel(q_ref, own_ref, far_ref, out_ref, log_ref):
    query = q_ref[0] * BF(HD**-0.5)
    share = query.shape[1]
    both = jnp.concatenate([own_ref[0], far_ref[0]], axis=0)
    keys, values = both[:, :share], both[:, share:].T
    parts = []
    for head in range(query.shape[1] // HD):
        scores = mm(keys, head_mask(query, head), NT)
        top = jnp.max(scores, axis=0, keepdims=True)
        shifted = jnp.exp(scores - top)
        total = jnp.sum(shifted, axis=0, keepdims=True)
        weights = (shifted * (1.0 / total)).astype(BF)
        parts.append(mm(values[head * HD : (head + 1) * HD], weights, NN))
        log_ref[0, head : head + 1, :] = top + jnp.log(total)
    out_ref[0] = jnp.concatenate(parts, axis=0).T.astype(BF)


def attend_specs(rows, share):
    return [
        pl.BlockSpec((1, rows, share), lambda s: (s, 0, 0)),
        pl.BlockSpec((1, rows, 2 * share), lambda s: (s, 0, 0)),
        pl.BlockSpec((1, rows, 2 * share), lambda s: (s ^ 1, 0, 0)),
    ]


def attend(query, own, far):
    slots, rows, share = query.shape
    heads = share // HD
    return pl.pallas_call(
        attend_kernel,
        grid=(slots,),
        in_specs=attend_specs(rows, share),
        out_specs=[
            pl.BlockSpec((1, rows, share), lambda s: (s, 0, 0)),
            pl.BlockSpec((1, heads, rows), lambda s: (s, 0, 0)),
        ],
        out_shape=[
            jax.ShapeDtypeStruct((slots, rows, share), BF),
            jax.ShapeDtypeStruct((slots, heads, rows), F32),
        ],
        name="attend",
        **LOCAL,
    )(query, own, far)


def feed_kernel(
    mixed_ref, start_ref, par_ref, a0, a1, a2, a3, bc0, bc1, bc2, bc3, select_ref,
    attended_ref, middle_ref, output_ref, hidden_ref, inner_ref, picked_ref,
):
    par = lambda k: par_ref[k : k + 1, :]
    share = mixed_ref.shape[2]
    attended = sum(
        mm(mixed_ref[s], weight[:, 3 * share :], NT) for s, weight in enumerate((a0, a1, a2, a3))
    )
    attended_ref[...] = attended
    middle = start_ref[...] + par(GATE_ONE) * attended
    middle_ref[...] = middle
    normed, _ = layer_norm(middle)
    hidden = normed * par(GAIN_TWO) * (1.0 + par(SCALE_TWO)) + par(SHIFT_TWO)
    hidden = hidden.astype(BF)
    hidden_ref[...] = hidden
    output = jnp.zeros(middle.shape, F32)
    for s, weight in enumerate((bc0, bc1, bc2, bc3)):
        inner = mm(hidden, weight[0], NN)
        inner_ref[s] = inner
        output = output + mm(gelu_tanh(inner).astype(BF), weight[1], NT)
    output_ref[...] = output
    final = middle + par(GATE_TWO) * (output + par(BIAS_DOWN))
    normed, _ = layer_norm(final)
    last = normed * (par(GAIN_LAST) * (1.0 + par(SCALE_LAST))) + par(SHIFT_LAST)
    picked_ref[...] = mm(select_ref[...], last.astype(BF), NN).astype(BF)


def feed(mixed, start, params, weights_a, weights_bc, select):
    rows, width = start.shape
    plain = jax.ShapeDtypeStruct((rows, width), F32)
    return pl.pallas_call(
        feed_kernel,
        out_shape=[
            plain,
            plain,
            plain,
            jax.ShapeDtypeStruct((rows, width), BF),
            jax.ShapeDtypeStruct((4, rows, width), F32),
            jax.ShapeDtypeStruct((select.shape[0], width), BF),
        ],
        name="feed",
        **LOCAL,
    )(mixed, start, params, *weights_a, *weights_bc, select)


SLOT_PLACES = ((1, 0, 0), (3, 0, 1), (0, 1, 0), (2, 1, 1))


def feed_back_kernel(
    rows_ref, select_ref, par_ref, middle_ref, output_ref, attended_ref, hidden_ref, inner_ref,
    a0, a1, a2, a3, bc0, bc1, bc2, bc3,
    d_middle_ref, d_attended_ref, d_mixed_ref, sent_ref, own_ref, vec_ref,
):
    par = lambda k: par_ref[k : k + 1, :]
    share = d_mixed_ref.shape[2]
    middle, output = middle_ref[...], output_ref[...]
    d_hidden = mm(select_ref[...], rows_ref[...], TN)
    final = middle + par(GATE_TWO) * (output + par(BIAS_DOWN))
    normed, inverse = layer_norm(final)
    d_normed = column_sum(d_hidden * normed)
    vec_ref[SHIFT_LAST : SHIFT_LAST + 1, :] = column_sum(d_hidden)
    vec_ref[SCALE_LAST : SCALE_LAST + 1, :] = d_normed * par(GAIN_LAST)
    vec_ref[GAIN_LAST : GAIN_LAST + 1, :] = d_normed * (1.0 + par(SCALE_LAST))
    d_final = norm_back(d_hidden * (par(GAIN_LAST) * (1.0 + par(SCALE_LAST))), normed, inverse)
    vec_ref[BIAS_DOWN : BIAS_DOWN + 1, :] = column_sum(d_final) * par(GATE_TWO)
    vec_ref[GATE_TWO : GATE_TWO + 1, :] = column_sum(d_final * (output + par(BIAS_DOWN)))
    d_output = (d_final * par(GATE_TWO)).astype(BF)
    hidden = hidden_ref[...]
    d_hidden = jnp.zeros(middle.shape, F32)
    weights = (bc0, bc1, bc2, bc3)
    for s, kept, place in SLOT_PLACES:
        out_ref = own_ref if kept else sent_ref
        inner = inner_ref[s]
        tangent = jnp.tanh(0.7978845608 * (inner + 0.044715 * inner * inner * inner))
        active = (0.5 * inner * (1.0 + tangent)).astype(BF)
        slope = 0.5 * (1.0 + tangent) + 0.5 * inner * (
            1.0 - tangent * tangent
        ) * 0.7978845608 * (1.0 + 0.134145 * inner * inner)
        d_inner = (mm(d_output, weights[s][1], NN) * slope).astype(BF)
        out_ref[place, 0] = mm(hidden, d_inner, TN).astype(BF)
        out_ref[place, 1] = mm(d_output, active, TN).astype(BF)
        d_hidden = d_hidden + mm(d_inner, weights[s][0], NT)
    normed, inverse = layer_norm(middle)
    d_normed = column_sum(d_hidden * normed)
    vec_ref[SHIFT_TWO : SHIFT_TWO + 1, :] = column_sum(d_hidden)
    vec_ref[SCALE_TWO : SCALE_TWO + 1, :] = d_normed * par(GAIN_TWO)
    vec_ref[GAIN_TWO : GAIN_TWO + 1, :] = d_normed * (1.0 + par(SCALE_TWO))
    d_middle = d_final + norm_back(
        d_hidden * par(GAIN_TWO) * (1.0 + par(SCALE_TWO)), normed, inverse
    )
    d_middle_ref[...] = d_middle
    vec_ref[GATE_ONE : GATE_ONE + 1, :] = column_sum(d_middle * attended_ref[...])
    d_attended = (d_middle * par(GATE_ONE)).astype(BF)
    d_attended_ref[...] = d_attended
    for s, weight in enumerate((a0, a1, a2, a3)):
        d_mixed_ref[s] = mm(d_attended, weight[:, 3 * share :], NN).astype(BF)
    for unused in (SHIFT_ONE, SCALE_ONE, GAIN_ONE):
        vec_ref[unused : unused + 1, :] = jnp.zeros_like(par(0))


def feed_back(
    d_rows, select, params, middle, output, attended, hidden, inner, weights_a, weights_bc
):
    rows, width = middle.shape
    half = jax.ShapeDtypeStruct((2, 2, width, width), BF)
    return pl.pallas_call(
        feed_back_kernel,
        out_shape=[
            jax.ShapeDtypeStruct((rows, width), F32),
            jax.ShapeDtypeStruct((rows, width), BF),
            jax.ShapeDtypeStruct((4, rows, width // 4), BF),
            half,
            half,
            jax.ShapeDtypeStruct(params.shape, F32),
        ],
        name="feed_back",
        **LOCAL,
    )(
        d_rows, select, params, middle, output, attended, hidden, inner, *weights_a, *weights_bc
    )


def attend_back_kernel(
    q_ref, own_ref, far_ref, grad_ref, log_ref, cos_ref, sin_ref, kcos_ref, ksin_ref,
    dq_ref, d_own_ref, d_far_ref,
):
    query, grad = q_ref[0], grad_ref[0]
    share = query.shape[1]
    both = jnp.concatenate([own_ref[0], far_ref[0]], axis=0)
    keys, values = both[:, :share], both[:, share:]
    turned_keys = keys.T
    scale = HD**-0.5
    rows = query.shape[0]
    dq = []
    dk = jnp.zeros(keys.shape, F32)
    dv = jnp.zeros(keys.shape, F32)
    for head in range(query.shape[1] // HD):
        query_one = head_mask(query * BF(scale), head)
        grad_one = head_mask(grad, head)
        scores = mm(keys, query_one, NT)
        weights = jnp.exp(scores - log_ref[0, head : head + 1, :])
        d_weights = mm(values, grad_one, NT)
        delta = jnp.sum(weights * d_weights, axis=0, keepdims=True)
        d_scores = (weights * (d_weights - delta)).astype(BF)
        dq.append(mm(turned_keys[head * HD : (head + 1) * HD], d_scores, NN))
        dk = dk + mm(d_scores, query_one, NN)
        dv = dv + mm(weights.astype(BF), grad_one, NN)
    dq = jnp.concatenate(dq, axis=0).T * scale
    dq_ref[0] = turned_back(dq, cos_ref[...], sin_ref[...]).astype(BF)
    dk = turned_back(dk, kcos_ref[...], ksin_ref[...])
    both = jnp.concatenate([dk, dv], axis=1)
    d_own_ref[0] = both[:rows]
    d_far_ref[0] = both[rows:].astype(BF)


def attend_back(query, own, far, grad, logs, cosine, sine, key_cosine, key_sine):
    slots, rows, share = query.shape
    heads = share // HD
    whole = lambda table: pl.BlockSpec(table.shape, lambda s: (0, 0))
    one, two, other = attend_specs(rows, share)
    return pl.pallas_call(
        attend_back_kernel,
        grid=(slots,),
        in_specs=[
            one, two, other, one, pl.BlockSpec((1, heads, rows), lambda s: (s, 0, 0)),
            whole(cosine), whole(sine), whole(key_cosine), whole(key_sine),
        ],
        out_specs=[one, two, two],
        out_shape=[
            jax.ShapeDtypeStruct((slots, rows, share), BF),
            jax.ShapeDtypeStruct((slots, rows, 2 * share), F32),
            jax.ShapeDtypeStruct((slots, rows, 2 * share), BF),
        ],
        name="attend_back",
        **LOCAL,
    )(query, own, far, grad, logs, cosine, sine, key_cosine, key_sine)


def slot_grads(dq_ref, d_own_ref, d_far_ref, s):
    return jnp.concatenate(
        [
            dq_ref[s],
            (d_own_ref[s] + d_far_ref[s ^ 1].astype(F32)).astype(BF),
        ],
        axis=1,
    )


def qkv_back_kernel(
    dq_ref, d_own_ref, d_far_ref, a0, a1, a2, a3, d_middle_ref, start_ref, par_ref, mask_ref,
    out_ref, grads_ref, vec_ref,
):
    par = lambda k: par_ref[k : k + 1, :]
    share = dq_ref.shape[2]
    rows = start_ref.shape[0]
    d_hidden = jnp.zeros(start_ref.shape, F32)
    for s, weight in enumerate((a0, a1, a2, a3)):
        grads = slot_grads(dq_ref, d_own_ref, d_far_ref, s)
        grads_ref[s] = grads
        d_hidden = d_hidden + mm(grads, weight[:, : 3 * share], NT)
    normed, inverse = layer_norm(start_ref[...])
    d_normed = column_sum(d_hidden * normed)
    vec_ref[0:1, :] = column_sum(d_hidden)
    vec_ref[1:2, :] = d_normed * par(GAIN_ONE)
    vec_ref[2:3, :] = d_normed * (1.0 + par(SCALE_ONE))
    d_start = d_middle_ref[...] + norm_back(
        d_hidden * par(GAIN_ONE) * (1.0 + par(SCALE_ONE)), normed, inverse
    )
    masked = column_sum(d_start * mask_ref[...])
    extra = out_ref.shape[1] - rows
    first = lax.broadcasted_iota(jnp.int32, (extra, 1), 0) == 0
    whole = jnp.concatenate([d_start, jnp.where(first, masked, 0.0)], axis=0).astype(BF)
    columns = out_ref.shape[2]
    for piece in range(out_ref.shape[0]):
        out_ref[piece] = whole[:, piece * columns : (piece + 1) * columns]


def qkv_back(dq, d_own, d_far, weights, d_middle, start, params, is_mask, padded, wide):
    rows, width = start.shape
    return pl.pallas_call(
        qkv_back_kernel,
        out_shape=[
            jax.ShapeDtypeStruct((wide, padded, width // wide), BF),
            jax.ShapeDtypeStruct((4, rows, 3 * width // 4), BF),
            jax.ShapeDtypeStruct((3, width), F32),
        ],
        name="qkv_back",
        **LOCAL,
    )(dq, d_own, d_far, *weights, d_middle, start, params, is_mask)


def qkv_grads_kernel(grads_ref, hidden_ref, d_attended_ref, mixed_ref, sent_ref, own_ref):
    for s, kept, place in SLOT_PLACES:
        out_ref = own_ref if kept else sent_ref
        out_ref[place] = jnp.concatenate(
            [
                mm(hidden_ref[...], grads_ref[s], TN),
                mm(d_attended_ref[...], mixed_ref[s], TN),
            ],
            axis=1,
        ).astype(BF)


def qkv_grads(grads, hidden, d_attended, mixed):
    width = hidden.shape[1]
    half = jax.ShapeDtypeStruct((2, width, width), BF)
    return pl.pallas_call(
        qkv_grads_kernel, out_shape=[half, half], name="qkv_grads", **BUSY
    )(grads, hidden, d_attended, mixed)


def rows_kernel(own_ref, other_ref, out_ref):
    step = pl.program_id(0)
    half = pl.num_programs(0) // 2

    @pl.when(step < half)
    def _():
        out_ref[...] = own_ref[...].astype(BF).astype(F32).T

    @pl.when((step >= half) & (step < 2 * half))
    def _():
        out_ref[...] = other_ref[...].astype(F32).T

    @pl.when(step == 2 * half)
    def _():
        out_ref[...] = jnp.zeros_like(out_ref)


def table_rows_of(own, other):
    width, entries = own.shape
    block = next(b for b in (1408, 1152, 384, 128) if entries % b == 0)
    half = entries // block
    return pl.pallas_call(
        rows_kernel,
        grid=(2 * half + 1,),
        in_specs=[
            pl.BlockSpec((width, block), lambda i: (0, jnp.minimum(i, half - 1))),
            pl.BlockSpec((width, block), lambda i: (0, jnp.clip(i - half, 0, half - 1))),
        ],
        out_specs=pl.BlockSpec((block, width), lambda i: (i, 0)),
        out_shape=jax.ShapeDtypeStruct((2 * entries + block, width), F32),
        name="table_rows",
        **BUSY,
    )(own, other)


def lookup_kernel(id_ref, table_ref, out_ref, scratch):
    block = scratch.shape[0]
    unroll = 16

    def body(step, _):
        for k in range(unroll):
            place = step * unroll + k
            scratch[pl.ds(place, 1), :] = table_ref[pl.ds(id_ref[0, 0, place], 1), :]
        return 0

    lax.fori_loop(0, block // unroll, body, 0)
    out_ref[...] = scratch[...].astype(BF)


def lookup(table, ids):
    count = ids.shape[0]
    block = min(2048, count)
    width = table.shape[1]
    return pl.pallas_call(
        lookup_kernel,
        grid=(count // block,),
        in_specs=[
            pl.BlockSpec((1, 1, block), lambda i: (i, 0, 0), memory_space=pltpu.SMEM),
            pl.BlockSpec(table.shape, lambda i: (0, 0), pipeline_mode=pl.Buffered(1)),
        ],
        out_specs=pl.BlockSpec((block, width), lambda i: (i, 0)),
        out_shape=jax.ShapeDtypeStruct((count, width), BF),
        scratch_shapes=[pltpu.VMEM((block, width), F32)],
        name="lookup",
        **LOCAL,
    )(ids.reshape(count // block, 1, block), table)


def collect_kernel(shift, first, key_ref, count_ref, grad_ref, *refs):
    step = pl.program_id(0)
    if first:
        out_ref, rows_ref = refs
        sum_ref = out_ref
    else:
        old_ref, out_ref, rows_ref, sum_ref = refs

    @pl.when(step == 0)
    def _():
        sum_ref[...] = jnp.zeros_like(sum_ref) if first else old_ref[...]

    rows_ref[...] = grad_ref[0].astype(F32)
    mask = (1 << shift) - 1
    count = count_ref[0, 0, 0]
    unroll = 8

    def group(item, _):
        keys = [key_ref[0, 0, item * unroll + k] for k in range(unroll)]
        targets = [lax.shift_right_logical(key, shift) for key in keys]
        olds = [sum_ref[pl.ds(target, 1), :] for target in targets]
        news = [rows_ref[pl.ds(key & mask, 1), :] for key in keys]
        sums = []
        for k in range(unroll):
            old = olds[k]
            if k:
                old = jnp.where(targets[k] == targets[k - 1], sums[k - 1], old)
            sums.append(old + news[k])
        for k in range(unroll):
            sum_ref[pl.ds(targets[k], 1), :] = sums[k]
        return 0

    def single(item, _):
        key = key_ref[0, 0, item]
        target = pl.ds(lax.shift_right_logical(key, shift), 1)
        sum_ref[target, :] = sum_ref[target, :] + rows_ref[pl.ds(key & mask, 1), :]
        return 0

    groups = lax.shift_right_logical(count, 3)
    lax.fori_loop(0, groups, group, 0)
    lax.fori_loop(groups * unroll, count, single, 0)

    if not first:

        @pl.when(step == pl.num_programs(0) - 1)
        def _():
            def turn(block, _):
                place = pl.ds(pl.multiple_of(block * 128, 128), 128)
                out_ref[:, place] = sum_ref[place, :].T
                return 0

            lax.fori_loop(0, sum_ref.shape[0] // 128, turn, 0)


def collect(keys, counts, grads, shift, before, entries):
    parts, tokens, width = grads.shape
    first = before is None
    out_dims = (entries, width) if first else (width, entries)
    scratch = [pltpu.VMEM((tokens, width), F32)]
    if not first:
        scratch.append(pltpu.VMEM((entries, width), F32))
    return pl.pallas_call(
        functools.partial(collect_kernel, shift, first),
        grid=(parts,),
        in_specs=[
            pl.BlockSpec((1, 1, tokens), lambda i: (i, 0, 0), memory_space=pltpu.SMEM),
            pl.BlockSpec((1, 1, 1), lambda i: (i, 0, 0), memory_space=pltpu.SMEM),
            pl.BlockSpec((1, tokens, width), lambda i: (i, 0, 0)),
        ]
        + ([] if first else [pl.BlockSpec((entries, width), lambda i: (0, 0), pipeline_mode=pl.Buffered(1))]),
        out_specs=pl.BlockSpec(out_dims, lambda i: (0, 0)),
        out_shape=jax.ShapeDtypeStruct(out_dims, F32),
        scratch_shapes=scratch,
        compiler_params=pltpu.CompilerParams(vmem_limit_bytes=VMEM_LIMIT),
        cost_estimate=FREE,
        name="collect",
    )(*[keys.reshape(parts, 1, tokens), counts.reshape(parts, 1, 1), grads] + ([] if first else [before]))


def local(
    token_ids, mask_slots, mask_counts,
    embedding, out_table, qkv_weight, proj_weight, up_weight, down_weight, mod_weight, vectors,
    embedding_first, out_table_first, qkv_first, proj_first, up_first, down_first, mod_first,
    vectors_first,
    embedding_second, out_table_second, qkv_second, proj_second, up_second, down_second,
    mod_second, vectors_second,
):
    masters = (
        embedding, out_table, qkv_weight, proj_weight, up_weight, down_weight, mod_weight, vectors,
    )
    firsts = (
        embedding_first, out_table_first, qkv_first, proj_first, up_first, down_first, mod_first,
        vectors_first,
    )
    seconds = (
        embedding_second, out_table_second, qkv_second, proj_second, up_second, down_second,
        mod_second, vectors_second,
    )
    wide = lax.axis_size("wide")
    narrow = lax.axis_size(NARROW)
    me = lax.axis_index("wide")
    group = lax.axis_index(NARROW)
    part = group & 1
    micro = group >> 1
    entries, share = embedding.shape
    width = share * wide
    vocab = entries * narrow
    micro_count, length = token_ids.shape[1:]
    capacity = mask_slots.shape[2]
    rows = length // 2
    pair_total = 5 * length // 16
    quarter = pair_total // 4
    loss_scale = 1.0 / (length * micro_count * wide)
    positions = jnp.arange(length, dtype=jnp.int32)

    tokens, slots, counts = token_ids[0], mask_slots[0], mask_counts[0]
    at_slot = slots[:, :, None] == positions[None, None, :]
    valid = jnp.arange(capacity)[None, :] < counts[:, None]
    masked = jnp.any(at_slot & valid[:, :, None], axis=1)
    targets = jnp.sum(jnp.where(at_slot, tokens[:, None, :], 0), axis=2)
    inputs = jnp.where(masked, vocab - 1, tokens)
    packed = jnp.concatenate(
        [inputs, targets, jnp.broadcast_to(counts[:, None], (micro_count, 128))], axis=1
    )
    packed_all = spread_wide(packed)
    inputs_all = packed_all[:, :, :length]
    targets_all = packed_all[:, :, length : length + capacity]
    counts_all = packed_all[:, :, length + capacity]

    shard_a = jnp.concatenate(
        [qkv_weight[0], qkv_weight[1], qkv_weight[2], proj_weight.T], axis=1
    ).astype(BF)
    wide_a = gather_wide(shard_a, 0)
    wide_bc = gather_wide(jnp.stack([up_weight.astype(BF), down_weight.T.astype(BF)]), 1)
    heads_width = width // narrow

    chunk = -(-entries // (128 * wide)) * 128
    spare = chunk * wide - entries
    table_own = jnp.pad(out_table.astype(BF), ((0, 0), (0, spare)))
    table_own = table_own.reshape(share, wide, chunk).transpose(1, 0, 2)
    real = me * chunk + jnp.arange(chunk) < entries

    moments = counts_all.astype(F32) / pair_total
    condition = jax.nn.silu(time_features(moments, mod_weight.shape[0]))
    condition_mine = lax.dynamic_index_in_dim(condition, micro, 1, keepdims=False)
    mod_part = jnp.dot(condition_mine, rounded(mod_weight), precision=HIGHEST)
    mod_share = mod_part.shape[1]
    exact = []
    rest = mod_part
    for _ in range(3):
        exact.append(rounded(rest))
        rest = rest - exact[-1]
    extra = jnp.concatenate(
        exact + [jnp.broadcast_to(rounded(vectors), (wide, vectors.shape[0]))], axis=1
    ).astype(BF)
    extra_rows = extra.shape[1] // share
    extra = extra.reshape(wide, extra_rows, share)
    extra = jnp.pad(extra, ((0, 0), (0, -extra_rows % 16), (0, 0)))

    table_rows = table_rows_of(embedding.T, xor_narrow(embedding.T.astype(BF), 1))
    inputs_all, table_rows = together(inputs_all, table_rows)
    half_ids = lax.dynamic_slice_in_dim(inputs_all, part * rows, rows, axis=2)
    half_ids = jnp.stack(
        [
            lax.dynamic_index_in_dim(half_ids, micro, 1, keepdims=False),
            lax.dynamic_index_in_dim(half_ids, 1 - micro, 1, keepdims=False),
        ]
    )
    inside, beside = half_ids - group * entries, half_ids - (group ^ 1) * entries
    inside_here = (inside >= 0) & (inside < entries)
    beside_here = (beside >= 0) & (beside < entries)
    places = jnp.where(
        inside_here, inside, jnp.where(beside_here, beside + entries, 2 * entries)
    )
    looked = lookup(table_rows, places.reshape(-1))
    looked = looked.reshape(2, wide, rows, share)
    start_part = looked[0] + xor_narrow(looked[1], 2)
    start_recv_in = jnp.concatenate([start_part, extra], axis=1)
    start_recv_in, wide_a = together(start_recv_in, wide_a)
    full_a = gather_narrow(wide_a)
    start_recv = swap_wide(start_recv_in)

    my_inputs = lax.dynamic_slice_in_dim(
        lax.dynamic_index_in_dim(inputs, micro, 0, keepdims=False), part * rows, rows, axis=0
    )
    small_rows = (9 * width + 3 * width + 8 * width) // wide // share
    padded = rows + 16 + -(-small_rows // 16) * 16
    padded = rows + 16 + 32
    mask_entry = vocab - 1
    ids = jnp.stack(
        [
            lax.dynamic_slice_in_dim(
                lax.dynamic_index_in_dim(inputs_all, (group ^ s) >> 1, 1, keepdims=False),
                ((group ^ s) & 1) * rows,
                rows,
                axis=1,
            )
            for s in range(narrow)
        ]
    )
    ids = jnp.concatenate(
        [
            jnp.where(ids == mask_entry, -1, ids),
            jnp.full((narrow, wide, 1), mask_entry, jnp.int32),
            jnp.full((narrow, wide, padded - rows - 1), -1, jnp.int32),
        ],
        axis=2,
    ).reshape(narrow, wide * padded)
    local_ids = ids - group * entries
    taken = (local_ids >= 0) & (local_ids < entries)
    shift = (wide * padded - 1).bit_length()
    sort_keys = jnp.where(
        taken,
        local_ids * (1 << shift) + jnp.arange(wide * padded, dtype=jnp.int32)[None, :],
        jnp.iinfo(jnp.int32).max,
    )
    hits = jnp.sum(taken.astype(jnp.int32), axis=1)
    start_recv, table_own, wide_bc, *full_a = together(start_recv, table_own, wide_bc, *full_a)
    across_bc = xor_narrow(wide_bc, 2)
    table_mine = swap_wide(table_own).reshape(width, chunk)
    extra = start_recv[:, rows : rows + extra_rows].astype(F32).reshape(wide, -1)
    vector_full = extra[:, 3 * mod_share :].reshape(-1)
    modulation = extra[:, :mod_share] + extra[:, mod_share : 2 * mod_share]
    modulation = (modulation + extra[:, 2 * mod_share : 3 * mod_share]).reshape(-1)
    modulation = modulation + vector_full[4 * width :]
    params = jnp.concatenate(
        [modulation.reshape(8, width), vector_full[: 4 * width].reshape(4, width)]
    )

    my_positions = part * rows + jnp.arange(rows, dtype=jnp.int32)
    far_positions = (1 - part) * rows + jnp.arange(rows, dtype=jnp.int32)
    key_cosine, key_sine = rotary_tables(jnp.concatenate([my_positions, far_positions]), HD)
    cosine, sine = key_cosine[:rows], key_sine[:rows]
    query, own_kv, hidden_one, start = project_qkv(start_recv, params, full_a, cosine, sine)
    query, sort_keys = together(query, sort_keys)
    sort_keys = lax.sort(sort_keys, dimension=1)
    far_kv = xor_narrow(own_kv, 1)
    mixed, logs = attend(query, own_kv, far_kv)
    mixed, sort_keys, hits, across_bc = together(mixed, sort_keys, hits, across_bc)
    full_bc = (wide_bc, xor_narrow(wide_bc, 1), across_bc, xor_narrow(across_bc, 1))
    tables = gather_narrow(table_mine)

    side = me // (wide // 2)
    low = me % (wide // 2)
    count_low = lax.dynamic_index_in_dim(
        lax.dynamic_index_in_dim(counts_all, low, 0, keepdims=False), micro, 0, keepdims=False
    )
    slot_row = lax.dynamic_index_in_dim(slots, micro, 0, keepdims=False)
    offset = jnp.arange(quarter, dtype=jnp.int32)
    order = jnp.concatenate(
        [
            s * (2 * quarter) + p * quarter + offset
            for p in (part, 1 - part)
            for s in (side, 1 - side)
        ]
    )
    from_low = order < count_low
    index = jnp.where(from_low, order, order - count_low)
    mine = from_low == (side == 0)
    wanted = jnp.sum(
        jnp.where(index[:, None] == jnp.arange(capacity)[None, :], slot_row[None, :], 0), axis=1
    )
    select = ((wanted[:, None] == my_positions[None, :]) & mine[:, None]).astype(BF)
    attended, middle, output, hidden_two, inner, picked = feed(
        mixed, start, params, full_a, full_bc, select
    )
    picked = picked[: 2 * quarter] + xor_narrow(picked[2 * quarter :], 1)
    row_part = picked[:quarter] + xor_wide(picked[quarter:], wide // 2)
    head_rows = spread_wide(row_part).reshape(wide * quarter, width)

    targets_mine = lax.dynamic_index_in_dim(targets_all, micro, 1, keepdims=False)
    counts_mine = lax.dynamic_index_in_dim(counts_all, micro, 1, keepdims=False)
    pairs = wide // 2
    both = jnp.concatenate([targets_mine[:pairs], targets_mine[pairs:]], axis=1)
    spot = jnp.stack([s * 2 * quarter + part * quarter + offset for s in (0, 1)])
    low_counts = counts_mine[:pairs, None, None]
    spot = jnp.where(spot[None] < low_counts, spot[None], capacity + spot[None] - low_counts)
    row_targets = jnp.sum(
        jnp.where(
            spot[..., None] == jnp.arange(2 * capacity)[None, None, None, :],
            both[:, None, None, :],
            0,
        ),
        axis=-1,
    )
    row_targets = row_targets.transpose(1, 0, 2).reshape(-1)
    target_owner = sum((row_targets >= k * entries).astype(jnp.int32) for k in range(1, narrow))
    target_rest = row_targets - target_owner * entries - me * chunk
    target_column = jnp.where(
        (target_rest >= 0) & (target_rest < chunk), (target_owner ^ group) * chunk + target_rest, -1
    )

    logits = [jnp.where(real[None, :], mm(head_rows, table, NN), -1e30) for table in tables]
    hitting = [
        jnp.arange(chunk)[None, :] + s * chunk == target_column[:, None] for s in range(narrow)
    ]
    top = functools.reduce(jnp.maximum, [jnp.max(value, axis=-1) for value in logits])
    total = sum(jnp.sum(jnp.exp(value - top[:, None]), axis=-1) for value in logits)
    target_logit = sum(
        jnp.sum(jnp.where(hit, value, 0.0), axis=-1) for hit, value in zip(hitting, logits)
    )
    stats = spread_wide(jnp.stack([top, total, target_logit]))
    top_all = jnp.max(stats[:, 0], axis=0)
    total_all = jnp.sum(stats[:, 1] * jnp.exp(stats[:, 0] - top_all[None]), axis=0)
    log_total = top_all + jnp.log(total_all)
    loss_part = jnp.sum(log_total - jnp.sum(stats[:, 2], axis=0))
    d_logits = [
        ((jnp.exp(value - log_total[:, None]) - hit.astype(F32)) * loss_scale).astype(BF)
        for hit, value in zip(hitting, logits)
    ]
    d_rows = sum(mm(grad, table, NT) for grad, table in zip(d_logits, tables))
    d_table_parts = [mm(head_rows, grad, TN) for grad in d_logits]
    d_recv = swap_wide(d_rows.astype(BF).reshape(wide, quarter, width))
    d_recv, *d_table_parts = together(d_recv, *d_table_parts)
    table_sent = [xor_narrow(d_table_parts[s].astype(BF), 1) for s in (1, 3)]
    d_mine = jnp.sum(d_recv.astype(F32), axis=0).astype(BF)
    d_sides = jnp.concatenate([d_mine, xor_wide(d_mine, wide // 2)])
    d_all = jnp.concatenate([d_sides, xor_narrow(d_sides, 1)])
    table_far = (d_table_parts[2] + table_sent[1].astype(F32)).astype(BF)
    d_all, table_far = together(d_all, table_far)
    half = width // 2
    table_from = [xor_narrow(table_far[:half], 2), xor_narrow(table_far[half:], 2)]

    d_middle, d_attended, d_mixed, bc_sent, bc_own, d_params = feed_back(
        d_all, select, params, middle, output, attended, hidden_two, inner, full_a, full_bc
    )
    d_mixed, table_from[0] = together(d_mixed, table_from[0])
    bc_near, bc_far = scatter_core(bc_sent, bc_own)
    d_query, d_own, d_far = attend_back(
        query, own_kv, far_kv, d_mixed, logs, cosine, sine, key_cosine, key_sine
    )
    d_query, d_own, d_far, table_from[1], bc_far = together(
        d_query, d_own, d_far, table_from[1], bc_far
    )
    b_from, c_from = xor_narrow(bc_far[0], 2), xor_narrow(bc_far[1], 2)
    d_far = xor_narrow(d_far, 1)
    is_mask = (my_inputs == mask_entry).astype(F32)[:, None]
    d_start_rows, d_projected, d_first = qkv_back(
        d_query, d_own, d_far, full_a, d_middle, start, params, is_mask, rows + 16, wide
    )

    d_start_rows, d_first, b_from = together(d_start_rows, d_first, b_from)
    d_params = jnp.concatenate([d_first[:2], d_params[2:8], d_first[2:3], d_params[9:]])
    d_modulation = d_params[:8].reshape(-1)
    d_vector = jnp.concatenate([d_params[8:].reshape(-1), d_modulation])
    small = jnp.concatenate(
        [d_modulation.reshape(wide, -1, share), d_vector.reshape(wide, -1, share)], axis=1
    ).astype(BF)
    small = jnp.pad(small, ((0, 0), (0, padded - rows - 16 - small_rows), (0, 0)))
    d_start_rows = jnp.concatenate([d_start_rows, small], axis=1)
    d_start_recv = swap_wide(d_start_rows)
    a_sent, a_own = qkv_grads(d_projected, hidden_one, d_attended, mixed)
    a_near, a_far = scatter_core(a_sent, a_own)
    a_far, c_from, d_start_recv = together(a_far, c_from, d_start_recv)
    d_b = scatter_wide((bc_near[0] + b_from.astype(F32)).reshape(wide, share, width))
    d_c = scatter_wide((bc_near[1] + c_from.astype(F32)).reshape(wide, share, width))
    d_table = d_table_parts[0] + table_sent[0].astype(F32)
    d_table = (d_table + jnp.concatenate(table_from).astype(F32)).astype(BF)
    d_table = swap_wide(d_table.reshape(wide, share, chunk)).astype(F32).transpose(1, 0, 2)
    d_table = d_table.reshape(share, chunk * wide)[:, :entries]
    a_from = xor_narrow(a_far, 2)
    d_a = scatter_wide((a_near + a_from.astype(F32)).reshape(wide, share, width))
    d_start_recv = d_start_recv.reshape(wide * padded, share)
    d_start_across = xor_narrow(d_start_recv, 2)
    d_near = jnp.stack([d_start_recv, xor_narrow(d_start_recv, 1)])
    d_embed = collect(sort_keys[:2], hits[:2], d_near, shift, None, entries)
    d_far = jnp.stack([d_start_across, xor_narrow(d_start_across, 1)])
    d_embed = collect(sort_keys[2:], hits[2:], d_far, shift, d_embed, entries)

    small = jnp.stack([d_near, d_far]).reshape(2, 2, wide, padded, share)
    small = small[:, :, :, rows + 16 : rows + 16 + small_rows].astype(F32)
    small = small.sum(axis=1).reshape(2, wide, -1)
    small, small_far = small[0], small[1]
    d_vectors = jnp.sum(small[:, mod_share:] + small_far[:, mod_share:], axis=0)
    condition_far = lax.dynamic_index_in_dim(condition, 1 - micro, 1, keepdims=False)
    d_mod_weight = lax.dot_general(
        condition_mine, small[:, :mod_share], TN, precision=HIGHEST
    ) + lax.dot_general(condition_far, small_far[:, :mod_share], TN, precision=HIGHEST)

    shards = (
        d_embed,
        d_table,
        jnp.stack([d_a[:, k * heads_width : (k + 1) * heads_width] for k in range(3)]),
        together(d_a[:, 3 * heads_width :].T)[0],
        d_b,
        d_c,
        d_mod_weight,
        d_vectors,
    )

    square = jnp.zeros((), F32)
    for grad in shards[:6]:
        square = square + jnp.sum(grad * grad)
    shared_square = jnp.sum(shards[6] * shards[6]) + jnp.sum(shards[7] * shards[7])
    square = square + shared_square / narrow
    sums = lax.all_to_all(
        jnp.broadcast_to(jnp.stack([loss_part / wide, square])[None, None], (wide * narrow, 1, 2)),
        ("wide",) + NARROW,
        0,
        0,
        tiled=True,
    )
    sums = jnp.sum(sums, axis=(0, 1))
    loss_sum = sums[0]
    grad_norm = jnp.sqrt(sums[1])
    factor = CLIP_NORM / jnp.maximum(grad_norm, CLIP_NORM)
    results = []
    for member in range(8):
        turn = (lambda value: value.T) if member in (0, 5) else (lambda value: value)
        master = turn(masters[member])
        grad = shards[member] * factor
        first = BETA_ONE * turn(firsts[member]) + (1.0 - BETA_ONE) * grad
        second = BETA_TWO * turn(seconds[member]) + (1.0 - BETA_TWO) * grad * grad
        stepped = (
            first / (1.0 - BETA_ONE**STEP) / (jnp.sqrt(second / (1.0 - BETA_TWO**STEP)) + ADAM_EPS)
        )
        decay = WEIGHT_DECAY if member < 7 else 0.0
        fresh = master - LEARN_RATES[member] * (stepped + decay * master)
        results.extend([turn(fresh), turn(first), turn(second)])
    return (loss_sum, grad_norm, *results)


def solution(mesh):
    shape = (mesh.shape["wide"], mesh.shape["narrow"] // 2, 2)
    mesh = jax.sharding.Mesh(mesh.devices.reshape(shape), ("wide",) + NARROW)
    weights = (
        P(NARROW, "wide"),
        P("wide", NARROW),
        P(None, "wide", NARROW),
        P(NARROW, "wide"),
        P("wide", NARROW),
        P(NARROW, "wide"),
        P(None, "wide"),
        P("wide"),
    )
    data = (P("wide", None, None), P("wide", None, None), P("wide", None))
    outs = [P(), P()]
    for spec in weights:
        outs.extend([spec] * 3)
    return jax.shard_map(
        local,
        mesh=mesh,
        in_specs=data + weights * 3,
        out_specs=tuple(outs),
        check_vma=False,
    )
```

time: 1130 us -> 768 us (0.68); the launches traced: 1110 us -> 760 us
  local copies, waits for them, and re-layouts: 353 us -> 91.9 us
  matrix products: 138 us -> 51.5 us
  starting transfers between devices: 143 us -> 69.3 us
  Pallas kernels: 95 us -> 166 us
  other arithmetic: 173 us -> 120 us
  waiting for transfers between devices: 182 us -> 226 us
  blocking collectives: 0 us -> 12.3 us
    dynamic_update_slice x34 -> x0, local copies, waits for them, and re-layouts: 127 us -> none  [the longest x14 100 us: swap_wide_async(): out = lax.dynamic_update_index_in_dim(out, pieces[k - 1], me ^ k, 0)]
    ppermute x31 -> x27, waiting for transfers between devices: 45.9 us -> 137 us  [xor_narrow(): lax.ppermute(value, NARROW, [(i, i ^ bits) for i in range(lax.axis_size(N...]
    dot_general x43 -> x12, matrix products: 135 us -> 49.5 us  [mm(): return lax.dot_general(a, b, dims, preferred_element_type=F32)]
    pallas_call x4 -> x10, Pallas kernels: 80.3 us -> 151 us  [the longest x2 30.8 us: collect(): pl.pallas_call(functools.partial(collect_kernel, shift, first), grid=(par...]
    ppermute x40 -> x14, waiting for transfers between devices: 104 us -> 39.5 us  [xor_wide(): lax.ppermute(value, 'wide', [(i, i ^ bits) for i in range(lax.axis_size('...]
    ppermute x40 -> x14, starting transfers between devices: 75.1 us -> 18.7 us  [xor_wide(): lax.ppermute(value, 'wide', [(i, i ^ bits) for i in range(lax.axis_size('...]
    unnamed x430 -> x181, local copies, waits for them, and re-layouts: 64.7 us -> 25.1 us
    slice x15 -> x11, local copies, waits for them, and re-layouts: 28.1 us -> 3.53 us  [the longest x1 0.74 us: local(): d_params[2:8]]
  transfers between devices with their start and end apart: 80 -> 51, of which waited for: 21 -> 26; matrix products, arithmetic and copies ran while one was open for 47% -> 22% of each run, Pallas kernels for 9% -> 19%
where the time goes in v2:
time: 768 us; the launch traced here: 760 us
  waiting for transfers between devices  226 us (29%)
  Pallas kernels  166 us (22%)
  other arithmetic  120 us (16%)
  local copies, waits for them, and re-layouts  91.9 us (12%)
  starting transfers between devices  69.3 us (9%)
  matrix products  51.5 us (7%)
  between operations  23.3 us (3%)
  blocking collectives  12.3 us (2%)
    ppermute x27, waiting for transfers between devices, xor_narrow(): lax.ppermute(value, NARROW, [(i, i ^ bits) for i in range(lax.axis_size(N...  137 us
    dot_general x12, matrix products, mm(): return lax.dot_general(a, b, dims, preferred_element_type=F32)  49.5 us
    all_to_all x7, waiting for transfers between devices, swap_wide(): return lax.all_to_all(value, 'wide', 0, 0, tiled=True)  40.8 us
    ppermute x14, waiting for transfers between devices, xor_wide(): lax.ppermute(value, 'wide', [(i, i ^ bits) for i in range(lax.axis_size('...  39.5 us
    all_to_all x7, starting transfers between devices, swap_wide(): return lax.all_to_all(value, 'wide', 0, 0, tiled=True)  31.3 us
    pallas_call x2, Pallas kernels, collect(): pl.pallas_call(functools.partial(collect_kernel, shift, first), grid=(par...  30.8 us
    unnamed x181, local copies, waits for them, and re-layouts  25.1 us
    pallas_call x1, Pallas kernels, attend_back(): pl.pallas_call(attend_back_kernel, grid=(slots,), in_specs=[one, two, oth...  25 us
  transfers between devices with their start and end apart: 51, of which 26 were waited for; matrix products, arithmetic and copies ran while one was open for 22% of the time, Pallas kernels for 19%

profile of v2, /device:TPU:0, one launch (start us, length us, event | category | flops | bytes accessed | tf_op | source)
XLA Modules:
  0.0 760.5 jit_solution(12680083857054908532)
XLA Ops:
  15.6 6.8 all-to-all-start
  23.4 7.5 all-to-all-done
  33.1 15.0 %table_rows.1.table_ref = f32[26752,96]{1,0:T(8,128)} custom-call(f32[96,12672]{1,0:T(8,128)} %bitcast.262, bf16[96,12672]{1,0:T(8,128)(2,1)} %collective-permute-done.other_ref), custom_call_target="tpu_custom_call" | custom-call | flops 10000000000 | bytes 40000000 | tf_op jit(solution)/shard_map/table_rows/pallas_call | solution.py:538
  49.5 15.0 %lookup.1 = bf16[8192,96]{1,0:T(8,128)(2,1)} custom-call(s32[4,1,2048]{2,1,0:T(1,128)} %and_select_fusion.id_ref, f32[26752,96]{1,0:T(8,128)} %table_rows.1.table_ref), custom_call_target="tpu_custom_call" | custom-call | tf_op jit(solution)/shard_map/lookup/pallas_call | solution.py:570
  69.1 16.1 %collective-permute-done.1 = bf16[8,512,96]{1,2,0:T(8,128)(2,1)} collective-permute-done((bf16[8,512,96]{1,2,0:T(8,128)(2,1)S(1)}, bf16[8,512,96]{1,2,0:T(8,128)(2,1)}, u32[]{:S(2)}, u32[]{:S(2)}) %collective-permute-start.1) | collective-permute-done | bytes 786464 | tf_op jit(solution)/shard_map/ppermute | solution.py:34
  89.1 4.2 all-to-all-start.1
  93.4 20.1 %collective-permute-done.3.a2 = bf16[768,768]{1,0:T(8,128)(2,1)S(1)} collective-permute-done((bf16[768,768]{1,0:T(8,128)(2,1)}, bf16[768,768]{1,0:T(8,128)(2,1)S(1)}, u32[]{:S(2)}, u32[]{:S(2)}) %collective-permute-start.3) | collective-permute-done | bytes 1179680 | tf_op jit(solution)/shard_map/ppermute | solution.py:34
  113.6 3.1 convert_element_type.241
  118.7 6.7 all-gather.5.cloned.1.call-done.bc0
  127.1 3.9 copy.320
  131.0 4.4 all-to-all-start.3
  147.3 8.1 %qkv.1 = (bf16[4,512,192]{2,1,0:T(8,128)(2,1)}, bf16[4,512,384]{2,1,0:T(8,128)(2,1)}, bf16[512,768]{1,0:T(8,128)(2,1)}, f32[512,768]{1,0:T(8,128)}) custom-call(bf16[8,560,96]{2,1,0:T(8,128)(2,1)} %copy.319.recv_ref, f32[12,768]{1,0:T(8,128)} %pad_maximum_fusion.12.par_ref, bf16[768,768]{1,0:T(8,128)(2,1)} %all-gather.3.cloned.1.call-done.a0, ...), custom_call_target="tpu_custom_call" | custom-call | tf_op jit(solution)/shard_map/qkv/pallas_call | solution.py:201
  159.2 14.7 %attend.1 = (bf16[4,512,192]{2,1,0:T(8,128)(2,1)}, f32[4,3,512]{2,1,0:T(4,128)}) custom-call(bf16[4,512,192]{2,1,0:T(8,128)(2,1)} %get-tuple-element.99.q_ref, bf16[4,512,384]{2,1,0:T(8,128)(2,1)} %get-tuple-element.100.own_ref, bf16[4,512,384]{2,1,0:T(8,128)(2,1)} %collective-permute-done.5.far_ref), custom_call_target="tpu_custom_call" | custom-call | tf_op jit(solution)/shard_map/attend/pallas_call | solution.py:248
  173.9 14.9 %collective-permute-done.6.bc2 = bf16[2,768,768]{2,1,0:T(8,128)(2,1)} collective-permute-done((bf16[2,768,768]{2,1,0:T(8,128)(2,1)}, bf16[2,768,768]{2,1,0:T(8,128)(2,1)}, u32[]{:S(2)}, u32[]{:S(2)}) %collective-permute-start.6) | collective-permute-done | bytes 2359328 | tf_op jit(solution)/shard_map/ppermute | solution.py:34
  188.8 4.7 all-to-all-done.3
  198.0 15.6 %feed.1 = (f32[512,768]{1,0:T(8,128)}, f32[512,768]{1,0:T(8,128)}, f32[512,768]{1,0:T(8,128)}, bf16[512,768]{1,0:T(8,128)(2,1)}, f32[4,512,768]{2,1,0:T(8,128)}, /*index=5*/bf16[320,768]{1,0:T(8,128)(2,1)}) custom-call(bf16[4,512,192]{2,1,0:T(8,128)(2,1)} %get-tuple-element.104.mixed_ref, f32[512,768]{1,0:T(8,128)} %get-tuple-element.105.start_ref, ...), custom_call_target="tpu_custom_call" | custom-call | tf_op jit(solution)/shard_map/feed/pallas_call | solution.py:296
  217.8 7.9 %collective-permute-done.10 = bf16[80,768]{1,0:T(8,128)(2,1)S(1)} collective-permute-done((bf16[80,768]{1,0:T(8,128)(2,1)S(1)}, bf16[80,768]{1,0:T(8,128)(2,1)S(1)}, u32[]{:S(2)}, u32[]{:S(2)}) %collective-permute-start.10) | collective-permute-done | bytes 122912 | tf_op jit(solution)/shard_map/ppermute | solution.py:40
  226.8 4.0 all-to-all-start.2
  230.8 19.0 %collective-permute-done.12 = bf16[768,1664]{1,0:T(8,128)(2,1)} collective-permute-done((bf16[768,1664]{1,0:T(8,128)(2,1)}, bf16[768,1664]{1,0:T(8,128)(2,1)}, u32[]{:S(2)}, u32[]{:S(2)}) %collective-permute-start.12) | collective-permute-done | bytes 2555936 | tf_op jit(solution)/shard_map/ppermute | solution.py:34
  256.7 3.7 fusion.92
  260.4 3.7 fusion.93
  264.1 3.7 fusion.94
  270.7 5.9 exponential_reduce_fusion
  276.6 12.3 %all_to_all.45 = f32[8,3,640]{2,1,0:T(4,128)S(1)} all-to-all(f32[8,3,640]{2,1,0:T(4,128)S(1)} %broadcast_in_dim.197), channel_id=1, replica_groups=mesh['wide'=8,'line'=2,'core'=2] {'wide'}, dimensions={0} | all-to-all | bytes 122880 | tf_op jit(solution)/shard_map/all_to_all | solution.py:44
  289.6 4.3 fusion.9
  294.0 5.6 fusion.95
  299.6 3.7 fusion.97
  305.3 5.6 add_convert_fusion.2
  310.9 3.7 all-to-all-start.5
  314.7 6.4 fusion.98
  321.1 3.8 fusion.99
  324.9 4.5 fusion.100
  329.5 4.1 fusion.73
  333.6 4.6 all-to-all-done.5
  338.3 8.4 %collective-permute-done.14 = bf16[80,768]{1,0:T(8,128)(2,1)S(1)} collective-permute-done((bf16[80,768]{1,0:T(8,128)(2,1)S(1)}, bf16[80,768]{1,0:T(8,128)(2,1)S(1)}, u32[]{:S(2)}, u32[]{:S(2)}) %collective-permute-start.14) | collective-permute-done | bytes 122912 | tf_op jit(solution)/shard_map/ppermute | solution.py:40
  349.1 3.7 add_convert_fusion.1
  352.8 24.9 %feed_back.1 = (f32[512,768]{1,0:T(8,128)}, bf16[512,768]{1,0:T(8,128)(2,1)}, bf16[4,512,192]{2,1,0:T(8,128)(2,1)}, bf16[2,2,768,768]{3,2,1,0:T(8,128)(2,1)}, bf...) custom-call(bf16[320,768]{1,0:T(8,128)(2,1)} %pad_maximum_fusion.7.rows_ref, ...), custom_call_target="tpu_custom_call" | custom-call | tf_op jit(solution)/shard_map/feed_back/pallas_call | solution.py:371
  380.4 28.9 %collective-permute-done.17 = bf16[384,1664]{1,0:T(8,128)(2,1)S(1)} collective-permute-done((bf16[384,1664]{1,0:T(8,128)(2,1)S(1)}, bf16[384,1664]{1,0:T(8,128)(2,1)S(1)}, u32[]{:S(2)}, u32[]{:S(2)}) %collective-permute-start.17) | collective-permute-done | bytes 1277984 | tf_op jit(solution)/shard_map/ppermute | solution.py:34
  410.3 25.0 %attend_back.1 = (bf16[4,512,192]{2,1,0:T(8,128)(2,1)}, f32[4,512,384]{2,1,0:T(8,128)}, bf16[4,512,384]{2,1,0:T(8,128)(2,1)}) custom-call(bf16[4,512,192]{2,1,0:T(8,128)(2,1)} %get-tuple-element.99.q_ref, bf16[4,512,384]{2,1,0:T(8,128)(2,1)} %get-tuple-element.100.own_ref, bf16[4,512,384]{2,1,0:T(8,128)(2,1)} %collective-permute-done.5.far_ref, ...), custom_call_target="tpu_custom_call" | custom-call | tf_op jit(solution)/shard_map/attend_back/pallas_call | solution.py:426
  435.3 3.3 convert_element_type.263
  450.1 9.8 %qkv_back.1 = (bf16[8,528,96]{2,1,0:T(8,128)(2,1)}, bf16[4,512,576]{2,1,0:T(8,128)(2,1)}, f32[3,768]{1,0:T(4,128)}) custom-call(bf16[4,512,192]{2,1,0:T(8,128)(2,1)} %get-tuple-element.129.dq_ref, f32[4,512,384]{2,1,0:T(8,128)} %get-tuple-element.130.d_own_ref, bf16[4,512,384]{2,1,0:T(8,128)(2,1)} %copy-done.25, ...), custom_call_target="tpu_custom_call" | custom-call | tf_op jit(solution)/shard_map/qkv_back/pallas_call | solution.py:485
  459.9 13.0 %collective-permute-done.23 = bf16[768,768]{1,0:T(8,128)(2,1)S(1)} collective-permute-done((bf16[768,768]{1,0:T(8,128)(2,1)}, bf16[768,768]{1,0:T(8,128)(2,1)S(1)}, u32[]{:S(2)}, u32[]{:S(2)}) %collective-permute-start.23) | collective-permute-done | bytes 1179680 | tf_op jit(solution)/shard_map/ppermute | solution.py:34
  477.6 4.0 all-to-all-start.6
  481.6 7.6 qkv_grads.1
  489.2 5.5 add_convert_fusion
  494.7 11.2 %all-to-all-done.6 = bf16[8,560,96]{1,2,0:T(8,128)(2,1)S(1)} async-done(((bf16[8,560,96]{1,2,0:T(8,128)(2,1)}), bf16[8,560,96]{1,2,0:T(8,128)(2,1)S(1)}, u32[]{:S(2)}, u32[]{:S(2)}) %all-to-all-start.6) | async-done | bytes 860192 | tf_op jit(solution)/shard_map/all_to_all | solution.py:44
  506.9 4.0 all-to-all-start.7
  518.2 20.6 %collective-permute-done.22 = bf16[768,768]{1,0:T(8,128)(2,1)} collective-permute-done((bf16[768,768]{1,0:T(8,128)(2,1)}, bf16[768,768]{1,0:T(8,128)(2,1)}, u32[]{:S(2)}, u32[]{:S(2)}) %collective-permute-start.22) | collective-permute-done | bytes 1179680 | tf_op jit(solution)/shard_map/ppermute | solution.py:34
  557.9 11.2 %all-to-all-done.7 = bf16[8,96,1664]{2,1,0:T(8,128)(2,1)S(1)} async-done(((bf16[8,96,1664]{2,1,0:T(8,128)(2,1)}), bf16[8,96,1664]{2,1,0:T(8,128)(2,1)S(1)}, u32[]{:S(2)}, u32[]{:S(2)}) %all-to-all-start.7) | async-done | bytes 2555936 | tf_op jit(solution)/shard_map/all_to_all | solution.py:44
  583.7 5.0 collective-permute-done.35
  592.5 4.5 collective-permute-done.40
  597.0 3.4 collective-permute-start.38
  607.8 3.5 pad_maximum_fusion.1.grad_ref
  611.3 10.1 %collect.2.refs_0_ = f32[12672,96]{1,0:T(8,128)} custom-call(s32[2,1,4480]{2,1,0:T(1,128)} %copy.332.key_ref, s32[2,1,1]{2,1,0:T(1,128)} %copy.333.count_ref, bf16[2,4480,96]{2,1,0:T(8,128)(2,1)} %pad_maximum_fusion.1.grad_ref), custom_call_target="tpu_custom_call" | custom-call | tf_op jit(solution)/shard_map/collect/pallas_call | solution.py:646
  623.7 3.2 stack.120
  626.9 3.2 stack.118
  635.7 3.3 stack.121
  644.1 3.5 pad_maximum_fusion.grad_ref
  647.7 20.7 %collect.3 = f32[96,12672]{1,0:T(8,128)} custom-call(s32[2,1,4480]{2,1,0:T(1,128)} %reshape.597.key_ref, s32[2,1,1]{2,1,0:T(1,128)} %copy.334.count_ref, bf16[2,4480,96]{2,1,0:T(8,128)(2,1)} %pad_maximum_fusion.grad_ref, f32[12672,96]{1,0:T(8,128)} %collect.2.refs_0_), custom_call_target="tpu_custom_call" | custom-call | tf_op jit(solution)/shard_map/collect/pallas_call | solution.py:646
  669.6 4.4 multiply_reduce_fusion
  688.5 9.1 %collective-permute-done.31 = bf16[96,768]{0,1:T(8,128)(2,1)} collective-permute-done((bf16[96,768]{0,1:T(8,128)(2,1)S(1)}, bf16[96,768]{0,1:T(8,128)(2,1)}, u32[]{:S(2)}, u32[]{:S(2)}) %collective-permute-start.31) | collective-permute-done | bytes 147488 | tf_op jit(solution)/shard_map/ppermute | solution.py:40
  703.5 3.9 all-to-all-start.8
  724.0 13.1 %fusion.29 = (f32[12672,96]{0,1:T(8,128)}, f32[12672,96]{0,1:T(8,128)}, f32[12672,96]{0,1:T(8,128)}) fusion(f32[96,12672]{1,0:T(8,128)} %collect.3, f32[]{:T(128)S(6)} %div.124, f32[12672,96]{0,1:T(8,128)} %param.46, f32[12672,96]{0,1:T(8,128)} %param.38, f32[12672,96]{0,1:T(8,128)} %param.30), kind=kLoop, calls=%fused_computation.81 | loop fusion | flops 18247680 | bytes 34062340 | tf_op jit(solution)/shard_map/transpose | solution.py:993
  737.3 10.4 %multiply_subtract_fusion = (f32[96,12672]{1,0:T(8,128)}, f32[96,12672]{1,0:T(8,128)}, f32[96,12672]{1,0:T(8,128)}) fusion(f32[96,12672]{1,0:T(8,128)} %param.31, f32[]{:T(128)S(6)} %div.124, bf16[96,13312]{1,0:T(8,128)(2,1)S(1)} %bitcast.261, f32[96,12672]{1,0:T(8,128)} %param.39, f32[96,12672]{1,0:T(8,128)} %param.47), kind=kLoop, calls=%fused_computation.18 | loop fusion | flops 20680704 | bytes 31629316 | tf_op jit(solution)/shard_map/sub | solution.py:1002
  (451 shorter events, 187.6 us)
Async XLA Ops:
  7.2 80.4 %all-gather.3.cloned.1.call-start = ((), (), s32[]{:S(2)}) async-start(), calls=%async_computation.9 | async-start | bytes 1327104 | tf_op jit(solution)/shard_map/all_gather | solution.py:54
  12.8 19.7 %copy-start.23 = (f32[128,768]{1,0:T(8,128)S(1)}, f32[128,768]{1,0:T(8,128)}, u32[]{:S(2)}) copy-start(f32[128,768]{1,0:T(8,128)} %param.36) | copy-start | bytes 1179652
  12.8 20.0 %collective-permute-start = (bf16[96,12672]{1,0:T(8,128)(2,1)S(1)}, bf16[96,12672]{1,0:T(8,128)(2,1)}, u32[]{:S(2)}, u32[]{:S(2)}) collective-permute-start(bf16[96,12672]{1,0:T(8,128)(2,1)S(1)} %bitcast_convert_fusion.3), channel_id=1, source_target_pairs={{0,1},{1,0},{2,3},{3,2},{4,5},{5,4},{6,7},{7,6},{8,9},{9,8},{10,11... | collective-permute-start | bytes 7299080 | tf_op jit(solution)/shard_map/ppermute | solution.py:34
  15.6 15.3 %all-to-all-start = ((s32[8,2,1408]{2,1,0:T(2,128)}), s32[8,2,1408]{2,1,0:T(2,128)S(1)}, u32[]{:S(2)}, u32[]{:S(2)}) async-start(s32[8,2,1408]{2,1,0:T(2,128)} %broadcast_in_dim.181), calls=%async_computation | async-start | bytes 180224 | tf_op jit(solution)/shard_map/all_to_all | solution.py:44
  22.4 103.1 %all-gather.5.cloned.1.call-start = ((), (), s32[]{:S(2)}) async-start(), calls=%async_computation.10 | async-start | bytes 2654208 | tf_op jit(solution)/shard_map/all_gather | solution.py:54
  30.9 17.2 %copy-start.43 = (s32[8,2,1408]{2,1,0:T(2,128)}, s32[8,2,1408]{2,1,0:T(2,128)S(1)}, u32[]{:S(2)}) copy-start(s32[8,2,1408]{2,1,0:T(2,128)S(1)} %all-to-all-done) | copy-start | bytes 270340
  66.8 18.4 %collective-permute-start.1 = (bf16[8,512,96]{1,2,0:T(8,128)(2,1)S(1)}, bf16[8,512,96]{1,2,0:T(8,128)(2,1)}, u32[]{:S(2)}, u32[]{:S(2)}) collective-permute-start(bf16[8,512,96]{1,2,0:T(8,128)(2,1)S(1)} %copy.310), channel_id=1, source_target_pairs={{0,2},{1,3},{2,0},{3,1},{4,6},{5,7},{6,4},{7,5},{8,10},{9,11},{10,... | collective-permute-start | bytes 2359304 | tf_op jit(solution)/shard_map/ppermute | solution.py:34
  87.6 26.0 %collective-permute-start.3 = (bf16[768,768]{1,0:T(8,128)(2,1)}, bf16[768,768]{1,0:T(8,128)(2,1)S(1)}, u32[]{:S(2)}, u32[]{:S(2)}) collective-permute-start(bf16[768,768]{1,0:T(8,128)(2,1)} %all-gather.3.cloned.1.call-done.a0), channel_id=1, source_target_pairs={{0,2},{1,3},{2,0},{3,1},{4,6},{5,7},{6,4},{7,5},{8,10},{9,11},{10,... | collective-permute-start | bytes 3538952 | tf_op jit(solution)/shard_map/ppermute | solution.py:34
  89.1 38.0 %all-to-all-start.1 = ((bf16[8,560,96]{1,2,0:T(8,128)(2,1)}), bf16[8,560,96]{1,2,0:T(8,128)(2,1)}, u32[]{:S(2)}, u32[]{:S(2)}) async-start(bf16[8,560,96]{1,2,0:T(8,128)(2,1)} %fusion.30), calls=%async_computation.1 | async-start | bytes 1966080 | tf_op jit(solution)/shard_map/all_to_all | solution.py:44
  93.4 32.1 %collective-permute-start.2 = (bf16[768,768]{1,0:T(8,128)(2,1)}, bf16[768,768]{1,0:T(8,128)(2,1)S(1)}, u32[]{:S(2)}, u32[]{:S(2)}) collective-permute-start(bf16[768,768]{1,0:T(8,128)(2,1)} %all-gather.3.cloned.1.call-done.a0), channel_id=1, source_target_pairs={{0,1},{1,0},{2,3},{3,2},{4,5},{5,4},{6,7},{7,6},{8,9},{9,8},{10,11... | collective-permute-start | bytes 3538952 | tf_op jit(solution)/shard_map/ppermute | solution.py:34
  113.6 13.6 %collective-permute-start.4 = (bf16[768,768]{1,0:T(8,128)(2,1)S(1)}, bf16[768,768]{1,0:T(8,128)(2,1)S(1)}, u32[]{:S(2)}, u32[]{:S(2)}) collective-permute-start(bf16[768,768]{1,0:T(8,128)(2,1)S(1)} %collective-permute-done.3.a2), channel_id=1, source_target_pairs={{0,1},{1,0},{2,3},{3,2},{4,5},{5,4},{6,7},{7,6},{8,9},{9,8},{10,11... | collective-permute-start | bytes 3538952 | tf_op jit(solution)/shard_map/ppermute | solution.py:34
  131.0 62.5 %all-to-all-start.3 = ((bf16[8,96,1664]{2,1,0:T(8,128)(2,1)}), bf16[8,96,1664]{2,1,0:T(8,128)(2,1)}, u32[]{:S(2)}, u32[]{:S(2)}) async-start(bf16[8,96,1664]{2,1,0:T(8,128)(2,1)} %copy.320), calls=%async_computation.3 | async-start | bytes 5111808 | tf_op jit(solution)/shard_map/all_to_all | solution.py:44
  135.5 38.4 %sort.9.cloned.1.call-start = ((), (), s32[]{:S(2)}) async-start(), calls=%async_computation.11 | async-start | bytes 215072 | tf_op jit(solution)/shard_map/sort | solution.py:820
  135.8 53.1 %collective-permute-start.6 = (bf16[2,768,768]{2,1,0:T(8,128)(2,1)}, bf16[2,768,768]{2,1,0:T(8,128)(2,1)}, u32[]{:S(2)}, u32[]{:S(2)}) collective-permute-start(bf16[2,768,768]{2,1,0:T(8,128)(2,1)} %all-gather.5.cloned.1.call-done.bc0), channel_id=1, source_target_pairs={{0,2},{1,3},{2,0},{3,1},{4,6},{5,7},{6,4},{7,5},{8,10},{9,11},{10,... | collective-permute-start | bytes 7077896 | tf_op jit(solution)/shard_map/ppermute | solution.py:34
  155.4 39.5 %copy-start.72 = (s32[1,2,256]{2,1,0:T(2,128)S(1)}, s32[1,2,256]{2,1,0:T(2,128)}, u32[]{:S(2)}) copy-start(s32[1,2,256]{2,1,0:T(2,128)} %param.28) | copy-start | bytes 6148
  155.4 39.5 %copy-start.76 = (s32[8,2,1]{0,1,2:T(2,128)S(1)}, s32[8,2,1]{0,1,2:T(2,128)}, u32[]{:S(2)}) copy-start(s32[8,2,1]{0,1,2:T(2,128)} %copy-done.75) | copy-start | bytes 196
  155.4 3.8 collective-permute-start.5
  157.2 40.8 %collective-permute-start.7 = (bf16[2,768,768]{2,1,0:T(8,128)(2,1)S(1)}, bf16[2,768,768]{2,1,0:T(8,128)(2,1)}, u32[]{:S(2)}, u32[]{:S(2)}) collective-permute-start(bf16[2,768,768]{2,1,0:T(8,128)(2,1)S(1)} %copy-done.6), channel_id=1, source_target_pairs={{0,1},{1,0},{2,3},{3,2},{4,5},{5,4},{6,7},{7,6},{8,9},{9,8},{10,11... | collective-permute-start | bytes 7077896 | tf_op jit(solution)/shard_map/ppermute | solution.py:34
  188.8 9.2 %collective-permute-start.8 = (bf16[2,768,768]{2,1,0:T(8,128)(2,1)}, bf16[2,768,768]{2,1,0:T(8,128)(2,1)}, u32[]{:S(2)}, u32[]{:S(2)}) collective-permute-start(bf16[2,768,768]{2,1,0:T(8,128)(2,1)} %collective-permute-done.6.bc2), channel_id=1, source_target_pairs={{0,1},{1,0},{2,3},{3,2},{4,5},{5,4},{6,7},{7,6},{8,9},{9,8},{10,11... | collective-permute-start | bytes 7077896 | tf_op jit(solution)/shard_map/ppermute | solution.py:34
  193.5 56.3 %collective-permute-start.12 = (bf16[768,1664]{1,0:T(8,128)(2,1)}, bf16[768,1664]{1,0:T(8,128)(2,1)}, u32[]{:S(2)}, u32[]{:S(2)}) collective-permute-start(bf16[768,1664]{1,0:T(8,128)(2,1)} %bitcast.24), channel_id=1, source_target_pairs={{0,2},{1,3},{2,0},{3,1},{4,6},{5,7},{6,4},{7,5},{8,10},{9,11},{10,... | collective-permute-start | bytes 7667720 | tf_op jit(solution)/shard_map/ppermute | solution.py:34
  213.6 37.4 %slice-start.6 = ((s32[8,2,1408]{2,1,0:T(2,128)}), s32[8,2,256]{2,1,0:T(2,128)S(1)}, s32[]{:S(2)}) async-start(s32[8,2,1408]{2,1,0:T(2,128)} %copy-done.43), calls=%async_computation.19 | async-start | bytes 32768 | tf_op jit(solution)/shard_map/slice | solution.py:711
  214.6 1.6 collective-permute-start.9
  217.2 8.6 %collective-permute-start.10 = (bf16[80,768]{1,0:T(8,128)(2,1)S(1)}, bf16[80,768]{1,0:T(8,128)(2,1)S(1)}, u32[]{:S(2)}, u32[]{:S(2)}) collective-permute-start(bf16[80,768]{1,0:T(8,128)(2,1)S(1)} %slice.303), channel_id=1, source_target_pairs={{0,16},{4,20},{8,24},{12,28},{16,0},{20,4},{24,8},{28,12},{1,17},{... | collective-permute-start | bytes 368648 | tf_op jit(solution)/shard_map/ppermute | solution.py:40
  226.8 29.9 %all-to-all-start.2 = ((bf16[8,80,768]{2,1,0:T(8,128)(2,1)}), bf16[8,80,768]{2,1,0:T(8,128)(2,1)S(1)}, u32[]{:S(2)}, u32[]{:S(2)}) async-start(bf16[8,80,768]{2,1,0:T(8,128)(2,1)} %broadcast_in_dim.191), calls=%async_computation.2 | async-start | bytes 1966080 | tf_op jit(solution)/shard_map/all_to_all | solution.py:44
  249.8 14.3 %collective-permute-start.13 = (bf16[768,1664]{1,0:T(8,128)(2,1)}, bf16[768,1664]{1,0:T(8,128)(2,1)}, u32[]{:S(2)}, u32[]{:S(2)}) collective-permute-start(bf16[768,1664]{1,0:T(8,128)(2,1)} %collective-permute-done.12), channel_id=1, source_target_pairs={{0,1},{1,0},{2,3},{3,2},{4,5},{5,4},{6,7},{7,6},{8,9},{9,8},{10,11... | collective-permute-start | bytes 7667720 | tf_op jit(solution)/shard_map/ppermute | solution.py:34
  251.0 16.8 %collective-permute-start.11 = (bf16[768,1664]{1,0:T(8,128)(2,1)}, bf16[768,1664]{1,0:T(8,128)(2,1)S(1)}, u32[]{:S(2)}, u32[]{:S(2)}) collective-permute-start(bf16[768,1664]{1,0:T(8,128)(2,1)} %bitcast.24), channel_id=1, source_target_pairs={{0,1},{1,0},{2,3},{3,2},{4,5},{5,4},{6,7},{7,6},{8,9},{9,8},{10,11... | collective-permute-start | bytes 7667720 | tf_op jit(solution)/shard_map/ppermute | solution.py:34
  267.8 37.5 %copy-start.4 = (f32[640,1664]{1,0:T(8,128)}, f32[640,1664]{1,0:T(8,128)S(1)}, u32[]{:S(2)}) copy-start(f32[640,1664]{1,0:T(8,128)S(1)} %fusion.94) | copy-start | bytes 12779524
  289.6 15.7 %copy-start.69 = (f32[640]{0:T(1024)}, f32[640]{0:T(1024)S(1)}, u32[]{:S(2)}) copy-start(f32[640]{0:T(1024)S(1)} %get-tuple-element.425) | copy-start | bytes 7684
  310.9 27.2 %all-to-all-start.5 = ((bf16[8,80,768]{2,1,0:T(8,128)(2,1)}), bf16[8,80,768]{2,1,0:T(8,128)(2,1)S(1)}, u32[]{:S(2)}, u32[]{:S(2)}) async-start(bf16[8,80,768]{2,1,0:T(8,128)(2,1)} %bitcast.31), calls=%async_computation.5 | async-start | bytes 1966080 | tf_op jit(solution)/shard_map/all_to_all | solution.py:44
  338.1 11.0 %collective-permute-start.16 = (bf16[768,1664]{1,0:T(8,128)(2,1)}, bf16[768,1664]{1,0:T(8,128)(2,1)}, u32[]{:S(2)}, u32[]{:S(2)}) collective-permute-start(bf16[768,1664]{1,0:T(8,128)(2,1)} %fusion.73), channel_id=1, source_target_pairs={{0,1},{1,0},{2,3},{3,2},{4,5},{5,4},{6,7},{7,6},{8,9},{9,8},{10,11... | collective-permute-start | bytes 7667720 | tf_op jit(solution)/shard_map/ppermute | solution.py:34
  338.2 8.4 %collective-permute-start.14 = (bf16[80,768]{1,0:T(8,128)(2,1)S(1)}, bf16[80,768]{1,0:T(8,128)(2,1)S(1)}, u32[]{:S(2)}, u32[]{:S(2)}) collective-permute-start(bf16[80,768]{1,0:T(8,128)(2,1)S(1)} %reduce_sum.261), channel_id=1, source_target_pairs={{0,16},{4,20},{8,24},{12,28},{16,0},{20,4},{24,8},{28,12},{1,17},{... | collective-permute-start | bytes 368648 | tf_op jit(solution)/shard_map/ppermute | solution.py:40
  346.7 1.6 collective-permute-start.15
  377.7 57.6 %collective-permute-start.19 = (bf16[2,2,768,768]{3,2,1,0:T(8,128)(2,1)}, bf16[2,2,768,768]{3,2,1,0:T(8,128)(2,1)}, u32[]{:S(2)}, u32[]{:S(2)}) collective-permute-start(bf16[2,2,768,768]{3,2,1,0:T(8,128)(2,1)} %get-tuple-element.128), channel_id=1, source_target_pairs={{0,1},{1,0},{2,3},{3,2},{4,5},{5,4},{6,7},{7,6},{8,9},{9,8},{10,11... | collective-permute-start | bytes 14155784 | tf_op jit(solution)/shard_map/ppermute | solution.py:34
  378.1 31.1 %collective-permute-start.17 = (bf16[384,1664]{1,0:T(8,128)(2,1)S(1)}, bf16[384,1664]{1,0:T(8,128)(2,1)S(1)}, u32[]{:S(2)}, u32[]{:S(2)}) collective-permute-start(bf16[384,1664]{1,0:T(8,128)(2,1)S(1)} %get-tuple-element.446), channel_id=1, source_target_pairs={{0,2},{1,3},{2,0},{3,1},{4,6},{5,7},{6,4},{7,5},{8,10},{9,11},{10,... | collective-permute-start | bytes 3833864 | tf_op jit(solution)/shard_map/ppermute | solution.py:34
  379.7 62.1 %collective-permute-start.18 = (bf16[384,1664]{1,0:T(8,128)(2,1)S(1)}, bf16[384,1664]{1,0:T(8,128)(2,1)S(1)}, u32[]{:S(2)}, u32[]{:S(2)}) collective-permute-start(bf16[384,1664]{1,0:T(8,128)(2,1)S(1)} %get-tuple-element.445), channel_id=1, source_target_pairs={{0,2},{1,3},{2,0},{3,1},{4,6},{5,7},{6,4},{7,5},{8,10},{9,11},{10,... | collective-permute-start | bytes 3833864 | tf_op jit(solution)/shard_map/ppermute | solution.py:34
  410.3 28.3 %slice-start.4 = ((s8[4718592]{0:T(1024)(128)(4,1)}), s8[524288]{0:T(1024)(128)(4,1)S(1)}, s32[]{:S(2)}) async-start(s8[4718592]{0:T(1024)(128)(4,1)} %bitcast.277), calls=%async_computation.17 | async-start | bytes 1048576
  442.8 6.2 collective-permute-start.20
  444.4 28.6 %collective-permute-start.23 = (bf16[768,768]{1,0:T(8,128)(2,1)}, bf16[768,768]{1,0:T(8,128)(2,1)S(1)}, u32[]{:S(2)}, u32[]{:S(2)}) collective-permute-start(bf16[768,768]{1,0:T(8,128)(2,1)} %get-tuple-element.447), channel_id=1, source_target_pairs={{0,2},{1,3},{2,0},{3,1},{4,6},{5,7},{6,4},{7,5},{8,10},{9,11},{10,... | collective-permute-start | bytes 3538952 | tf_op jit(solution)/shard_map/ppermute | solution.py:34
  445.7 43.5 %collective-permute-start.27 = (bf16[768,1664]{1,0:T(8,128)(2,1)}, bf16[768,1664]{1,0:T(8,128)(2,1)}, u32[]{:S(2)}, u32[]{:S(2)}) collective-permute-start(bf16[768,1664]{1,0:T(8,128)(2,1)} %fusion.99), channel_id=1, source_target_pairs={{0,1},{1,0},{2,3},{3,2},{4,5},{5,4},{6,7},{7,6},{8,9},{9,8},{10,11... | collective-permute-start | bytes 7667720 | tf_op jit(solution)/shard_map/ppermute | solution.py:34
  477.6 28.4 %all-to-all-start.6 = ((bf16[8,560,96]{1,2,0:T(8,128)(2,1)}), bf16[8,560,96]{1,2,0:T(8,128)(2,1)S(1)}, u32[]{:S(2)}, u32[]{:S(2)}) async-start(bf16[8,560,96]{1,2,0:T(8,128)(2,1)} %copy.326), calls=%async_computation.6 | async-start | bytes 1966080 | tf_op jit(solution)/shard_map/all_to_all | solution.py:44
  489.2 23.1 %collective-permute-start.21 = (bf16[2,768,768]{2,1,0:T(8,128)(2,1)}, bf16[2,768,768]{2,1,0:T(8,128)(2,1)}, u32[]{:S(2)}, u32[]{:S(2)}) collective-permute-start(bf16[2,768,768]{2,1,0:T(8,128)(2,1)} %get-tuple-element.137), channel_id=1, source_target_pairs={{0,1},{1,0},{2,3},{3,2},{4,5},{5,4},{6,7},{7,6},{8,9},{9,8},{10,11... | collective-permute-start | bytes 7077896 | tf_op jit(solution)/shard_map/ppermute | solution.py:34
  506.9 62.2 %all-to-all-start.7 = ((bf16[8,96,1664]{2,1,0:T(8,128)(2,1)}), bf16[8,96,1664]{2,1,0:T(8,128)(2,1)S(1)}, u32[]{:S(2)}, u32[]{:S(2)}) async-start(bf16[8,96,1664]{2,1,0:T(8,128)(2,1)} %bitcast.43), calls=%async_computation.7 | async-start | bytes 5111808 | tf_op jit(solution)/shard_map/all_to_all | solution.py:44
  510.9 27.9 %collective-permute-start.22 = (bf16[768,768]{1,0:T(8,128)(2,1)}, bf16[768,768]{1,0:T(8,128)(2,1)}, u32[]{:S(2)}, u32[]{:S(2)}) collective-permute-start(bf16[768,768]{1,0:T(8,128)(2,1)} %get-tuple-element.448), channel_id=1, source_target_pairs={{0,2},{1,3},{2,0},{3,1},{4,6},{5,7},{6,4},{7,5},{8,10},{9,11},{10,... | collective-permute-start | bytes 3538952 | tf_op jit(solution)/shard_map/ppermute | solution.py:34
  512.3 26.6 %slice-start = ((s8[4718592]{0:T(1024)(128)(4,1)}), s8[524288]{0:T(1024)(128)(4,1)S(1)}, s32[]{:S(2)}) async-start(s8[4718592]{0:T(1024)(128)(4,1)} %bitcast.263), calls=%async_computation.13 | async-start | bytes 1048576
  512.3 26.5 %slice-start.1 = ((s8[4718592]{0:T(1024)(128)(4,1)}), s8[4194304]{0:T(1024)(128)(4,1)S(1)}, s32[]{:S(2)}) async-start(s8[4718592]{0:T(1024)(128)(4,1)} %bitcast.263), calls=%async_computation.14 | async-start | bytes 8388608
  514.5 24.3 %copy-start.31 = (bf16[768,768]{1,0:T(8,128)(2,1)S(1)}, bf16[768,768]{1,0:T(8,128)(2,1)}, u32[]{:S(2)}) copy-start(bf16[768,768]{1,0:T(8,128)(2,1)} %copy-done.30) | copy-start | bytes 3538948
  541.7 31.0 %collective-permute-start.33 = (bf16[4,96,768]{2,1,0:T(8,128)(2,1)}, bf16[4,96,768]{2,1,0:T(8,128)(2,1)}, u32[]{:S(2)}, u32[]{:S(2)}) collective-permute-start(bf16[4,96,768]{2,1,0:T(8,128)(2,1)} %fusion.33), channel_id=1, source_target_pairs={{0,4},{4,0},{8,12},{12,8},{16,20},{20,16},{24,28},{28,24},{1,5},{5... | collective-permute-start | bytes 1769480 | tf_op jit(solution)/shard_map/ppermute | solution.py:40
  545.0 31.7 %collective-permute-start.37 = (bf16[4,96,768]{2,1,0:T(8,128)(2,1)}, bf16[4,96,768]{2,1,0:T(8,128)(2,1)}, u32[]{:S(2)}, u32[]{:S(2)}) collective-permute-start(bf16[4,96,768]{2,1,0:T(8,128)(2,1)} %fusion.34), channel_id=1, source_target_pairs={{0,4},{4,0},{8,12},{12,8},{16,20},{20,16},{24,28},{28,24},{1,5},{5... | collective-permute-start | bytes 1769480 | tf_op jit(solution)/shard_map/ppermute | solution.py:40
  553.5 52.0 %collective-permute-start.24 = (bf16[4480,96]{0,1:T(8,128)(2,1)}, bf16[4480,96]{0,1:T(8,128)(2,1)}, u32[]{:S(2)}, u32[]{:S(2)}) collective-permute-start(bf16[4480,96]{0,1:T(8,128)(2,1)} %reshape.603), channel_id=1, source_target_pairs={{0,2},{1,3},{2,0},{3,1},{4,6},{5,7},{6,4},{7,5},{8,10},{9,11},{10,... | collective-permute-start | bytes 2580488 | tf_op jit(solution)/shard_map/ppermute | solution.py:34
  554.8 50.7 %collective-permute-start.26 = (bf16[4480,96]{0,1:T(8,128)(2,1)}, bf16[4480,96]{0,1:T(8,128)(2,1)}, u32[]{:S(2)}, u32[]{:S(2)}) collective-permute-start(bf16[4480,96]{0,1:T(8,128)(2,1)} %reshape.603), channel_id=1, source_target_pairs={{0,1},{1,0},{2,3},{3,2},{4,5},{5,4},{6,7},{7,6},{8,9},{9,8},{10,11... | collective-permute-start | bytes 2580488 | tf_op jit(solution)/shard_map/ppermute | solution.py:34
  557.1 72.9 %collective-permute-start.28 = (bf16[768,768]{1,0:T(8,128)(2,1)}, bf16[768,768]{1,0:T(8,128)(2,1)}, u32[]{:S(2)}, u32[]{:S(2)}) collective-permute-start(bf16[768,768]{1,0:T(8,128)(2,1)} %fusion.28), channel_id=1, source_target_pairs={{0,2},{1,3},{2,0},{3,1},{4,6},{5,7},{6,4},{7,5},{8,10},{9,11},{10,... | collective-permute-start | bytes 3538952 | tf_op jit(solution)/shard_map/ppermute | solution.py:34
  574.4 7.1 collective-permute-start.36
  576.7 11.9 %collective-permute-start.35 = (bf16[96,768]{1,0:T(8,128)(2,1)S(1)}, bf16[96,768]{1,0:T(8,128)(2,1)S(1)}, u32[]{:S(2)}, u32[]{:S(2)}) collective-permute-start(bf16[96,768]{1,0:T(8,128)(2,1)S(1)} %get-tuple-element.463), channel_id=1, source_target_pairs={{0,16},{4,20},{8,24},{12,28},{16,0},{20,4},{24,8},{28,12},{1,17},{... | collective-permute-start | bytes 442376 | tf_op jit(solution)/shard_map/ppermute | solution.py:40
  581.5 11.0 %collective-permute-start.34 = (bf16[96,768]{1,0:T(8,128)(2,1)S(1)}, bf16[96,768]{1,0:T(8,128)(2,1)S(1)}, u32[]{:S(2)}, u32[]{:S(2)}) collective-permute-start(bf16[96,768]{1,0:T(8,128)(2,1)S(1)} %get-tuple-element.461), channel_id=1, source_target_pairs={{0,8},{4,12},{8,0},{12,4},{16,24},{20,28},{24,16},{28,20},{1,9},{5... | collective-permute-start | bytes 442376 | tf_op jit(solution)/shard_map/ppermute | solution.py:40
  588.7 8.4 %collective-permute-start.40 = (bf16[96,768]{1,0:T(8,128)(2,1)S(1)}, bf16[96,768]{1,0:T(8,128)(2,1)S(1)}, u32[]{:S(2)}, u32[]{:S(2)}) collective-permute-start(bf16[96,768]{1,0:T(8,128)(2,1)S(1)} %get-tuple-element.459), channel_id=1, source_target_pairs={{0,24},{4,28},{8,16},{12,20},{16,8},{20,12},{24,0},{28,4},{1,25},{... | collective-permute-start | bytes 442376 | tf_op jit(solution)/shard_map/ppermute | solution.py:40
  592.5 10.1 %collective-permute-start.39 = (bf16[96,768]{1,0:T(8,128)(2,1)S(1)}, bf16[96,768]{1,0:T(8,128)(2,1)S(1)}, u32[]{:S(2)}, u32[]{:S(2)}) collective-permute-start(bf16[96,768]{1,0:T(8,128)(2,1)S(1)} %get-tuple-element.460), channel_id=1, source_target_pairs={{0,16},{4,20},{8,24},{12,28},{16,0},{20,4},{24,8},{28,12},{1,17},{... | collective-permute-start | bytes 442376 | tf_op jit(solution)/shard_map/ppermute | solution.py:40
  597.0 7.0 collective-permute-start.38
  605.5 30.2 %collective-permute-start.25 = (bf16[4480,96]{0,1:T(8,128)(2,1)}, bf16[4480,96]{0,1:T(8,128)(2,1)}, u32[]{:S(2)}, u32[]{:S(2)}) collective-permute-start(bf16[4480,96]{0,1:T(8,128)(2,1)} %collective-permute-done.24), channel_id=1, source_target_pairs={{0,1},{1,0},{2,3},{3,2},{4,5},{5,4},{6,7},{7,6},{8,9},{9,8},{10,11... | collective-permute-start | bytes 2580488 | tf_op jit(solution)/shard_map/ppermute | solution.py:34
  635.0 39.0 %collective-permute-start.29 = (bf16[4,96,768]{2,1,0:T(8,128)(2,1)}, bf16[4,96,768]{2,1,0:T(8,128)(2,1)}, u32[]{:S(2)}, u32[]{:S(2)}) collective-permute-start(bf16[4,96,768]{2,1,0:T(8,128)(2,1)} %fusion.32), channel_id=1, source_target_pairs={{0,4},{4,0},{8,12},{12,8},{16,20},{20,16},{24,28},{28,24},{1,5},{5... | collective-permute-start | bytes 1769480 | tf_op jit(solution)/shard_map/ppermute | solution.py:40
  647.7 20.8 %copy-start.68 = (f32[8,1,128]{2,1,0:T(1,128)S(1)}, f32[8,1,128]{2,1,0:T(1,128)}, u32[]{:S(2)}) copy-start(f32[8,1,128]{2,1,0:T(1,128)} %get-tuple-element.494) | copy-start | bytes 12292
  677.1 11.5 %collective-permute-start.32 = (bf16[96,768]{0,1:T(8,128)(2,1)}, bf16[96,768]{0,1:T(8,128)(2,1)}, u32[]{:S(2)}, u32[]{:S(2)}) collective-permute-start(bf16[96,768]{0,1:T(8,128)(2,1)} %bitcast.293), channel_id=1, source_target_pairs={{0,24},{4,28},{8,16},{12,20},{16,8},{20,12},{24,0},{28,4},{1,25},{... | collective-permute-start | bytes 442376 | tf_op jit(solution)/shard_map/ppermute | solution.py:40
  679.3 18.4 %collective-permute-start.31 = (bf16[96,768]{0,1:T(8,128)(2,1)S(1)}, bf16[96,768]{0,1:T(8,128)(2,1)}, u32[]{:S(2)}, u32[]{:S(2)}) collective-permute-start(bf16[96,768]{0,1:T(8,128)(2,1)S(1)} %bitcast.294), channel_id=1, source_target_pairs={{0,16},{4,20},{8,24},{12,28},{16,0},{20,4},{24,8},{28,12},{1,17},{... | collective-permute-start | bytes 442376 | tf_op jit(solution)/shard_map/ppermute | solution.py:40
  680.4 17.3 %collective-permute-start.30 = (bf16[96,768]{0,1:T(8,128)(2,1)}, bf16[96,768]{0,1:T(8,128)(2,1)}, u32[]{:S(2)}, u32[]{:S(2)}) collective-permute-start(bf16[96,768]{0,1:T(8,128)(2,1)} %bitcast.50), channel_id=1, source_target_pairs={{0,8},{4,12},{8,0},{12,4},{16,24},{20,28},{24,16},{28,20},{1,9},{5... | collective-permute-start | bytes 442376 | tf_op jit(solution)/shard_map/ppermute | solution.py:40
  703.5 10.8 %all-to-all-start.8 = ((f32[32,1,2]{2,1,0:T(1,128)}), f32[32,1,2]{2,1,0:T(1,128)}, u32[]{:S(2)}, u32[]{:S(2)}) async-start(f32[32,1,2]{2,1,0:T(1,128)} %broadcast_in_dim.198), calls=%async_computation.8 | async-start | bytes 32768 | tf_op jit(solution)/shard_map/all_to_all | solution.py:980
  (74 other events, 410.9 us)
Sparse Core Ops, SparseCore 0:
  10.8 44.3 all-gather.2
  58.0 67.4 all-gather.4
  157.3 13.4 sort.11.cloned.1.call-done
  (1 shorter events, 0.0 us)

commit v3 on v2

--- a/solution.py
+++ b/solution.py
@@ -54,17 +54,21 @@
     return lax.all_gather(value, "wide", axis=axis, tiled=True)
 
 
-def scatter_wide(value):
+def scatter_pair(value):
     count = lax.axis_size("wide")
     if count != 8:
-        return lax.psum_scatter(value, "wide", scatter_dimension=0)
-    me = lax.axis_index("wide")
-    side = me & 1
+        return value
+    side = lax.axis_index("wide") & 1
     pairs = value.reshape((4, 2) + value.shape[1:])
     kept = lax.dynamic_index_in_dim(pairs, side, 1, keepdims=False)
     sent = lax.dynamic_index_in_dim(pairs, 1 - side, 1, keepdims=False).astype(BF)
-    half = kept.astype(F32) + xor_wide(sent, 1).astype(F32)
-    depth = me >> 1
+    return kept + xor_wide(sent, 1).astype(F32)
+
+
+def scatter_line(half):
+    if lax.axis_size("wide") != 8:
+        return lax.psum_scatter(half, "wide", scatter_dimension=0)
+    depth = lax.axis_index("wide") >> 1
     total = lax.dynamic_index_in_dim(half, depth, 0, keepdims=False)
     low = half.astype(BF)
     for k in (1, 2, 3):
@@ -314,7 +318,8 @@
 def feed_back_kernel(
     rows_ref, select_ref, par_ref, middle_ref, output_ref, attended_ref, hidden_ref, inner_ref,
     a0, a1, a2, a3, bc0, bc1, bc2, bc3,
-    d_middle_ref, d_attended_ref, d_mixed_ref, sent_ref, own_ref, vec_ref,
+    d_middle_ref, d_attended_ref, d_mixed_ref, b_sent_ref, c_sent_ref, b_own_ref, c_own_ref,
+    vec_ref,
 ):
     par = lambda k: par_ref[k : k + 1, :]
     share = d_mixed_ref.shape[2]
@@ -334,7 +339,7 @@
     d_hidden = jnp.zeros(middle.shape, F32)
     weights = (bc0, bc1, bc2, bc3)
     for s, kept, place in SLOT_PLACES:
-        out_ref = own_ref if kept else sent_ref
+        b_ref, c_ref = (b_own_ref, c_own_ref) if kept else (b_sent_ref, c_sent_ref)
         inner = inner_ref[s]
         tangent = jnp.tanh(0.7978845608 * (inner + 0.044715 * inner * inner * inner))
         active = (0.5 * inner * (1.0 + tangent)).astype(BF)
@@ -342,8 +347,8 @@
             1.0 - tangent * tangent
         ) * 0.7978845608 * (1.0 + 0.134145 * inner * inner)
         d_inner = (mm(d_output, weights[s][1], NN) * slope).astype(BF)
-        out_ref[place, 0] = mm(hidden, d_inner, TN).astype(BF)
-        out_ref[place, 1] = mm(d_output, active, TN).astype(BF)
+        b_ref[place] = mm(hidden, d_inner, TN).astype(BF)
+        c_ref[place] = mm(d_output, active, TN).astype(BF)
         d_hidden = d_hidden + mm(d_inner, weights[s][0], NT)
     normed, inverse = layer_norm(middle)
     d_normed = column_sum(d_hidden * normed)
@@ -367,7 +372,7 @@
     d_rows, select, params, middle, output, attended, hidden, inner, weights_a, weights_bc
 ):
     rows, width = middle.shape
-    half = jax.ShapeDtypeStruct((2, 2, width, width), BF)
+    half = jax.ShapeDtypeStruct((2, width, width), BF)
     return pl.pallas_call(
         feed_back_kernel,
         out_shape=[
@@ -376,10 +381,12 @@
             jax.ShapeDtypeStruct((4, rows, width // 4), BF),
             half,
             half,
+            half,
+            half,
             jax.ShapeDtypeStruct(params.shape, F32),
         ],
         name="feed_back",
-        **LOCAL,
+        **BUSY,
     )(
         d_rows, select, params, middle, output, attended, hidden, inner, *weights_a, *weights_bc
     )
@@ -494,6 +501,15 @@
     )(dq, d_own, d_far, *weights, d_middle, start, params, is_mask)
 
 
+def flip(value):
+    def kernel(value_ref, out_ref):
+        out_ref[...] = value_ref[...].T
+
+    return pl.pallas_call(
+        kernel, out_shape=jax.ShapeDtypeStruct(value.shape[::-1], value.dtype), name="flip", **LOCAL
+    )(value)
+
+
 def qkv_grads_kernel(grads_ref, hidden_ref, d_attended_ref, mixed_ref, sent_ref, own_ref):
     for s, kept, place in SLOT_PLACES:
         out_ref = own_ref if kept else sent_ref
@@ -520,11 +536,11 @@
 
     @pl.when(step < half)
     def _():
-        out_ref[...] = own_ref[...].astype(BF).astype(F32).T
+        out_ref[...] = own_ref[...].astype(BF).T.astype(F32)
 
     @pl.when((step >= half) & (step < 2 * half))
     def _():
-        out_ref[...] = other_ref[...].astype(F32).T
+        out_ref[...] = other_ref[...].T.astype(F32)
 
     @pl.when(step == 2 * half)
     def _():
@@ -582,83 +598,73 @@
     )(ids.reshape(count // block, 1, block), table)
 
 
-def collect_kernel(shift, first, key_ref, count_ref, grad_ref, *refs):
-    step = pl.program_id(0)
+def collect_kernel(shift, first, key_ref, count_ref, one_ref, two_ref, *refs):
     if first:
         out_ref, rows_ref = refs
         sum_ref = out_ref
+        sum_ref[...] = jnp.zeros_like(sum_ref)
     else:
         old_ref, out_ref, rows_ref, sum_ref = refs
-
-    @pl.when(step == 0)
-    def _():
-        sum_ref[...] = jnp.zeros_like(sum_ref) if first else old_ref[...]
-
-    rows_ref[...] = grad_ref[0].astype(F32)
+        sum_ref[...] = old_ref[...]
     mask = (1 << shift) - 1
-    count = count_ref[0, 0, 0]
     unroll = 8
-
-    def group(item, _):
-        keys = [key_ref[0, 0, item * unroll + k] for k in range(unroll)]
-        targets = [lax.shift_right_logical(key, shift) for key in keys]
-        olds = [sum_ref[pl.ds(target, 1), :] for target in targets]
-        news = [rows_ref[pl.ds(key & mask, 1), :] for key in keys]
-        sums = []
-        for k in range(unroll):
-            old = olds[k]
-            if k:
-                old = jnp.where(targets[k] == targets[k - 1], sums[k - 1], old)
-            sums.append(old + news[k])
-        for k in range(unroll):
-            sum_ref[pl.ds(targets[k], 1), :] = sums[k]
-        return 0
-
-    def single(item, _):
-        key = key_ref[0, 0, item]
-        target = pl.ds(lax.shift_right_logical(key, shift), 1)
-        sum_ref[target, :] = sum_ref[target, :] + rows_ref[pl.ds(key & mask, 1), :]
-        return 0
-
-    groups = lax.shift_right_logical(count, 3)
-    lax.fori_loop(0, groups, group, 0)
-    lax.fori_loop(groups * unroll, count, single, 0)
+    for part, grad_ref in enumerate((one_ref, two_ref)):
+        rows_ref[...] = grad_ref[...].astype(F32)
+        count = count_ref[part]
+
+        def group(item, _, part=part):
+            keys = [key_ref[part, item * unroll + k] for k in range(unroll)]
+            targets = [lax.shift_right_logical(key, shift) for key in keys]
+            olds = [sum_ref[pl.ds(target, 1), :] for target in targets]
+            news = [rows_ref[pl.ds(key & mask, 1), :] for key in keys]
+            sums = []
+            for k in range(unroll):
+                old = olds[k]
+                if k:
+                    old = jnp.where(targets[k] == targets[k - 1], sums[k - 1], old)
+                sums.append(old + news[k])
+            for k in range(unroll):
+                sum_ref[pl.ds(targets[k], 1), :] = sums[k]
+            return 0
+
+        def single(item, _, part=part):
+            key = key_ref[part, item]
+            target = pl.ds(lax.shift_right_logical(key, shift), 1)
+            sum_ref[target, :] = sum_ref[target, :] + rows_ref[pl.ds(key & mask, 1), :]
+            return 0
+
+        groups = lax.shift_right_logical(count, 3)
+        lax.fori_loop(0, groups, group, 0)
+        lax.fori_loop(groups * unroll, count, single, 0)
 
     if not first:
 
-        @pl.when(step == pl.num_programs(0) - 1)
-        def _():
-            def turn(block, _):
-                place = pl.ds(pl.multiple_of(block * 128, 128), 128)
-                out_ref[:, place] = sum_ref[place, :].T
-                return 0
-
-            lax.fori_loop(0, sum_ref.shape[0] // 128, turn, 0)
+        def turn(block, _):
+            place = pl.ds(pl.multiple_of(block * 128, 128), 128)
+            out_ref[:, place] = sum_ref[place, :].T
+            return 0
+
+        lax.fori_loop(0, sum_ref.shape[0] // 128, turn, 0)
 
 
 def collect(keys, counts, grads, shift, before, entries):
-    parts, tokens, width = grads.shape
+    tokens, width = grads[0].shape
     first = before is None
     out_dims = (entries, width) if first else (width, entries)
     scratch = [pltpu.VMEM((tokens, width), F32)]
     if not first:
         scratch.append(pltpu.VMEM((entries, width), F32))
+    smem = pl.BlockSpec(memory_space=pltpu.SMEM)
+    vmem = pl.BlockSpec(memory_space=pltpu.VMEM)
     return pl.pallas_call(
         functools.partial(collect_kernel, shift, first),
-        grid=(parts,),
-        in_specs=[
-            pl.BlockSpec((1, 1, tokens), lambda i: (i, 0, 0), memory_space=pltpu.SMEM),
-            pl.BlockSpec((1, 1, 1), lambda i: (i, 0, 0), memory_space=pltpu.SMEM),
-            pl.BlockSpec((1, tokens, width), lambda i: (i, 0, 0)),
-        ]
-        + ([] if first else [pl.BlockSpec((entries, width), lambda i: (0, 0), pipeline_mode=pl.Buffered(1))]),
-        out_specs=pl.BlockSpec(out_dims, lambda i: (0, 0)),
+        in_specs=[smem, smem] + [vmem] * (2 if first else 3),
+        out_specs=vmem,
         out_shape=jax.ShapeDtypeStruct(out_dims, F32),
         scratch_shapes=scratch,
-        compiler_params=pltpu.CompilerParams(vmem_limit_bytes=VMEM_LIMIT),
-        cost_estimate=FREE,
         name="collect",
-    )(*[keys.reshape(parts, 1, tokens), counts.reshape(parts, 1, 1), grads] + ([] if first else [before]))
+        **LOCAL,
+    )(keys, counts, *grads, *([] if first else [before]))
 
 
 def local(
@@ -714,15 +720,18 @@
     shard_a = jnp.concatenate(
         [qkv_weight[0], qkv_weight[1], qkv_weight[2], proj_weight.T], axis=1
     ).astype(BF)
-    wide_a = gather_wide(shard_a, 0)
-    wide_bc = gather_wide(jnp.stack([up_weight.astype(BF), down_weight.T.astype(BF)]), 1)
+    wide_all = gather_wide(
+        jnp.stack([shard_a, up_weight.astype(BF), down_weight.T.astype(BF)]), 1
+    )
+    wide_a, wide_bc = wide_all[0], wide_all[1:]
     heads_width = width // narrow
 
     chunk = -(-entries // (128 * wide)) * 128
     spare = chunk * wide - entries
     table_own = jnp.pad(out_table.astype(BF), ((0, 0), (0, spare)))
     table_own = table_own.reshape(share, wide, chunk).transpose(1, 0, 2)
-    real = me * chunk + jnp.arange(chunk) < entries
+    cuts = [(0, chunk)]
+    table_own = [table_own[:, :, low:high] for low, high in cuts]
 
     moments = counts_all.astype(F32) / pair_total
     condition = jax.nn.silu(time_features(moments, mod_weight.shape[0]))
@@ -742,7 +751,6 @@
     extra = jnp.pad(extra, ((0, 0), (0, -extra_rows % 16), (0, 0)))
 
     table_rows = table_rows_of(embedding.T, xor_narrow(embedding.T.astype(BF), 1))
-    inputs_all, table_rows = together(inputs_all, table_rows)
     half_ids = lax.dynamic_slice_in_dim(inputs_all, part * rows, rows, axis=2)
     half_ids = jnp.stack(
         [
@@ -799,9 +807,12 @@
         jnp.iinfo(jnp.int32).max,
     )
     hits = jnp.sum(taken.astype(jnp.int32), axis=1)
-    start_recv, table_own, wide_bc, *full_a = together(start_recv, table_own, wide_bc, *full_a)
+    wide_bc, *full_a = together(wide_bc, *full_a)
+    start_recv, *table_own = together(start_recv, *table_own)
+    table_mine = [
+        swap_wide(piece).reshape(width, high - low) for piece, (low, high) in zip(table_own, cuts)
+    ]
     across_bc = xor_narrow(wide_bc, 2)
-    table_mine = swap_wide(table_own).reshape(width, chunk)
     extra = start_recv[:, rows : rows + extra_rows].astype(F32).reshape(wide, -1)
     vector_full = extra[:, 3 * mod_share :].reshape(-1)
     modulation = extra[:, :mod_share] + extra[:, mod_share : 2 * mod_share]
@@ -820,9 +831,11 @@
     sort_keys = lax.sort(sort_keys, dimension=1)
     far_kv = xor_narrow(own_kv, 1)
     mixed, logs = attend(query, own_kv, far_kv)
-    mixed, sort_keys, hits, across_bc = together(mixed, sort_keys, hits, across_bc)
+    mixed, sort_keys, hits, across_bc, *table_mine = together(
+        mixed, sort_keys, hits, across_bc, *table_mine
+    )
     full_bc = (wide_bc, xor_narrow(wide_bc, 1), across_bc, xor_narrow(across_bc, 1))
-    tables = gather_narrow(table_mine)
+    tables = [gather_narrow(piece) for piece in table_mine]
 
     side = me // (wide // 2)
     low = me % (wide // 2)
@@ -874,10 +887,19 @@
         (target_rest >= 0) & (target_rest < chunk), (target_owner ^ group) * chunk + target_rest, -1
     )
 
-    logits = [jnp.where(real[None, :], mm(head_rows, table, NN), -1e30) for table in tables]
-    hitting = [
-        jnp.arange(chunk)[None, :] + s * chunk == target_column[:, None] for s in range(narrow)
+    columns = [
+        (slot, piece, slot * chunk + low + jnp.arange(high - low))
+        for piece, (low, high) in enumerate(cuts)
+        for slot in range(narrow)
     ]
+    tables = [tables[piece][slot] for slot, piece, _ in columns]
+    logits = [
+        jnp.where(
+            (me * chunk + at - slot * chunk < entries)[None, :], mm(head_rows, table, NN), -1e30
+        )
+        for table, (slot, _, at) in zip(tables, columns)
+    ]
+    hitting = [at[None, :] == target_column[:, None] for _, _, at in columns]
     top = functools.reduce(jnp.maximum, [jnp.max(value, axis=-1) for value in logits])
     total = sum(jnp.sum(jnp.exp(value - top[:, None]), axis=-1) for value in logits)
     target_logit = sum(
@@ -896,34 +918,49 @@
     d_table_parts = [mm(head_rows, grad, TN) for grad in d_logits]
     d_recv = swap_wide(d_rows.astype(BF).reshape(wide, quarter, width))
     d_recv, *d_table_parts = together(d_recv, *d_table_parts)
-    table_sent = [xor_narrow(d_table_parts[s].astype(BF), 1) for s in (1, 3)]
+    d_table_parts = [
+        d_table_parts[piece * narrow : (piece + 1) * narrow] for piece in range(len(cuts))
+    ]
+    table_sent = [[xor_narrow(parts[s].astype(BF), 1) for s in (1, 3)] for parts in d_table_parts]
     d_mine = jnp.sum(d_recv.astype(F32), axis=0).astype(BF)
     d_sides = jnp.concatenate([d_mine, xor_wide(d_mine, wide // 2)])
     d_all = jnp.concatenate([d_sides, xor_narrow(d_sides, 1)])
-    table_far = (d_table_parts[2] + table_sent[1].astype(F32)).astype(BF)
-    d_all, table_far = together(d_all, table_far)
-    half = width // 2
-    table_from = [xor_narrow(table_far[:half], 2), xor_narrow(table_far[half:], 2)]
-
-    d_middle, d_attended, d_mixed, bc_sent, bc_own, d_params = feed_back(
+    table_far = [
+        (parts[2] + sent[1].astype(F32)).astype(BF)
+        for parts, sent in zip(d_table_parts, table_sent)
+    ]
+    d_all, *table_far = together(d_all, *table_far)
+    table_from = [xor_narrow(far, 2) for far in table_far]
+
+    d_middle, d_attended, d_mixed, b_sent, c_sent, b_own, c_own, d_params = feed_back(
         d_all, select, params, middle, output, attended, hidden_two, inner, full_a, full_bc
     )
-    d_mixed, table_from[0] = together(d_mixed, table_from[0])
-    bc_near, bc_far = scatter_core(bc_sent, bc_own)
+    def table_sum(piece):
+        value = d_table_parts[piece][0] + table_sent[piece][0].astype(F32)
+        value = (value + table_from[piece].astype(F32)).astype(BF)
+        return value.reshape(wide, share, value.shape[1])
+
     d_query, d_own, d_far = attend_back(
         query, own_kv, far_kv, d_mixed, logs, cosine, sine, key_cosine, key_sine
     )
-    d_query, d_own, d_far, table_from[1], bc_far = together(
-        d_query, d_own, d_far, table_from[1], bc_far
-    )
-    b_from, c_from = xor_narrow(bc_far[0], 2), xor_narrow(bc_far[1], 2)
-    d_far = xor_narrow(d_far, 1)
+    d_query, d_own, d_far, b_sent, c_sent = together(d_query, d_own, d_far, b_sent, c_sent)
+    b_near, b_far = scatter_core(b_sent, b_own)
+    c_near, c_far = scatter_core(c_sent, c_own)
+    d_query, d_own, d_far, *table_from = together(d_query, d_own, d_far, *table_from)
+    d_far, b_far, c_far = together(xor_narrow(d_far, 1), b_far, c_far)
+    b_from, c_from = xor_narrow(b_far, 2), xor_narrow(c_far, 2)
     is_mask = (my_inputs == mask_entry).astype(F32)[:, None]
     d_start_rows, d_projected, d_first = qkv_back(
         d_query, d_own, d_far, full_a, d_middle, start, params, is_mask, rows + 16, wide
     )
 
-    d_start_rows, d_first, b_from = together(d_start_rows, d_first, b_from)
+    d_table = [table_sum(piece) for piece in range(len(cuts))]
+    d_start_rows, d_projected, d_first, b_from = together(
+        d_start_rows, d_projected, d_first, b_from
+    )
+    a_sent, a_own = qkv_grads(d_projected, hidden_one, d_attended, mixed)
+    a_near, a_far = scatter_core(a_sent, a_own)
+    d_start_rows, d_first, c_from, *d_table = together(d_start_rows, d_first, c_from, *d_table)
     d_params = jnp.concatenate([d_first[:2], d_params[2:8], d_first[2:3], d_params[9:]])
     d_modulation = d_params[:8].reshape(-1)
     d_vector = jnp.concatenate([d_params[8:].reshape(-1), d_modulation])
@@ -933,28 +970,37 @@
     small = jnp.pad(small, ((0, 0), (0, padded - rows - 16 - small_rows), (0, 0)))
     d_start_rows = jnp.concatenate([d_start_rows, small], axis=1)
     d_start_recv = swap_wide(d_start_rows)
-    a_sent, a_own = qkv_grads(d_projected, hidden_one, d_attended, mixed)
-    a_near, a_far = scatter_core(a_sent, a_own)
-    a_far, c_from, d_start_recv = together(a_far, c_from, d_start_recv)
-    d_b = scatter_wide((bc_near[0] + b_from.astype(F32)).reshape(wide, share, width))
-    d_c = scatter_wide((bc_near[1] + c_from.astype(F32)).reshape(wide, share, width))
-    d_table = d_table_parts[0] + table_sent[0].astype(F32)
-    d_table = (d_table + jnp.concatenate(table_from).astype(F32)).astype(BF)
-    d_table = swap_wide(d_table.reshape(wide, share, chunk)).astype(F32).transpose(1, 0, 2)
-    d_table = d_table.reshape(share, chunk * wide)[:, :entries]
     a_from = xor_narrow(a_far, 2)
-    d_a = scatter_wide((a_near + a_from.astype(F32)).reshape(wide, share, width))
+    b_half, c_half = [
+        scatter_pair((near + other.astype(F32)).reshape(wide, share, width))
+        for near, other in ((b_near, b_from), (c_near, c_from))
+    ]
+    a_from, d_start_recv, b_half, c_half, *d_table = together(
+        a_from, d_start_recv, b_half, c_half, *d_table
+    )
+    d_table = [swap_wide(piece) for piece in d_table]
     d_start_recv = d_start_recv.reshape(wide * padded, share)
     d_start_across = xor_narrow(d_start_recv, 2)
-    d_near = jnp.stack([d_start_recv, xor_narrow(d_start_recv, 1)])
+    d_near = (d_start_recv, xor_narrow(d_start_recv, 1))
     d_embed = collect(sort_keys[:2], hits[:2], d_near, shift, None, entries)
-    d_far = jnp.stack([d_start_across, xor_narrow(d_start_across, 1)])
+    d_start_across, d_embed = together(d_start_across, d_embed)
+    d_start_corner = xor_narrow(d_start_across, 1)
+    a_from, b_half, c_half, d_start_corner = together(a_from, b_half, c_half, d_start_corner)
+    a_half = scatter_pair((a_near + a_from.astype(F32)).reshape(wide, share, width))
+    d_b, d_c, d_a = scatter_line(b_half), scatter_line(c_half), scatter_line(a_half)
+    d_far = (d_start_across, d_start_corner)
     d_embed = collect(sort_keys[2:], hits[2:], d_far, shift, d_embed, entries)
-
-    small = jnp.stack([d_near, d_far]).reshape(2, 2, wide, padded, share)
-    small = small[:, :, :, rows + 16 : rows + 16 + small_rows].astype(F32)
-    small = small.sum(axis=1).reshape(2, wide, -1)
-    small, small_far = small[0], small[1]
+    d_embed, *d_table = together(d_embed, *d_table)
+    d_table = jnp.concatenate(d_table, axis=2).astype(F32).transpose(1, 0, 2)
+    d_table = d_table.reshape(share, chunk * wide)[:, :entries]
+
+    small, small_far = [
+        sum(
+            part.reshape(wide, padded, share)[:, rows + 16 : rows + 16 + small_rows].astype(F32)
+            for part in parts
+        ).reshape(wide, -1)
+        for parts in (d_near, d_far)
+    ]
     d_vectors = jnp.sum(small[:, mod_share:] + small_far[:, mod_share:], axis=0)
     condition_far = lax.dynamic_index_in_dim(condition, 1 - micro, 1, keepdims=False)
     d_mod_weight = lax.dot_general(
@@ -965,7 +1011,7 @@
         d_embed,
         d_table,
         jnp.stack([d_a[:, k * heads_width : (k + 1) * heads_width] for k in range(3)]),
-        together(d_a[:, 3 * heads_width :].T)[0],
+        flip(d_a[:, 3 * heads_width :]),
         d_b,
         d_c,
         d_mod_weight,

time: 768 us -> 697 us (0.908)
  waiting for transfers between devices: 226 us -> 169 us
  local copies, waits for them, and re-layouts: 91.9 us -> 62.8 us
  other arithmetic: 120 us -> 112 us
  blocking collectives: 12.3 us -> 20.3 us
    ppermute x27, waiting for transfers between devices: 137 us -> 86.3 us  [xor_narrow(): lax.ppermute(value, NARROW, [(i, i ^ bits) for i in range(lax.axis_size(N...]
    unnamed x181 -> x161, local copies, waits for them, and re-layouts: 25.1 us -> 13.5 us
    all_to_all x0 -> x1, blocking collectives: none -> 9.7 us  [local(): lax.all_to_all(jnp.broadcast_to(jnp.stack([loss_part / wide, square])[Non...]
    another operation x3 -> x0, local copies, waits for them, and re-layouts: 9.63 us -> none  [the longest x2 6.47 us: local(): d_far = jnp.stack([d_start_across, xor_narrow(d_start_across, 1)])]
    pallas_call x2 -> x3, Pallas kernels: 30.8 us -> 37.2 us  [the longest x2 35.6 us: collect(): pl.pallas_call(functools.partial(collect_kernel, shift, first), in_specs=...]
  transfers between devices with their start and end apart: 51 -> 49, of which waited for: 26 -> 21; matrix products, arithmetic and copies ran while one was open for 22% -> 20% of each run, Pallas kernels for 19% -> 25%
where the time goes in v3:
time: 697 us; the launch traced here: 689 us
  Pallas kernels  173 us (25%)
  waiting for transfers between devices  169 us (24%)
  other arithmetic  112 us (16%)
  starting transfers between devices  70.6 us (10%)
  local copies, waits for them, and re-layouts  62.8 us (9%)
  matrix products  57.1 us (8%)
  between operations  23.8 us (3%)
  blocking collectives  20.3 us (3%)
    ppermute x27, waiting for transfers between devices, xor_narrow(): lax.ppermute(value, NARROW, [(i, i ^ bits) for i in range(lax.axis_size(N...  86.3 us
    dot_general x12, matrix products, mm(): return lax.dot_general(a, b, dims, preferred_element_type=F32)  52.7 us
    ppermute x14, waiting for transfers between devices, xor_wide(): lax.ppermute(value, 'wide', [(i, i ^ bits) for i in range(lax.axis_size('...  45.5 us
    all_to_all x7, waiting for transfers between devices, swap_wide(): return lax.all_to_all(value, 'wide', 0, 0, tiled=True)  37.3 us
    pallas_call x2, Pallas kernels, collect(): pl.pallas_call(functools.partial(collect_kernel, shift, first), in_specs=...  35.6 us
    all_to_all x7, starting transfers between devices, swap_wide(): return lax.all_to_all(value, 'wide', 0, 0, tiled=True)  33.6 us
    pallas_call x1, Pallas kernels, attend_back(): pl.pallas_call(attend_back_kernel, grid=(slots,), in_specs=[one, two, oth...  25.1 us
    pallas_call x1, Pallas kernels, feed_back(): pl.pallas_call(feed_back_kernel, out_shape=[jax.ShapeDtypeStruct((rows, w...  25 us
  transfers between devices with their start and end apart: 49, of which 21 were waited for; matrix products, arithmetic and copies ran while one was open for 20% of the time, Pallas kernels for 25%

profile of v3, /device:TPU:0, one launch (start us, length us, event | category | flops | bytes accessed | tf_op | source)
XLA Modules:
  0.0 688.8 jit_solution(7331359301670899911)
XLA Ops:
  17.2 6.8 all-to-all-start
  24.1 8.4 %all-to-all-done = s32[8,2,1408]{2,1,0:T(2,128)S(1)} async-done(((s32[8,2,1408]{2,1,0:T(2,128)}), s32[8,2,1408]{2,1,0:T(2,128)S(1)}, u32[]{:S(2)}, u32[]{:S(2)}) %all-to-all-start) | async-done | bytes 90144 | tf_op jit(solution)/shard_map/all_to_all | solution.py:44
  36.7 15.0 %table_rows.1.table_ref = f32[26752,96]{1,0:T(8,128)} custom-call(f32[96,12672]{1,0:T(8,128)} %bitcast.246, bf16[96,12672]{1,0:T(8,128)(2,1)} %collective-permute-done.other_ref), custom_call_target="tpu_custom_call" | custom-call | flops 10000000000 | bytes 40000000 | tf_op jit(solution)/shard_map/table_rows/pallas_call | solution.py:554
  51.7 15.0 %lookup.1 = bf16[8192,96]{1,0:T(8,128)(2,1)} custom-call(s32[4,1,2048]{2,1,0:T(1,128)} %and_select_fusion.id_ref, f32[26752,96]{1,0:T(8,128)} %table_rows.1.table_ref), custom_call_target="tpu_custom_call" | custom-call | tf_op jit(solution)/shard_map/lookup/pallas_call | solution.py:586
  71.4 16.2 %collective-permute-done.1 = bf16[8,512,96]{1,2,0:T(8,128)(2,1)} collective-permute-done((bf16[8,512,96]{1,2,0:T(8,128)(2,1)S(1)}, bf16[8,512,96]{1,2,0:T(8,128)(2,1)}, u32[]{:S(2)}, u32[]{:S(2)}) %collective-permute-start.1) | collective-permute-done | bytes 786464 | tf_op jit(solution)/shard_map/ppermute | solution.py:34
  91.4 3.6 all-to-all-start.1
  101.2 17.0 %all-to-all-done.1 = bf16[8,560,96]{1,2,0:T(8,128)(2,1)S(1)} async-done(((bf16[8,560,96]{1,2,0:T(8,128)(2,1)}), bf16[8,560,96]{1,2,0:T(8,128)(2,1)S(1)}, u32[]{:S(2)}, u32[]{:S(2)}) %all-to-all-start.1) | async-done | bytes 860192 | tf_op jit(solution)/shard_map/all_to_all | solution.py:44
  118.2 3.8 copy.203
  122.0 4.4 all-to-all-start.2
  129.8 3.2 slice.301.bc0
  142.1 7.9 %qkv.1 = (bf16[4,512,192]{2,1,0:T(8,128)(2,1)}, bf16[4,512,384]{2,1,0:T(8,128)(2,1)}, bf16[512,768]{1,0:T(8,128)(2,1)}, f32[512,768]{1,0:T(8,128)}) custom-call(bf16[8,560,96]{2,1,0:T(8,128)(2,1)} %copy.202.recv_ref, f32[12,768]{1,0:T(8,128)} %pad_maximum_fusion.7.par_ref, bf16[768,768]{1,0:T(8,128)(2,1)} %copy-done.3, bf16[768,768]{1,0:T(8,128)(2,1)} %copy-done.5, ...), custom_call_target="tpu_custom_call" | custom-call | tf_op jit(solution)/shard_map/qkv/pallas_call | solution.py:205
  154.9 14.7 %attend.1 = (bf16[4,512,192]{2,1,0:T(8,128)(2,1)}, f32[4,3,512]{2,1,0:T(4,128)}) custom-call(bf16[4,512,192]{2,1,0:T(8,128)(2,1)} %get-tuple-element.118.q_ref, bf16[4,512,384]{2,1,0:T(8,128)(2,1)} %get-tuple-element.119.own_ref, bf16[4,512,384]{2,1,0:T(8,128)(2,1)} %copy-done.12), custom_call_target="tpu_custom_call" | custom-call | tf_op jit(solution)/shard_map/attend/pallas_call | solution.py:252
  169.7 17.1 %collective-permute-done.6.bc2 = bf16[2,768,768]{2,1,0:T(8,128)(2,1)} collective-permute-done((bf16[2,768,768]{2,1,0:T(8,128)(2,1)}, bf16[2,768,768]{2,1,0:T(8,128)(2,1)}, u32[]{:S(2)}, u32[]{:S(2)}) %collective-permute-start.6) | collective-permute-done | bytes 2359328 | tf_op jit(solution)/shard_map/ppermute | solution.py:34
  192.9 15.7 %feed.1 = (f32[512,768]{1,0:T(8,128)}, f32[512,768]{1,0:T(8,128)}, f32[512,768]{1,0:T(8,128)}, bf16[512,768]{1,0:T(8,128)(2,1)}, f32[4,512,768]{2,1,0:T(8,128)}, /*index=5*/bf16[320,768]{1,0:T(8,128)(2,1)}) custom-call(bf16[4,512,192]{2,1,0:T(8,128)(2,1)} %get-tuple-element.124.mixed_ref, f32[512,768]{1,0:T(8,128)} %get-tuple-element.125.start_ref, ...), custom_call_target="tpu_custom_call" | custom-call | tf_op jit(solution)/shard_map/feed/pallas_call | solution.py:300
  212.2 2.8 collective-permute-start.10
  215.1 6.3 collective-permute-done.10
  222.4 6.2 all-to-all-start.3
  228.8 16.1 %collective-permute-done.12 = bf16[768,1664]{1,0:T(8,128)(2,1)} collective-permute-done((bf16[768,1664]{1,0:T(8,128)(2,1)}, bf16[768,1664]{1,0:T(8,128)(2,1)}, u32[]{:S(2)}, u32[]{:S(2)}) %collective-permute-start.12) | collective-permute-done | bytes 2555936 | tf_op jit(solution)/shard_map/ppermute | solution.py:34
  245.6 7.6 %all-to-all-done.3 = bf16[8,80,768]{2,1,0:T(8,128)(2,1)S(1)} async-done(((bf16[8,80,768]{2,1,0:T(8,128)(2,1)}), bf16[8,80,768]{2,1,0:T(8,128)(2,1)S(1)}, u32[]{:S(2)}, u32[]{:S(2)}) %all-to-all-start.3) | async-done | bytes 983072 | tf_op jit(solution)/shard_map/all_to_all | solution.py:44
  253.2 4.1 select_reduce_fusion.4
  257.3 3.8 select_reduce_fusion.2
  261.1 3.8 select_reduce_fusion.3
  264.8 3.8 select_reduce_fusion.1
  268.6 6.0 exponential_reduce_fusion
  274.7 10.6 %all_to_all.45 = f32[8,3,640]{2,1,0:T(4,128)S(1)} all-to-all(f32[8,3,640]{2,1,0:T(4,128)S(1)} %broadcast_in_dim.206), channel_id=1, replica_groups=mesh['wide'=8,'line'=2,'core'=2] {'wide'}, dimensions={0} | all-to-all | bytes 122880 | tf_op jit(solution)/shard_map/all_to_all | solution.py:44
  286.0 4.4 fusion.8
  290.5 5.2 fusion.95
  295.7 3.7 fusion.97
  299.4 3.7 fusion.96
  303.1 5.6 add_convert_fusion.2
  308.8 3.8 all-to-all-start.5
  312.6 6.6 fusion.98
  319.2 3.8 fusion.99
  323.0 4.5 fusion.100
  327.6 4.1 fusion.76
  331.6 4.3 all-to-all-done.5
  336.2 8.4 %collective-permute-done.14 = bf16[80,768]{1,0:T(8,128)(2,1)S(1)} collective-permute-done((bf16[80,768]{1,0:T(8,128)(2,1)S(1)}, bf16[80,768]{1,0:T(8,128)(2,1)S(1)}, u32[]{:S(2)}, u32[]{:S(2)}) %collective-permute-start.14) | collective-permute-done | bytes 122912 | tf_op jit(solution)/shard_map/ppermute | solution.py:40
  347.0 3.7 add_convert_fusion.1
  352.2 25.0 %feed_back.1 = (f32[512,768]{1,0:T(8,128)}, bf16[512,768]{1,0:T(8,128)(2,1)}, bf16[4,512,192]{2,1,0:T(8,128)(2,1)}, bf16[2,768,768]{2,1,0:T(8,128)(2,1)}, bf16[2...) custom-call(bf16[320,768]{1,0:T(8,128)(2,1)} %pad_maximum_fusion.3.rows, ...), custom_call_target="tpu_custom_call" | custom-call | flops 10000000000 | bytes 40000000 | tf_op jit(solution)/shard_map/feed_back/pallas_call | solution.py:376
  377.2 25.1 %attend_back.1 = (bf16[4,512,192]{2,1,0:T(8,128)(2,1)}, f32[4,512,384]{2,1,0:T(8,128)}, bf16[4,512,384]{2,1,0:T(8,128)(2,1)}) custom-call(bf16[4,512,192]{2,1,0:T(8,128)(2,1)} %get-tuple-element.118.q_ref, bf16[4,512,384]{2,1,0:T(8,128)(2,1)} %get-tuple-element.119.own_ref, bf16[4,512,384]{2,1,0:T(8,128)(2,1)} %copy-done.12, ...), custom_call_target="tpu_custom_call" | custom-call | tf_op jit(solution)/shard_map/attend_back/pallas_call | solution.py:433
  402.9 5.5 collective-permute-done.17
  421.2 10.0 %qkv_back.1 = (bf16[8,528,96]{2,1,0:T(8,128)(2,1)}, bf16[4,512,576]{2,1,0:T(8,128)(2,1)}, f32[3,768]{1,0:T(4,128)}) custom-call(bf16[4,512,192]{2,1,0:T(8,128)(2,1)} %get-tuple-element.151.dq_ref, f32[4,512,384]{2,1,0:T(8,128)} %get-tuple-element.152.d_own_ref, bf16[4,512,384]{2,1,0:T(8,128)(2,1)} %copy-done.28, bf16[768,768]{1,0:T(8,128)(2,1)} %copy-done.3, ...), custom_call_target="tpu_custom_call" | custom-call | tf_op jit(solution)/shard_map/qkv_back/pallas_call | solution.py:492
  431.2 15.5 %collective-permute-done.21 = bf16[768,768]{1,0:T(8,128)(2,1)} collective-permute-done((bf16[768,768]{1,0:T(8,128)(2,1)}, bf16[768,768]{1,0:T(8,128)(2,1)}, u32[]{:S(2)}, u32[]{:S(2)}) %collective-permute-start.21) | collective-permute-done | bytes 1179680 | tf_op jit(solution)/shard_map/ppermute | solution.py:34
  446.7 7.4 %qkv_grads.1 = (bf16[2,768,768]{2,1,0:T(8,128)(2,1)}, bf16[2,768,768]{2,1,0:T(8,128)(2,1)}) custom-call(bf16[4,512,576]{2,1,0:T(8,128)(2,1)} %get-tuple-element.164.grads_ref, bf16[512,768]{1,0:T(8,128)(2,1)} %get-tuple-element.165.hidden_ref, bf16[512,768]{1,0:T(8,128)(2,1)} %get-tuple-element.166.d_attended_ref, ...), custom_call_target="tpu_custom_call" | custom-call | flops 10000000000 | bytes 40000000 | tf_op jit(solution)/shard_map/qkv_grads/pallas_call | solution.py:528
  455.6 5.5 add_convert_fusion
  461.0 10.0 %collective-permute-done.24 = bf16[768,768]{1,0:T(8,128)(2,1)} collective-permute-done((bf16[768,768]{1,0:T(8,128)(2,1)}, bf16[768,768]{1,0:T(8,128)(2,1)}, u32[]{:S(2)}, u32[]{:S(2)}) %collective-permute-start.24) | collective-permute-done | bytes 1179680 | tf_op jit(solution)/shard_map/ppermute | solution.py:34
  474.2 4.3 all-to-all-start.6
  483.3 2.8 convert_element_type.306
  493.8 11.3 %collective-permute-done.26 = bf16[4,96,768]{2,1,0:T(8,128)(2,1)S(1)} collective-permute-done((bf16[4,96,768]{2,1,0:T(8,128)(2,1)S(1)}, bf16[4,96,768]{2,1,0:T(8,128)(2,1)S(1)}, u32[]{:S(2)}, u32[]{:S(2)}) %collective-permute-start.26) | collective-permute-done | bytes 589856 | tf_op jit(solution)/shard_map/ppermute | solution.py:40
  507.5 9.1 %collective-permute-done.27 = bf16[4,96,768]{2,1,0:T(8,128)(2,1)} collective-permute-done((bf16[4,96,768]{2,1,0:T(8,128)(2,1)S(1)}, bf16[4,96,768]{2,1,0:T(8,128)(2,1)}, u32[]{:S(2)}, u32[]{:S(2)}) %collective-permute-start.27) | collective-permute-done | bytes 589856 | tf_op jit(solution)/shard_map/ppermute | solution.py:40
  521.7 4.6 all-to-all-start.7
  529.9 12.3 %collect.2.refs_0_ = f32[12672,96]{1,0:T(8,128)} custom-call(s32[2,4480]{1,0:T(2,128)} %get-tuple-element.265.key_ref, s32[2]{0:T(128)} %get-tuple-element.293.count_ref, bf16[4480,96]{1,0:T(8,128)(2,1)} %bitcast.250, bf16[4480,96]{1,0:T(8,128)(2,1)} %copy.215.two_ref), custom_call_target="tpu_custom_call" | custom-call | tf_op jit(solution)/shard_map/collect/pallas_call | solution.py:659
  554.6 2.7 fusion.18
  560.8 3.3 collective-permute-start.37
  566.0 3.3 collective-permute-start.40
  572.3 2.9 multiply_reduce_fusion.1
  577.9 23.2 %collect.3 = f32[96,12672]{1,0:T(8,128)} custom-call(s32[2,4480]{1,0:T(2,128)} %get-tuple-element.266.key_ref, s32[2]{0:T(128)} %get-tuple-element.294.count_ref, bf16[4480,96]{1,0:T(8,128)(2,1)} %copy.216.one_ref, bf16[4480,96]{1,0:T(8,128)(2,1)} %copy.217.two_ref, f32[12672,96]{1,0:T(8,128)} %collect.2.refs_0_), custom_call_target="tpu_custom_call" | custom-call | tf_op jit(solution)/shard_map/collect/pallas_call | solution.py:659
  606.2 3.3 collective-permute-start.34
  610.7 6.6 collective-permute-done.39
  619.6 3.4 collective-permute-done.33
  627.7 4.2 multiply_reduce_fusion
  639.7 9.7 %all_to_all.46 = f32[32,1,2]{2,1,0:T(1,128)S(1)} all-to-all(f32[32,1,2]{2,1,0:T(1,128)S(1)} %broadcast_in_dim.207), channel_id=1, replica_groups=mesh['wide'=8,'line'=2,'core'=2] {'wide','line','core'}, dimensions={0} | all-to-all | bytes 512 | tf_op jit(solution)/shard_map/all_to_all | solution.py:1026
  650.8 13.1 %fusion.33 = (f32[12672,96]{0,1:T(8,128)}, f32[12672,96]{0,1:T(8,128)}, f32[12672,96]{0,1:T(8,128)}) fusion(f32[96,12672]{1,0:T(8,128)} %collect.3, f32[]{:T(128)S(6)} %div.124, f32[12672,96]{0,1:T(8,128)} %param.46, f32[12672,96]{0,1:T(8,128)} %param.38, f32[12672,96]{0,1:T(8,128)} %param.30), kind=kLoop, calls=%fused_computation.81 | loop fusion | flops 18247680 | bytes 34062340 | tf_op jit(solution)/shard_map/transpose | solution.py:1039
  664.0 10.4 %multiply_subtract_fusion = (f32[96,12672]{1,0:T(8,128)}, f32[96,12672]{1,0:T(8,128)}, f32[96,12672]{1,0:T(8,128)}) fusion(f32[96,12672]{1,0:T(8,128)} %param.31, f32[]{:T(128)S(6)} %div.124, bf16[96,13312]{1,0:T(8,128)(2,1)S(1)} %bitcast.245, f32[96,12672]{1,0:T(8,128)} %param.39, f32[96,12672]{1,0:T(8,128)} %param.47), kind=kLoop, calls=%fused_computation.18 | loop fusion | flops 20680704 | bytes 31629316 | tf_op jit(solution)/shard_map/sub | solution.py:1048
  (420 shorter events, 148.6 us)
Async XLA Ops:
  7.2 82.8 %all-gather.2.cloned.1.call-start = ((), (), s32[]{:S(2)}) async-start(), calls=%async_computation.9 | async-start | bytes 3981312 | tf_op jit(solution)/shard_map/all_gather | solution.py:54
  12.2 23.5 %copy-start.25 = (f32[128,768]{1,0:T(8,128)S(1)}, f32[128,768]{1,0:T(8,128)}, u32[]{:S(2)}) copy-start(f32[128,768]{1,0:T(8,128)} %param.36) | copy-start | bytes 1179652
  14.9 21.8 %collective-permute-start = (bf16[96,12672]{1,0:T(8,128)(2,1)S(1)}, bf16[96,12672]{1,0:T(8,128)(2,1)}, u32[]{:S(2)}, u32[]{:S(2)}) collective-permute-start(bf16[96,12672]{1,0:T(8,128)(2,1)S(1)} %bitcast_convert_fusion.4), channel_id=1, source_target_pairs={{0,1},{1,0},{2,3},{3,2},{4,5},{5,4},{6,7},{7,6},{8,9},{9,8},{10,11... | collective-permute-start | bytes 7299080 | tf_op jit(solution)/shard_map/ppermute | solution.py:34
  17.2 15.4 %all-to-all-start = ((s32[8,2,1408]{2,1,0:T(2,128)}), s32[8,2,1408]{2,1,0:T(2,128)S(1)}, u32[]{:S(2)}, u32[]{:S(2)}) async-start(s32[8,2,1408]{2,1,0:T(2,128)} %broadcast_in_dim.187), calls=%async_computation | async-start | bytes 180224 | tf_op jit(solution)/shard_map/all_to_all | solution.py:44
  32.6 19.1 %copy-start.40 = (s32[8,2,1408]{2,1,0:T(2,128)}, s32[8,2,1408]{2,1,0:T(2,128)S(1)}, u32[]{:S(2)}) copy-start(s32[8,2,1408]{2,1,0:T(2,128)S(1)} %all-to-all-done) | copy-start | bytes 270340
  35.7 16.0 %copy-start.57 = (f32[8,1,128]{2,1,0:T(1,128)}, f32[8,1,128]{2,1,0:T(1,128)S(1)}, u32[]{:S(2)}) copy-start(f32[8,1,128]{2,1,0:T(1,128)S(1)} %get-tuple-element.280) | copy-start | bytes 12292
  68.9 18.7 %collective-permute-start.1 = (bf16[8,512,96]{1,2,0:T(8,128)(2,1)S(1)}, bf16[8,512,96]{1,2,0:T(8,128)(2,1)}, u32[]{:S(2)}, u32[]{:S(2)}) collective-permute-start(bf16[8,512,96]{1,2,0:T(8,128)(2,1)S(1)} %copy.193), channel_id=1, source_target_pairs={{0,2},{1,3},{2,0},{3,1},{4,6},{5,7},{6,4},{7,5},{8,10},{9,11},{10,... | collective-permute-start | bytes 2359304 | tf_op jit(solution)/shard_map/ppermute | solution.py:34
  91.4 35.3 %copy-start.3 = (bf16[768,768]{1,0:T(8,128)(2,1)}, bf16[768,768]{1,0:T(8,128)(2,1)S(1)}, u32[]{:S(2)}) copy-start(bf16[768,768]{1,0:T(8,128)(2,1)S(1)} %slice_bitcast_fusion.a0) | copy-start | bytes 3538948
  91.4 26.8 %all-to-all-start.1 = ((bf16[8,560,96]{1,2,0:T(8,128)(2,1)}), bf16[8,560,96]{1,2,0:T(8,128)(2,1)S(1)}, u32[]{:S(2)}, u32[]{:S(2)}) async-start(bf16[8,560,96]{1,2,0:T(8,128)(2,1)} %fusion.34), calls=%async_computation.1 | async-start | bytes 1966080 | tf_op jit(solution)/shard_map/all_to_all | solution.py:44
  95.0 31.8 %collective-permute-start.3 = (bf16[768,768]{1,0:T(8,128)(2,1)S(1)}, bf16[768,768]{1,0:T(8,128)(2,1)S(1)}, u32[]{:S(2)}, u32[]{:S(2)}) collective-permute-start(bf16[768,768]{1,0:T(8,128)(2,1)S(1)} %slice_bitcast_fusion.a0), channel_id=1, source_target_pairs={{0,2},{1,3},{2,0},{3,1},{4,6},{5,7},{6,4},{7,5},{8,10},{9,11},{10,... | collective-permute-start | bytes 3538952 | tf_op jit(solution)/shard_map/ppermute | solution.py:34
  122.0 64.8 %all-to-all-start.2 = ((bf16[8,96,1664]{2,1,0:T(8,128)(2,1)}), bf16[8,96,1664]{2,1,0:T(8,128)(2,1)}, u32[]{:S(2)}, u32[]{:S(2)}) async-start(bf16[8,96,1664]{2,1,0:T(8,128)(2,1)} %copy.203), calls=%async_computation.2 | async-start | bytes 5111808 | tf_op jit(solution)/shard_map/all_to_all | solution.py:44
  126.4 43.3 %sort.9.cloned.1.call-start = ((), (), s32[]{:S(2)}) async-start(), calls=%async_computation.10 | async-start | bytes 215072 | tf_op jit(solution)/shard_map/sort | solution.py:831
  126.7 6.3 collective-permute-start.2
  126.8 6.2 collective-permute-start.4
  133.0 53.8 %collective-permute-start.6 = (bf16[2,768,768]{2,1,0:T(8,128)(2,1)}, bf16[2,768,768]{2,1,0:T(8,128)(2,1)}, u32[]{:S(2)}, u32[]{:S(2)}) collective-permute-start(bf16[2,768,768]{2,1,0:T(8,128)(2,1)} %slice.301.bc0), channel_id=1, source_target_pairs={{0,2},{1,3},{2,0},{3,1},{4,6},{5,7},{6,4},{7,5},{8,10},{9,11},{10,... | collective-permute-start | bytes 7077896 | tf_op jit(solution)/shard_map/ppermute | solution.py:34
  150.0 38.3 %copy-start.66 = (s32[1,2,256]{2,1,0:T(2,128)S(1)}, s32[1,2,256]{2,1,0:T(2,128)}, u32[]{:S(2)}) copy-start(s32[1,2,256]{2,1,0:T(2,128)} %param.28) | copy-start | bytes 6148
  150.0 38.4 %copy-start.70 = (s32[8,2,1]{0,1,2:T(2,128)S(1)}, s32[8,2,1]{0,1,2:T(2,128)}, u32[]{:S(2)}) copy-start(s32[8,2,1]{0,1,2:T(2,128)} %copy-done.69) | copy-start | bytes 196
  150.0 3.7 collective-permute-start.5
  150.1 40.5 %copy-start.63 = (s32[512]{0:T(512)S(1)}, s32[512]{0:T(512)}, u32[]{:S(2)}) copy-start(s32[512]{0:T(512)} %copy-done.62) | copy-start | bytes 6148
  151.3 40.3 %collective-permute-start.7 = (bf16[2,768,768]{2,1,0:T(8,128)(2,1)}, bf16[2,768,768]{2,1,0:T(8,128)(2,1)}, u32[]{:S(2)}, u32[]{:S(2)}) collective-permute-start(bf16[2,768,768]{2,1,0:T(8,128)(2,1)} %slice.301.bc0), channel_id=1, source_target_pairs={{0,1},{1,0},{2,3},{3,2},{4,5},{5,4},{6,7},{7,6},{8,9},{9,8},{10,11... | collective-permute-start | bytes 7077896 | tf_op jit(solution)/shard_map/ppermute | solution.py:34
  186.8 4.8 collective-permute-start.8
  186.8 58.2 %collective-permute-start.12 = (bf16[768,1664]{1,0:T(8,128)(2,1)}, bf16[768,1664]{1,0:T(8,128)(2,1)}, u32[]{:S(2)}, u32[]{:S(2)}) collective-permute-start(bf16[768,1664]{1,0:T(8,128)(2,1)} %bitcast.20), channel_id=1, source_target_pairs={{0,2},{1,3},{2,0},{3,1},{4,6},{5,7},{6,4},{7,5},{8,10},{9,11},{10,... | collective-permute-start | bytes 7667720 | tf_op jit(solution)/shard_map/ppermute | solution.py:34
  208.7 20.1 %slice-start.4 = ((s32[8,2,1408]{2,1,0:T(2,128)}), s32[8,2,256]{2,1,0:T(2,128)S(1)}, s32[]{:S(2)}) async-start(s32[8,2,1408]{2,1,0:T(2,128)} %copy-done.40), calls=%async_computation.16 | async-start | bytes 32768 | tf_op jit(solution)/shard_map/slice | solution.py:717
  209.7 1.6 collective-permute-start.9
  212.2 9.2 %collective-permute-start.10 = (bf16[80,768]{1,0:T(8,128)(2,1)S(1)}, bf16[80,768]{1,0:T(8,128)(2,1)S(1)}, u32[]{:S(2)}, u32[]{:S(2)}) collective-permute-start(bf16[80,768]{1,0:T(8,128)(2,1)S(1)} %slice.305), channel_id=1, source_target_pairs={{0,16},{4,20},{8,24},{12,28},{16,0},{20,4},{24,8},{28,12},{1,17},{... | collective-permute-start | bytes 368648 | tf_op jit(solution)/shard_map/ppermute | solution.py:40
  222.4 30.8 %all-to-all-start.3 = ((bf16[8,80,768]{2,1,0:T(8,128)(2,1)}), bf16[8,80,768]{2,1,0:T(8,128)(2,1)S(1)}, u32[]{:S(2)}, u32[]{:S(2)}) async-start(bf16[8,80,768]{2,1,0:T(8,128)(2,1)} %broadcast_in_dim.197), calls=%async_computation.3 | async-start | bytes 1966080 | tf_op jit(solution)/shard_map/all_to_all | solution.py:44
  228.7 32.4 %collective-permute-start.11 = (bf16[768,1664]{1,0:T(8,128)(2,1)}, bf16[768,1664]{1,0:T(8,128)(2,1)}, u32[]{:S(2)}, u32[]{:S(2)}) collective-permute-start(bf16[768,1664]{1,0:T(8,128)(2,1)} %bitcast.20), channel_id=1, source_target_pairs={{0,1},{1,0},{2,3},{3,2},{4,5},{5,4},{6,7},{7,6},{8,9},{9,8},{10,11... | collective-permute-start | bytes 7667720 | tf_op jit(solution)/shard_map/ppermute | solution.py:34
  245.0 19.9 %collective-permute-start.13 = (bf16[768,1664]{1,0:T(8,128)(2,1)}, bf16[768,1664]{1,0:T(8,128)(2,1)}, u32[]{:S(2)}, u32[]{:S(2)}) collective-permute-start(bf16[768,1664]{1,0:T(8,128)(2,1)} %collective-permute-done.12), channel_id=1, source_target_pairs={{0,1},{1,0},{2,3},{3,2},{4,5},{5,4},{6,7},{7,6},{8,9},{9,8},{10,11... | collective-permute-start | bytes 7667720 | tf_op jit(solution)/shard_map/ppermute | solution.py:34
  268.6 34.5 %copy-start.14 = (f32[640,1664]{1,0:T(8,128)}, f32[640,1664]{1,0:T(8,128)S(1)}, u32[]{:S(2)}) copy-start(f32[640,1664]{1,0:T(8,128)S(1)} %get-tuple-element.296) | copy-start | bytes 12779524
  308.8 27.2 %all-to-all-start.5 = ((bf16[8,80,768]{2,1,0:T(8,128)(2,1)}), bf16[8,80,768]{2,1,0:T(8,128)(2,1)S(1)}, u32[]{:S(2)}, u32[]{:S(2)}) async-start(bf16[8,80,768]{2,1,0:T(8,128)(2,1)} %bitcast.274), calls=%async_computation.5 | async-start | bytes 1966080 | tf_op jit(solution)/shard_map/all_to_all | solution.py:44
  335.9 11.0 %collective-permute-start.16 = (bf16[768,1664]{1,0:T(8,128)(2,1)}, bf16[768,1664]{1,0:T(8,128)(2,1)}, u32[]{:S(2)}, u32[]{:S(2)}) collective-permute-start(bf16[768,1664]{1,0:T(8,128)(2,1)} %fusion.76), channel_id=1, source_target_pairs={{0,1},{1,0},{2,3},{3,2},{4,5},{5,4},{6,7},{7,6},{8,9},{9,8},{10,11... | collective-permute-start | bytes 7667720 | tf_op jit(solution)/shard_map/ppermute | solution.py:34
  336.1 8.4 %collective-permute-start.14 = (bf16[80,768]{1,0:T(8,128)(2,1)S(1)}, bf16[80,768]{1,0:T(8,128)(2,1)S(1)}, u32[]{:S(2)}, u32[]{:S(2)}) collective-permute-start(bf16[80,768]{1,0:T(8,128)(2,1)S(1)} %reduce_sum.252), channel_id=1, source_target_pairs={{0,16},{4,20},{8,24},{12,28},{16,0},{20,4},{24,8},{28,12},{1,17},{... | collective-permute-start | bytes 368648 | tf_op jit(solution)/shard_map/ppermute | solution.py:40
  344.6 1.6 collective-permute-start.15
  350.7 57.7 %collective-permute-start.17 = (bf16[768,1664]{1,0:T(8,128)(2,1)S(1)}, bf16[768,1664]{1,0:T(8,128)(2,1)}, u32[]{:S(2)}, u32[]{:S(2)}) collective-permute-start(bf16[768,1664]{1,0:T(8,128)(2,1)S(1)} %add_convert_fusion.1), channel_id=1, source_target_pairs={{0,2},{1,3},{2,0},{3,1},{4,6},{5,7},{6,4},{7,5},{8,10},{9,11},{10,... | collective-permute-start | bytes 7667720 | tf_op jit(solution)/shard_map/ppermute | solution.py:34
  402.3 6.5 collective-permute-start.19
  402.4 8.1 %collective-permute-start.20 = (bf16[2,768,768]{2,1,0:T(8,128)(2,1)}, bf16[2,768,768]{2,1,0:T(8,128)(2,1)S(1)}, u32[]{:S(2)}, u32[]{:S(2)}) collective-permute-start(bf16[2,768,768]{2,1,0:T(8,128)(2,1)} %get-tuple-element.157), channel_id=1, source_target_pairs={{0,1},{1,0},{2,3},{3,2},{4,5},{5,4},{6,7},{7,6},{8,9},{9,8},{10,11... | collective-permute-start | bytes 7077896 | tf_op jit(solution)/shard_map/ppermute | solution.py:34
  408.4 8.0 %collective-permute-start.18 = (bf16[4,512,384]{2,1,0:T(8,128)(2,1)}, bf16[4,512,384]{2,1,0:T(8,128)(2,1)S(1)}, u32[]{:S(2)}, u32[]{:S(2)}) collective-permute-start(bf16[4,512,384]{2,1,0:T(8,128)(2,1)} %get-tuple-element.153), channel_id=1, source_target_pairs={{0,1},{1,0},{2,3},{3,2},{4,5},{5,4},{6,7},{7,6},{8,9},{9,8},{10,11... | collective-permute-start | bytes 4718600 | tf_op jit(solution)/shard_map/ppermute | solution.py:34
  408.4 47.2 %collective-permute-start.25 = (bf16[768,1664]{1,0:T(8,128)(2,1)}, bf16[768,1664]{1,0:T(8,128)(2,1)S(1)}, u32[]{:S(2)}, u32[]{:S(2)}) collective-permute-start(bf16[768,1664]{1,0:T(8,128)(2,1)} %fusion.99), channel_id=1, source_target_pairs={{0,1},{1,0},{2,3},{3,2},{4,5},{5,4},{6,7},{7,6},{8,9},{9,8},{10,11... | collective-permute-start | bytes 7667720 | tf_op jit(solution)/shard_map/ppermute | solution.py:34
  417.5 29.2 %collective-permute-start.21 = (bf16[768,768]{1,0:T(8,128)(2,1)}, bf16[768,768]{1,0:T(8,128)(2,1)}, u32[]{:S(2)}, u32[]{:S(2)}) collective-permute-start(bf16[768,768]{1,0:T(8,128)(2,1)} %fusion.30), channel_id=1, source_target_pairs={{0,2},{1,3},{2,0},{3,1},{4,6},{5,7},{6,4},{7,5},{8,10},{9,11},{10,... | collective-permute-start | bytes 3538952 | tf_op jit(solution)/shard_map/ppermute | solution.py:34
  420.6 50.4 %collective-permute-start.24 = (bf16[768,768]{1,0:T(8,128)(2,1)}, bf16[768,768]{1,0:T(8,128)(2,1)}, u32[]{:S(2)}, u32[]{:S(2)}) collective-permute-start(bf16[768,768]{1,0:T(8,128)(2,1)} %fusion.31), channel_id=1, source_target_pairs={{0,2},{1,3},{2,0},{3,1},{4,6},{5,7},{6,4},{7,5},{8,10},{9,11},{10,... | collective-permute-start | bytes 3538952 | tf_op jit(solution)/shard_map/ppermute | solution.py:34
  454.1 29.3 %collective-permute-start.22 = (bf16[2,768,768]{2,1,0:T(8,128)(2,1)}, bf16[2,768,768]{2,1,0:T(8,128)(2,1)}, u32[]{:S(2)}, u32[]{:S(2)}) collective-permute-start(bf16[2,768,768]{2,1,0:T(8,128)(2,1)} %get-tuple-element.168), channel_id=1, source_target_pairs={{0,1},{1,0},{2,3},{3,2},{4,5},{5,4},{6,7},{7,6},{8,9},{9,8},{10,11... | collective-permute-start | bytes 7077896 | tf_op jit(solution)/shard_map/ppermute | solution.py:34
  455.6 15.4 %copy-start.71 = (f32[3,768]{1,0:T(4,128)S(1)}, f32[3,768]{1,0:T(4,128)}, u32[]{:S(2)}) copy-start(f32[3,768]{1,0:T(4,128)} %get-tuple-element.176) | copy-start | bytes 27652
  474.2 43.6 %all-to-all-start.6 = ((bf16[8,560,96]{1,2,0:T(8,128)(2,1)}), bf16[8,560,96]{1,2,0:T(8,128)(2,1)S(1)}, u32[]{:S(2)}, u32[]{:S(2)}) async-start(bf16[8,560,96]{1,2,0:T(8,128)(2,1)} %copy.209), calls=%async_computation.6 | async-start | bytes 1966080 | tf_op jit(solution)/shard_map/all_to_all | solution.py:44
  481.2 23.9 %collective-permute-start.26 = (bf16[4,96,768]{2,1,0:T(8,128)(2,1)S(1)}, bf16[4,96,768]{2,1,0:T(8,128)(2,1)S(1)}, u32[]{:S(2)}, u32[]{:S(2)}) collective-permute-start(bf16[4,96,768]{2,1,0:T(8,128)(2,1)S(1)} %fusion.35), channel_id=1, source_target_pairs={{0,4},{4,0},{8,12},{12,8},{16,20},{20,16},{24,28},{28,24},{1,5},{5... | collective-permute-start | bytes 1769480 | tf_op jit(solution)/shard_map/ppermute | solution.py:40
  487.5 30.3 %collective-permute-start.23 = (bf16[768,768]{1,0:T(8,128)(2,1)}, bf16[768,768]{1,0:T(8,128)(2,1)}, u32[]{:S(2)}, u32[]{:S(2)}) collective-permute-start(bf16[768,768]{1,0:T(8,128)(2,1)} %fusion.32), channel_id=1, source_target_pairs={{0,2},{1,3},{2,0},{3,1},{4,6},{5,7},{6,4},{7,5},{8,10},{9,11},{10,... | collective-permute-start | bytes 3538952 | tf_op jit(solution)/shard_map/ppermute | solution.py:34
  492.7 23.9 %collective-permute-start.27 = (bf16[4,96,768]{2,1,0:T(8,128)(2,1)S(1)}, bf16[4,96,768]{2,1,0:T(8,128)(2,1)}, u32[]{:S(2)}, u32[]{:S(2)}) collective-permute-start(bf16[4,96,768]{2,1,0:T(8,128)(2,1)S(1)} %fusion.36), channel_id=1, source_target_pairs={{0,4},{4,0},{8,12},{12,8},{16,20},{20,16},{24,28},{28,24},{1,5},{5... | collective-permute-start | bytes 1769480 | tf_op jit(solution)/shard_map/ppermute | solution.py:40
  493.8 22.8 %copy-start.11 = (f32[768,768]{1,0:T(8,128)S(1)}, f32[768,768]{1,0:T(8,128)}, u32[]{:S(2)}) copy-start(f32[768,768]{1,0:T(8,128)} %copy-done.10) | copy-start | bytes 7077892
  520.3 21.9 %collective-permute-start.28 = (bf16[4480,96]{0,1:T(8,128)(2,1)}, bf16[4480,96]{0,1:T(8,128)(2,1)}, u32[]{:S(2)}, u32[]{:S(2)}) collective-permute-start(bf16[4480,96]{0,1:T(8,128)(2,1)} %copy.213), channel_id=1, source_target_pairs={{0,2},{1,3},{2,0},{3,1},{4,6},{5,7},{6,4},{7,5},{8,10},{9,11},{10,... | collective-permute-start | bytes 2580488 | tf_op jit(solution)/shard_map/ppermute | solution.py:34
  521.7 5.8 collective-permute-start.29
  521.7 105.9 %all-to-all-start.7 = ((bf16[8,96,1664]{2,1,0:T(8,128)(2,1)}), bf16[8,96,1664]{2,1,0:T(8,128)(2,1)}, u32[]{:S(2)}, u32[]{:S(2)}) async-start(bf16[8,96,1664]{2,1,0:T(8,128)(2,1)} %bitcast.251), calls=%async_computation.7 | async-start | bytes 5111808 | tf_op jit(solution)/shard_map/all_to_all | solution.py:44
  542.2 10.1 %collective-permute-start.30 = (bf16[4480,96]{0,1:T(8,128)(2,1)}, bf16[4480,96]{0,1:T(8,128)(2,1)}, u32[]{:S(2)}, u32[]{:S(2)}) collective-permute-start(bf16[4480,96]{0,1:T(8,128)(2,1)} %collective-permute-done.28), channel_id=1, source_target_pairs={{0,1},{1,0},{2,3},{3,2},{4,5},{5,4},{6,7},{7,6},{8,9},{9,8},{10,11... | collective-permute-start | bytes 2580488 | tf_op jit(solution)/shard_map/ppermute | solution.py:34
  558.3 14.1 %copy-start.64 = (f32[8,1,128]{2,1,0:T(1,128)S(1)}, f32[8,1,128]{2,1,0:T(1,128)}, u32[]{:S(2)}) copy-start(f32[8,1,128]{2,1,0:T(1,128)} %get-tuple-element.279) | copy-start | bytes 12292
  558.3 46.7 %collective-permute-start.31 = (bf16[4,96,768]{2,1,0:T(8,128)(2,1)}, bf16[4,96,768]{2,1,0:T(8,128)(2,1)}, u32[]{:S(2)}, u32[]{:S(2)}) collective-permute-start(bf16[4,96,768]{2,1,0:T(8,128)(2,1)} %fusion.37), channel_id=1, source_target_pairs={{0,4},{4,0},{8,12},{12,8},{16,20},{20,16},{24,28},{28,24},{1,5},{5... | collective-permute-start | bytes 1769480 | tf_op jit(solution)/shard_map/ppermute | solution.py:40
  560.8 40.4 %collective-permute-start.37 = (bf16[96,768]{1,0:T(8,128)(2,1)}, bf16[96,768]{1,0:T(8,128)(2,1)}, u32[]{:S(2)}, u32[]{:S(2)}) collective-permute-start(bf16[96,768]{1,0:T(8,128)(2,1)} %get-tuple-element.250), channel_id=1, source_target_pairs={{0,24},{4,28},{8,16},{12,20},{16,8},{20,12},{24,0},{28,4},{1,25},{... | collective-permute-start | bytes 442376 | tf_op jit(solution)/shard_map/ppermute | solution.py:40
  564.0 37.6 %collective-permute-start.36 = (bf16[96,768]{1,0:T(8,128)(2,1)}, bf16[96,768]{1,0:T(8,128)(2,1)}, u32[]{:S(2)}, u32[]{:S(2)}) collective-permute-start(bf16[96,768]{1,0:T(8,128)(2,1)} %get-tuple-element.251), channel_id=1, source_target_pairs={{0,16},{4,20},{8,24},{12,28},{16,0},{20,4},{24,8},{28,12},{1,17},{... | collective-permute-start | bytes 442376 | tf_op jit(solution)/shard_map/ppermute | solution.py:40
  564.0 38.3 %collective-permute-start.35 = (bf16[96,768]{1,0:T(8,128)(2,1)}, bf16[96,768]{1,0:T(8,128)(2,1)}, u32[]{:S(2)}, u32[]{:S(2)}) collective-permute-start(bf16[96,768]{1,0:T(8,128)(2,1)} %get-tuple-element.249), channel_id=1, source_target_pairs={{0,8},{4,12},{8,0},{12,4},{16,24},{20,28},{24,16},{28,20},{1,9},{5... | collective-permute-start | bytes 442376 | tf_op jit(solution)/shard_map/ppermute | solution.py:40
  566.0 43.6 %collective-permute-start.40 = (bf16[96,768]{1,0:T(8,128)(2,1)}, bf16[96,768]{1,0:T(8,128)(2,1)}, u32[]{:S(2)}, u32[]{:S(2)}) collective-permute-start(bf16[96,768]{1,0:T(8,128)(2,1)} %get-tuple-element.247), channel_id=1, source_target_pairs={{0,24},{4,28},{8,16},{12,20},{16,8},{20,12},{24,0},{28,4},{1,25},{... | collective-permute-start | bytes 442376 | tf_op jit(solution)/shard_map/ppermute | solution.py:40
  577.9 23.3 %copy-start.49 = (bf16[96,768]{1,0:T(8,128)(2,1)S(1)}, bf16[96,768]{1,0:T(8,128)(2,1)}, u32[]{:S(2)}) copy-start(bf16[96,768]{1,0:T(8,128)(2,1)} %get-tuple-element.248) | copy-start | bytes 442372
  577.9 23.7 %copy-start.48 = (bf16[96,768]{1,0:T(8,128)(2,1)S(1)}, bf16[96,768]{1,0:T(8,128)(2,1)}, u32[]{:S(2)}) copy-start(bf16[96,768]{1,0:T(8,128)(2,1)} %get-tuple-element.246) | copy-start | bytes 442372
  601.2 16.1 %collective-permute-start.39 = (bf16[96,768]{1,0:T(8,128)(2,1)S(1)}, bf16[96,768]{1,0:T(8,128)(2,1)S(1)}, u32[]{:S(2)}, u32[]{:S(2)}) collective-permute-start(bf16[96,768]{1,0:T(8,128)(2,1)S(1)} %copy-done.49), channel_id=1, source_target_pairs={{0,16},{4,20},{8,24},{12,28},{16,0},{20,4},{24,8},{28,12},{1,17},{... | collective-permute-start | bytes 442376 | tf_op jit(solution)/shard_map/ppermute | solution.py:40
  601.6 15.7 %collective-permute-start.38 = (bf16[96,768]{1,0:T(8,128)(2,1)S(1)}, bf16[96,768]{1,0:T(8,128)(2,1)S(1)}, u32[]{:S(2)}, u32[]{:S(2)}) collective-permute-start(bf16[96,768]{1,0:T(8,128)(2,1)S(1)} %copy-done.48), channel_id=1, source_target_pairs={{0,8},{4,12},{8,0},{12,4},{16,24},{20,28},{24,16},{28,20},{1,9},{5... | collective-permute-start | bytes 442376 | tf_op jit(solution)/shard_map/ppermute | solution.py:40
  606.2 13.4 %collective-permute-start.34 = (bf16[96,768]{1,0:T(8,128)(2,1)S(1)}, bf16[96,768]{1,0:T(8,128)(2,1)S(1)}, u32[]{:S(2)}, u32[]{:S(2)}) collective-permute-start(bf16[96,768]{1,0:T(8,128)(2,1)S(1)} %get-tuple-element.253), channel_id=1, source_target_pairs={{0,24},{4,28},{8,16},{12,20},{16,8},{20,12},{24,0},{28,4},{1,25},{... | collective-permute-start | bytes 442376 | tf_op jit(solution)/shard_map/ppermute | solution.py:40
  609.6 13.5 %collective-permute-start.33 = (bf16[96,768]{1,0:T(8,128)(2,1)S(1)}, bf16[96,768]{1,0:T(8,128)(2,1)S(1)}, u32[]{:S(2)}, u32[]{:S(2)}) collective-permute-start(bf16[96,768]{1,0:T(8,128)(2,1)S(1)} %get-tuple-element.254), channel_id=1, source_target_pairs={{0,16},{4,20},{8,24},{12,28},{16,0},{20,4},{24,8},{28,12},{1,17},{... | collective-permute-start | bytes 442376 | tf_op jit(solution)/shard_map/ppermute | solution.py:40
  609.6 13.5 %collective-permute-start.32 = (bf16[96,768]{1,0:T(8,128)(2,1)S(1)}, bf16[96,768]{1,0:T(8,128)(2,1)S(1)}, u32[]{:S(2)}, u32[]{:S(2)}) collective-permute-start(bf16[96,768]{1,0:T(8,128)(2,1)S(1)} %get-tuple-element.252), channel_id=1, source_target_pairs={{0,8},{4,12},{8,0},{12,4},{16,24},{20,28},{24,16},{28,20},{1,9},{5... | collective-permute-start | bytes 442376 | tf_op jit(solution)/shard_map/ppermute | solution.py:40
  (64 other events, 326.3 us)
Sparse Core Ops, SparseCore 0:
  12.2 69.7 all-gather.1
  151.4 13.4 sort.11.cloned.1.call-done
  (1 shorter events, 0.0 us)

commit v4 on v3

--- a/solution.py
+++ b/solution.py
@@ -948,16 +948,20 @@
     c_near, c_far = scatter_core(c_sent, c_own)
     d_query, d_own, d_far, *table_from = together(d_query, d_own, d_far, *table_from)
     d_far, b_far, c_far = together(xor_narrow(d_far, 1), b_far, c_far)
-    b_from, c_from = xor_narrow(b_far, 2), xor_narrow(c_far, 2)
+    b_from = xor_narrow(b_far, 2)
+    c_pair = [
+        scatter_pair(value.astype(F32).reshape(wide, share, width)) for value in (c_near, c_far)
+    ]
     is_mask = (my_inputs == mask_entry).astype(F32)[:, None]
     d_start_rows, d_projected, d_first = qkv_back(
         d_query, d_own, d_far, full_a, d_middle, start, params, is_mask, rows + 16, wide
     )
 
     d_table = [table_sum(piece) for piece in range(len(cuts))]
-    d_start_rows, d_projected, d_first, b_from = together(
-        d_start_rows, d_projected, d_first, b_from
-    )
+    d_start_rows, d_projected, d_first, b_from, *c_pair = together(
+        d_start_rows, d_projected, d_first, b_from, *c_pair
+    )
+    c_from = xor_narrow(c_pair[1].astype(BF), 2)
     a_sent, a_own = qkv_grads(d_projected, hidden_one, d_attended, mixed)
     a_near, a_far = scatter_core(a_sent, a_own)
     d_start_rows, d_first, c_from, *d_table = together(d_start_rows, d_first, c_from, *d_table)
@@ -971,10 +975,8 @@
     d_start_rows = jnp.concatenate([d_start_rows, small], axis=1)
     d_start_recv = swap_wide(d_start_rows)
     a_from = xor_narrow(a_far, 2)
-    b_half, c_half = [
-        scatter_pair((near + other.astype(F32)).reshape(wide, share, width))
-        for near, other in ((b_near, b_from), (c_near, c_from))
-    ]
+    b_half = scatter_pair((b_near + b_from.astype(F32)).reshape(wide, share, width))
+    c_half = c_pair[0] + c_from.astype(F32)
     a_from, d_start_recv, b_half, c_half, *d_table = together(
         a_from, d_start_recv, b_half, c_half, *d_table
     )

time: 697 us -> 693 us (level)
    ppermute x27, waiting for transfers between devices: 86.3 us -> 70.2 us  [xor_narrow(): lax.ppermute(value, NARROW, [(i, i ^ bits) for i in range(lax.axis_size(N...]
    ppermute x14 -> x15, waiting for transfers between devices: 45.5 us -> 56.4 us  [xor_wide(): lax.ppermute(value, 'wide', [(i, i ^ bits) for i in range(lax.axis_size('...]
    ppermute x14 -> x15, starting transfers between devices: 20.6 us -> 21.5 us  [xor_wide(): lax.ppermute(value, 'wide', [(i, i ^ bits) for i in range(lax.axis_size('...]
  transfers between devices with their start and end apart: 49 -> 50, of which waited for: 21 -> 20; matrix products, arithmetic and copies ran while one was open for 20% -> 21% of each run, Pallas kernels for 25% -> 25%
where the time goes in v4:
time: 693 us; the launch traced here: 686 us
  Pallas kernels  173 us (25%)
  waiting for transfers between devices  164 us (24%)
  other arithmetic  114 us (16%)
  starting transfers between devices  72.4 us (10%)
  local copies, waits for them, and re-layouts  60.7 us (9%)
  matrix products  57.1 us (8%)
  between operations  23.8 us (3%)
  blocking collectives  20.9 us (3%)
    ppermute x27, waiting for transfers between devices, xor_narrow(): lax.ppermute(value, NARROW, [(i, i ^ bits) for i in range(lax.axis_size(N...  70.2 us
    ppermute x15, waiting for transfers between devices, xor_wide(): lax.ppermute(value, 'wide', [(i, i ^ bits) for i in range(lax.axis_size('...  56.4 us
    dot_general x12, matrix products, mm(): return lax.dot_general(a, b, dims, preferred_element_type=F32)  52.7 us
    all_to_all x7, waiting for transfers between devices, swap_wide(): return lax.all_to_all(value, 'wide', 0, 0, tiled=True)  37.2 us
    pallas_call x2, Pallas kernels, collect(): pl.pallas_call(functools.partial(collect_kernel, shift, first), in_specs=...  35.3 us
    all_to_all x7, starting transfers between devices, swap_wide(): return lax.all_to_all(value, 'wide', 0, 0, tiled=True)  34.8 us
    pallas_call x1, Pallas kernels, attend_back(): pl.pallas_call(attend_back_kernel, grid=(slots,), in_specs=[one, two, oth...  25.2 us
    pallas_call x1, Pallas kernels, feed_back(): pl.pallas_call(feed_back_kernel, out_shape=[jax.ShapeDtypeStruct((rows, w...  25.1 us
  transfers between devices with their start and end apart: 50, of which 20 were waited for; matrix products, arithmetic and copies ran while one was open for 21% of the time, Pallas kernels for 25%

profile of v4, /device:TPU:0, one launch (start us, length us, event | category | flops | bytes accessed | tf_op | source)
XLA Modules:
  0.0 685.8 jit_solution(12670919355621934551)
XLA Ops:
  12.2 2.7 bitcast_convert_fusion.5
  17.2 6.8 all-to-all-start
  24.1 8.4 %all-to-all-done = s32[8,2,1408]{2,1,0:T(2,128)S(1)} async-done(((s32[8,2,1408]{2,1,0:T(2,128)}), s32[8,2,1408]{2,1,0:T(2,128)S(1)}, u32[]{:S(2)}, u32[]{:S(2)}) %all-to-all-start) | async-done | bytes 90144 | tf_op jit(solution)/shard_map/all_to_all | solution.py:44
  36.7 15.0 %table_rows.1.table_ref = f32[26752,96]{1,0:T(8,128)} custom-call(f32[96,12672]{1,0:T(8,128)} %bitcast.252, bf16[96,12672]{1,0:T(8,128)(2,1)} %collective-permute-done.other_ref), custom_call_target="tpu_custom_call" | custom-call | flops 10000000000 | bytes 40000000 | tf_op jit(solution)/shard_map/table_rows/pallas_call | solution.py:554
  51.6 15.0 %lookup.1 = bf16[8192,96]{1,0:T(8,128)(2,1)} custom-call(s32[4,1,2048]{2,1,0:T(1,128)} %and_select_fusion.id_ref, f32[26752,96]{1,0:T(8,128)} %table_rows.1.table_ref), custom_call_target="tpu_custom_call" | custom-call | tf_op jit(solution)/shard_map/lookup/pallas_call | solution.py:586
  71.4 16.2 %collective-permute-done.1 = bf16[8,512,96]{1,2,0:T(8,128)(2,1)} collective-permute-done((bf16[8,512,96]{1,2,0:T(8,128)(2,1)S(1)}, bf16[8,512,96]{1,2,0:T(8,128)(2,1)}, u32[]{:S(2)}, u32[]{:S(2)}) %collective-permute-start.1) | collective-permute-done | bytes 786464 | tf_op jit(solution)/shard_map/ppermute | solution.py:34
  91.3 3.6 all-to-all-start.1
  101.1 17.0 %all-to-all-done.1 = bf16[8,560,96]{1,2,0:T(8,128)(2,1)S(1)} async-done(((bf16[8,560,96]{1,2,0:T(8,128)(2,1)}), bf16[8,560,96]{1,2,0:T(8,128)(2,1)S(1)}, u32[]{:S(2)}, u32[]{:S(2)}) %all-to-all-start.1) | async-done | bytes 860192 | tf_op jit(solution)/shard_map/all_to_all | solution.py:44
  118.1 3.8 copy.210
  122.0 4.4 all-to-all-start.2
  129.7 3.2 slice.301.bc0
  142.0 8.0 %qkv.1 = (bf16[4,512,192]{2,1,0:T(8,128)(2,1)}, bf16[4,512,384]{2,1,0:T(8,128)(2,1)}, bf16[512,768]{1,0:T(8,128)(2,1)}, f32[512,768]{1,0:T(8,128)}) custom-call(bf16[8,560,96]{2,1,0:T(8,128)(2,1)} %copy.209.recv_ref, f32[12,768]{1,0:T(8,128)} %pad_maximum_fusion.7.par_ref, bf16[768,768]{1,0:T(8,128)(2,1)} %copy-done.2, bf16[768,768]{1,0:T(8,128)(2,1)} %copy-done.4, ...), custom_call_target="tpu_custom_call" | custom-call | tf_op jit(solution)/shard_map/qkv/pallas_call | solution.py:205
  154.9 14.7 %attend.1 = (bf16[4,512,192]{2,1,0:T(8,128)(2,1)}, f32[4,3,512]{2,1,0:T(4,128)}) custom-call(bf16[4,512,192]{2,1,0:T(8,128)(2,1)} %get-tuple-element.120.q_ref, bf16[4,512,384]{2,1,0:T(8,128)(2,1)} %get-tuple-element.121.own_ref, bf16[4,512,384]{2,1,0:T(8,128)(2,1)} %copy-done.10), custom_call_target="tpu_custom_call" | custom-call | tf_op jit(solution)/shard_map/attend/pallas_call | solution.py:252
  169.7 17.0 %collective-permute-done.6.bc2 = bf16[2,768,768]{2,1,0:T(8,128)(2,1)} collective-permute-done((bf16[2,768,768]{2,1,0:T(8,128)(2,1)}, bf16[2,768,768]{2,1,0:T(8,128)(2,1)}, u32[]{:S(2)}, u32[]{:S(2)}) %collective-permute-start.6) | collective-permute-done | bytes 2359328 | tf_op jit(solution)/shard_map/ppermute | solution.py:34
  192.9 15.7 %feed.1 = (f32[512,768]{1,0:T(8,128)}, f32[512,768]{1,0:T(8,128)}, f32[512,768]{1,0:T(8,128)}, bf16[512,768]{1,0:T(8,128)(2,1)}, f32[4,512,768]{2,1,0:T(8,128)}, /*index=5*/bf16[320,768]{1,0:T(8,128)(2,1)}) custom-call(bf16[4,512,192]{2,1,0:T(8,128)(2,1)} %get-tuple-element.126.mixed_ref, f32[512,768]{1,0:T(8,128)} %get-tuple-element.127.start_ref, ...), custom_call_target="tpu_custom_call" | custom-call | tf_op jit(solution)/shard_map/feed/pallas_call | solution.py:300
  212.1 2.8 collective-permute-start.10
  215.0 6.3 collective-permute-done.10
  222.3 6.2 all-to-all-start.3
  228.7 16.2 %collective-permute-done.12 = bf16[768,1664]{1,0:T(8,128)(2,1)} collective-permute-done((bf16[768,1664]{1,0:T(8,128)(2,1)}, bf16[768,1664]{1,0:T(8,128)(2,1)}, u32[]{:S(2)}, u32[]{:S(2)}) %collective-permute-start.12) | collective-permute-done | bytes 2555936 | tf_op jit(solution)/shard_map/ppermute | solution.py:34
  245.5 7.5 %all-to-all-done.3 = bf16[8,80,768]{2,1,0:T(8,128)(2,1)S(1)} async-done(((bf16[8,80,768]{2,1,0:T(8,128)(2,1)}), bf16[8,80,768]{2,1,0:T(8,128)(2,1)S(1)}, u32[]{:S(2)}, u32[]{:S(2)}) %all-to-all-start.3) | async-done | bytes 983072 | tf_op jit(solution)/shard_map/all_to_all | solution.py:44
  253.0 4.1 select_reduce_fusion.4
  257.2 3.8 select_reduce_fusion.2
  260.9 3.8 select_reduce_fusion.3
  264.7 3.8 select_reduce_fusion.1
  268.5 6.0 exponential_reduce_fusion
  274.6 10.6 %all_to_all.45 = f32[8,3,640]{2,1,0:T(4,128)S(1)} all-to-all(f32[8,3,640]{2,1,0:T(4,128)S(1)} %broadcast_in_dim.206), channel_id=1, replica_groups=mesh['wide'=8,'line'=2,'core'=2] {'wide'}, dimensions={0} | all-to-all | bytes 122880 | tf_op jit(solution)/shard_map/all_to_all | solution.py:44
  285.9 4.4 fusion.8
  290.3 5.2 fusion.94
  295.6 3.7 fusion.96
  299.3 3.7 fusion.95
  303.0 5.6 add_convert_fusion.2
  308.6 3.8 all-to-all-start.5
  312.4 6.6 fusion.97
  319.1 3.8 fusion.98
  322.9 4.5 fusion.99
  327.4 4.1 fusion.75
  331.5 4.3 all-to-all-done.5
  336.0 8.4 %collective-permute-done.14 = bf16[80,768]{1,0:T(8,128)(2,1)S(1)} collective-permute-done((bf16[80,768]{1,0:T(8,128)(2,1)S(1)}, bf16[80,768]{1,0:T(8,128)(2,1)S(1)}, u32[]{:S(2)}, u32[]{:S(2)}) %collective-permute-start.14) | collective-permute-done | bytes 122912 | tf_op jit(solution)/shard_map/ppermute | solution.py:40
  346.8 3.7 add_convert_fusion.1
  352.0 25.1 %feed_back.1 = (f32[512,768]{1,0:T(8,128)}, bf16[512,768]{1,0:T(8,128)(2,1)}, bf16[4,512,192]{2,1,0:T(8,128)(2,1)}, bf16[2,768,768]{2,1,0:T(8,128)(2,1)}, bf16[2...) custom-call(bf16[320,768]{1,0:T(8,128)(2,1)} %pad_maximum_fusion.3.rows, ...), custom_call_target="tpu_custom_call" | custom-call | flops 10000000000 | bytes 40000000 | tf_op jit(solution)/shard_map/feed_back/pallas_call | solution.py:376
  377.1 25.2 %attend_back.1 = (bf16[4,512,192]{2,1,0:T(8,128)(2,1)}, f32[4,512,384]{2,1,0:T(8,128)}, bf16[4,512,384]{2,1,0:T(8,128)(2,1)}) custom-call(bf16[4,512,192]{2,1,0:T(8,128)(2,1)} %get-tuple-element.120.q_ref, bf16[4,512,384]{2,1,0:T(8,128)(2,1)} %get-tuple-element.121.own_ref, bf16[4,512,384]{2,1,0:T(8,128)(2,1)} %copy-done.10, ...), custom_call_target="tpu_custom_call" | custom-call | tf_op jit(solution)/shard_map/attend_back/pallas_call | solution.py:433
  402.8 5.4 collective-permute-done.17
  410.8 3.8 convert_element_type.314
  424.3 11.8 %collective-permute-done.22 = bf16[4,96,768]{2,1,0:T(8,128)(2,1)} collective-permute-done((bf16[4,96,768]{2,1,0:T(8,128)(2,1)}, bf16[4,96,768]{2,1,0:T(8,128)(2,1)}, u32[]{:S(2)}, u32[]{:S(2)}) %collective-permute-start.22) | collective-permute-done | bytes 589856 | tf_op jit(solution)/shard_map/ppermute | solution.py:40
  438.6 9.8 %qkv_back.1 = (bf16[8,528,96]{2,1,0:T(8,128)(2,1)}, bf16[4,512,576]{2,1,0:T(8,128)(2,1)}, f32[3,768]{1,0:T(4,128)}) custom-call(bf16[4,512,192]{2,1,0:T(8,128)(2,1)} %get-tuple-element.153.dq_ref, f32[4,512,384]{2,1,0:T(8,128)} %get-tuple-element.154.d_own_ref, bf16[4,512,384]{2,1,0:T(8,128)(2,1)} %copy-done.27, bf16[768,768]{1,0:T(8,128)(2,1)} %copy-done.2, ...), custom_call_target="tpu_custom_call" | custom-call | tf_op jit(solution)/shard_map/qkv_back/pallas_call | solution.py:492
  450.4 7.4 %qkv_grads.1 = (bf16[2,768,768]{2,1,0:T(8,128)(2,1)}, bf16[2,768,768]{2,1,0:T(8,128)(2,1)}) custom-call(bf16[4,512,576]{2,1,0:T(8,128)(2,1)} %get-tuple-element.167.grads_ref, bf16[512,768]{1,0:T(8,128)(2,1)} %get-tuple-element.168.hidden_ref, bf16[512,768]{1,0:T(8,128)(2,1)} %get-tuple-element.169.d_attended_ref, ...), custom_call_target="tpu_custom_call" | custom-call | flops 10000000000 | bytes 40000000 | tf_op jit(solution)/shard_map/qkv_grads/pallas_call | solution.py:528
  460.7 6.2 add_convert_fusion
  468.7 6.6 collective-permute-done.26
  477.8 4.3 all-to-all-start.6
  489.8 18.1 %collective-permute-done.28 = bf16[4,96,768]{2,1,0:T(8,128)(2,1)S(1)} collective-permute-done((bf16[4,96,768]{2,1,0:T(8,128)(2,1)S(1)}, bf16[4,96,768]{2,1,0:T(8,128)(2,1)S(1)}, u32[]{:S(2)}, u32[]{:S(2)}) %collective-permute-start.28) | collective-permute-done | bytes 589856 | tf_op jit(solution)/shard_map/ppermute | solution.py:40
  509.3 4.1 collective-permute-done.25
  517.0 5.7 all-to-all-start.7
  526.3 12.2 %collect.2.refs_0_ = f32[12672,96]{1,0:T(8,128)} custom-call(s32[2,4480]{1,0:T(2,128)} %get-tuple-element.271.key_ref, s32[2]{0:T(128)} %get-tuple-element.299.count_ref, bf16[4480,96]{1,0:T(8,128)(2,1)} %bitcast.256, bf16[4480,96]{1,0:T(8,128)(2,1)} %copy.223.two_ref), custom_call_target="tpu_custom_call" | custom-call | tf_op jit(solution)/shard_map/collect/pallas_call | solution.py:659
  557.0 3.3 collective-permute-start.38
  562.2 3.3 collective-permute-start.41
  568.6 2.9 multiply_reduce_fusion.1
  574.2 23.0 %collect.3 = f32[96,12672]{1,0:T(8,128)} custom-call(s32[2,4480]{1,0:T(2,128)} %get-tuple-element.272.key_ref, s32[2]{0:T(128)} %get-tuple-element.300.count_ref, bf16[4480,96]{1,0:T(8,128)(2,1)} %copy.224.one_ref, bf16[4480,96]{1,0:T(8,128)(2,1)} %copy.225.two_ref, f32[12672,96]{1,0:T(8,128)} %collect.2.refs_0_), custom_call_target="tpu_custom_call" | custom-call | tf_op jit(solution)/shard_map/collect/pallas_call | solution.py:659
  602.1 3.3 collective-permute-start.35
  606.6 7.2 %collective-permute-done.40 = bf16[96,768]{1,0:T(8,128)(2,1)S(1)} collective-permute-done((bf16[96,768]{1,0:T(8,128)(2,1)S(1)}, bf16[96,768]{1,0:T(8,128)(2,1)S(1)}, u32[]{:S(2)}, u32[]{:S(2)}) %collective-permute-start.40) | collective-permute-done | bytes 147488 | tf_op jit(solution)/shard_map/ppermute | solution.py:40
  615.5 3.9 collective-permute-done.34
  624.0 4.2 multiply_reduce_fusion
  636.1 10.3 %all_to_all.46 = f32[32,1,2]{2,1,0:T(1,128)S(1)} all-to-all(f32[32,1,2]{2,1,0:T(1,128)S(1)} %broadcast_in_dim.207), channel_id=1, replica_groups=mesh['wide'=8,'line'=2,'core'=2] {'wide','line','core'}, dimensions={0} | all-to-all | bytes 512 | tf_op jit(solution)/shard_map/all_to_all | solution.py:1028
  647.8 13.1 %fusion.31 = (f32[12672,96]{0,1:T(8,128)}, f32[12672,96]{0,1:T(8,128)}, f32[12672,96]{0,1:T(8,128)}) fusion(f32[96,12672]{1,0:T(8,128)} %collect.3, f32[]{:T(128)S(6)} %div.124, f32[12672,96]{0,1:T(8,128)} %param.46, f32[12672,96]{0,1:T(8,128)} %param.38, f32[12672,96]{0,1:T(8,128)} %param.30), kind=kLoop, calls=%fused_computation.82 | loop fusion | flops 18247680 | bytes 34062340 | tf_op jit(solution)/shard_map/transpose | solution.py:1041
  660.9 10.4 %multiply_subtract_fusion = (f32[96,12672]{1,0:T(8,128)}, f32[96,12672]{1,0:T(8,128)}, f32[96,12672]{1,0:T(8,128)}) fusion(f32[96,12672]{1,0:T(8,128)} %param.31, f32[]{:T(128)S(6)} %div.124, bf16[96,13312]{1,0:T(8,128)(2,1)S(1)} %bitcast.251, f32[96,12672]{1,0:T(8,128)} %param.39, f32[96,12672]{1,0:T(8,128)} %param.47), kind=kLoop, calls=%fused_computation.18 | loop fusion | flops 20680704 | bytes 31629316 | tf_op jit(solution)/shard_map/sub | solution.py:1050
  (429 shorter events, 146.9 us)
Async XLA Ops:
  7.2 82.8 %all-gather.2.cloned.1.call-start = ((), (), s32[]{:S(2)}) async-start(), calls=%async_computation.9 | async-start | bytes 3981312 | tf_op jit(solution)/shard_map/all_gather | solution.py:54
  12.2 23.5 %copy-start.24 = (f32[128,768]{1,0:T(8,128)S(1)}, f32[128,768]{1,0:T(8,128)}, u32[]{:S(2)}) copy-start(f32[128,768]{1,0:T(8,128)} %param.36) | copy-start | bytes 1179652
  14.9 21.8 %collective-permute-start = (bf16[96,12672]{1,0:T(8,128)(2,1)S(1)}, bf16[96,12672]{1,0:T(8,128)(2,1)}, u32[]{:S(2)}, u32[]{:S(2)}) collective-permute-start(bf16[96,12672]{1,0:T(8,128)(2,1)S(1)} %bitcast_convert_fusion.5), channel_id=1, source_target_pairs={{0,1},{1,0},{2,3},{3,2},{4,5},{5,4},{6,7},{7,6},{8,9},{9,8},{10,11... | collective-permute-start | bytes 7299080 | tf_op jit(solution)/shard_map/ppermute | solution.py:34
  17.2 15.4 %all-to-all-start = ((s32[8,2,1408]{2,1,0:T(2,128)}), s32[8,2,1408]{2,1,0:T(2,128)S(1)}, u32[]{:S(2)}, u32[]{:S(2)}) async-start(s32[8,2,1408]{2,1,0:T(2,128)} %broadcast_in_dim.187), calls=%async_computation | async-start | bytes 180224 | tf_op jit(solution)/shard_map/all_to_all | solution.py:44
  32.5 19.1 %copy-start.42 = (s32[8,2,1408]{2,1,0:T(2,128)}, s32[8,2,1408]{2,1,0:T(2,128)S(1)}, u32[]{:S(2)}) copy-start(s32[8,2,1408]{2,1,0:T(2,128)S(1)} %all-to-all-done) | copy-start | bytes 270340
  35.7 16.0 %copy-start.59 = (f32[8,1,128]{2,1,0:T(1,128)}, f32[8,1,128]{2,1,0:T(1,128)S(1)}, u32[]{:S(2)}) copy-start(f32[8,1,128]{2,1,0:T(1,128)S(1)} %get-tuple-element.286) | copy-start | bytes 12292
  68.9 18.7 %collective-permute-start.1 = (bf16[8,512,96]{1,2,0:T(8,128)(2,1)S(1)}, bf16[8,512,96]{1,2,0:T(8,128)(2,1)}, u32[]{:S(2)}, u32[]{:S(2)}) collective-permute-start(bf16[8,512,96]{1,2,0:T(8,128)(2,1)S(1)} %copy.200), channel_id=1, source_target_pairs={{0,2},{1,3},{2,0},{3,1},{4,6},{5,7},{6,4},{7,5},{8,10},{9,11},{10,... | collective-permute-start | bytes 2359304 | tf_op jit(solution)/shard_map/ppermute | solution.py:34
  91.3 35.3 %copy-start.2 = (bf16[768,768]{1,0:T(8,128)(2,1)}, bf16[768,768]{1,0:T(8,128)(2,1)S(1)}, u32[]{:S(2)}) copy-start(bf16[768,768]{1,0:T(8,128)(2,1)S(1)} %slice_bitcast_fusion.a0) | copy-start | bytes 3538948
  91.3 26.8 %all-to-all-start.1 = ((bf16[8,560,96]{1,2,0:T(8,128)(2,1)}), bf16[8,560,96]{1,2,0:T(8,128)(2,1)S(1)}, u32[]{:S(2)}, u32[]{:S(2)}) async-start(bf16[8,560,96]{1,2,0:T(8,128)(2,1)} %fusion.32), calls=%async_computation.1 | async-start | bytes 1966080 | tf_op jit(solution)/shard_map/all_to_all | solution.py:44
  94.9 31.8 %collective-permute-start.3 = (bf16[768,768]{1,0:T(8,128)(2,1)S(1)}, bf16[768,768]{1,0:T(8,128)(2,1)S(1)}, u32[]{:S(2)}, u32[]{:S(2)}) collective-permute-start(bf16[768,768]{1,0:T(8,128)(2,1)S(1)} %slice_bitcast_fusion.a0), channel_id=1, source_target_pairs={{0,2},{1,3},{2,0},{3,1},{4,6},{5,7},{6,4},{7,5},{8,10},{9,11},{10,... | collective-permute-start | bytes 3538952 | tf_op jit(solution)/shard_map/ppermute | solution.py:34
  122.0 64.8 %all-to-all-start.2 = ((bf16[8,96,1664]{2,1,0:T(8,128)(2,1)}), bf16[8,96,1664]{2,1,0:T(8,128)(2,1)}, u32[]{:S(2)}, u32[]{:S(2)}) async-start(bf16[8,96,1664]{2,1,0:T(8,128)(2,1)} %copy.210), calls=%async_computation.2 | async-start | bytes 5111808 | tf_op jit(solution)/shard_map/all_to_all | solution.py:44
  126.4 43.3 %sort.9.cloned.1.call-start = ((), (), s32[]{:S(2)}) async-start(), calls=%async_computation.10 | async-start | bytes 215072 | tf_op jit(solution)/shard_map/sort | solution.py:831
  126.6 6.3 collective-permute-start.2
  126.7 6.2 collective-permute-start.4
  133.0 53.7 %collective-permute-start.6 = (bf16[2,768,768]{2,1,0:T(8,128)(2,1)}, bf16[2,768,768]{2,1,0:T(8,128)(2,1)}, u32[]{:S(2)}, u32[]{:S(2)}) collective-permute-start(bf16[2,768,768]{2,1,0:T(8,128)(2,1)} %slice.301.bc0), channel_id=1, source_target_pairs={{0,2},{1,3},{2,0},{3,1},{4,6},{5,7},{6,4},{7,5},{8,10},{9,11},{10,... | collective-permute-start | bytes 7077896 | tf_op jit(solution)/shard_map/ppermute | solution.py:34
  150.0 38.3 %copy-start.68 = (s32[1,2,256]{2,1,0:T(2,128)S(1)}, s32[1,2,256]{2,1,0:T(2,128)}, u32[]{:S(2)}) copy-start(s32[1,2,256]{2,1,0:T(2,128)} %param.28) | copy-start | bytes 6148
  150.0 38.3 %copy-start.72 = (s32[8,2,1]{0,1,2:T(2,128)S(1)}, s32[8,2,1]{0,1,2:T(2,128)}, u32[]{:S(2)}) copy-start(s32[8,2,1]{0,1,2:T(2,128)} %copy-done.71) | copy-start | bytes 196
  150.0 3.7 collective-permute-start.5
  150.1 40.5 %copy-start.65 = (s32[512]{0:T(512)S(1)}, s32[512]{0:T(512)}, u32[]{:S(2)}) copy-start(s32[512]{0:T(512)} %copy-done.64) | copy-start | bytes 6148
  151.3 40.2 %collective-permute-start.7 = (bf16[2,768,768]{2,1,0:T(8,128)(2,1)}, bf16[2,768,768]{2,1,0:T(8,128)(2,1)}, u32[]{:S(2)}, u32[]{:S(2)}) collective-permute-start(bf16[2,768,768]{2,1,0:T(8,128)(2,1)} %slice.301.bc0), channel_id=1, source_target_pairs={{0,1},{1,0},{2,3},{3,2},{4,5},{5,4},{6,7},{7,6},{8,9},{9,8},{10,11... | collective-permute-start | bytes 7077896 | tf_op jit(solution)/shard_map/ppermute | solution.py:34
  186.7 4.8 collective-permute-start.8
  186.7 58.2 %collective-permute-start.12 = (bf16[768,1664]{1,0:T(8,128)(2,1)}, bf16[768,1664]{1,0:T(8,128)(2,1)}, u32[]{:S(2)}, u32[]{:S(2)}) collective-permute-start(bf16[768,1664]{1,0:T(8,128)(2,1)} %bitcast.20), channel_id=1, source_target_pairs={{0,2},{1,3},{2,0},{3,1},{4,6},{5,7},{6,4},{7,5},{8,10},{9,11},{10,... | collective-permute-start | bytes 7667720 | tf_op jit(solution)/shard_map/ppermute | solution.py:34
  208.6 20.1 %slice-start.4 = ((s32[8,2,1408]{2,1,0:T(2,128)}), s32[8,2,256]{2,1,0:T(2,128)S(1)}, s32[]{:S(2)}) async-start(s32[8,2,1408]{2,1,0:T(2,128)} %copy-done.42), calls=%async_computation.16 | async-start | bytes 32768 | tf_op jit(solution)/shard_map/slice | solution.py:717
  209.5 1.6 collective-permute-start.9
  212.1 9.2 %collective-permute-start.10 = (bf16[80,768]{1,0:T(8,128)(2,1)S(1)}, bf16[80,768]{1,0:T(8,128)(2,1)S(1)}, u32[]{:S(2)}, u32[]{:S(2)}) collective-permute-start(bf16[80,768]{1,0:T(8,128)(2,1)S(1)} %slice.305), channel_id=1, source_target_pairs={{0,16},{4,20},{8,24},{12,28},{16,0},{20,4},{24,8},{28,12},{1,17},{... | collective-permute-start | bytes 368648 | tf_op jit(solution)/shard_map/ppermute | solution.py:40
  222.3 30.7 %all-to-all-start.3 = ((bf16[8,80,768]{2,1,0:T(8,128)(2,1)}), bf16[8,80,768]{2,1,0:T(8,128)(2,1)S(1)}, u32[]{:S(2)}, u32[]{:S(2)}) async-start(bf16[8,80,768]{2,1,0:T(8,128)(2,1)} %broadcast_in_dim.197), calls=%async_computation.3 | async-start | bytes 1966080 | tf_op jit(solution)/shard_map/all_to_all | solution.py:44
  228.5 32.4 %collective-permute-start.11 = (bf16[768,1664]{1,0:T(8,128)(2,1)}, bf16[768,1664]{1,0:T(8,128)(2,1)}, u32[]{:S(2)}, u32[]{:S(2)}) collective-permute-start(bf16[768,1664]{1,0:T(8,128)(2,1)} %bitcast.20), channel_id=1, source_target_pairs={{0,1},{1,0},{2,3},{3,2},{4,5},{5,4},{6,7},{7,6},{8,9},{9,8},{10,11... | collective-permute-start | bytes 7667720 | tf_op jit(solution)/shard_map/ppermute | solution.py:34
  244.9 19.8 %collective-permute-start.13 = (bf16[768,1664]{1,0:T(8,128)(2,1)}, bf16[768,1664]{1,0:T(8,128)(2,1)}, u32[]{:S(2)}, u32[]{:S(2)}) collective-permute-start(bf16[768,1664]{1,0:T(8,128)(2,1)} %collective-permute-done.12), channel_id=1, source_target_pairs={{0,1},{1,0},{2,3},{3,2},{4,5},{5,4},{6,7},{7,6},{8,9},{9,8},{10,11... | collective-permute-start | bytes 7667720 | tf_op jit(solution)/shard_map/ppermute | solution.py:34
  268.5 34.5 %copy-start.13 = (f32[640,1664]{1,0:T(8,128)}, f32[640,1664]{1,0:T(8,128)S(1)}, u32[]{:S(2)}) copy-start(f32[640,1664]{1,0:T(8,128)S(1)} %get-tuple-element.302) | copy-start | bytes 12779524
  308.6 27.2 %all-to-all-start.5 = ((bf16[8,80,768]{2,1,0:T(8,128)(2,1)}), bf16[8,80,768]{2,1,0:T(8,128)(2,1)S(1)}, u32[]{:S(2)}, u32[]{:S(2)}) async-start(bf16[8,80,768]{2,1,0:T(8,128)(2,1)} %bitcast.281), calls=%async_computation.5 | async-start | bytes 1966080 | tf_op jit(solution)/shard_map/all_to_all | solution.py:44
  335.8 11.0 %collective-permute-start.16 = (bf16[768,1664]{1,0:T(8,128)(2,1)}, bf16[768,1664]{1,0:T(8,128)(2,1)}, u32[]{:S(2)}, u32[]{:S(2)}) collective-permute-start(bf16[768,1664]{1,0:T(8,128)(2,1)} %fusion.75), channel_id=1, source_target_pairs={{0,1},{1,0},{2,3},{3,2},{4,5},{5,4},{6,7},{7,6},{8,9},{9,8},{10,11... | collective-permute-start | bytes 7667720 | tf_op jit(solution)/shard_map/ppermute | solution.py:34
  336.0 8.4 %collective-permute-start.14 = (bf16[80,768]{1,0:T(8,128)(2,1)S(1)}, bf16[80,768]{1,0:T(8,128)(2,1)S(1)}, u32[]{:S(2)}, u32[]{:S(2)}) collective-permute-start(bf16[80,768]{1,0:T(8,128)(2,1)S(1)} %reduce_sum.252), channel_id=1, source_target_pairs={{0,16},{4,20},{8,24},{12,28},{16,0},{20,4},{24,8},{28,12},{1,17},{... | collective-permute-start | bytes 368648 | tf_op jit(solution)/shard_map/ppermute | solution.py:40
  344.4 1.6 collective-permute-start.15
  350.5 57.7 %collective-permute-start.17 = (bf16[768,1664]{1,0:T(8,128)(2,1)S(1)}, bf16[768,1664]{1,0:T(8,128)(2,1)}, u32[]{:S(2)}, u32[]{:S(2)}) collective-permute-start(bf16[768,1664]{1,0:T(8,128)(2,1)S(1)} %add_convert_fusion.1), channel_id=1, source_target_pairs={{0,2},{1,3},{2,0},{3,1},{4,6},{5,7},{6,4},{7,5},{8,10},{9,11},{10,... | collective-permute-start | bytes 7667720 | tf_op jit(solution)/shard_map/ppermute | solution.py:34
  402.3 6.4 collective-permute-start.19
  402.3 8.5 %collective-permute-start.20 = (bf16[2,768,768]{2,1,0:T(8,128)(2,1)}, bf16[2,768,768]{2,1,0:T(8,128)(2,1)}, u32[]{:S(2)}, u32[]{:S(2)}) collective-permute-start(bf16[2,768,768]{2,1,0:T(8,128)(2,1)} %get-tuple-element.159), channel_id=1, source_target_pairs={{0,1},{1,0},{2,3},{3,2},{4,5},{5,4},{6,7},{7,6},{8,9},{9,8},{10,11... | collective-permute-start | bytes 7077896 | tf_op jit(solution)/shard_map/ppermute | solution.py:34
  408.2 8.9 %collective-permute-start.18 = (bf16[4,512,384]{2,1,0:T(8,128)(2,1)}, bf16[4,512,384]{2,1,0:T(8,128)(2,1)S(1)}, u32[]{:S(2)}, u32[]{:S(2)}) collective-permute-start(bf16[4,512,384]{2,1,0:T(8,128)(2,1)} %get-tuple-element.155), channel_id=1, source_target_pairs={{0,1},{1,0},{2,3},{3,2},{4,5},{5,4},{6,7},{7,6},{8,9},{9,8},{10,11... | collective-permute-start | bytes 4718600 | tf_op jit(solution)/shard_map/ppermute | solution.py:34
  408.2 52.5 %collective-permute-start.27 = (bf16[768,1664]{1,0:T(8,128)(2,1)}, bf16[768,1664]{1,0:T(8,128)(2,1)}, u32[]{:S(2)}, u32[]{:S(2)}) collective-permute-start(bf16[768,1664]{1,0:T(8,128)(2,1)} %fusion.98), channel_id=1, source_target_pairs={{0,1},{1,0},{2,3},{3,2},{4,5},{5,4},{6,7},{7,6},{8,9},{9,8},{10,11... | collective-permute-start | bytes 7667720 | tf_op jit(solution)/shard_map/ppermute | solution.py:34
  417.1 33.3 %collective-permute-start.21 = (bf16[768,768]{1,0:T(8,128)(2,1)}, bf16[768,768]{1,0:T(8,128)(2,1)S(1)}, u32[]{:S(2)}, u32[]{:S(2)}) collective-permute-start(bf16[768,768]{1,0:T(8,128)(2,1)} %fusion.28), channel_id=1, source_target_pairs={{0,2},{1,3},{2,0},{3,1},{4,6},{5,7},{6,4},{7,5},{8,10},{9,11},{10,... | collective-permute-start | bytes 3538952 | tf_op jit(solution)/shard_map/ppermute | solution.py:34
  419.5 16.5 %collective-permute-start.22 = (bf16[4,96,768]{2,1,0:T(8,128)(2,1)}, bf16[4,96,768]{2,1,0:T(8,128)(2,1)}, u32[]{:S(2)}, u32[]{:S(2)}) collective-permute-start(bf16[4,96,768]{2,1,0:T(8,128)(2,1)} %fusion.33), channel_id=1, source_target_pairs={{0,4},{4,0},{8,12},{12,8},{16,20},{20,16},{24,28},{28,24},{1,5},{5... | collective-permute-start | bytes 1769480 | tf_op jit(solution)/shard_map/ppermute | solution.py:40
  421.6 26.8 %collective-permute-start.23 = (bf16[4,96,768]{2,1,0:T(8,128)(2,1)}, bf16[4,96,768]{2,1,0:T(8,128)(2,1)}, u32[]{:S(2)}, u32[]{:S(2)}) collective-permute-start(bf16[4,96,768]{2,1,0:T(8,128)(2,1)} %fusion.34), channel_id=1, source_target_pairs={{0,4},{4,0},{8,12},{12,8},{16,20},{20,16},{24,28},{28,24},{1,5},{5... | collective-permute-start | bytes 1769480 | tf_op jit(solution)/shard_map/ppermute | solution.py:40
  457.8 24.2 %collective-permute-start.24 = (bf16[2,768,768]{2,1,0:T(8,128)(2,1)}, bf16[2,768,768]{2,1,0:T(8,128)(2,1)}, u32[]{:S(2)}, u32[]{:S(2)}) collective-permute-start(bf16[2,768,768]{2,1,0:T(8,128)(2,1)} %get-tuple-element.171), channel_id=1, source_target_pairs={{0,1},{1,0},{2,3},{3,2},{4,5},{5,4},{6,7},{7,6},{8,9},{9,8},{10,11... | collective-permute-start | bytes 7077896 | tf_op jit(solution)/shard_map/ppermute | solution.py:34
  459.5 15.8 %collective-permute-start.26 = (bf16[4,96,768]{2,1,0:T(8,128)(2,1)S(1)}, bf16[4,96,768]{2,1,0:T(8,128)(2,1)S(1)}, u32[]{:S(2)}, u32[]{:S(2)}) collective-permute-start(bf16[4,96,768]{2,1,0:T(8,128)(2,1)S(1)} %copy-done.36), channel_id=1, source_target_pairs={{0,2},{1,3},{2,0},{3,1},{4,6},{5,7},{6,4},{7,5},{8,10},{9,11},{10,... | collective-permute-start | bytes 1769480 | tf_op jit(solution)/shard_map/ppermute | solution.py:34
  477.8 31.5 %all-to-all-start.6 = ((bf16[8,560,96]{1,2,0:T(8,128)(2,1)}), bf16[8,560,96]{1,2,0:T(8,128)(2,1)S(1)}, u32[]{:S(2)}, u32[]{:S(2)}) async-start(bf16[8,560,96]{1,2,0:T(8,128)(2,1)} %copy.218), calls=%async_computation.6 | async-start | bytes 1966080 | tf_op jit(solution)/shard_map/all_to_all | solution.py:44
  485.7 22.4 %copy-start.12 = (f32[4,96,768]{2,1,0:T(8,128)S(1)}, f32[4,96,768]{2,1,0:T(8,128)}, u32[]{:S(2)}) copy-start(f32[4,96,768]{2,1,0:T(8,128)} %bitcast_add_fusion.4) | copy-start | bytes 3538948
  485.7 22.4 %copy-start.38 = (bf16[4,96,768]{2,1,0:T(8,128)(2,1)S(1)}, bf16[4,96,768]{2,1,0:T(8,128)(2,1)}, u32[]{:S(2)}) copy-start(bf16[4,96,768]{2,1,0:T(8,128)(2,1)} %copy-done.37) | copy-start | bytes 1769476
  485.7 27.6 %collective-permute-start.25 = (bf16[768,768]{1,0:T(8,128)(2,1)}, bf16[768,768]{1,0:T(8,128)(2,1)}, u32[]{:S(2)}, u32[]{:S(2)}) collective-permute-start(bf16[768,768]{1,0:T(8,128)(2,1)} %fusion.30), channel_id=1, source_target_pairs={{0,2},{1,3},{2,0},{3,1},{4,6},{5,7},{6,4},{7,5},{8,10},{9,11},{10,... | collective-permute-start | bytes 3538952 | tf_op jit(solution)/shard_map/ppermute | solution.py:34
  487.8 20.2 %collective-permute-start.28 = (bf16[4,96,768]{2,1,0:T(8,128)(2,1)S(1)}, bf16[4,96,768]{2,1,0:T(8,128)(2,1)S(1)}, u32[]{:S(2)}, u32[]{:S(2)}) collective-permute-start(bf16[4,96,768]{2,1,0:T(8,128)(2,1)S(1)} %fusion.35), channel_id=1, source_target_pairs={{0,4},{4,0},{8,12},{12,8},{16,20},{20,16},{24,28},{28,24},{1,5},{5... | collective-permute-start | bytes 1769480 | tf_op jit(solution)/shard_map/ppermute | solution.py:40
  515.8 22.7 %collective-permute-start.29 = (bf16[4480,96]{0,1:T(8,128)(2,1)}, bf16[4480,96]{0,1:T(8,128)(2,1)}, u32[]{:S(2)}, u32[]{:S(2)}) collective-permute-start(bf16[4480,96]{0,1:T(8,128)(2,1)} %copy.221), channel_id=1, source_target_pairs={{0,2},{1,3},{2,0},{3,1},{4,6},{5,7},{6,4},{7,5},{8,10},{9,11},{10,... | collective-permute-start | bytes 2580488 | tf_op jit(solution)/shard_map/ppermute | solution.py:34
  517.0 7.0 %collective-permute-start.30 = (bf16[4480,96]{0,1:T(8,128)(2,1)}, bf16[4480,96]{0,1:T(8,128)(2,1)}, u32[]{:S(2)}, u32[]{:S(2)}) collective-permute-start(bf16[4480,96]{0,1:T(8,128)(2,1)} %copy.221), channel_id=1, source_target_pairs={{0,1},{1,0},{2,3},{3,2},{4,5},{5,4},{6,7},{7,6},{8,9},{9,8},{10,11... | collective-permute-start | bytes 2580488 | tf_op jit(solution)/shard_map/ppermute | solution.py:34
  517.0 107.0 %all-to-all-start.7 = ((bf16[8,96,1664]{2,1,0:T(8,128)(2,1)}), bf16[8,96,1664]{2,1,0:T(8,128)(2,1)}, u32[]{:S(2)}, u32[]{:S(2)}) async-start(bf16[8,96,1664]{2,1,0:T(8,128)(2,1)} %bitcast.257), calls=%async_computation.7 | async-start | bytes 5111808 | tf_op jit(solution)/shard_map/all_to_all | solution.py:44
  538.5 9.8 %collective-permute-start.31 = (bf16[4480,96]{0,1:T(8,128)(2,1)}, bf16[4480,96]{0,1:T(8,128)(2,1)}, u32[]{:S(2)}, u32[]{:S(2)}) collective-permute-start(bf16[4480,96]{0,1:T(8,128)(2,1)} %collective-permute-done.29), channel_id=1, source_target_pairs={{0,1},{1,0},{2,3},{3,2},{4,5},{5,4},{6,7},{7,6},{8,9},{9,8},{10,11... | collective-permute-start | bytes 2580488 | tf_op jit(solution)/shard_map/ppermute | solution.py:34
  554.2 46.7 %collective-permute-start.32 = (bf16[4,96,768]{2,1,0:T(8,128)(2,1)}, bf16[4,96,768]{2,1,0:T(8,128)(2,1)}, u32[]{:S(2)}, u32[]{:S(2)}) collective-permute-start(bf16[4,96,768]{2,1,0:T(8,128)(2,1)} %fusion.36), channel_id=1, source_target_pairs={{0,4},{4,0},{8,12},{12,8},{16,20},{20,16},{24,28},{28,24},{1,5},{5... | collective-permute-start | bytes 1769480 | tf_op jit(solution)/shard_map/ppermute | solution.py:40
  557.0 40.2 %collective-permute-start.38 = (bf16[96,768]{1,0:T(8,128)(2,1)}, bf16[96,768]{1,0:T(8,128)(2,1)}, u32[]{:S(2)}, u32[]{:S(2)}) collective-permute-start(bf16[96,768]{1,0:T(8,128)(2,1)} %get-tuple-element.256), channel_id=1, source_target_pairs={{0,24},{4,28},{8,16},{12,20},{16,8},{20,12},{24,0},{28,4},{1,25},{... | collective-permute-start | bytes 442376 | tf_op jit(solution)/shard_map/ppermute | solution.py:40
  560.3 37.8 %collective-permute-start.37 = (bf16[96,768]{1,0:T(8,128)(2,1)}, bf16[96,768]{1,0:T(8,128)(2,1)}, u32[]{:S(2)}, u32[]{:S(2)}) collective-permute-start(bf16[96,768]{1,0:T(8,128)(2,1)} %get-tuple-element.257), channel_id=1, source_target_pairs={{0,16},{4,20},{8,24},{12,28},{16,0},{20,4},{24,8},{28,12},{1,17},{... | collective-permute-start | bytes 442376 | tf_op jit(solution)/shard_map/ppermute | solution.py:40
  560.3 38.2 %collective-permute-start.36 = (bf16[96,768]{1,0:T(8,128)(2,1)}, bf16[96,768]{1,0:T(8,128)(2,1)}, u32[]{:S(2)}, u32[]{:S(2)}) collective-permute-start(bf16[96,768]{1,0:T(8,128)(2,1)} %get-tuple-element.255), channel_id=1, source_target_pairs={{0,8},{4,12},{8,0},{12,4},{16,24},{20,28},{24,16},{28,20},{1,9},{5... | collective-permute-start | bytes 442376 | tf_op jit(solution)/shard_map/ppermute | solution.py:40
  562.2 43.2 %collective-permute-start.41 = (bf16[96,768]{1,0:T(8,128)(2,1)}, bf16[96,768]{1,0:T(8,128)(2,1)}, u32[]{:S(2)}, u32[]{:S(2)}) collective-permute-start(bf16[96,768]{1,0:T(8,128)(2,1)} %get-tuple-element.253), channel_id=1, source_target_pairs={{0,24},{4,28},{8,16},{12,20},{16,8},{20,12},{24,0},{28,4},{1,25},{... | collective-permute-start | bytes 442376 | tf_op jit(solution)/shard_map/ppermute | solution.py:40
  574.2 23.1 %copy-start.51 = (bf16[96,768]{1,0:T(8,128)(2,1)S(1)}, bf16[96,768]{1,0:T(8,128)(2,1)}, u32[]{:S(2)}) copy-start(bf16[96,768]{1,0:T(8,128)(2,1)} %get-tuple-element.254) | copy-start | bytes 442372
  574.2 23.9 %copy-start.50 = (bf16[96,768]{1,0:T(8,128)(2,1)S(1)}, bf16[96,768]{1,0:T(8,128)(2,1)}, u32[]{:S(2)}) copy-start(bf16[96,768]{1,0:T(8,128)(2,1)} %get-tuple-element.252) | copy-start | bytes 442372
  597.2 16.5 %collective-permute-start.40 = (bf16[96,768]{1,0:T(8,128)(2,1)S(1)}, bf16[96,768]{1,0:T(8,128)(2,1)S(1)}, u32[]{:S(2)}, u32[]{:S(2)}) collective-permute-start(bf16[96,768]{1,0:T(8,128)(2,1)S(1)} %copy-done.51), channel_id=1, source_target_pairs={{0,16},{4,20},{8,24},{12,28},{16,0},{20,4},{24,8},{28,12},{1,17},{... | collective-permute-start | bytes 442376 | tf_op jit(solution)/shard_map/ppermute | solution.py:40
  598.1 15.7 %collective-permute-start.39 = (bf16[96,768]{1,0:T(8,128)(2,1)S(1)}, bf16[96,768]{1,0:T(8,128)(2,1)S(1)}, u32[]{:S(2)}, u32[]{:S(2)}) collective-permute-start(bf16[96,768]{1,0:T(8,128)(2,1)S(1)} %copy-done.50), channel_id=1, source_target_pairs={{0,8},{4,12},{8,0},{12,4},{16,24},{20,28},{24,16},{28,20},{1,9},{5... | collective-permute-start | bytes 442376 | tf_op jit(solution)/shard_map/ppermute | solution.py:40
  602.1 13.4 %collective-permute-start.35 = (bf16[96,768]{1,0:T(8,128)(2,1)S(1)}, bf16[96,768]{1,0:T(8,128)(2,1)S(1)}, u32[]{:S(2)}, u32[]{:S(2)}) collective-permute-start(bf16[96,768]{1,0:T(8,128)(2,1)S(1)} %get-tuple-element.259), channel_id=1, source_target_pairs={{0,24},{4,28},{8,16},{12,20},{16,8},{20,12},{24,0},{28,4},{1,25},{... | collective-permute-start | bytes 442376 | tf_op jit(solution)/shard_map/ppermute | solution.py:40
  605.5 13.9 %collective-permute-start.34 = (bf16[96,768]{1,0:T(8,128)(2,1)S(1)}, bf16[96,768]{1,0:T(8,128)(2,1)S(1)}, u32[]{:S(2)}, u32[]{:S(2)}) collective-permute-start(bf16[96,768]{1,0:T(8,128)(2,1)S(1)} %get-tuple-element.260), channel_id=1, source_target_pairs={{0,16},{4,20},{8,24},{12,28},{16,0},{20,4},{24,8},{28,12},{1,17},{... | collective-permute-start | bytes 442376 | tf_op jit(solution)/shard_map/ppermute | solution.py:40
  605.5 13.9 %collective-permute-start.33 = (bf16[96,768]{1,0:T(8,128)(2,1)S(1)}, bf16[96,768]{1,0:T(8,128)(2,1)S(1)}, u32[]{:S(2)}, u32[]{:S(2)}) collective-permute-start(bf16[96,768]{1,0:T(8,128)(2,1)S(1)} %get-tuple-element.258), channel_id=1, source_target_pairs={{0,8},{4,12},{8,0},{12,4},{16,24},{20,28},{24,16},{28,20},{1,9},{5... | collective-permute-start | bytes 442376 | tf_op jit(solution)/shard_map/ppermute | solution.py:40
  (67 other events, 369.1 us)
Sparse Core Ops, SparseCore 0:
  12.2 69.7 all-gather.1
  151.4 13.4 sort.11.cloned.1.call-done
  (1 shorter events, 0.0 us)

commit v5 on v4

--- a/solution.py
+++ b/solution.py
@@ -65,16 +65,23 @@
     return kept + xor_wide(sent, 1).astype(F32)
 
 
+def line_pieces(half):
+    if lax.axis_size("wide") != 8:
+        return [lax.psum_scatter(half, "wide", scatter_dimension=0)]
+    depth = lax.axis_index("wide") >> 1
+    low = half.astype(BF)
+    return [lax.dynamic_index_in_dim(half, depth, 0, keepdims=False)] + [
+        xor_wide(lax.dynamic_index_in_dim(low, depth ^ k, 0, keepdims=False), 2 * k)
+        for k in (1, 2, 3)
+    ]
+
+
+def total_of(pieces):
+    return sum(piece.astype(F32) for piece in pieces)
+
+
 def scatter_line(half):
-    if lax.axis_size("wide") != 8:
-        return lax.psum_scatter(half, "wide", scatter_dimension=0)
-    depth = lax.axis_index("wide") >> 1
-    total = lax.dynamic_index_in_dim(half, depth, 0, keepdims=False)
-    low = half.astype(BF)
-    for k in (1, 2, 3):
-        piece = lax.dynamic_index_in_dim(low, depth ^ k, 0, keepdims=False)
-        total = total + xor_wide(piece, 2 * k).astype(F32)
-    return total
+    return total_of(line_pieces(half))
 
 
 def scatter_core(sent, own):
@@ -989,12 +996,16 @@
     d_start_corner = xor_narrow(d_start_across, 1)
     a_from, b_half, c_half, d_start_corner = together(a_from, b_half, c_half, d_start_corner)
     a_half = scatter_pair((a_near + a_from.astype(F32)).reshape(wide, share, width))
-    d_b, d_c, d_a = scatter_line(b_half), scatter_line(c_half), scatter_line(a_half)
+    d_b, d_c = scatter_line(b_half), scatter_line(c_half)
+    a_pieces = line_pieces(a_half)
     d_far = (d_start_across, d_start_corner)
     d_embed = collect(sort_keys[2:], hits[2:], d_far, shift, d_embed, entries)
     d_embed, *d_table = together(d_embed, *d_table)
     d_table = jnp.concatenate(d_table, axis=2).astype(F32).transpose(1, 0, 2)
     d_table = d_table.reshape(share, chunk * wide)[:, :entries]
+    square = jnp.sum(d_embed * d_embed) + jnp.sum(d_table * d_table)
+    square, *a_pieces = together(square, *a_pieces)
+    d_a = total_of(a_pieces)
 
     small, small_far = [
         sum(
@@ -1020,8 +1031,7 @@
         d_vectors,
     )
 
-    square = jnp.zeros((), F32)
-    for grad in shards[:6]:
+    for grad in shards[2:6]:
         square = square + jnp.sum(grad * grad)
     shared_square = jnp.sum(shards[6] * shards[6]) + jnp.sum(shards[7] * shards[7])
     square = square + shared_square / narrow

time: 693 us -> 692 us (level)
  transfers between devices with their start and end apart: 50 -> 50, of which waited for: 20 -> 20; matrix products, arithmetic and copies ran while one was open for 21% -> 22% of each run, Pallas kernels for 25% -> 25%
where the time goes in v5:
time: 692 us; the launch traced here: 684 us
  Pallas kernels  173 us (25%)
  waiting for transfers between devices  160 us (23%)
  other arithmetic  115 us (17%)
  starting transfers between devices  72.1 us (10%)
  local copies, waits for them, and re-layouts  61.5 us (9%)
  matrix products  57.1 us (8%)
  between operations  23.9 us (3%)
  blocking collectives  21.7 us (3%)
    ppermute x27, waiting for transfers between devices, xor_narrow(): lax.ppermute(value, NARROW, [(i, i ^ bits) for i in range(lax.axis_size(N...  70.2 us
    dot_general x12, matrix products, mm(): return lax.dot_general(a, b, dims, preferred_element_type=F32)  52.7 us
    ppermute x15, waiting for transfers between devices, xor_wide(): lax.ppermute(value, 'wide', [(i, i ^ bits) for i in range(lax.axis_size('...  52.4 us
    all_to_all x7, waiting for transfers between devices, swap_wide(): return lax.all_to_all(value, 'wide', 0, 0, tiled=True)  37.2 us
    pallas_call x2, Pallas kernels, collect(): pl.pallas_call(functools.partial(collect_kernel, shift, first), in_specs=...  35.4 us
    all_to_all x7, starting transfers between devices, swap_wide(): return lax.all_to_all(value, 'wide', 0, 0, tiled=True)  34.8 us
    pallas_call x1, Pallas kernels, attend_back(): pl.pallas_call(attend_back_kernel, grid=(slots,), in_specs=[one, two, oth...  25.2 us
    pallas_call x1, Pallas kernels, feed_back(): pl.pallas_call(feed_back_kernel, out_shape=[jax.ShapeDtypeStruct((rows, w...  25.1 us
  transfers between devices with their start and end apart: 50, of which 20 were waited for; matrix products, arithmetic and copies ran while one was open for 22% of the time, Pallas kernels for 25%

profile of v5, /device:TPU:0, one launch (start us, length us, event | category | flops | bytes accessed | tf_op | source)
XLA Modules:
  0.0 684.0 jit_solution(10808784963752722630)
XLA Ops:
  12.2 2.7 bitcast_convert_fusion.5
  17.2 6.8 all-to-all-start
  24.1 8.4 %all-to-all-done = s32[8,2,1408]{2,1,0:T(2,128)S(1)} async-done(((s32[8,2,1408]{2,1,0:T(2,128)}), s32[8,2,1408]{2,1,0:T(2,128)S(1)}, u32[]{:S(2)}, u32[]{:S(2)}) %all-to-all-start) | async-done | bytes 90144 | tf_op jit(solution)/shard_map/all_to_all | solution.py:44
  36.7 15.0 %table_rows.1.table_ref = f32[26752,96]{1,0:T(8,128)} custom-call(f32[96,12672]{1,0:T(8,128)} %bitcast.248, bf16[96,12672]{1,0:T(8,128)(2,1)} %collective-permute-done.other_ref), custom_call_target="tpu_custom_call" | custom-call | flops 10000000000 | bytes 40000000 | tf_op jit(solution)/shard_map/table_rows/pallas_call | solution.py:561
  51.6 15.0 %lookup.1 = bf16[8192,96]{1,0:T(8,128)(2,1)} custom-call(s32[4,1,2048]{2,1,0:T(1,128)} %and_select_fusion.id_ref, f32[26752,96]{1,0:T(8,128)} %table_rows.1.table_ref), custom_call_target="tpu_custom_call" | custom-call | tf_op jit(solution)/shard_map/lookup/pallas_call | solution.py:593
  71.4 16.2 %collective-permute-done.1 = bf16[8,512,96]{1,2,0:T(8,128)(2,1)} collective-permute-done((bf16[8,512,96]{1,2,0:T(8,128)(2,1)S(1)}, bf16[8,512,96]{1,2,0:T(8,128)(2,1)}, u32[]{:S(2)}, u32[]{:S(2)}) %collective-permute-start.1) | collective-permute-done | bytes 786464 | tf_op jit(solution)/shard_map/ppermute | solution.py:34
  91.3 3.6 all-to-all-start.1
  96.4 2.6 convert_element_type.290
  101.1 17.0 %all-to-all-done.1 = bf16[8,560,96]{1,2,0:T(8,128)(2,1)S(1)} async-done(((bf16[8,560,96]{1,2,0:T(8,128)(2,1)}), bf16[8,560,96]{1,2,0:T(8,128)(2,1)S(1)}, u32[]{:S(2)}, u32[]{:S(2)}) %all-to-all-start.1) | async-done | bytes 860192 | tf_op jit(solution)/shard_map/all_to_all | solution.py:44
  118.1 3.8 copy.210
  122.0 4.4 all-to-all-start.2
  129.7 3.2 slice.301.bc0
  142.0 8.0 %qkv.1 = (bf16[4,512,192]{2,1,0:T(8,128)(2,1)}, bf16[4,512,384]{2,1,0:T(8,128)(2,1)}, bf16[512,768]{1,0:T(8,128)(2,1)}, f32[512,768]{1,0:T(8,128)}) custom-call(bf16[8,560,96]{2,1,0:T(8,128)(2,1)} %copy.209.recv_ref, f32[12,768]{1,0:T(8,128)} %pad_maximum_fusion.7.par_ref, bf16[768,768]{1,0:T(8,128)(2,1)} %copy-done.2, bf16[768,768]{1,0:T(8,128)(2,1)} %copy-done.4, ...), custom_call_target="tpu_custom_call" | custom-call | tf_op jit(solution)/shard_map/qkv/pallas_call | solution.py:212
  154.9 14.7 %attend.1 = (bf16[4,512,192]{2,1,0:T(8,128)(2,1)}, f32[4,3,512]{2,1,0:T(4,128)}) custom-call(bf16[4,512,192]{2,1,0:T(8,128)(2,1)} %get-tuple-element.125.q_ref, bf16[4,512,384]{2,1,0:T(8,128)(2,1)} %get-tuple-element.126.own_ref, bf16[4,512,384]{2,1,0:T(8,128)(2,1)} %copy-done.10), custom_call_target="tpu_custom_call" | custom-call | tf_op jit(solution)/shard_map/attend/pallas_call | solution.py:259
  169.7 17.0 %collective-permute-done.6.bc2 = bf16[2,768,768]{2,1,0:T(8,128)(2,1)} collective-permute-done((bf16[2,768,768]{2,1,0:T(8,128)(2,1)}, bf16[2,768,768]{2,1,0:T(8,128)(2,1)}, u32[]{:S(2)}, u32[]{:S(2)}) %collective-permute-start.6) | collective-permute-done | bytes 2359328 | tf_op jit(solution)/shard_map/ppermute | solution.py:34
  192.9 15.7 %feed.1 = (f32[512,768]{1,0:T(8,128)}, f32[512,768]{1,0:T(8,128)}, f32[512,768]{1,0:T(8,128)}, bf16[512,768]{1,0:T(8,128)(2,1)}, f32[4,512,768]{2,1,0:T(8,128)}, /*index=5*/bf16[320,768]{1,0:T(8,128)(2,1)}) custom-call(bf16[4,512,192]{2,1,0:T(8,128)(2,1)} %get-tuple-element.131.mixed_ref, f32[512,768]{1,0:T(8,128)} %get-tuple-element.132.start_ref, ...), custom_call_target="tpu_custom_call" | custom-call | tf_op jit(solution)/shard_map/feed/pallas_call | solution.py:307
  212.1 2.8 collective-permute-start.10
  215.0 6.3 collective-permute-done.10
  222.3 6.2 all-to-all-start.3
  228.7 16.2 %collective-permute-done.12 = bf16[768,1664]{1,0:T(8,128)(2,1)} collective-permute-done((bf16[768,1664]{1,0:T(8,128)(2,1)}, bf16[768,1664]{1,0:T(8,128)(2,1)}, u32[]{:S(2)}, u32[]{:S(2)}) %collective-permute-start.12) | collective-permute-done | bytes 2555936 | tf_op jit(solution)/shard_map/ppermute | solution.py:34
  245.5 7.5 %all-to-all-done.3 = bf16[8,80,768]{2,1,0:T(8,128)(2,1)S(1)} async-done(((bf16[8,80,768]{2,1,0:T(8,128)(2,1)}), bf16[8,80,768]{2,1,0:T(8,128)(2,1)S(1)}, u32[]{:S(2)}, u32[]{:S(2)}) %all-to-all-start.3) | async-done | bytes 983072 | tf_op jit(solution)/shard_map/all_to_all | solution.py:44
  253.0 4.1 select_reduce_fusion.4
  257.2 3.8 select_reduce_fusion.2
  260.9 3.8 select_reduce_fusion.3
  264.7 3.8 select_reduce_fusion.1
  268.5 6.0 exponential_reduce_fusion
  274.6 10.6 %all_to_all.45 = f32[8,3,640]{2,1,0:T(4,128)S(1)} all-to-all(f32[8,3,640]{2,1,0:T(4,128)S(1)} %broadcast_in_dim.206), channel_id=1, replica_groups=mesh['wide'=8,'line'=2,'core'=2] {'wide'}, dimensions={0} | all-to-all | bytes 122880 | tf_op jit(solution)/shard_map/all_to_all | solution.py:44
  285.9 4.4 fusion.8
  290.3 5.2 fusion.92
  295.6 3.7 fusion.94
  299.3 3.7 fusion.93
  303.0 5.6 add_convert_fusion.2
  308.6 3.8 all-to-all-start.5
  312.4 6.6 fusion.95
  319.1 3.8 fusion.96
  322.9 4.5 fusion.97
  327.4 4.1 fusion.73
  331.5 4.3 all-to-all-done.5
  336.0 8.4 %collective-permute-done.14 = bf16[80,768]{1,0:T(8,128)(2,1)S(1)} collective-permute-done((bf16[80,768]{1,0:T(8,128)(2,1)S(1)}, bf16[80,768]{1,0:T(8,128)(2,1)S(1)}, u32[]{:S(2)}, u32[]{:S(2)}) %collective-permute-start.14) | collective-permute-done | bytes 122912 | tf_op jit(solution)/shard_map/ppermute | solution.py:40
  346.8 3.7 add_convert_fusion.1
  352.0 25.1 %feed_back.1 = (f32[512,768]{1,0:T(8,128)}, bf16[512,768]{1,0:T(8,128)(2,1)}, bf16[4,512,192]{2,1,0:T(8,128)(2,1)}, bf16[2,768,768]{2,1,0:T(8,128)(2,1)}, bf16[2...) custom-call(bf16[320,768]{1,0:T(8,128)(2,1)} %pad_maximum_fusion.3.rows, ...), custom_call_target="tpu_custom_call" | custom-call | flops 10000000000 | bytes 40000000 | tf_op jit(solution)/shard_map/feed_back/pallas_call | solution.py:383
  377.1 25.2 %attend_back.1 = (bf16[4,512,192]{2,1,0:T(8,128)(2,1)}, f32[4,512,384]{2,1,0:T(8,128)}, bf16[4,512,384]{2,1,0:T(8,128)(2,1)}) custom-call(bf16[4,512,192]{2,1,0:T(8,128)(2,1)} %get-tuple-element.125.q_ref, bf16[4,512,384]{2,1,0:T(8,128)(2,1)} %get-tuple-element.126.own_ref, bf16[4,512,384]{2,1,0:T(8,128)(2,1)} %copy-done.10, ...), custom_call_target="tpu_custom_call" | custom-call | tf_op jit(solution)/shard_map/attend_back/pallas_call | solution.py:440
  402.8 5.4 collective-permute-done.17
  410.8 3.8 convert_element_type.314
  424.3 11.8 %collective-permute-done.22 = bf16[4,96,768]{2,1,0:T(8,128)(2,1)} collective-permute-done((bf16[4,96,768]{2,1,0:T(8,128)(2,1)}, bf16[4,96,768]{2,1,0:T(8,128)(2,1)}, u32[]{:S(2)}, u32[]{:S(2)}) %collective-permute-start.22) | collective-permute-done | bytes 589856 | tf_op jit(solution)/shard_map/ppermute | solution.py:40
  438.6 9.8 %qkv_back.1 = (bf16[8,528,96]{2,1,0:T(8,128)(2,1)}, bf16[4,512,576]{2,1,0:T(8,128)(2,1)}, f32[3,768]{1,0:T(4,128)}) custom-call(bf16[4,512,192]{2,1,0:T(8,128)(2,1)} %get-tuple-element.158.dq_ref, f32[4,512,384]{2,1,0:T(8,128)} %get-tuple-element.159.d_own_ref, bf16[4,512,384]{2,1,0:T(8,128)(2,1)} %copy-done.27, bf16[768,768]{1,0:T(8,128)(2,1)} %copy-done.2, ...), custom_call_target="tpu_custom_call" | custom-call | tf_op jit(solution)/shard_map/qkv_back/pallas_call | solution.py:499
  450.4 7.4 %qkv_grads.1 = (bf16[2,768,768]{2,1,0:T(8,128)(2,1)}, bf16[2,768,768]{2,1,0:T(8,128)(2,1)}) custom-call(bf16[4,512,576]{2,1,0:T(8,128)(2,1)} %get-tuple-element.172.grads_ref, bf16[512,768]{1,0:T(8,128)(2,1)} %get-tuple-element.173.hidden_ref, bf16[512,768]{1,0:T(8,128)(2,1)} %get-tuple-element.174.d_attended_ref, ...), custom_call_target="tpu_custom_call" | custom-call | flops 10000000000 | bytes 40000000 | tf_op jit(solution)/shard_map/qkv_grads/pallas_call | solution.py:535
  460.7 6.2 add_convert_fusion
  468.7 6.6 collective-permute-done.26
  477.8 4.3 all-to-all-start.6
  490.4 17.6 %collective-permute-done.28 = bf16[4,96,768]{2,1,0:T(8,128)(2,1)S(1)} collective-permute-done((bf16[4,96,768]{2,1,0:T(8,128)(2,1)S(1)}, bf16[4,96,768]{2,1,0:T(8,128)(2,1)S(1)}, u32[]{:S(2)}, u32[]{:S(2)}) %collective-permute-start.28) | collective-permute-done | bytes 589856 | tf_op jit(solution)/shard_map/ppermute | solution.py:40
  509.3 4.1 collective-permute-done.25
  517.0 5.7 all-to-all-start.7
  525.7 12.3 %collect.2.refs_0_ = f32[12672,96]{1,0:T(8,128)} custom-call(s32[2,4480]{1,0:T(2,128)} %get-tuple-element.281.key_ref, s32[2]{0:T(128)} %get-tuple-element.309.count_ref, bf16[4480,96]{1,0:T(8,128)(2,1)} %bitcast.252, bf16[4480,96]{1,0:T(8,128)(2,1)} %copy.223.two_ref), custom_call_target="tpu_custom_call" | custom-call | tf_op jit(solution)/shard_map/collect/pallas_call | solution.py:666
  550.5 2.6 fusion.18
  556.6 3.3 collective-permute-start.38
  561.8 3.3 collective-permute-start.41
  568.2 2.9 multiply_reduce_fusion.1
  573.8 23.1 %collect.3 = f32[96,12672]{1,0:T(8,128)} custom-call(s32[2,4480]{1,0:T(2,128)} %get-tuple-element.282.key_ref, s32[2]{0:T(128)} %get-tuple-element.310.count_ref, bf16[4480,96]{1,0:T(8,128)(2,1)} %copy.224.one_ref, bf16[4480,96]{1,0:T(8,128)(2,1)} %copy.225.two_ref, f32[12672,96]{1,0:T(8,128)} %collect.2.refs_0_), custom_call_target="tpu_custom_call" | custom-call | tf_op jit(solution)/shard_map/collect/pallas_call | solution.py:666
  602.1 4.7 collective-permute-done.40
  615.9 4.2 multiply_reduce_fusion
  633.6 11.1 %all_to_all.46 = f32[32,1,2]{2,1,0:T(1,128)S(1)} all-to-all(f32[32,1,2]{2,1,0:T(1,128)S(1)} %broadcast_in_dim.207), channel_id=1, replica_groups=mesh['wide'=8,'line'=2,'core'=2] {'wide','line','core'}, dimensions={0} | all-to-all | bytes 512 | tf_op jit(solution)/shard_map/all_to_all | solution.py:1038
  646.0 13.1 %fusion.31 = (f32[12672,96]{0,1:T(8,128)}, f32[12672,96]{0,1:T(8,128)}, f32[12672,96]{0,1:T(8,128)}) fusion(f32[96,12672]{1,0:T(8,128)} %collect.3, f32[]{:T(128)S(6)} %div.124, f32[12672,96]{0,1:T(8,128)} %param.46, f32[12672,96]{0,1:T(8,128)} %param.38, f32[12672,96]{0,1:T(8,128)} %param.30), kind=kLoop, calls=%fused_computation.82 | loop fusion | flops 18247680 | bytes 34062340 | tf_op jit(solution)/shard_map/transpose | solution.py:1051
  659.2 10.4 %multiply_subtract_fusion = (f32[96,12672]{1,0:T(8,128)}, f32[96,12672]{1,0:T(8,128)}, f32[96,12672]{1,0:T(8,128)}) fusion(f32[96,12672]{1,0:T(8,128)} %param.31, f32[]{:T(128)S(6)} %div.124, bf16[96,13312]{1,0:T(8,128)(2,1)S(1)} %bitcast.247, f32[96,12672]{1,0:T(8,128)} %param.39, f32[96,12672]{1,0:T(8,128)} %param.47), kind=kLoop, calls=%fused_computation.18 | loop fusion | flops 20680704 | bytes 31629316 | tf_op jit(solution)/shard_map/sub | solution.py:1060
  (430 shorter events, 149.2 us)
Async XLA Ops:
  7.2 82.8 %all-gather.2.cloned.1.call-start = ((), (), s32[]{:S(2)}) async-start(), calls=%async_computation.9 | async-start | bytes 3981312 | tf_op jit(solution)/shard_map/all_gather | solution.py:54
  12.2 23.5 %copy-start.24 = (f32[128,768]{1,0:T(8,128)S(1)}, f32[128,768]{1,0:T(8,128)}, u32[]{:S(2)}) copy-start(f32[128,768]{1,0:T(8,128)} %param.36) | copy-start | bytes 1179652
  14.9 21.8 %collective-permute-start = (bf16[96,12672]{1,0:T(8,128)(2,1)S(1)}, bf16[96,12672]{1,0:T(8,128)(2,1)}, u32[]{:S(2)}, u32[]{:S(2)}) collective-permute-start(bf16[96,12672]{1,0:T(8,128)(2,1)S(1)} %bitcast_convert_fusion.5), channel_id=1, source_target_pairs={{0,1},{1,0},{2,3},{3,2},{4,5},{5,4},{6,7},{7,6},{8,9},{9,8},{10,11... | collective-permute-start | bytes 7299080 | tf_op jit(solution)/shard_map/ppermute | solution.py:34
  17.2 15.4 %all-to-all-start = ((s32[8,2,1408]{2,1,0:T(2,128)}), s32[8,2,1408]{2,1,0:T(2,128)S(1)}, u32[]{:S(2)}, u32[]{:S(2)}) async-start(s32[8,2,1408]{2,1,0:T(2,128)} %broadcast_in_dim.187), calls=%async_computation | async-start | bytes 180224 | tf_op jit(solution)/shard_map/all_to_all | solution.py:44
  32.5 19.1 %copy-start.42 = (s32[8,2,1408]{2,1,0:T(2,128)}, s32[8,2,1408]{2,1,0:T(2,128)S(1)}, u32[]{:S(2)}) copy-start(s32[8,2,1408]{2,1,0:T(2,128)S(1)} %all-to-all-done) | copy-start | bytes 270340
  35.7 16.0 %copy-start.59 = (f32[8,1,128]{2,1,0:T(1,128)}, f32[8,1,128]{2,1,0:T(1,128)S(1)}, u32[]{:S(2)}) copy-start(f32[8,1,128]{2,1,0:T(1,128)S(1)} %get-tuple-element.296) | copy-start | bytes 12292
  68.9 18.7 %collective-permute-start.1 = (bf16[8,512,96]{1,2,0:T(8,128)(2,1)S(1)}, bf16[8,512,96]{1,2,0:T(8,128)(2,1)}, u32[]{:S(2)}, u32[]{:S(2)}) collective-permute-start(bf16[8,512,96]{1,2,0:T(8,128)(2,1)S(1)} %copy.200), channel_id=1, source_target_pairs={{0,2},{1,3},{2,0},{3,1},{4,6},{5,7},{6,4},{7,5},{8,10},{9,11},{10,... | collective-permute-start | bytes 2359304 | tf_op jit(solution)/shard_map/ppermute | solution.py:34
  91.3 35.3 %copy-start.2 = (bf16[768,768]{1,0:T(8,128)(2,1)}, bf16[768,768]{1,0:T(8,128)(2,1)S(1)}, u32[]{:S(2)}) copy-start(bf16[768,768]{1,0:T(8,128)(2,1)S(1)} %slice_bitcast_fusion.a0) | copy-start | bytes 3538948
  91.3 26.8 %all-to-all-start.1 = ((bf16[8,560,96]{1,2,0:T(8,128)(2,1)}), bf16[8,560,96]{1,2,0:T(8,128)(2,1)S(1)}, u32[]{:S(2)}, u32[]{:S(2)}) async-start(bf16[8,560,96]{1,2,0:T(8,128)(2,1)} %fusion.32), calls=%async_computation.1 | async-start | bytes 1966080 | tf_op jit(solution)/shard_map/all_to_all | solution.py:44
  94.9 31.8 %collective-permute-start.3 = (bf16[768,768]{1,0:T(8,128)(2,1)S(1)}, bf16[768,768]{1,0:T(8,128)(2,1)S(1)}, u32[]{:S(2)}, u32[]{:S(2)}) collective-permute-start(bf16[768,768]{1,0:T(8,128)(2,1)S(1)} %slice_bitcast_fusion.a0), channel_id=1, source_target_pairs={{0,2},{1,3},{2,0},{3,1},{4,6},{5,7},{6,4},{7,5},{8,10},{9,11},{10,... | collective-permute-start | bytes 3538952 | tf_op jit(solution)/shard_map/ppermute | solution.py:34
  122.0 64.8 %all-to-all-start.2 = ((bf16[8,96,1664]{2,1,0:T(8,128)(2,1)}), bf16[8,96,1664]{2,1,0:T(8,128)(2,1)}, u32[]{:S(2)}, u32[]{:S(2)}) async-start(bf16[8,96,1664]{2,1,0:T(8,128)(2,1)} %copy.210), calls=%async_computation.2 | async-start | bytes 5111808 | tf_op jit(solution)/shard_map/all_to_all | solution.py:44
  126.4 43.3 %sort.9.cloned.1.call-start = ((), (), s32[]{:S(2)}) async-start(), calls=%async_computation.10 | async-start | bytes 215072 | tf_op jit(solution)/shard_map/sort | solution.py:838
  126.6 6.3 collective-permute-start.2
  126.7 6.2 collective-permute-start.4
  133.0 53.7 %collective-permute-start.6 = (bf16[2,768,768]{2,1,0:T(8,128)(2,1)}, bf16[2,768,768]{2,1,0:T(8,128)(2,1)}, u32[]{:S(2)}, u32[]{:S(2)}) collective-permute-start(bf16[2,768,768]{2,1,0:T(8,128)(2,1)} %slice.301.bc0), channel_id=1, source_target_pairs={{0,2},{1,3},{2,0},{3,1},{4,6},{5,7},{6,4},{7,5},{8,10},{9,11},{10,... | collective-permute-start | bytes 7077896 | tf_op jit(solution)/shard_map/ppermute | solution.py:34
  150.0 38.3 %copy-start.68 = (s32[1,2,256]{2,1,0:T(2,128)S(1)}, s32[1,2,256]{2,1,0:T(2,128)}, u32[]{:S(2)}) copy-start(s32[1,2,256]{2,1,0:T(2,128)} %param.28) | copy-start | bytes 6148
  150.0 38.3 %copy-start.72 = (s32[8,2,1]{0,1,2:T(2,128)S(1)}, s32[8,2,1]{0,1,2:T(2,128)}, u32[]{:S(2)}) copy-start(s32[8,2,1]{0,1,2:T(2,128)} %copy-done.71) | copy-start | bytes 196
  150.0 3.7 collective-permute-start.5
  150.1 40.5 %copy-start.65 = (s32[512]{0:T(512)S(1)}, s32[512]{0:T(512)}, u32[]{:S(2)}) copy-start(s32[512]{0:T(512)} %copy-done.64) | copy-start | bytes 6148
  151.3 40.2 %collective-permute-start.7 = (bf16[2,768,768]{2,1,0:T(8,128)(2,1)}, bf16[2,768,768]{2,1,0:T(8,128)(2,1)}, u32[]{:S(2)}, u32[]{:S(2)}) collective-permute-start(bf16[2,768,768]{2,1,0:T(8,128)(2,1)} %slice.301.bc0), channel_id=1, source_target_pairs={{0,1},{1,0},{2,3},{3,2},{4,5},{5,4},{6,7},{7,6},{8,9},{9,8},{10,11... | collective-permute-start | bytes 7077896 | tf_op jit(solution)/shard_map/ppermute | solution.py:34
  186.7 4.8 collective-permute-start.8
  186.7 58.2 %collective-permute-start.12 = (bf16[768,1664]{1,0:T(8,128)(2,1)}, bf16[768,1664]{1,0:T(8,128)(2,1)}, u32[]{:S(2)}, u32[]{:S(2)}) collective-permute-start(bf16[768,1664]{1,0:T(8,128)(2,1)} %bitcast.20), channel_id=1, source_target_pairs={{0,2},{1,3},{2,0},{3,1},{4,6},{5,7},{6,4},{7,5},{8,10},{9,11},{10,... | collective-permute-start | bytes 7667720 | tf_op jit(solution)/shard_map/ppermute | solution.py:34
  208.6 20.1 %slice-start.4 = ((s32[8,2,1408]{2,1,0:T(2,128)}), s32[8,2,256]{2,1,0:T(2,128)S(1)}, s32[]{:S(2)}) async-start(s32[8,2,1408]{2,1,0:T(2,128)} %copy-done.42), calls=%async_computation.16 | async-start | bytes 32768 | tf_op jit(solution)/shard_map/slice | solution.py:724
  209.5 1.6 collective-permute-start.9
  212.1 9.2 %collective-permute-start.10 = (bf16[80,768]{1,0:T(8,128)(2,1)S(1)}, bf16[80,768]{1,0:T(8,128)(2,1)S(1)}, u32[]{:S(2)}, u32[]{:S(2)}) collective-permute-start(bf16[80,768]{1,0:T(8,128)(2,1)S(1)} %slice.305), channel_id=1, source_target_pairs={{0,16},{4,20},{8,24},{12,28},{16,0},{20,4},{24,8},{28,12},{1,17},{... | collective-permute-start | bytes 368648 | tf_op jit(solution)/shard_map/ppermute | solution.py:40
  222.3 30.7 %all-to-all-start.3 = ((bf16[8,80,768]{2,1,0:T(8,128)(2,1)}), bf16[8,80,768]{2,1,0:T(8,128)(2,1)S(1)}, u32[]{:S(2)}, u32[]{:S(2)}) async-start(bf16[8,80,768]{2,1,0:T(8,128)(2,1)} %broadcast_in_dim.197), calls=%async_computation.3 | async-start | bytes 1966080 | tf_op jit(solution)/shard_map/all_to_all | solution.py:44
  228.5 32.4 %collective-permute-start.11 = (bf16[768,1664]{1,0:T(8,128)(2,1)}, bf16[768,1664]{1,0:T(8,128)(2,1)}, u32[]{:S(2)}, u32[]{:S(2)}) collective-permute-start(bf16[768,1664]{1,0:T(8,128)(2,1)} %bitcast.20), channel_id=1, source_target_pairs={{0,1},{1,0},{2,3},{3,2},{4,5},{5,4},{6,7},{7,6},{8,9},{9,8},{10,11... | collective-permute-start | bytes 7667720 | tf_op jit(solution)/shard_map/ppermute | solution.py:34
  244.9 19.8 %collective-permute-start.13 = (bf16[768,1664]{1,0:T(8,128)(2,1)}, bf16[768,1664]{1,0:T(8,128)(2,1)}, u32[]{:S(2)}, u32[]{:S(2)}) collective-permute-start(bf16[768,1664]{1,0:T(8,128)(2,1)} %collective-permute-done.12), channel_id=1, source_target_pairs={{0,1},{1,0},{2,3},{3,2},{4,5},{5,4},{6,7},{7,6},{8,9},{9,8},{10,11... | collective-permute-start | bytes 7667720 | tf_op jit(solution)/shard_map/ppermute | solution.py:34
  268.5 34.5 %copy-start.13 = (f32[640,1664]{1,0:T(8,128)}, f32[640,1664]{1,0:T(8,128)S(1)}, u32[]{:S(2)}) copy-start(f32[640,1664]{1,0:T(8,128)S(1)} %get-tuple-element.312) | copy-start | bytes 12779524
  308.6 27.2 %all-to-all-start.5 = ((bf16[8,80,768]{2,1,0:T(8,128)(2,1)}), bf16[8,80,768]{2,1,0:T(8,128)(2,1)S(1)}, u32[]{:S(2)}, u32[]{:S(2)}) async-start(bf16[8,80,768]{2,1,0:T(8,128)(2,1)} %bitcast.277), calls=%async_computation.5 | async-start | bytes 1966080 | tf_op jit(solution)/shard_map/all_to_all | solution.py:44
  335.8 11.0 %collective-permute-start.16 = (bf16[768,1664]{1,0:T(8,128)(2,1)}, bf16[768,1664]{1,0:T(8,128)(2,1)}, u32[]{:S(2)}, u32[]{:S(2)}) collective-permute-start(bf16[768,1664]{1,0:T(8,128)(2,1)} %fusion.73), channel_id=1, source_target_pairs={{0,1},{1,0},{2,3},{3,2},{4,5},{5,4},{6,7},{7,6},{8,9},{9,8},{10,11... | collective-permute-start | bytes 7667720 | tf_op jit(solution)/shard_map/ppermute | solution.py:34
  336.0 8.4 %collective-permute-start.14 = (bf16[80,768]{1,0:T(8,128)(2,1)S(1)}, bf16[80,768]{1,0:T(8,128)(2,1)S(1)}, u32[]{:S(2)}, u32[]{:S(2)}) collective-permute-start(bf16[80,768]{1,0:T(8,128)(2,1)S(1)} %reduce_sum.252), channel_id=1, source_target_pairs={{0,16},{4,20},{8,24},{12,28},{16,0},{20,4},{24,8},{28,12},{1,17},{... | collective-permute-start | bytes 368648 | tf_op jit(solution)/shard_map/ppermute | solution.py:40
  344.4 1.6 collective-permute-start.15
  350.5 57.7 %collective-permute-start.17 = (bf16[768,1664]{1,0:T(8,128)(2,1)S(1)}, bf16[768,1664]{1,0:T(8,128)(2,1)}, u32[]{:S(2)}, u32[]{:S(2)}) collective-permute-start(bf16[768,1664]{1,0:T(8,128)(2,1)S(1)} %add_convert_fusion.1), channel_id=1, source_target_pairs={{0,2},{1,3},{2,0},{3,1},{4,6},{5,7},{6,4},{7,5},{8,10},{9,11},{10,... | collective-permute-start | bytes 7667720 | tf_op jit(solution)/shard_map/ppermute | solution.py:34
  402.3 6.4 collective-permute-start.19
  402.3 8.5 %collective-permute-start.20 = (bf16[2,768,768]{2,1,0:T(8,128)(2,1)}, bf16[2,768,768]{2,1,0:T(8,128)(2,1)}, u32[]{:S(2)}, u32[]{:S(2)}) collective-permute-start(bf16[2,768,768]{2,1,0:T(8,128)(2,1)} %get-tuple-element.164), channel_id=1, source_target_pairs={{0,1},{1,0},{2,3},{3,2},{4,5},{5,4},{6,7},{7,6},{8,9},{9,8},{10,11... | collective-permute-start | bytes 7077896 | tf_op jit(solution)/shard_map/ppermute | solution.py:34
  408.2 8.9 %collective-permute-start.18 = (bf16[4,512,384]{2,1,0:T(8,128)(2,1)}, bf16[4,512,384]{2,1,0:T(8,128)(2,1)S(1)}, u32[]{:S(2)}, u32[]{:S(2)}) collective-permute-start(bf16[4,512,384]{2,1,0:T(8,128)(2,1)} %get-tuple-element.160), channel_id=1, source_target_pairs={{0,1},{1,0},{2,3},{3,2},{4,5},{5,4},{6,7},{7,6},{8,9},{9,8},{10,11... | collective-permute-start | bytes 4718600 | tf_op jit(solution)/shard_map/ppermute | solution.py:34
  408.2 52.5 %collective-permute-start.27 = (bf16[768,1664]{1,0:T(8,128)(2,1)}, bf16[768,1664]{1,0:T(8,128)(2,1)}, u32[]{:S(2)}, u32[]{:S(2)}) collective-permute-start(bf16[768,1664]{1,0:T(8,128)(2,1)} %fusion.96), channel_id=1, source_target_pairs={{0,1},{1,0},{2,3},{3,2},{4,5},{5,4},{6,7},{7,6},{8,9},{9,8},{10,11... | collective-permute-start | bytes 7667720 | tf_op jit(solution)/shard_map/ppermute | solution.py:34
  417.1 33.3 %collective-permute-start.21 = (bf16[768,768]{1,0:T(8,128)(2,1)}, bf16[768,768]{1,0:T(8,128)(2,1)S(1)}, u32[]{:S(2)}, u32[]{:S(2)}) collective-permute-start(bf16[768,768]{1,0:T(8,128)(2,1)} %fusion.28), channel_id=1, source_target_pairs={{0,2},{1,3},{2,0},{3,1},{4,6},{5,7},{6,4},{7,5},{8,10},{9,11},{10,... | collective-permute-start | bytes 3538952 | tf_op jit(solution)/shard_map/ppermute | solution.py:34
  419.5 16.5 %collective-permute-start.22 = (bf16[4,96,768]{2,1,0:T(8,128)(2,1)}, bf16[4,96,768]{2,1,0:T(8,128)(2,1)}, u32[]{:S(2)}, u32[]{:S(2)}) collective-permute-start(bf16[4,96,768]{2,1,0:T(8,128)(2,1)} %fusion.33), channel_id=1, source_target_pairs={{0,4},{4,0},{8,12},{12,8},{16,20},{20,16},{24,28},{28,24},{1,5},{5... | collective-permute-start | bytes 1769480 | tf_op jit(solution)/shard_map/ppermute | solution.py:40
  421.6 26.8 %collective-permute-start.23 = (bf16[4,96,768]{2,1,0:T(8,128)(2,1)}, bf16[4,96,768]{2,1,0:T(8,128)(2,1)}, u32[]{:S(2)}, u32[]{:S(2)}) collective-permute-start(bf16[4,96,768]{2,1,0:T(8,128)(2,1)} %fusion.34), channel_id=1, source_target_pairs={{0,4},{4,0},{8,12},{12,8},{16,20},{20,16},{24,28},{28,24},{1,5},{5... | collective-permute-start | bytes 1769480 | tf_op jit(solution)/shard_map/ppermute | solution.py:40
  457.8 24.2 %collective-permute-start.24 = (bf16[2,768,768]{2,1,0:T(8,128)(2,1)}, bf16[2,768,768]{2,1,0:T(8,128)(2,1)}, u32[]{:S(2)}, u32[]{:S(2)}) collective-permute-start(bf16[2,768,768]{2,1,0:T(8,128)(2,1)} %get-tuple-element.176), channel_id=1, source_target_pairs={{0,1},{1,0},{2,3},{3,2},{4,5},{5,4},{6,7},{7,6},{8,9},{9,8},{10,11... | collective-permute-start | bytes 7077896 | tf_op jit(solution)/shard_map/ppermute | solution.py:34
  459.5 15.8 %collective-permute-start.26 = (bf16[4,96,768]{2,1,0:T(8,128)(2,1)S(1)}, bf16[4,96,768]{2,1,0:T(8,128)(2,1)S(1)}, u32[]{:S(2)}, u32[]{:S(2)}) collective-permute-start(bf16[4,96,768]{2,1,0:T(8,128)(2,1)S(1)} %copy-done.36), channel_id=1, source_target_pairs={{0,2},{1,3},{2,0},{3,1},{4,6},{5,7},{6,4},{7,5},{8,10},{9,11},{10,... | collective-permute-start | bytes 1769480 | tf_op jit(solution)/shard_map/ppermute | solution.py:34
  477.8 31.5 %all-to-all-start.6 = ((bf16[8,560,96]{1,2,0:T(8,128)(2,1)}), bf16[8,560,96]{1,2,0:T(8,128)(2,1)S(1)}, u32[]{:S(2)}, u32[]{:S(2)}) async-start(bf16[8,560,96]{1,2,0:T(8,128)(2,1)} %copy.218), calls=%async_computation.6 | async-start | bytes 1966080 | tf_op jit(solution)/shard_map/all_to_all | solution.py:44
  485.7 22.4 %copy-start.12 = (f32[4,96,768]{2,1,0:T(8,128)S(1)}, f32[4,96,768]{2,1,0:T(8,128)}, u32[]{:S(2)}) copy-start(f32[4,96,768]{2,1,0:T(8,128)} %bitcast_add_fusion.4) | copy-start | bytes 3538948
  485.7 22.4 %copy-start.38 = (bf16[4,96,768]{2,1,0:T(8,128)(2,1)S(1)}, bf16[4,96,768]{2,1,0:T(8,128)(2,1)}, u32[]{:S(2)}) copy-start(bf16[4,96,768]{2,1,0:T(8,128)(2,1)} %copy-done.37) | copy-start | bytes 1769476
  485.7 27.6 %collective-permute-start.25 = (bf16[768,768]{1,0:T(8,128)(2,1)}, bf16[768,768]{1,0:T(8,128)(2,1)}, u32[]{:S(2)}, u32[]{:S(2)}) collective-permute-start(bf16[768,768]{1,0:T(8,128)(2,1)} %fusion.30), channel_id=1, source_target_pairs={{0,2},{1,3},{2,0},{3,1},{4,6},{5,7},{6,4},{7,5},{8,10},{9,11},{10,... | collective-permute-start | bytes 3538952 | tf_op jit(solution)/shard_map/ppermute | solution.py:34
  487.8 20.2 %collective-permute-start.28 = (bf16[4,96,768]{2,1,0:T(8,128)(2,1)S(1)}, bf16[4,96,768]{2,1,0:T(8,128)(2,1)S(1)}, u32[]{:S(2)}, u32[]{:S(2)}) collective-permute-start(bf16[4,96,768]{2,1,0:T(8,128)(2,1)S(1)} %fusion.35), channel_id=1, source_target_pairs={{0,4},{4,0},{8,12},{12,8},{16,20},{20,16},{24,28},{28,24},{1,5},{5... | collective-permute-start | bytes 1769480 | tf_op jit(solution)/shard_map/ppermute | solution.py:40
  515.8 22.1 %collective-permute-start.29 = (bf16[4480,96]{0,1:T(8,128)(2,1)}, bf16[4480,96]{0,1:T(8,128)(2,1)}, u32[]{:S(2)}, u32[]{:S(2)}) collective-permute-start(bf16[4480,96]{0,1:T(8,128)(2,1)} %copy.221), channel_id=1, source_target_pairs={{0,2},{1,3},{2,0},{3,1},{4,6},{5,7},{6,4},{7,5},{8,10},{9,11},{10,... | collective-permute-start | bytes 2580488 | tf_op jit(solution)/shard_map/ppermute | solution.py:34
  517.0 6.4 collective-permute-start.30
  517.0 98.9 %all-to-all-start.7 = ((bf16[8,96,1664]{2,1,0:T(8,128)(2,1)}), bf16[8,96,1664]{2,1,0:T(8,128)(2,1)}, u32[]{:S(2)}, u32[]{:S(2)}) async-start(bf16[8,96,1664]{2,1,0:T(8,128)(2,1)} %bitcast.253), calls=%async_computation.7 | async-start | bytes 5111808 | tf_op jit(solution)/shard_map/all_to_all | solution.py:44
  538.0 10.2 %collective-permute-start.31 = (bf16[4480,96]{0,1:T(8,128)(2,1)}, bf16[4480,96]{0,1:T(8,128)(2,1)}, u32[]{:S(2)}, u32[]{:S(2)}) collective-permute-start(bf16[4480,96]{0,1:T(8,128)(2,1)} %collective-permute-done.29), channel_id=1, source_target_pairs={{0,1},{1,0},{2,3},{3,2},{4,5},{5,4},{6,7},{7,6},{8,9},{9,8},{10,11... | collective-permute-start | bytes 2580488 | tf_op jit(solution)/shard_map/ppermute | solution.py:34
  554.0 55.5 %collective-permute-start.32 = (bf16[4,96,768]{2,1,0:T(8,128)(2,1)}, bf16[4,96,768]{2,1,0:T(8,128)(2,1)}, u32[]{:S(2)}, u32[]{:S(2)}) collective-permute-start(bf16[4,96,768]{2,1,0:T(8,128)(2,1)} %fusion.36), channel_id=1, source_target_pairs={{0,4},{4,0},{8,12},{12,8},{16,20},{20,16},{24,28},{28,24},{1,5},{5... | collective-permute-start | bytes 1769480 | tf_op jit(solution)/shard_map/ppermute | solution.py:40
  556.6 40.3 %collective-permute-start.38 = (bf16[96,768]{1,0:T(8,128)(2,1)}, bf16[96,768]{1,0:T(8,128)(2,1)}, u32[]{:S(2)}, u32[]{:S(2)}) collective-permute-start(bf16[96,768]{1,0:T(8,128)(2,1)} %get-tuple-element.266), channel_id=1, source_target_pairs={{0,24},{4,28},{8,16},{12,20},{16,8},{20,12},{24,0},{28,4},{1,25},{... | collective-permute-start | bytes 442376 | tf_op jit(solution)/shard_map/ppermute | solution.py:40
  559.9 39.8 %collective-permute-start.37 = (bf16[96,768]{1,0:T(8,128)(2,1)}, bf16[96,768]{1,0:T(8,128)(2,1)}, u32[]{:S(2)}, u32[]{:S(2)}) collective-permute-start(bf16[96,768]{1,0:T(8,128)(2,1)} %get-tuple-element.267), channel_id=1, source_target_pairs={{0,16},{4,20},{8,24},{12,28},{16,0},{20,4},{24,8},{28,12},{1,17},{... | collective-permute-start | bytes 442376 | tf_op jit(solution)/shard_map/ppermute | solution.py:40
  559.9 39.8 %collective-permute-start.36 = (bf16[96,768]{1,0:T(8,128)(2,1)}, bf16[96,768]{1,0:T(8,128)(2,1)}, u32[]{:S(2)}, u32[]{:S(2)}) collective-permute-start(bf16[96,768]{1,0:T(8,128)(2,1)} %get-tuple-element.265), channel_id=1, source_target_pairs={{0,8},{4,12},{8,0},{12,4},{16,24},{20,28},{24,16},{28,20},{1,9},{5... | collective-permute-start | bytes 442376 | tf_op jit(solution)/shard_map/ppermute | solution.py:40
  561.8 40.3 %collective-permute-start.41 = (bf16[96,768]{1,0:T(8,128)(2,1)}, bf16[96,768]{1,0:T(8,128)(2,1)}, u32[]{:S(2)}, u32[]{:S(2)}) collective-permute-start(bf16[96,768]{1,0:T(8,128)(2,1)} %get-tuple-element.263), channel_id=1, source_target_pairs={{0,24},{4,28},{8,16},{12,20},{16,8},{20,12},{24,0},{28,4},{1,25},{... | collective-permute-start | bytes 442376 | tf_op jit(solution)/shard_map/ppermute | solution.py:40
  573.8 23.2 %copy-start.51 = (bf16[96,768]{1,0:T(8,128)(2,1)S(1)}, bf16[96,768]{1,0:T(8,128)(2,1)}, u32[]{:S(2)}) copy-start(bf16[96,768]{1,0:T(8,128)(2,1)} %get-tuple-element.264) | copy-start | bytes 442372
  573.8 25.9 %copy-start.50 = (bf16[96,768]{1,0:T(8,128)(2,1)S(1)}, bf16[96,768]{1,0:T(8,128)(2,1)}, u32[]{:S(2)}) copy-start(bf16[96,768]{1,0:T(8,128)(2,1)} %get-tuple-element.262) | copy-start | bytes 442372
  596.9 9.9 %collective-permute-start.40 = (bf16[96,768]{1,0:T(8,128)(2,1)S(1)}, bf16[96,768]{1,0:T(8,128)(2,1)S(1)}, u32[]{:S(2)}, u32[]{:S(2)}) collective-permute-start(bf16[96,768]{1,0:T(8,128)(2,1)S(1)} %copy-done.51), channel_id=1, source_target_pairs={{0,16},{4,20},{8,24},{12,28},{16,0},{20,4},{24,8},{28,12},{1,17},{... | collective-permute-start | bytes 442376 | tf_op jit(solution)/shard_map/ppermute | solution.py:40
  599.7 8.1 %collective-permute-start.39 = (bf16[96,768]{1,0:T(8,128)(2,1)S(1)}, bf16[96,768]{1,0:T(8,128)(2,1)S(1)}, u32[]{:S(2)}, u32[]{:S(2)}) collective-permute-start(bf16[96,768]{1,0:T(8,128)(2,1)S(1)} %copy-done.50), channel_id=1, source_target_pairs={{0,8},{4,12},{8,0},{12,4},{16,24},{20,28},{24,16},{28,20},{1,9},{5... | collective-permute-start | bytes 442376 | tf_op jit(solution)/shard_map/ppermute | solution.py:40
  611.5 13.8 %collective-permute-start.33 = (bf16[96,768]{1,0:T(8,128)(2,1)}, bf16[96,768]{1,0:T(8,128)(2,1)S(1)}, u32[]{:S(2)}, u32[]{:S(2)}) collective-permute-start(bf16[96,768]{1,0:T(8,128)(2,1)} %get-tuple-element.270), channel_id=1, source_target_pairs={{0,8},{4,12},{8,0},{12,4},{16,24},{20,28},{24,16},{28,20},{1,9},{5... | collective-permute-start | bytes 442376 | tf_op jit(solution)/shard_map/ppermute | solution.py:40
  611.5 13.8 %collective-permute-start.34 = (bf16[96,768]{1,0:T(8,128)(2,1)}, bf16[96,768]{1,0:T(8,128)(2,1)S(1)}, u32[]{:S(2)}, u32[]{:S(2)}) collective-permute-start(bf16[96,768]{1,0:T(8,128)(2,1)} %get-tuple-element.269), channel_id=1, source_target_pairs={{0,16},{4,20},{8,24},{12,28},{16,0},{20,4},{24,8},{28,12},{1,17},{... | collective-permute-start | bytes 442376 | tf_op jit(solution)/shard_map/ppermute | solution.py:40
  613.3 12.0 %collective-permute-start.35 = (bf16[96,768]{1,0:T(8,128)(2,1)}, bf16[96,768]{1,0:T(8,128)(2,1)}, u32[]{:S(2)}, u32[]{:S(2)}) collective-permute-start(bf16[96,768]{1,0:T(8,128)(2,1)} %get-tuple-element.268), channel_id=1, source_target_pairs={{0,24},{4,28},{8,16},{12,20},{16,8},{20,12},{24,0},{28,4},{1,25},{... | collective-permute-start | bytes 442376 | tf_op jit(solution)/shard_map/ppermute | solution.py:40
  (67 other events, 368.6 us)
Sparse Core Ops, SparseCore 0:
  12.2 69.7 all-gather.1
  151.4 13.4 sort.11.cloned.1.call-done
  (1 shorter events, 0.0 us)
